TPU v7x, 32 devices: a whole 2x2x4 slice. The times are simulated.
32 devices in a mesh: dp: 8 (over y, x, core), mp: 4 (over z).
Axes of the slice: x: 2, y: 2, z: 4, core: 2. Of those that a mesh axis runs over, the one named last changes fastest.
Arguments:
- tokens: bfloat16 [16384, 768], P('dp'), may hold values from -6 to 6
- segment_ids: int32 [32, 512], P('dp'), may hold values from 0 to 3, never falling along the last dimension, each value on 1 to 256 neighbouring positions
- pad_mask: int32 [32, 512], P('dp'), may hold values 0 or 1
- top_index: int32 [32, 32, 32], P('dp'), may hold values from 0 to 511
- query_emb: bfloat16 [32, 32, 128], P('dp'), may hold values from -6 to 6
- score_cot: float32 [32, 32, 32], P('dp'), may hold values from -6 to 6
- gain_attn: bfloat16 [768], replicated, may hold values from 0.25 to 1.75
- w_query: bfloat16 [768, 768], P(None, 'mp'), may hold values from -0.02734375 to 0.02734375
- w_key: bfloat16 [768, 768], P(None, 'mp'), may hold values from -0.21875 to 0.21875
- w_value: bfloat16 [768, 768], P(None, 'mp'), may hold values from -0.21875 to 0.21875
- w_out: bfloat16 [768, 768], P('mp'), may hold values from -1.75 to 1.75
- rel_table: bfloat16 [32, 12], P(None, 'mp'), may hold values from -4 to 4
- gain_ffn: bfloat16 [768], replicated, may hold values from 0.25 to 1.75
- w_gate: bfloat16 [768, 3072], P(None, 'mp'), may hold values from -0.21875 to 0.21875
- w_up: bfloat16 [768, 3072], P(None, 'mp'), may hold values from -0.21875 to 0.21875
- w_down: bfloat16 [3072, 768], P('mp'), may hold values from -0.109375 to 0.109375
- gain_final: bfloat16 [768], replicated, may hold values from 0.25 to 1.75
- w_proj: bfloat16 [768, 128], replicated, may hold values from -0.21875 to 0.21875
Outputs:
- scores: float32 [32, 32, 32], P('dp')
- input_grad: float32 [16384, 768], P('dp')
- grad_gain_attn: float32 [768], replicated
- grad_w_query: float32 [768, 768], P(None, 'mp')
- grad_w_key: float32 [768, 768], P(None, 'mp')
- grad_w_value: float32 [768, 768], P(None, 'mp')
- grad_w_out: float32 [768, 768], P('mp')
- grad_rel_table: float32 [32, 12], P(None, 'mp')
- grad_gain_ffn: float32 [768], replicated
- grad_w_gate: float32 [768, 3072], P(None, 'mp')
- grad_w_up: float32 [768, 3072], P(None, 'mp')
- grad_w_down: float32 [3072, 768], P('mp')
- grad_gain_final: float32 [768], replicated
- grad_w_proj: float32 [768, 128], replicated
Inputs may be any that keep to these rules, and one draw needn't show every extreme that they name: `segment_ids`: within each row the ids never fall; each id covers 1 to 256 positions, one exactly 256.
All inputs are finite; a program needn't handle non-finite values. No bound on the sum of `pad_mask` on one device may be relied on, other than what follows from the above.
Results may differ from a plain program's by a relative error of at most 0.023.
Values may be sent and summed in bfloat16 or wider, within the bound.
No kernel may reach another device: no remote copies, remote signals or barrier semaphores. Data moves between devices by JAX's collectives and lax.ppermute only.
A program may use at most 128 MiB of HBM per device.

v0:
```python
import jax
import jax.numpy as jnp
from jax import lax
from jax.sharding import PartitionSpec as P

highest = lax.Precision.HIGHEST
masked_logit = -1e30


def bucket_onehot(length, buckets):
    places = jnp.arange(length, dtype=jnp.int32)
    offset = places[None, :] - places[:, None]
    distance = jnp.abs(offset)
    far_bucket = 8 + sum(
        ((distance >= threshold).astype(jnp.int32) for threshold in (12, 16, 23, 32, 46, 64, 91))
    )
    bucket = jnp.where(distance < 8, distance, far_bucket) + 16 * (offset > 0).astype(jnp.int32)
    return (bucket.reshape(-1, 1) == jnp.arange(buckets, dtype=jnp.int32)[None, :]).astype(
        jnp.float32
    )


def rms_norm(values, gain):
    scale = lax.rsqrt(jnp.mean(values * values, axis=-1, keepdims=True) + 1e-06)
    return values * scale * gain


def rms_back(values, gain, grad_out):
    scale = lax.rsqrt(jnp.mean(values * values, axis=-1, keepdims=True) + 1e-06)
    weighted = grad_out * gain
    grad_gain = jnp.sum(grad_out * values * scale, axis=0)
    grad_values = scale * weighted - values * (scale * scale * scale) * jnp.mean(
        weighted * values, axis=-1, keepdims=True
    )
    return (grad_values, grad_gain)


def left_product(left, right):
    return jnp.einsum("ta,tb->ab", left, right, preferred_element_type=jnp.float32)


def back_product(grad, weight):
    return jnp.einsum("tb,ab->ta", grad, weight, preferred_element_type=jnp.float32)


def row_logits(query_row, key_row, mask_row, bias):
    logits = (
        jnp.einsum("qhd,khd->hqk", query_row, key_row, preferred_element_type=jnp.float32) + bias
    )
    return jnp.where(mask_row[None], logits, masked_logit)


def local(
    tokens,
    segment_ids,
    pad_mask,
    top_index,
    query_emb,
    score_cot,
    gain_attn,
    w_query,
    w_key,
    w_value,
    w_out,
    rel_table,
    gain_ffn,
    w_gate,
    w_up,
    w_down,
    gain_final,
    w_proj,
):
    row_count, length = segment_ids.shape
    heads = rel_table.shape[1]
    head_size = w_query.shape[1] // heads
    embed_width = w_proj.shape[1]
    picks_count = top_index.shape[1] * top_index.shape[2]
    inputs = tokens.astype(jnp.float32)
    attn_gain = gain_attn.astype(jnp.float32)
    ffn_gain = gain_ffn.astype(jnp.float32)
    final_gain = gain_final.astype(jnp.float32)
    bucket_hot = bucket_onehot(length, rel_table.shape[0])
    bias = (
        jnp.dot(bucket_hot, rel_table.astype(jnp.float32), precision=highest)
        .reshape(length, length, heads)
        .transpose(2, 0, 1)
    )
    allowed = (segment_ids[:, :, None] == segment_ids[:, None, :]) & (
        (pad_mask[:, None, :] == 1) | jnp.eye(length, dtype=bool)[None]
    )
    normed_attn = rms_norm(inputs, attn_gain).astype(jnp.bfloat16)

    def project(weight):
        return (
            jnp.dot(normed_attn, weight, preferred_element_type=jnp.float32)
            .astype(jnp.bfloat16)
            .reshape(row_count, length, heads, head_size)
        )

    query = project(w_query)
    keys = project(w_key)
    values = project(w_value)

    def forward_row(items):
        query_row, key_row, value_row, mask_row = items
        logits = row_logits(query_row, key_row, mask_row, bias)
        largest = jnp.max(logits, axis=-1, keepdims=True)
        log_total = largest + jnp.log(jnp.sum(jnp.exp(logits - largest), axis=-1, keepdims=True))
        probs = jnp.exp(logits - log_total)
        mixed_row = jnp.einsum(
            "hqk,khd->qhd",
            probs.astype(jnp.bfloat16),
            value_row,
            preferred_element_type=jnp.float32,
        )
        return (mixed_row.astype(jnp.bfloat16), log_total)

    mixed, log_totals = lax.map(forward_row, (query, keys, values, allowed))
    mixed_flat = mixed.reshape(row_count * length, heads * head_size)
    attn_term = jnp.dot(mixed_flat, w_out, preferred_element_type=jnp.float32).astype(jnp.bfloat16)
    hidden_attn = inputs + lax.psum(attn_term, "mp").astype(jnp.float32)
    normed_ffn = rms_norm(hidden_attn, ffn_gain).astype(jnp.bfloat16)
    gate = jnp.dot(normed_ffn, w_gate, preferred_element_type=jnp.float32)
    up_proj = jnp.dot(normed_ffn, w_up, preferred_element_type=jnp.float32)
    inner = (jax.nn.gelu(gate, approximate=True) * up_proj).astype(jnp.bfloat16)
    ffn_term = jnp.dot(inner, w_down, preferred_element_type=jnp.float32).astype(jnp.bfloat16)
    hidden_ffn = hidden_attn + lax.psum(ffn_term, "mp").astype(jnp.float32)
    normed_final = rms_norm(hidden_ffn, final_gain).astype(jnp.bfloat16)
    embed = jnp.dot(normed_final, w_proj, preferred_element_type=jnp.float32)
    inverse = lax.rsqrt(jnp.sum(embed * embed, axis=-1, keepdims=True) + 1e-06)
    padding = pad_mask.reshape(-1, 1).astype(jnp.float32)
    unit = (embed * inverse * padding).astype(jnp.bfloat16).reshape(row_count, length, embed_width)
    picks = top_index.reshape(row_count, picks_count)
    pick_hot = (picks[:, :, None] == jnp.arange(length, dtype=jnp.int32)[None, None, :]).astype(
        jnp.bfloat16
    )
    chosen = jnp.einsum("rps,rse->rpe", pick_hot, unit, preferred_element_type=jnp.float32)
    queries = query_emb.astype(jnp.float32)
    chosen = chosen.reshape(query_emb.shape[0], query_emb.shape[1], top_index.shape[2], embed_width)
    result = jnp.sum(chosen * queries[:, :, None, :], axis=-1)
    grad_chosen = (
        (score_cot[:, :, :, None] * queries[:, :, None, :])
        .astype(jnp.bfloat16)
        .reshape(row_count, picks_count, embed_width)
    )
    grad_unit = (
        jnp.einsum(
            "rps,rpe->rse", pick_hot, grad_chosen, preferred_element_type=jnp.float32
        ).reshape(-1, embed_width)
        * padding
    )
    grad_embed = inverse * grad_unit - embed * (inverse * inverse * inverse) * jnp.sum(
        grad_unit * embed, axis=-1, keepdims=True
    )
    grad_embed = grad_embed.astype(jnp.bfloat16)
    grad_proj = left_product(normed_final, grad_embed)
    grad_normed_final = back_product(grad_embed, w_proj)
    grad_hidden_ffn, grad_gfinal = rms_back(hidden_ffn, final_gain, grad_normed_final)
    grad_ffn_term = grad_hidden_ffn.astype(jnp.bfloat16)
    grad_down = left_product(inner, grad_ffn_term)
    grad_inner = back_product(grad_ffn_term, w_down)
    unused, gelu_pull = jax.vjp(
        lambda gate_in, up_in: jax.nn.gelu(gate_in, approximate=True) * up_in, gate, up_proj
    )
    grad_gate_full, grad_up_full = gelu_pull(grad_inner)
    grad_gate_low = grad_gate_full.astype(jnp.bfloat16)
    grad_up_low = grad_up_full.astype(jnp.bfloat16)
    grad_gate = left_product(normed_ffn, grad_gate_low)
    grad_up = left_product(normed_ffn, grad_up_low)
    grad_normed_ffn = back_product(grad_gate_low, w_gate) + back_product(grad_up_low, w_up)
    grad_normed_ffn = lax.psum(grad_normed_ffn.astype(jnp.bfloat16), "mp").astype(jnp.float32)
    grad_from_ffn, grad_gffn = rms_back(hidden_attn, ffn_gain, grad_normed_ffn)
    grad_hidden_attn = grad_hidden_ffn + grad_from_ffn
    grad_attn_term = grad_hidden_attn.astype(jnp.bfloat16)
    grad_wout = left_product(mixed_flat, grad_attn_term)
    grad_mixed = (
        back_product(grad_attn_term, w_out)
        .astype(jnp.bfloat16)
        .reshape(row_count, length, heads, head_size)
    )

    def backward_row(logit_sum, items):
        query_row, key_row, value_row, mask_row, total_row, grad_row = items
        probs = jnp.exp(row_logits(query_row, key_row, mask_row, bias) - total_row)
        grad_probs = jnp.einsum(
            "qhd,khd->hqk", grad_row, value_row, preferred_element_type=jnp.float32
        )
        grad_value_row = jnp.einsum(
            "hqk,qhd->khd", probs.astype(jnp.bfloat16), grad_row, preferred_element_type=jnp.float32
        )
        grad_logits = probs * (grad_probs - jnp.sum(grad_probs * probs, axis=-1, keepdims=True))
        logits_low = grad_logits.astype(jnp.bfloat16)
        grad_query_row = jnp.einsum(
            "hqk,khd->qhd", logits_low, key_row, preferred_element_type=jnp.float32
        )
        grad_key_row = jnp.einsum(
            "hqk,qhd->khd", logits_low, query_row, preferred_element_type=jnp.float32
        )
        return (
            logit_sum + grad_logits,
            (
                grad_query_row.astype(jnp.bfloat16),
                grad_key_row.astype(jnp.bfloat16),
                grad_value_row.astype(jnp.bfloat16),
            ),
        )

    logit_start = jnp.zeros((heads, length, length), jnp.float32)
    logit_sum, (grad_query, grad_keys, grad_values) = lax.scan(
        backward_row, logit_start, (query, keys, values, allowed, log_totals, grad_mixed)
    )
    grad_table = jnp.dot(logit_sum.reshape(heads, length * length), bucket_hot, precision=highest).T
    flat_shape = (row_count * length, heads * head_size)
    grad_query = grad_query.reshape(flat_shape)
    grad_keys = grad_keys.reshape(flat_shape)
    grad_values = grad_values.reshape(flat_shape)
    grad_wquery = left_product(normed_attn, grad_query)
    grad_wkey = left_product(normed_attn, grad_keys)
    grad_wvalue = left_product(normed_attn, grad_values)
    grad_normed_attn = (
        back_product(grad_query, w_query)
        + back_product(grad_keys, w_key)
        + back_product(grad_values, w_value)
    )
    grad_normed_attn = lax.psum(grad_normed_attn.astype(jnp.bfloat16), "mp").astype(jnp.float32)
    grad_from_attn, grad_gattn = rms_back(inputs, attn_gain, grad_normed_attn)
    input_grad = grad_hidden_attn + grad_from_attn
    (
        grad_gattn,
        grad_wquery,
        grad_wkey,
        grad_wvalue,
        grad_wout,
        grad_table,
        grad_gffn,
        grad_gate,
        grad_up,
        grad_down,
        grad_gfinal,
        grad_proj,
    ) = lax.psum(
        (
            grad_gattn,
            grad_wquery,
            grad_wkey,
            grad_wvalue,
            grad_wout,
            grad_table,
            grad_gffn,
            grad_gate,
            grad_up,
            grad_down,
            grad_gfinal,
            grad_proj,
        ),
        "dp",
    )
    return (
        result,
        input_grad,
        grad_gattn,
        grad_wquery,
        grad_wkey,
        grad_wvalue,
        grad_wout,
        grad_table,
        grad_gffn,
        grad_gate,
        grad_up,
        grad_down,
        grad_gfinal,
        grad_proj,
    )


def solution(mesh):
    return jax.shard_map(
        local,
        mesh=mesh,
        in_specs=(
            P("dp", None),
            P("dp", None),
            P("dp", None),
            P("dp", None, None),
            P("dp", None, None),
            P("dp", None, None),
            P(),
            P(None, "mp"),
            P(None, "mp"),
            P(None, "mp"),
            P("mp", None),
            P(None, "mp"),
            P(),
            P(None, "mp"),
            P(None, "mp"),
            P("mp", None),
            P(),
            P(),
        ),
        out_specs=(
            P("dp", None, None),
            P("dp", None),
            P(),
            P(None, "mp"),
            P(None, "mp"),
            P(None, "mp"),
            P("mp", None),
            P(None, "mp"),
            P(),
            P(None, "mp"),
            P(None, "mp"),
            P("mp", None),
            P(),
            P(),
        ),
        check_vma=False,
    )
```

profile of v0, /device:TPU:0, one launch (start us, length us, event | category | flops | bytes accessed | tf_op | source)
XLA Modules:
  0.0 867.2 jit_solution(17086425817584775725)
XLA Ops:
  9.7 2.7 fusion.72
  20.1 3.1 convolution_convert_fusion.6
  23.9 3.1 convolution_convert_fusion.7
  32.1 5.3 fusion.50
  37.4 2.6 copy.104
  40.1 3.6 copy.72
  43.7 3.4 or_and_fusion
  48.0 23.9 %while.29 = (s32[]{:T(128)}, bf16[4,512,3,64]{1,3,2,0:T(8,128)(2,1)}, f32[4,3,512,1]{2,1,3,0:T(4,128)}, bf16[4,512,3,64]{1,3,2,0:T(8,128)(2,1)S(1)}, pred[4,512,...) while((s32[]{:T(128)}, ...), condition=%wide.region_4.5_spmd, body=%wide.region_1.4_spmd.sunk | while | flops 206928384 | bytes 14211181 | solution.py:118
  49.0 2.7 fusion.167
  54.9 2.7 fusion.167
  60.9 2.7 fusion.167
  66.9 2.7 fusion.167
  74.8 2.7 convolution_convert_fusion.3
  78.2 123.3 %all-reduce.8.cloned.1.call-done = bf16[2048,768]{1,0:T(8,128)(2,1)} async-done(((bf16[2048,768]{1,0:T(8,128)(2,1)}), bf16[2048,768]{1,0:T(8,128)(2,1)}) %all-reduce.8.cloned.1.call-update) | async-done | bytes 3145744 | tf_op jit(solution)/shard_map/psum | solution.py:121
  201.5 4.1 multiply_reduce_fusion.4
  207.7 2.6 fusion.92
  210.4 5.3 multiply_convert_fusion.2
  217.3 4.0 convolution_convert_fusion.2
  227.9 3.8 fusion.53
  231.7 109.8 %all-reduce.10.cloned.1.call-done = bf16[2048,768]{1,0:T(8,128)(2,1)} async-done(((bf16[2048,768]{1,0:T(8,128)(2,1)}), bf16[2048,768]{1,0:T(8,128)(2,1)}) %all-reduce.10.cloned.1.call-update) | async-done | bytes 3145744 | tf_op jit(solution)/shard_map/psum | solution.py:127
  341.5 5.4 multiply_reduce_fusion.3
  353.7 3.3 multiply_reduce_fusion.1
  359.6 11.8 %multiply_convert_fusion = (bf16[2048,768]{1,0:T(8,128)(2,1)S(1)}, bf16[2048,768]{1,0:T(8,128)(2,1)S(1)}) fusion(f32[2048,768]{1,0:T(8,128)} %copy-done.67, f32[2048,768]{1,0:T(8,128)} %get-tuple-element.308, bf16[768,768]{1,0:T(8,128)(2,1)S(1)} %copy-done, f32[2048,768]{1,0:T(8,128)S(1)} %multiply_subtract_fusion), kind=kOutput, calls=%fused_computation.103 | convolution fusion | flops 2455240704 | bytes 26345472 | tf_op jit(solution)/shard_map/tb,ab->ta/dot_general | solution.py:43
  371.5 2.7 fusion.93
  374.2 4.1 add_convert_fusion.1
  378.4 6.9 fusion.97
  385.3 113.2 %all-reduce.12.cloned.1.call-done = bf16[2048,768]{1,0:T(8,128)(2,1)} async-done(((bf16[2048,768]{1,0:T(8,128)(2,1)}), bf16[2048,768]{1,0:T(8,128)(2,1)}) %all-reduce.12.cloned.1.call-update) | async-done | bytes 3145744 | tf_op jit(solution)/shard_map/psum | solution.py:171
  498.6 6.4 fusion.64
  505.1 4.9 fusion.61
  510.0 2.7 copy-done.11
  519.5 49.3 %while.30 = (s32[]{:T(128)}, f32[3,512,512]{1,2,0:T(8,128)}, bf16[4,512,3,64]{1,3,2,0:T(8,128)(2,1)}, bf16[4,512,3,64]{1,3,2,0:T(8,128)(2,1)}, bf16[4,512,3,64]{...) while((s32[]{:T(128)}, f32[3,512,512]{1,2,0:T(8,128)}, ...), condition=%wide.region_17.18_spmd.clone, body=%wide.region_15.17_spmd.clone.sunk | while | flops 512260608 | bytes 60986580 | solution.py:209
  521.2 2.8 subtract_exponential_fusion.2
  533.4 2.8 subtract_exponential_fusion.2
  545.7 2.9 subtract_exponential_fusion.2
  558.0 2.9 subtract_exponential_fusion.2
  574.7 2.8 add_convert_fusion
  578.6 3.8 fusion.98
  582.4 7.1 fusion.96
  589.5 4.2 fusion.84
  603.8 3.5 multiply_reduce_fusion.5
  608.0 3.6 copy.87
  611.5 4.2 copy.102
  615.8 15.9 %fusion.49 = f32[32,3]{0,1:T(4,128)S(1)} fusion(f32[3,262144]{1,0:T(4,128)S(1)} %bitcast.227, s32[262144]{0:T(1024)S(1)} %copy-done.36), kind=kOutput, calls=%fused_computation.58 | convolution fusion | flops 310378496 | bytes 4194688 | tf_op jit(solution)/shard_map/dot_general | solution.py:212
  631.7 66.1 %all-reduce.14.cloned.1.call-done = bf16[2048,768]{1,0:T(8,128)(2,1)} async-done(((bf16[2048,768]{1,0:T(8,128)(2,1)}), bf16[2048,768]{1,0:T(8,128)(2,1)}) %all-reduce.14.cloned.1.call-update) | async-done | bytes 3145744 | tf_op jit(solution)/shard_map/psum | solution.py:225
  697.8 4.9 fusion.78
  702.7 25.9 %all-reduce = (f32[768]{0:T(1024)}, f32[32,3]{0,1:T(4,128)}, f32[768]{0:T(1024)}, f32[768]{0:T(1024)}) all-reduce(f32[768]{0:T(1024)S(1)} %get-tuple-element.231, f32[32,3]{0,1:T(4,128)S(1)} %fusion.49, f32[768]{0:T(1024)S(1)} %get-tuple-element.229, f32[768]{0:T(1024)S(1)} %copy-done.58), channel_id=1, replica_groups=mesh['dp'=8,'mp'=4] {'dp'}, use_global_device_ids=true, to_apply=%region_21.22 | all-reduce | flops 2400 | bytes 19200 | tf_op jit(solution)/shard_map/psum | solution.py:241
  728.6 9.1 %fusion.59 = f32[2048,768]{1,0:T(8,128)} fusion(f32[2048,768]{1,0:T(8,128)} %copy-done.11, bf16[2048,768]{1,0:T(8,128)(2,1)} %all-reduce.14.cloned.1.call-done, bf16[2048,768]{1,0:T(8,128)(2,1)} %param.22, f32[2048]{0:T(1024)S(1)} %broadcast_multiply_fusion, f32[2048]{0:T(1024)S(1)} %copy-done.54, f32[768]{0:T(1024)S(1)} %copy-done.51, f32[2048]{0:T(1024)S(1)} %copy-done.47), kind=kLoop, calls=%fused_computation.80 | loop fusion | flops 12582912 | bytes 18902016 | tf_op jit(solution)/shard_map/add | solution.py:227
  737.6 110.0 %all-reduce.16.cloned.1.call-done = (f32[768,192]{0,1:T(8,128)}, f32[768,192]{0,1:T(8,128)}, f32[768,192]{0,1:T(8,128)}, f32[192,768]{1,0:T(8,128)}, f32[768,768...) async-done(((f32[768,192]{0,1:T(8,128)}, f32[768,192]{0,1:T(8,128)}, f32[768,192]{0,1:T(8,128)}, f32[192,768]{1,0:T(8,128)}, ...) | async-done | bytes 9830416 | tf_op jit(solution)/shard_map/psum | solution.py:241
  (279 shorter events, 128.4 us)
Async XLA Ops:
  7.2 210.1 %copy-start = (bf16[768,768]{1,0:T(8,128)(2,1)S(1)}, bf16[768,768]{1,0:T(8,128)(2,1)}, u32[]{:S(2)}) copy-start(bf16[768,768]{1,0:T(8,128)(2,1)} %param.37) | copy-start | bytes 3538948
  7.2 194.3 %all-reduce.8.cloned.1.call-start = ((), (), s32[]{:S(2)}) async-start(), calls=%async_computation | async-start | bytes 6291456 | tf_op jit(solution)/shard_map/psum | solution.py:121
  9.7 5.8 copy-start.50
  9.7 5.8 copy-start.2
  13.0 3.3 copy-start.46
  27.0 5.1 copy-start.64
  32.1 5.3 copy-start.35
  40.1 3.6 copy-start.56
  71.9 2.9 copy-start.33
  77.5 264.0 %all-reduce.10.cloned.1.call-start = ((), (), s32[]{:S(2)}) async-start(), calls=%async_computation.1 | async-start | bytes 6291456 | tf_op jit(solution)/shard_map/psum | solution.py:127
  78.2 128.0 %copy-start.48 = (f32[768]{0:T(1024)}, f32[768]{0:T(1024)S(1)}, u32[]{:S(2)}) copy-start(f32[768]{0:T(1024)S(1)} %convert_element_type.211) | copy-start | bytes 9220
  201.5 4.7 copy-start.3
  201.5 4.7 copy-start.6
  210.3 5.3 copy-start.67
  221.3 277.3 %all-reduce.12.cloned.1.call-start = ((), (), s32[]{:S(2)}) async-start(), calls=%async_computation.2 | async-start | bytes 6291456 | tf_op jit(solution)/shard_map/psum | solution.py:171
  341.5 5.4 copy-start.4
  341.5 5.6 copy-start.7
  341.5 6.5 copy-start.16
  341.5 6.5 copy-start.52
  353.7 3.3 copy-start.31
  359.6 11.8 %copy-start.12 = (f32[2048,768]{1,0:T(8,128)}, f32[2048,768]{1,0:T(8,128)S(1)}, u32[]{:S(2)}) copy-start(f32[2048,768]{1,0:T(8,128)S(1)} %multiply_subtract_fusion) | copy-start | bytes 18874372
  359.6 11.8 %copy-start.61 = (bf16[768,768]{1,0:T(8,128)(2,1)S(1)}, bf16[768,768]{1,0:T(8,128)(2,1)}, u32[]{:S(2)}) copy-start(bf16[768,768]{1,0:T(8,128)(2,1)} %param.35) | copy-start | bytes 3538948
  371.4 2.8 copy-start.66
  378.3 319.5 %all-reduce.14.cloned.1.call-start = ((), (), s32[]{:S(2)}) async-start(), calls=%async_computation.3 | async-start | bytes 6291456 | tf_op jit(solution)/shard_map/psum | solution.py:225
  378.4 120.2 %copy-start.49 = (f32[768]{0:T(1024)S(1)}, f32[768]{0:T(1024)}, u32[]{:S(2)}) copy-start(f32[768]{0:T(1024)} %copy-done.48) | copy-start | bytes 9220
  385.3 119.7 %copy-start.53 = (f32[2048]{0:T(1024)S(1)}, f32[2048]{0:T(1024)}, u32[]{:S(2)}) copy-start(f32[2048]{0:T(1024)} %get-tuple-element.301) | copy-start | bytes 24580
  498.5 6.4 copy-start.5
  498.5 6.4 copy-start.8
  498.5 6.5 copy-start.17
  505.1 7.6 copy-start.34
  541.3 2.8 copy-start.10
  553.6 2.8 copy-start.10
  568.9 2.9 copy-start.24
  577.6 270.1 %all-reduce.16.cloned.1.call-start = ((), (), s32[]{:S(2)}) async-start(), calls=%async_computation.4 | async-start | bytes 19660800 | tf_op jit(solution)/shard_map/psum | solution.py:241
  578.6 10.9 %slice-start.2 = ((s8[6291456]{0:T(1024)(128)(4,1)}), s8[4194304]{0:T(1024)(128)(4,1)S(1)}, s32[]{:S(2)}) async-start(s8[6291456]{0:T(1024)(128)(4,1)} %bitcast.213), calls=%async_computation.7 | async-start | bytes 8388608
  582.4 7.1 slice-start.3
  582.4 7.1 copy-start.27
  589.5 4.2 copy-start.14
  593.7 4.9 slice-start
  595.3 3.2 slice-start.1
  611.5 4.2 copy-start.36
  615.8 82.0 %copy-start.47 = (f32[2048]{0:T(1024)S(1)}, f32[2048]{0:T(1024)}, u32[]{:S(2)}) copy-start(f32[2048]{0:T(1024)} %copy-done.46) | copy-start | bytes 24580
  615.8 82.0 %copy-start.51 = (f32[768]{0:T(1024)S(1)}, f32[768]{0:T(1024)}, u32[]{:S(2)}) copy-start(f32[768]{0:T(1024)} %copy-done.50) | copy-start | bytes 9220
  631.7 71.0 %copy-start.58 = (f32[768]{0:T(1024)S(1)}, f32[768]{0:T(1024)}, u32[]{:S(2)}) copy-start(f32[768]{0:T(1024)} %get-tuple-element.227) | copy-start | bytes 9220
  631.7 96.9 %copy-start.54 = (f32[2048]{0:T(1024)S(1)}, f32[2048]{0:T(1024)}, u32[]{:S(2)}) copy-start(f32[2048]{0:T(1024)} %get-tuple-element.299) | copy-start | bytes 24580
  847.7 5.9 copy-start.37
  847.7 6.7 copy-start.30
  855.8 4.7 copy-start.1
  (35 other events, 64.1 us)
Sparse Core Ops, SparseCore 0:
  77.7 123.7 all-reduce.7
  221.4 120.0 all-reduce.9
  378.4 120.0 all-reduce.11
  577.7 120.0 all-reduce.13
  703.5 144.1 all-reduce.15
where the time goes:
time: 875 us; the launch traced here: 867 us
  waiting for transfers between devices  523 us (60%)
  matrix products  154 us (18%)
  local copies, waits for them, and re-layouts  80.8 us (9%)
  other arithmetic  68.3 us (8%)
  blocking collectives  25.9 us (3%)
  between operations  14.8 us (2%)
    psum x1, waiting for transfers between devices, local(): hidden_attn = inputs + lax.psum(attn_term, 'mp').astype(jnp.float32)  123 us
    psum x1, waiting for transfers between devices, local(): lax.psum(grad_normed_ffn.astype(jnp.bfloat16), 'mp').astype(jnp.float32)  113 us
    psum x1, waiting for transfers between devices, local(): lax.psum((grad_gattn, grad_wquery, grad_wkey, grad_wvalue, grad_wout, gra...  110 us
    psum x1, waiting for transfers between devices, local(): hidden_ffn = hidden_attn + lax.psum(ffn_term, 'mp').astype(jnp.float32)  110 us
    psum x1, waiting for transfers between devices, local(): lax.psum(grad_normed_attn.astype(jnp.bfloat16), 'mp').astype(jnp.float32)  66.1 us
    unnamed x158, local copies, waits for them, and re-layouts  37.1 us
    dot_general x8, matrix products, left_product(): jnp.einsum('ta,tb->ab', left, right, preferred_element_type=jnp.float32)  28.5 us
    dot_general x8, matrix products, back_product(): jnp.einsum('tb,ab->ta', grad, weight, preferred_element_type=jnp.float32)  28 us
  transfers between devices with their start and end apart: 5, of which 5 were waited for; matrix products, arithmetic and copies ran while one was open for 9% of the time, Pallas kernels for 0%

commit v1 on v0

v1 whole, which is shorter than its diff:
```python
import functools
import math

import jax
import jax.numpy as jnp
import numpy as np
from jax import lax
from jax.experimental import pallas as pl
from jax.experimental.pallas import tpu as pltpu
from jax.sharding import Mesh
from jax.sharding import PartitionSpec as P

f32 = jnp.float32
bf16 = jnp.bfloat16
eps = 1e-06
masked_logit = -1e30
gelu_c = math.sqrt(2.0 / math.pi)
CORE, XBIT, YBIT = "core", "x", "y"
group = ("y", "x", "core")
dp = ("out",) + group
span = 1024
tile = 128


def bucket_hot(buckets, length):
    column = np.arange(span)
    base = length - tile
    offset = np.where(column < base + length, column - base, column - span - base)
    distance = np.abs(offset)
    far = 8 + sum((distance >= t).astype(np.int32) for t in (12, 16, 23, 32, 46, 64, 91))
    bucket = np.where(distance < 8, distance, far) + 16 * (offset > 0)
    hot = (bucket[None, :] == np.arange(tile)[:, None]) & (np.arange(tile)[:, None] < buckets)
    return hot.astype(np.float32)


def dot(a, b, dims=((1,), (0,))):
    return lax.dot_general(a, b, (dims, ((), ())), preferred_element_type=f32)


def rms_scale(v):
    return lax.rsqrt(jnp.mean(v * v, axis=-1, keepdims=True) + eps)


def rms_back(v, gain, grad):
    s = rms_scale(v)
    w = grad * gain
    value = s * w - v * ((s * s * s) * jnp.mean(w * v, axis=-1, keepdims=True))
    return value, jnp.sum(grad * v * s, axis=0, keepdims=True)


def params(mib):
    return pltpu.CompilerParams(
        vmem_limit_bytes=mib << 20, dimension_semantics=("arbitrary",)
    )


def whole(shape):
    return pl.BlockSpec(shape, lambda *_: (0,) * len(shape))


ANY = pl.BlockSpec(memory_space=pl.ANY)


class Place:
    def __init__(self):
        self.n_out, self.n_mp = lax.axis_size("out"), lax.axis_size("mp")
        self.c, self.x, self.y = (lax.axis_index(name) for name in ("core", "x", "y"))
        self.z = lax.axis_index("mp")
        self.p = self.c * 4 + self.y * 2 + self.x

    def swap(self, v, name):
        return lax.ppermute(v, name, [(0, 1), (1, 0)])

    def shift(self, v, k):
        n = self.n_mp
        return lax.ppermute(v, "mp", [(i, (i + k) % n) for i in range(n)])

    def offsets(self, rows):
        half = rows // 2
        out = []
        for flip in (0, 4):
            p = self.p ^ flip
            for other, extra in (
                (0, 0), (1, 0), (0, half), (2, half), (2, 0), (3, 0), (1, half), (3, half),
            ):
                out.append((p ^ other) * rows + extra)
        return jnp.stack(out + [self.z, self.c, self.x, self.y]).astype(jnp.int32)

    def first_round(self, a, b, after=()):
        return stack_pairs(a, self.swap(a, XBIT), b, self.swap(b, YBIT), after)

    def second_round(self, sa, sb):
        near = [sa, sb, self.swap(sa, YBIT), self.swap(sb, XBIT)]
        return near + [self.swap(t, CORE) for t in near]


def pick(v, axis, index):
    return lax.dynamic_index_in_dim(v, index, axis, keepdims=False)


def halves(v, axis):
    half = v.shape[axis] // 2
    return (
        lax.slice_in_dim(v, 0, half, axis=axis),
        lax.slice_in_dim(v, half, 2 * half, axis=axis),
    )


def chunk_copies(offs, own, arrays, dst, sems, first=0):
    slots, rows, width = dst.shape
    half = rows // 16
    pairs = [
        (ref, dst.at[0, :, pl.ds(column, ref.shape[1])]) for ref, column in own
    ]
    for at in range(16):
        src = arrays[at // 2].at[at % 2]
        if src.shape[2] != width:
            src = src.at[:, :, pl.ds(first, width)]
        start = pl.multiple_of(offs[at], 16)
        pairs.append((src, dst.at[pl.ds(1, slots - 1), pl.ds(start, half), :]))
    return [pltpu.make_async_copy(s, d, sems.at[i]) for i, (s, d) in enumerate(pairs)]


copies_per_chunk = 20


def gathered_copies(gathered, dst, sems, shard=None):
    full = gathered.shape[4]
    out = []
    for at, (c, y, x) in enumerate(np.ndindex(2, 2, 2)):
        rows = pl.ds(at * full, full)
        if shard is None:
            out.append((gathered.at[y, x, c], dst.at[:, rows, :]))
        else:
            out.append((gathered.at[y, x, c, shard], dst.at[rows, :]))
    return [pltpu.make_async_copy(s, d, sems.at[i]) for i, (s, d) in enumerate(out)]


def split_kernel(slots, *refs):
    a_ref, b_ref = refs[-2:]
    half = a_ref.shape[1]
    for k in range(slots):
        a_ref[k] = refs[k][:half, :]
        b_ref[k] = refs[k][half:, :]


def split(arrays, after=()):
    rows, width = arrays[0].shape
    out = (len(arrays), rows // 2, width)
    return pl.pallas_call(
        functools.partial(split_kernel, len(arrays)),
        grid=(1,),
        in_specs=[whole(arrays[0].shape)] * len(arrays) + [ANY] * len(after),
        out_specs=[whole(out)] * 2,
        out_shape=[jax.ShapeDtypeStruct(out, bf16)] * 2,
        compiler_params=params(16),
        name="split",
    )(*arrays, *after)


def skew(base):
    t = jnp.broadcast_to(base, (8, span))
    row = lax.broadcasted_iota(jnp.int32, (8, span), 0)
    for step in (1, 2, 4):
        t = jnp.where((row & step) != 0, pltpu.roll(t, step, 1), t)
    while t.shape[0] < tile:
        t = jnp.concatenate([t, pltpu.roll(t, t.shape[0], 1)], axis=0)
    return t


def unskew(t):
    while t.shape[0] > 8:
        n = t.shape[0] // 2
        t = t[:n] + pltpu.roll(t[n:], span - n, 1)
    row = lax.broadcasted_iota(jnp.int32, (8, span), 0)
    for step in (1, 2, 4):
        t = jnp.where((row & step) != 0, pltpu.roll(t, span - step, 1), t)
    return jnp.sum(t, axis=0, keepdims=True)


def fill_mask(mask, segs, pads, seg_cols, row):
    length = mask.shape[0]
    rows = segs.shape[0]
    chosen = lax.broadcasted_iota(jnp.int32, (rows, length), 0) == row
    seg_k = jnp.sum(jnp.where(chosen, segs, 0.0), axis=0, keepdims=True)
    pad_k = jnp.sum(jnp.where(chosen, pads, 0.0), axis=0, keepdims=True)
    code = jnp.where(pad_k == 1.0, seg_k, -1.0)
    lane = lax.broadcasted_iota(jnp.int32, seg_cols.shape, 1)
    seg_q = jnp.sum(jnp.where(lane == row, seg_cols, 0.0), axis=1, keepdims=True)
    q = lax.broadcasted_iota(jnp.int32, (tile, length), 0)
    k = lax.broadcasted_iota(jnp.int32, (tile, length), 1)
    for a in range(length // tile):
        own = seg_q[a * tile : (a + 1) * tile]
        ok = (own == code) | (q + a * tile == k)
        mask[a * tile : (a + 1) * tile, :] = jnp.where(ok, 0.0, masked_logit)


def fill_bias(bias, table, hot, heads):
    base = dot(table, hot[0 : table.shape[1], :])
    for h in range(heads):
        bias[h] = skew(base[h : h + 1, :])


def normalize(x_ref, gain, normed):
    for a in range(x_ref.shape[0] // tile):
        rows = slice(a * tile, (a + 1) * tile)
        v = x_ref[rows, :].astype(f32)
        normed[rows, :] = (v * rms_scale(v) * gain).astype(bf16)


def attend_kernel(
    first, heads, size, sc, x_ref, seg_ref, pad_ref, segc_ref, gain_ref, w_ref, hot_ref,
    out_ref, normed, qkv, mask, bias,
):
    length = x_ref.shape[0]
    wide = heads * size
    buckets = 32
    row = lax.rem(sc[16] + first + pl.program_id(0), seg_ref.shape[0])
    normalize(x_ref, gain_ref[...], normed)
    qkv[...] = dot(normed[...], w_ref[: 3 * wide, :], ((1,), (1,))).astype(bf16)
    fill_mask(mask, seg_ref[...], pad_ref[...], segc_ref[...], row)

    @pl.when(pl.program_id(0) == 0)
    def _():
        fill_bias(bias, w_ref[3 * wide : 3 * wide + 16, :tile][:, :buckets], hot_ref, heads)

    for h in range(heads):
        q_at, k_at, v_at = h * size, wide + h * size, 2 * wide + h * size
        keys = qkv[:, k_at : k_at + size]
        values = qkv[:, v_at : v_at + size]
        for a in range(length // tile):
            rows = slice(a * tile, (a + 1) * tile)
            at = length - tile - a * tile
            s = dot(qkv[rows, q_at : q_at + size], keys, ((1,), (1,)))
            s = s + bias[h, :, at : at + length] + mask[rows, :]
            e = jnp.exp(s - jnp.max(s, axis=1, keepdims=True))
            p = (e * (1.0 / jnp.sum(e, axis=1, keepdims=True))).astype(bf16)
            out_ref[0, rows, q_at : q_at + size] = dot(p, values).astype(bf16)
    out_ref[0, length:, :] = w_ref[3 * wide : 3 * wide + 16, :wide]


def attend(first, offs, tokens, segs, pads, seg_cols, gain, w_qkv, hot, heads, size):
    rows, length = segs.shape
    d = tokens.shape[1]
    wide = heads * size
    grid = pltpu.PrefetchScalarGridSpec(
        num_scalar_prefetch=1,
        grid=(rows,),
        in_specs=[
            pl.BlockSpec((length, d), lambda i, sc: (lax.rem(sc[16] + first + i, rows), 0)),
            whole(segs.shape),
            whole(pads.shape),
            whole(seg_cols.shape),
            whole(gain.shape),
            whole(w_qkv.shape),
            whole(hot.shape),
        ],
        out_specs=pl.BlockSpec((1, length + 16, wide), lambda i, sc: (i, 0, 0)),
        scratch_shapes=[
            pltpu.VMEM((length, d), bf16),
            pltpu.VMEM((length, 3 * wide), bf16),
            pltpu.VMEM((length, length), f32),
            pltpu.VMEM((heads, tile, span), f32),
        ],
    )
    return pl.pallas_call(
        functools.partial(attend_kernel, first, heads, size),
        grid_spec=grid,
        out_shape=jax.ShapeDtypeStruct((rows, length + 16, wide), bf16),
        compiler_params=params(24),
        cost_estimate=pl.CostEstimate(
            flops=rows * (2 * length * d * 3 * wide + 4 * wide * length * length),
            bytes_accessed=4 << 20,
            transcendentals=rows * heads * length * length,
        ),
        name="attend",
    )(offs, tokens, segs, pads, seg_cols, gain, w_qkv, hot)


def high_low(v):
    high = v.astype(bf16)
    return high, (v - high.astype(f32)).astype(bf16)


def attend_back_kernel(
    slot, last, heads, size, n_after, sc, x_ref, seg_ref, pad_ref, segc_ref, gain_ref, hot_ref,
    gm_ref, mixed_ref, *refs,
):
    refs = list(refs)
    acc_in = refs.pop(0) if slot else None
    if last:
        gha_ref, gat_ref, fin_ref, mid_ref, score_ref = refs[:5]
        tables, refs = refs[5 : 5 + slot], refs[5 + slot :]
    w_ref = refs[0]
    refs = refs[1 + n_after + (1 if slot else 0) :]
    left_ref, table_out = refs[:2]
    if last:
        dx_ref, both_ref, small_ref, acc = refs[2:6]
        refs = refs[6:]
    else:
        acc, refs = refs[2], refs[3:]
    w, sems, normed, qkv, mask, bias, probs, dlog, skewed, diag, dqkv = refs
    length, d = x_ref.shape
    wide = heads * size
    row = sc[16]
    gain = gain_ref[...]
    blocks = length // tile
    shard = lax.rem(row + 4 - slot, 4)
    copies = gathered_copies(w_ref, w, sems, shard)
    for copy in copies:
        copy.start()
    normalize(x_ref, gain, normed)
    fill_mask(mask, seg_ref[...], pad_ref[...], segc_ref[...], row)
    fill_bias(bias, mixed_ref[length:, :tile][:, :32], hot_ref, heads)
    diag[...] = jnp.zeros_like(diag)
    for copy in copies:
        copy.wait()
    qkv[...] = dot(normed[...], w[: 3 * wide, :], ((1,), (1,))).astype(bf16)
    for h in range(heads):
        q_at, k_at, v_at = h * size, wide + h * size, 2 * wide + h * size
        here = slice(q_at, q_at + size)
        query = qkv[:, q_at : q_at + size]
        keys = qkv[:, k_at : k_at + size]
        values = qkv[:, v_at : v_at + size]
        grad = gm_ref[0, :, here]
        skewed[...] = jnp.zeros_like(skewed)
        for a in range(blocks):
            rows = slice(a * tile, (a + 1) * tile)
            at = length - tile - a * tile
            s = dot(query[rows], keys, ((1,), (1,)))
            s = s + bias[h, :, at : at + length] + mask[rows, :]
            e = jnp.exp(s - jnp.max(s, axis=1, keepdims=True))
            p = e * (1.0 / jnp.sum(e, axis=1, keepdims=True))
            probs[rows, :] = p.astype(bf16)
            gp = dot(grad[rows], values, ((1,), (1,)))
            gl = p * (gp - jnp.sum(gp * p, axis=1, keepdims=True))
            dlog[rows, :] = gl.astype(bf16)
            skewed[:, at : at + length] += gl
        diag[h : h + 1, :] = unskew(skewed[...])
        for part, value in (
            (0, dot(dlog[...], keys)),
            (1, dot(dlog[...], query, ((0,), (0,)))),
            (2, dot(probs[...], grad, ((0,), (0,)))),
        ):
            value = value.astype(bf16)
            left_ref[0, part, :, here] = value
            dqkv[:, part * wide + q_at : part * wide + q_at + size] = value
    left_ref[0, 3] = mixed_ref[:length, :]
    high, low = high_low(diag[...])
    table = dot(high, hot_ref[...], ((1,), (1,))) + dot(low, hot_ref[...], ((1,), (1,)))
    table_out[...] = table
    value = dot(dqkv[...], w[: 3 * wide, :])
    acc[...] = value if acc_in is None else acc_in[...] + value
    if not last:
        return
    total = jnp.zeros((1, d), f32)
    for a in range(blocks):
        rows = slice(a * tile, (a + 1) * tile)
        back, part = rms_back(x_ref[rows, :].astype(f32), gain, acc[rows, :])
        dx_ref[rows, :] = (gha_ref[rows, :] + back).astype(bf16)
        total = total + part
    both_ref[0] = normed[...]
    both_ref[1] = gat_ref[...]
    dx_ref[length:, :] = jnp.zeros((dx_ref.shape[0] - length, d), bf16)
    n = score_ref.shape[0] // 16
    cols = score_ref.shape[1]
    high, low = high_low(score_ref[...])
    for i in range(n):
        rows = slice(16 * i, 16 * i + 16)
        dx_ref[length : length + 16, 2 * i * tile : 2 * i * tile + cols] = high[rows]
        dx_ref[length : length + 16, (2 * i + 1) * tile : (2 * i + 1) * tile + cols] = low[rows]
    line = lax.broadcasted_iota(jnp.int32, (8, d), 0)
    gains = jnp.where(
        line == 0, total, jnp.where(line == 1, fin_ref[...], jnp.where(line == 2, mid_ref[...], 0.0))
    )
    line = lax.broadcasted_iota(jnp.int32, (8, tile), 0)
    column = lax.broadcasted_iota(jnp.int32, (8, tile), 1)

    def turned(value, at):
        place = jnp.where(column == line + at, 1.0, 0.0).astype(bf16)
        high, low = high_low(value)
        return dot(high, place, ((0,), (0,))) + dot(low, place, ((0,), (0,)))

    gains = turned(gains, 0)
    for k, value in enumerate([t[...] for t in tables] + [table]):
        small_ref[k] = gains.astype(bf16)
        small_ref[k, 0:tile, :] = (gains[0:tile] + turned(value, tile // 2)).astype(bf16)


def attend_back(
    slot, common, grad_mixed, mixed, acc, left, finish, weights, heads, size, after=()
):
    offs, tokens, segs, pads, seg_cols, gain, hot = common
    rows, length = segs.shape
    d = tokens.shape[1]
    slots = grad_mixed.shape[0]
    wide = heads * size
    last = slot == slots - 1
    args = [offs, tokens, segs, pads, seg_cols, gain, hot, grad_mixed, mixed]
    specs = [
        pl.BlockSpec((length, d), lambda i, sc: (sc[16], 0)),
        whole(segs.shape),
        whole(pads.shape),
        whole(seg_cols.shape),
        whole(gain.shape),
        whole(hot.shape),
        pl.BlockSpec((1, length, wide), lambda i, sc: (slot, 0, 0)),
        whole(mixed.shape),
    ]
    if slot:
        args.append(acc)
        specs.append(whole(acc.shape))
    if last:
        args += finish
        specs += [whole(v.shape) for v in finish]
    args += [weights] + ([left] if slot else []) + list(after)
    specs += [ANY] * (1 + len(after) + (1 if slot else 0))
    out_specs = [
        pl.BlockSpec((1, 4, length, wide), lambda i, sc: (slot, 0, 0, 0)),
        whole((8, tile)),
    ]
    out_shape = [
        jax.ShapeDtypeStruct((slots, 4, length, wide), bf16),
        jax.ShapeDtypeStruct((8, tile), f32),
    ]
    scratch = []
    if last:
        for shape in ((length + 16, d), (2, length, d), (slots, d, tile)):
            out_specs.append(whole(shape))
            out_shape.append(jax.ShapeDtypeStruct(shape, bf16))
        scratch = [pltpu.VMEM((length, d), f32)]
    else:
        out_specs.append(whole((length, d)))
        out_shape.append(jax.ShapeDtypeStruct((length, d), f32))
    grid = pltpu.PrefetchScalarGridSpec(
        num_scalar_prefetch=1,
        grid=(1,),
        in_specs=specs,
        out_specs=out_specs,
        scratch_shapes=scratch
        + [
            pltpu.VMEM((8 * weights.shape[4], d), bf16),
            pltpu.SemaphoreType.DMA((8,)),
            pltpu.VMEM((length, d), bf16),
            pltpu.VMEM((length, 3 * wide), bf16),
            pltpu.VMEM((length, length), f32),
            pltpu.VMEM((heads, tile, span), f32),
            pltpu.VMEM((length, length), bf16),
            pltpu.VMEM((length, length), bf16),
            pltpu.VMEM((tile, span), f32),
            pltpu.VMEM((8, span), f32),
            pltpu.VMEM((length, 3 * wide), bf16),
        ],
    )
    return pl.pallas_call(
        functools.partial(attend_back_kernel, slot, last, heads, size, len(after)),
        grid_spec=grid,
        out_shape=out_shape,
        input_output_aliases={len(args) - len(after) - 1: 0} if slot else {},
        compiler_params=params(58),
        cost_estimate=pl.CostEstimate(
            flops=12 * length * d * wide + 14 * wide * length * length,
            bytes_accessed=16 << 20,
            transcendentals=heads * length * length,
        ),
        name=f"attend_back{slot}",
    )(*args)


def ffn_in_kernel(n_after, sc, x_ref, gain_ref, *refs):
    slots = 4
    mixed, own, arrays = refs[:slots], refs[slots : slots + 3], refs[slots + 3 : slots + 11]
    refs = refs[slots + 11 + n_after :]
    hid_ref, normed_ref, act_ref, dact_ref, inner_ref, w, sems = refs
    length, d = x_ref.shape
    slot = pl.program_id(0)
    hidden = act_ref.shape[2]
    copies = chunk_copies(sc, zip(own, (0, hidden, 2 * hidden)), arrays, w, sems)

    @pl.when(slot == 0)
    def _():
        for copy in copies:
            copy.start()
        for copy in copies:
            copy.wait()
        gain = gain_ref[...]
        for a in range(length // tile):
            rows = slice(a * tile, (a + 1) * tile)
            h = x_ref[rows, :].astype(f32)
            for k in range(slots):
                h = h + dot(mixed[k][rows, :], w[k, :, 2 * hidden :], ((1,), (1,)))
            hid_ref[rows, :] = h
            normed_ref[rows, :] = (h * rms_scale(h) * gain).astype(bf16)

    def step(n, carry):
        at = pl.multiple_of(n * 256, 256)
        cols = pl.ds(at, 256)
        normed = normed_ref[...]
        gate = dot(normed, w[slot, :, cols])
        up = dot(normed, w[slot, :, pl.ds(at + hidden, 256)])
        t = jnp.tanh(gelu_c * (gate + 0.044715 * gate * gate * gate))
        half = 0.5 * (1.0 + t)
        act = gate * half
        slope = half + 0.5 * gate * (1.0 - t * t) * (
            gelu_c * (1.0 + 3 * 0.044715 * gate * gate)
        )
        act_ref[0, :, cols] = act.astype(bf16)
        dact_ref[0, :, cols] = (up * slope).astype(bf16)
        inner_ref[0, :, cols] = (act * up).astype(bf16)
        return carry

    lax.fori_loop(0, hidden // 256, step, 0)


def ffn_in(offs, tokens, gain, mixed, own, arrays, length, after=()):
    d = tokens.shape[1]
    slots = len(mixed)
    hidden = own[0].shape[1]
    width = arrays[0].shape[3]
    per_slot = pl.BlockSpec((1, length, hidden), lambda i, sc: (i, 0, 0))
    grid = pltpu.PrefetchScalarGridSpec(
        num_scalar_prefetch=1,
        grid=(slots,),
        in_specs=[
            pl.BlockSpec((length, d), lambda i, sc: (sc[16], 0)),
            whole(gain.shape),
        ]
        + [whole(m.shape) for m in mixed]
        + [ANY] * (11 + len(after)),
        out_specs=[whole((length, d)), whole((length, d))] + [per_slot] * 3,
        scratch_shapes=[
            pltpu.VMEM((slots, d, width), bf16),
            pltpu.SemaphoreType.DMA((copies_per_chunk,)),
        ],
    )
    three = jax.ShapeDtypeStruct((slots, length, hidden), bf16)
    return pl.pallas_call(
        functools.partial(ffn_in_kernel, len(after)),
        grid_spec=grid,
        out_shape=[
            jax.ShapeDtypeStruct((length, d), f32),
            jax.ShapeDtypeStruct((length, d), bf16),
            three,
            three,
            three,
        ],
        compiler_params=params(58),
        cost_estimate=pl.CostEstimate(
            flops=2 * length * d * (d + 2 * slots * hidden),
            bytes_accessed=24 << 20,
            transcendentals=slots * length * hidden,
        ),
        name="ffn_in",
    )(offs, tokens, gain, *mixed, *own, *arrays, *after)


def middle_kernel(
    sc, hid_ref, inner_ref, act_ref, dact_ref, gfin_ref, gffn_ref, wp_ref, padc_ref, query_ref,
    cot_ref, top_ref, *refs,
):
    slots = 4
    own, first, second = refs[:3], refs[3:11], refs[11]
    (
        score_ref, nfin, ge, gain_fin_ref, gain_ffn_ref, gft_ref, gg_ref, gu_ref, gha_ref,
        gat_ref, gm_ref,
    ) = refs[12:23]
    w, wd, w_sems, d_sems, acc, embed, unit = refs[23:]
    length, d = hid_ref.shape
    hidden = wd.shape[1]
    step = pl.program_id(0)
    w_copies = chunk_copies(sc, zip(own, (0, hidden, 2 * hidden)), first, w, w_sems)
    d_copies = gathered_copies(second, wd, d_sems)

    def shard(k):
        return lax.rem(sc[16] + slots - k, slots)

    blocks = length // tile

    @pl.when(step == 0)
    def _():
        for copy in d_copies + w_copies:
            copy.start()
        acc[...] = hid_ref[...]
        for copy in d_copies:
            copy.wait()

    @pl.when(step < slots)
    def _():
        acc[...] += dot(inner_ref[0], wd[shard(step)])

    @pl.when(step == slots - 1)
    def _():
        lane = lax.broadcasted_iota(jnp.int32, padc_ref.shape, 1)
        pad = jnp.sum(jnp.where(lane == sc[16], padc_ref[...], 0.0), axis=1, keepdims=True)
        gain = gfin_ref[...]
        for a in range(blocks):
            rows = slice(a * tile, (a + 1) * tile)
            h = acc[rows, :]
            n = (h * rms_scale(h) * gain).astype(bf16)
            nfin[rows, :] = n
            e = dot(n, wp_ref[...])
            embed[rows, :] = e
            inverse = lax.rsqrt(jnp.sum(e * e, axis=1, keepdims=True) + eps)
            unit[rows, :] = (e * inverse * pad[rows]).astype(bf16)
        query = query_ref[0]
        cot = cot_ref[0]
        top = top_ref[0]
        scored = dot(query, unit[...], ((1,), (1,)))
        place = lax.broadcasted_iota(jnp.int32, scored.shape, 1)
        out_lane = lax.broadcasted_iota(jnp.int32, cot.shape, 1)
        chosen = jnp.zeros_like(cot)
        weight = jnp.zeros_like(scored)
        for j in range(top.shape[1]):
            here = place == top[:, j : j + 1]
            mine = jnp.sum(jnp.where(here, scored, 0.0), axis=1, keepdims=True)
            chosen = jnp.where(out_lane == j, mine, chosen)
            weight = weight + jnp.where(here, cot[:, j : j + 1], 0.0)
        score_ref[...] = chosen
        high = weight.astype(bf16)
        low = (weight - high.astype(f32)).astype(bf16)
        gunit = dot(high, query, ((0,), (0,))) + dot(low, query, ((0,), (0,)))
        total = jnp.zeros((1, d), f32)
        for a in range(blocks):
            rows = slice(a * tile, (a + 1) * tile)
            e = embed[rows, :]
            inverse = lax.rsqrt(jnp.sum(e * e, axis=1, keepdims=True) + eps)
            u = gunit[rows] * pad[rows]
            cube = (inverse * inverse * inverse) * jnp.sum(u * e, axis=1, keepdims=True)
            g = (inverse * u - e * cube).astype(bf16)
            ge[rows, :] = g
            back, part = rms_back(acc[rows, :], gain, dot(g, wp_ref[...], ((1,), (1,))))
            total = total + part
            gha_ref[rows, :] = back
            gft_ref[rows, :] = back.astype(bf16)
        gain_fin_ref[...] = total
        acc[...] = jnp.zeros_like(acc)
        for copy in w_copies:
            copy.wait()

    @pl.when(step >= slots)
    def _():
        k = step - slots

        def part(n, carry):
            cols = pl.ds(pl.multiple_of(n * 256, 256), 256)
            gi = dot(gft_ref[...], wd[shard(k), cols, :], ((1,), (1,)))
            gg_ref[0, :, cols] = (gi * dact_ref[0, :, cols].astype(f32)).astype(bf16)
            gu_ref[0, :, cols] = (gi * act_ref[0, :, cols].astype(f32)).astype(bf16)
            return carry

        lax.fori_loop(0, hidden // 256, part, 0)
        acc[...] += dot(gg_ref[0], w[k, :, :hidden], ((1,), (1,))) + dot(
            gu_ref[0], w[k, :, hidden : 2 * hidden], ((1,), (1,))
        )

    @pl.when(step == 2 * slots - 1)
    def _():
        gain = gffn_ref[...]
        total = jnp.zeros((1, d), f32)
        for a in range(blocks):
            rows = slice(a * tile, (a + 1) * tile)
            back, part = rms_back(hid_ref[rows, :], gain, acc[rows, :])
            total = total + part
            g = gha_ref[rows, :] + back
            gha_ref[rows, :] = g
            g = g.astype(bf16)
            gat_ref[rows, :] = g
            for k in range(slots):
                gm_ref[k, rows, :] = dot(g, w[k, :, 2 * hidden :]).astype(bf16)
        gain_ffn_ref[...] = total


def middle(
    offs, hid, inner, act, dact, gain_final, gain_ffn, w_proj, pad_cols, query, cot, top,
    own, first, second,
):
    length, d = hid.shape
    slots, _, hidden = inner.shape
    width = first[0].shape[3]
    wide = width - 2 * hidden
    e = w_proj.shape[1]

    def row_block(v):
        return pl.BlockSpec((1,) + v.shape[1:], lambda i, sc: (sc[16], 0, 0))

    early = pl.BlockSpec((1, length, hidden), lambda i, sc: (jnp.minimum(i, slots - 1), 0, 0))
    late = pl.BlockSpec((1, length, hidden), lambda i, sc: (jnp.maximum(i - slots, 0), 0, 0))
    chunk = jax.ShapeDtypeStruct((slots, length, hidden), bf16)
    grid = pltpu.PrefetchScalarGridSpec(
        num_scalar_prefetch=1,
        grid=(2 * slots,),
        in_specs=[
            whole(hid.shape),
            early,
            late,
            late,
            whole(gain_final.shape),
            whole(gain_ffn.shape),
            whole(w_proj.shape),
            whole(pad_cols.shape),
            row_block(query),
            row_block(cot),
            row_block(top),
        ]
        + [ANY] * 12,
        out_specs=[
            whole(cot.shape[1:]),
            whole((length, d)),
            whole((length, e)),
            whole((1, d)),
            whole((1, d)),
            whole((length, d)),
            late,
            late,
            whole((length, d)),
            whole((length, d)),
            whole((slots, length, wide)),
        ],
        scratch_shapes=[
            pltpu.VMEM((slots, d, width), bf16),
            pltpu.VMEM((slots, hidden, d), bf16),
            pltpu.SemaphoreType.DMA((copies_per_chunk,)),
            pltpu.SemaphoreType.DMA((copies_per_chunk,)),
            pltpu.VMEM((length, d), f32),
            pltpu.VMEM((length, e), f32),
            pltpu.VMEM((length, e), bf16),
        ],
    )
    return pl.pallas_call(
        middle_kernel,
        grid_spec=grid,
        out_shape=[
            jax.ShapeDtypeStruct(cot.shape[1:], f32),
            jax.ShapeDtypeStruct((length, d), bf16),
            jax.ShapeDtypeStruct((length, e), bf16),
            jax.ShapeDtypeStruct((1, d), f32),
            jax.ShapeDtypeStruct((1, d), f32),
            jax.ShapeDtypeStruct((length, d), bf16),
            chunk,
            chunk,
            jax.ShapeDtypeStruct((length, d), f32),
            jax.ShapeDtypeStruct((length, d), bf16),
            jax.ShapeDtypeStruct((slots, length, wide), bf16),
        ],
        compiler_params=params(58),
        cost_estimate=pl.CostEstimate(
            flops=2 * length * d * (4 * slots * hidden + d),
            bytes_accessed=32 << 20,
            transcendentals=length,
        ),
        name="middle",
    )(
        offs, hid, inner, act, dact, gain_final, gain_ffn, w_proj, pad_cols, query, cot, top,
        *own, *first, second,
    )


def keep_parts(sc, out, refs):
    send_a, keep_a, send_b, keep_b = refs
    half = send_a.shape[2]
    x, y = sc[18], sc[19]

    def rows(y, x, extra):
        at = pl.multiple_of((2 * y + x) * (2 * half) + extra, 16)
        return out[pl.ds(at, half), :]

    for other in range(2):
        send_a[0, other] = rows(other, 1 - x, 0)
        keep_a[0, other] = rows(other, x, 0)
        send_b[0, other] = rows(1 - y, other, half)
        keep_b[0, other] = rows(y, other, half)


def parts_of(slots, rows, width):
    part = (1, 2, rows // 8, width)
    spec = pl.BlockSpec(part, lambda i, sc: (i, 0, 0, 0))
    return [spec] * 4, [jax.ShapeDtypeStruct((slots,) + part[1:], bf16)] * 4


def product_kernel(lefts, pairs, keep, sc, *refs):
    left_refs, right_refs = refs[:lefts], refs[lefts : lefts + len(pairs)]
    refs = refs[lefts + len(pairs) :]
    out = refs[-1] if keep else refs[-1].at[0]
    at = 0
    for right_ref, which in zip(right_refs, pairs):
        right = right_ref[...]
        left = left_refs[which][...]
        left, right = (v.reshape(v.shape[-2:]) for v in (left, right))
        cols = slice(at, at + right.shape[1])
        value = dot(left, right, ((0,), (0,)))
        if keep:
            value = value + refs[0][0, :, cols].astype(f32)
        out[:, cols] = value.astype(bf16)
        at += right.shape[1]
    if keep:
        keep_parts(sc, out, refs[1:5])


def products(offs, lefts, rights, slots, got=None):
    keep = got is not None
    length, half = lefts[0].shape[-2], lefts[0].shape[-1] // 2
    width = sum(right.shape[-1] for right, _ in rights)

    def which(sc):
        return sc[17] if keep else 1 - sc[17]

    specs = []
    for left in lefts:
        if left.ndim == 3:
            specs.append(pl.BlockSpec((1, length, half), lambda i, sc: (i, 0, which(sc))))
        else:
            specs.append(pl.BlockSpec((length, half), lambda i, sc: (0, which(sc))))
    for right, _ in rights:
        if right.ndim == 3:
            specs.append(pl.BlockSpec((1,) + right.shape[1:], lambda i, sc: (i, 0, 0)))
        else:
            specs.append(whole(right.shape))
    args = list(lefts) + [right for right, _ in rights]
    block = pl.BlockSpec((1, half, width), lambda i, sc: (i, 0, 0))
    out_specs, out_shape = block, jax.ShapeDtypeStruct((slots, half, width), bf16)
    scratch = []
    if keep:
        specs.append(block)
        args.append(got)
        out_specs, out_shape = parts_of(slots, half, width)
        scratch = [pltpu.VMEM((half, width), bf16)]
    return pl.pallas_call(
        functools.partial(product_kernel, len(lefts), [i for _, i in rights], keep),
        grid_spec=pltpu.PrefetchScalarGridSpec(
            num_scalar_prefetch=1,
            grid=(slots,),
            in_specs=specs,
            out_specs=out_specs,
            scratch_shapes=scratch,
        ),
        out_shape=out_shape,
        compiler_params=params(48),
        cost_estimate=cheap,
        name="products_keep" if keep else "products_send",
    )(offs, *args)


cheap = pl.CostEstimate(flops=1 << 20, bytes_accessed=1 << 16, transcendentals=0)


def attn_product_kernel(keep, sc, la, lb, ra, rb, small, *refs):
    out = refs[-1] if keep else refs[-1].at[0]
    quarter, d = la.shape[3], ra.shape[2]
    for left, right, at in ((la, ra, 0), (lb, rb, quarter)):
        value = dot(left[0, 0], right[0], ((0,), (0,)))
        if keep:
            value = value + refs[0][0, at : at + quarter, :d].astype(f32)
        out[at : at + quarter, :d] = value.astype(bf16)
    value = small[0]
    if keep:
        value = add(value, refs[0][0, :, d:])
    out[:, d:] = value
    if keep:
        keep_parts(sc, out, refs[1:5])


def attn_products(offs, left, both, small, got=None):
    keep = got is not None
    slots, _, length, quarter = left.shape
    d = both.shape[2]
    width = d + small.shape[2]
    half = 2 * quarter

    def which(sc):
        return sc[17] if keep else 1 - sc[17]

    block = pl.BlockSpec((1, half, width), lambda i, sc: (i, 0, 0))
    specs = [
        pl.BlockSpec((1, 1, length, quarter), lambda i, sc: (i, 2 * which(sc), 0, 0)),
        pl.BlockSpec((1, 1, length, quarter), lambda i, sc: (i, 2 * which(sc) + 1, 0, 0)),
        pl.BlockSpec((1, length, d), lambda i, sc: (0, 0, 0)),
        pl.BlockSpec((1, length, d), lambda i, sc: (which(sc), 0, 0)),
        pl.BlockSpec((1, half, small.shape[2]), lambda i, sc: (i, which(sc), 0)),
    ]
    args = [left, left, both, both, small]
    out_specs, out_shape = block, jax.ShapeDtypeStruct((slots, half, width), bf16)
    scratch = []
    if keep:
        specs.append(block)
        args.append(got)
        out_specs, out_shape = parts_of(slots, half, width)
        scratch = [pltpu.VMEM((half, width), bf16)]
    return pl.pallas_call(
        functools.partial(attn_product_kernel, keep),
        grid_spec=pltpu.PrefetchScalarGridSpec(
            num_scalar_prefetch=1,
            grid=(slots,),
            in_specs=specs,
            out_specs=out_specs,
            scratch_shapes=scratch,
        ),
        out_shape=out_shape,
        compiler_params=params(48),
        cost_estimate=cheap,
        name="attn_keep" if keep else "attn_send",
    )(offs, *args)


def add(a, b):
    return (a.astype(f32) + b.astype(f32)).astype(bf16)


def second_kernel(sc, ka, ra, kb, rb, *refs):
    send_a, keep_a, send_b, keep_b = refs[-4:]
    x, y = sc[18], sc[19]
    send_a[0] = add(ka[0, 1 - y], ra[0, 1 - y])
    keep_a[0] = add(ka[0, y], ra[0, y])
    send_b[0] = add(kb[0, 1 - x], rb[0, 1 - x])
    keep_b[0] = add(kb[0, x], rb[0, x])


def second_sums(offs, *arrays, after=()):
    slots, _, half, width = arrays[0].shape
    into = pl.BlockSpec((1, 2, half, width), lambda i, sc: (i, 0, 0, 0))
    out = pl.BlockSpec((1, half, width), lambda i, sc: (i, 0, 0))
    return pl.pallas_call(
        second_kernel,
        grid_spec=pltpu.PrefetchScalarGridSpec(
            num_scalar_prefetch=1,
            grid=(slots,),
            in_specs=[into] * 4 + [ANY] * len(after),
            out_specs=[out] * 4,
        ),
        out_shape=[jax.ShapeDtypeStruct((slots, half, width), bf16)] * 4,
        compiler_params=params(48),
        cost_estimate=cheap,
        name="second_sums",
    )(offs, *arrays, *after)


def third_kernel(ka, ra, kb, rb, *refs):
    half = ka.shape[1]
    for k, out in enumerate(refs[-ka.shape[0] :]):
        out[:half, :] = add(ka[k], ra[k])
        out[half:, :] = add(kb[k], rb[k])


def third_sums(*arrays, after=()):
    slots, half, width = arrays[0].shape
    shape = (2 * half, width)
    return pl.pallas_call(
        third_kernel,
        grid=(1,),
        in_specs=[whole(arrays[0].shape)] * 4 + [ANY] * len(after),
        out_specs=[whole(shape)] * slots,
        out_shape=[jax.ShapeDtypeStruct(shape, bf16)] * slots,
        compiler_params=params(48),
        cost_estimate=cheap,
        name="third_sums",
    )(*arrays, *after)


def last_kernel(*refs):
    t = [ref[...].astype(f32) for ref in refs[:4]]
    refs[-1][...] = ((t[0] + t[2]) + (t[1] + t[3])).astype(refs[-1].dtype)


def last_sum(arrays, dtype, after=()):
    shape = arrays[0].shape
    return pl.pallas_call(
        last_kernel,
        grid=(1,),
        in_specs=[whole(shape)] * 4 + [ANY] * len(after),
        out_specs=whole(shape),
        out_shape=jax.ShapeDtypeStruct(shape, dtype),
        compiler_params=params(48),
        cost_estimate=cheap,
        name="last_sum",
    )(*arrays, *after)


def stack_kernel(a, xa, b, yb, *refs):
    sa, sb = refs[-2:]
    sa[0], sa[1], sb[0], sb[1] = a[...], xa[...], b[...], yb[...]


def stack_pairs(a, xa, b, yb, after):
    out = (2,) + a.shape
    return pl.pallas_call(
        stack_kernel,
        grid=(1,),
        in_specs=[whole(a.shape)] * 4 + [ANY] * len(after),
        out_specs=[whole(out)] * 2,
        out_shape=[jax.ShapeDtypeStruct(out, bf16)] * 2,
        compiler_params=params(48),
        cost_estimate=cheap,
        name="stack_pairs",
    )(a, xa, b, yb, *after)


class Reduce:
    def __init__(self, place, offs, kept):
        self.place, self.offs, self.kept = place, offs, kept

    def first(self, after=()):
        send_a, keep_a, send_b, keep_b = self.kept
        ra, rb = self.place.swap(send_a, XBIT), self.place.swap(send_b, YBIT)
        self.kept = second_sums(self.offs, keep_a, ra, keep_b, rb, after=after)

    def second(self, after=()):
        send_a, keep_a, send_b, keep_b = self.kept
        ra, rb = self.place.swap(send_a, YBIT), self.place.swap(send_b, XBIT)
        self.kept = third_sums(keep_a, ra, keep_b, rb, after=after)

    def third(self, after=()):
        p = self.place
        t = [self.kept[0]] + [p.shift(self.kept[k], -k) for k in range(1, p.n_mp)]
        if p.n_out > 1:
            return lax.psum(last_sum(t, f32, after), "out").astype(bf16)
        return last_sum(t, bf16, after)


def gathered(v):
    rows, width = v.shape
    out = lax.all_gather(v, group, tiled=False).reshape(2, 2, 2, rows, width)
    return out.transpose(2, 0, 1, 3, 4).reshape(8 * rows, width).astype(f32)


def unpack_kernel(offs, *refs):
    arrays, outs, small, full = refs[:8], refs[8:-2], refs[-2], refs[-1]
    for at in range(16):
        value = arrays[at // 2][at % 2]
        rows = pl.ds(pl.multiple_of(offs[at], 16), value.shape[0])
        full[rows, :] = value.astype(f32)
    rows, d = outs[0].shape
    for i, out in enumerate(outs):
        out[...] = full[i * rows : (i + 1) * rows, :d]
    small[...] = full[:, d:]


def unpack(offs, arrays, count, small):
    half, width = arrays[0].shape[1:]
    rows, d = 16 * half, width - small
    shapes = [(rows // count, d)] * count + [(rows, small)]
    return pl.pallas_call(
        unpack_kernel,
        grid_spec=pltpu.PrefetchScalarGridSpec(
            num_scalar_prefetch=1,
            grid=(1,),
            in_specs=[whole(v.shape) for v in arrays],
            out_specs=[whole(s) for s in shapes],
            scratch_shapes=[pltpu.VMEM((rows, width), f32)],
        ),
        out_shape=[jax.ShapeDtypeStruct(s, f32) for s in shapes],
        compiler_params=params(24),
        cost_estimate=cheap,
        name="unpack",
    )(offs, *arrays)


def spread_rows(place, v, length):
    n = place.n_mp
    right = left = v
    slots = [v] + [None] * (n - 1)
    for k in range(1, n):
        right = lax.ppermute(right, "mp", [(i, i + 1) for i in range(n - 1)])
        left = lax.ppermute(left, "mp", [(i + 1, i) for i in range(n - 1)])
        for at, value in ((k, right), (n - k, left)):
            slots[at] = value if slots[at] is None else slots[at] + value
    out = jnp.zeros((n, length) + v.shape[1:], f32)
    rest = jnp.zeros((n, v.shape[0] - length) + v.shape[1:], v.dtype)
    for k in range(n):
        at = (place.z - k) % n
        out = lax.dynamic_update_index_in_dim(out, slots[k][:length].astype(f32), at, 0)
        rest = lax.dynamic_update_index_in_dim(rest, slots[k][length:], at, 0)
    return out, rest


def local(
    tokens, segment_ids, pad_mask, top_index, query_emb, score_cot, gain_attn, w_query, w_key,
    w_value, w_out, rel_table, gain_ffn, w_gate, w_up, w_down, gain_final, w_proj,
):
    place = Place()
    slots = place.n_mp
    rows, length = segment_ids.shape
    d = tokens.shape[1]
    heads = rel_table.shape[1]
    size = w_query.shape[1] // heads
    wide = heads * size
    hot = jnp.asarray(bucket_hot(rel_table.shape[0], length), bf16)
    segs, pads = segment_ids.astype(f32), pad_mask.astype(f32)
    seg_cols, pad_cols = segs.T, pads.T
    gain_a, gain_f, gain_l = (
        g.astype(f32).reshape(1, d) for g in (gain_attn, gain_ffn, gain_final)
    )
    offs = place.offsets(d // 8)

    buckets = rel_table.shape[0]
    table = jnp.zeros((64, d), bf16).at[:heads, :buckets].set(rel_table.T)
    w_qkv = jnp.concatenate([w_query.T, w_key.T, w_value.T, table])
    w_out_t = w_out.T
    eighth = d // 8

    def piece(*arrays):
        parts = []
        for v in arrays:
            rows = v.shape[0] // 8
            parts.append(lax.dynamic_slice_in_dim(v, place.p * rows, rows, 0))
        return jnp.concatenate(parts, axis=1) if len(parts) > 1 else parts[0]

    def all_pieces(v):
        out = lax.all_gather(piece(v), group + ("mp",))
        return out.reshape((2, 2, 2, slots) + out.shape[1:])

    common = (offs, tokens, segs, pads, seg_cols, gain_a)
    piece1 = piece(w_gate, w_up, w_out_t)
    z1 = [place.shift(piece1, k) for k in range(1, slots)]
    all_down = all_pieces(w_down)
    all_qkv = all_pieces(w_qkv)
    attended = attend(1, *common, w_qkv, hot, heads, size)
    mixed = [attended[slots - 1]] + [place.shift(attended[k - 1], k) for k in range(1, slots)]
    s1 = place.first_round(*split(z1, (attended,)), mixed[1:])
    first = place.second_round(*s1)
    own = (w_gate, w_up, w_out_t)
    hid, normed_ffn, act, dact, inner = ffn_in(
        offs, tokens, gain_f, mixed, own, first, length
    )
    score, nfin, ge, gain_fin, gain_mid, gft, gg, gu, gha, gat, gm = middle(
        offs, hid, inner, act, dact, gain_l, gain_f, w_proj, pad_cols, query_emb, score_cot,
        top_index, own, first, all_down,
    )

    down_sides = ([inner, nfin], [(gft, 0), (ge, 1)])
    gu_sides = ([normed_ffn], [(gg, 0), (gu, 0)])
    down_got = place.swap(products(offs, *down_sides, slots), CORE)
    gu_got = place.swap(products(offs, *gu_sides, slots), CORE)
    down = Reduce(place, offs, products(offs, *down_sides, slots, down_got))
    gate_up = Reduce(place, offs, products(offs, *gu_sides, slots, gu_got))
    kept_gu = (gate_up.kept[0], gate_up.kept[2])
    down.first(kept_gu)

    finish = [gha, gat, gain_fin, gain_mid, score]

    def back(slot, acc, left, after):
        return attend_back(
            slot, common + (hot,), gm, mixed[slot], acc, left, finish, all_qkv, heads, size, after
        )

    left, table0, acc = back(0, None, None, kept_gu + (down.kept[0], down.kept[2]))
    down.second((table0,))
    left, table1, acc = back(1, acc, left, tuple(down.kept[1:]))
    down = down.third((table1,))
    gate_up.first((table1,))
    left, table2, acc = back(2, acc, left, (gate_up.kept[0], gate_up.kept[2]))
    gate_up.second((table2,))
    finish += [table0, table1, table2]
    left, _, dx, both, small = back(3, acc, left, tuple(gate_up.kept[1:]))
    gate_up = gate_up.third((both,))
    attn_got = place.swap(attn_products(offs, left, both, small), CORE)
    attn = Reduce(place, offs, attn_products(offs, left, both, small, attn_got))
    attn.first()
    attn.second()
    attn = place.second_round(*place.first_round(*halves(attn.third(), 0)))
    grad_q, grad_k, grad_v, grad_out, small = unpack(offs, attn, 4, small.shape[2])
    grad_down = gathered(down)
    grad_gu = gathered(gate_up)
    hidden = w_gate.shape[1]

    input_grad, packed = spread_rows(place, dx, length)
    input_grad = input_grad.reshape(rows * length, d)
    n, m = score.shape
    packed = packed.astype(f32).reshape(slots, 16, d // 128, 128)[:, :, : 2 * (n // 16), :m]
    packed = packed[:, :, 0::2] + packed[:, :, 1::2]
    scores = packed.transpose(0, 2, 1, 3).reshape(slots, n, m)
    return (
        scores,
        input_grad,
        small[:, 0],
        grad_q.T,
        grad_k.T,
        grad_v.T,
        grad_out,
        small[:buckets, 64 : 64 + heads],
        small[:, 2],
        grad_gu[:, :hidden],
        grad_gu[:, hidden:],
        grad_down[:, :d],
        small[:, 1],
        grad_down[:, d:],
    )


def solution(mesh):
    n_dp, n_mp = mesh.shape["dp"], mesh.shape["mp"]
    mesh = Mesh(mesh.devices.reshape(n_dp // 8, 2, 2, 2, n_mp), dp + ("mp",))
    return jax.shard_map(
        local,
        mesh=mesh,
        in_specs=(
            P(dp, None),
            P(dp, None),
            P(dp, None),
            P(dp, None, None),
            P(dp, None, None),
            P(dp, None, None),
            P(),
            P(None, "mp"),
            P(None, "mp"),
            P(None, "mp"),
            P("mp", None),
            P(None, "mp"),
            P(),
            P(None, "mp"),
            P(None, "mp"),
            P("mp", None),
            P(),
            P(),
        ),
        out_specs=(
            P(dp, None, None),
            P(dp, None),
            P(),
            P(None, "mp"),
            P(None, "mp"),
            P(None, "mp"),
            P("mp", None),
            P(None, "mp"),
            P(),
            P(None, "mp"),
            P(None, "mp"),
            P("mp", None),
            P(),
            P(),
        ),
        check_vma=False,
    )
```

time: 875 us -> 495 us (0.57)
  waiting for transfers between devices: 523 us -> 148 us
  Pallas kernels: 0 us -> 180 us
  matrix products: 154 us -> 0 us
  starting transfers between devices: 0.67 us -> 86.4 us
  other arithmetic: 68.3 us -> 17.9 us
  local copies, waits for them, and re-layouts: 80.8 us -> 41.1 us
  blocking collectives: 25.9 us -> 0 us
    psum x5 -> x0, waiting for transfers between devices: 522 us -> none  [the longest x1 123 us: local(): hidden_attn = inputs + lax.psum(attn_term, 'mp').astype(jnp.float32)]
    pallas_call x0 -> x26, Pallas kernels: none -> 180 us  [the longest x4 54.4 us: attend_back(): pl.pallas_call(functools.partial(attend_back_kernel, slot, last, heads, s...]
    dot_general x56 -> x0, matrix products: 154 us -> none  [the longest x8 28.5 us: left_product(): jnp.einsum('ta,tb->ab', left, right, preferred_element_type=jnp.float32)]
    ppermute x0 -> x52, waiting for transfers between devices: none -> 148 us  [the longest x31 78.6 us: swap(): return lax.ppermute(v, name, [(0, 1), (1, 0)])]
    ppermute x0 -> x52, starting transfers between devices: none -> 86 us  [the longest x15 42 us: shift(): return lax.ppermute(v, 'mp', [(i, (i + k) % n) for i in range(n)])]
    psum x1 -> x0, blocking collectives: 25.9 us -> none  [local(): lax.psum((grad_gattn, grad_wquery, grad_wkey, grad_wvalue, grad_wout, gra...]
    reduce_sum x9 -> x0, other arithmetic: 25.2 us -> none  [the longest x3 12.2 us: rms_norm(): scale = lax.rsqrt(jnp.mean(values * values, axis=-1, keepdims=True) + 1e-06)]
    while x24 -> x0, local copies, waits for them, and re-layouts: 15 us -> none  [the longest x4 6.66 us: local(): lax.scan(backward_row, logit_start, (query, keys, values, allowed, log_to...]
  transfers between devices with their start and end apart: 5 -> 56, of which waited for: 5 -> 26; matrix products, arithmetic and copies ran while one was open for 9% -> 7% of each run, Pallas kernels for 0% -> 37%
where the time goes in v1:
time: 495 us; the launch traced here: 488 us
  Pallas kernels  180 us (36%)
  waiting for transfers between devices  148 us (30%)
  starting transfers between devices  86.4 us (17%)
  local copies, waits for them, and re-layouts  41.1 us (8%)
  other arithmetic  17.9 us (4%)
  between operations  14.9 us (3%)
    ppermute x31, waiting for transfers between devices, swap(): return lax.ppermute(v, name, [(0, 1), (1, 0)])  78.6 us
    ppermute x15, waiting for transfers between devices, shift(): return lax.ppermute(v, 'mp', [(i, (i + k) % n) for i in range(n)])  54.4 us
    pallas_call x4, Pallas kernels, attend_back(): pl.pallas_call(functools.partial(attend_back_kernel, slot, last, heads, s...  54.4 us
    ppermute x15, starting transfers between devices, shift(): return lax.ppermute(v, 'mp', [(i, (i + k) % n) for i in range(n)])  42 us
    pallas_call x1, Pallas kernels, middle(): pl.pallas_call(middle_kernel, grid_spec=grid, out_shape=[jax.ShapeDtypeSt...  32.2 us
    ppermute x31, starting transfers between devices, swap(): return lax.ppermute(v, name, [(0, 1), (1, 0)])  23.7 us
    pallas_call x4, Pallas kernels, products(): pl.pallas_call(functools.partial(product_kernel, len(lefts), [i for _, i...  23.4 us
    unnamed x136, local copies, waits for them, and re-layouts  22.8 us
  transfers between devices with their start and end apart: 56, of which 26 were waited for; matrix products, arithmetic and copies ran while one was open for 7% of the time, Pallas kernels for 37%

profile of v1, /device:TPU:0, one launch (start us, length us, event | category | flops | bytes accessed | tf_op | source)
XLA Modules:
  0.0 488.0 jit_solution(4723834644090873647)
XLA Ops:
  12.4 3.0 collective-permute-start.3
  15.4 2.6 collective-permute-start.4
  23.5 22.7 %attend.1.refs_3_ = bf16[4,528,192]{2,1,0:T(8,128)(2,1)S(1)} custom-call(s32[20]{0:T(128)S(1)} %stack.83.sc.offs, bf16[2048,768]{1,0:T(8,128)(2,1)S(1)} %copy-done.2, f32[4,512]{1,0:T(4,128)S(1)} %convert_element_type.38.seg_ref, f32[4,512]{1,0:T(4,128)S(1)} %get-tuple-element.246.pad_ref, f32[512,4]{1,0:T(8,128)S(1)} %bitcast.89, ...), custom_call_target="tpu_custom_call" | custom-call | flops 2617245696 | bytes 4194304 | tf_op jit(solution)/shard_map/attend/pallas_call | solution.py:266
  51.5 5.4 %collective-permute-start = (bf16[528,192]{1,0:T(8,128)(2,1)S(1)}, bf16[528,192]{1,0:T(8,128)(2,1)S(1)}, u32[]{:S(2)}, u32[]{:S(2)}) collective-permute-start(bf16[528,192]{1,0:T(8,128)(2,1)S(1)} %get-tuple-element.241), channel_id=1, source_target_pairs={{0,1},{1,2},{2,3},{3,0},{4,5},{5,6},{6,7},{7,4},{8,9},{9,10},{10,1... | collective-permute-start | bytes 608264 | tf_op jit(solution)/shard_map/ppermute | solution.py:76
  59.2 7.8 %collective-permute-done.refs_0_.refs_1_.mixed_ref = bf16[528,192]{1,0:T(8,128)(2,1)S(1)} collective-permute-done((bf16[528,192]{1,0:T(8,128)(2,1)S(1)}, bf16[528,192]{1,0:T(8,128)(2,1)S(1)}, u32[]{:S(2)}, u32[]{:S(2)}) %collective-permute-start) | collective-permute-done | bytes 202784 | tf_op jit(solution)/shard_map/ppermute | solution.py:76
  67.0 12.3 %collective-permute-done.1.refs_1_.refs_2_.mixed_ref = bf16[528,192]{1,0:T(8,128)(2,1)S(1)} collective-permute-done((bf16[528,192]{1,0:T(8,128)(2,1)S(1)}, bf16[528,192]{1,0:T(8,128)(2,1)S(1)}, u32[]{:S(2)}, u32[]{:S(2)}) %collective-permute-start.1) | collective-permute-done | bytes 202784 | tf_op jit(solution)/shard_map/ppermute | solution.py:76
  82.4 30.3 %collective-permute-done.8.refs_9_.refs_5_ = bf16[2,3,48,1728]{3,2,1,0:T(8,128)(2,1)} collective-permute-done((bf16[2,3,48,1728]{3,2,1,0:T(8,128)(2,1)S(1)}, bf16[2,3,48,1728]{3,2,1,0:T(8,128)(2,1)}, u32[]{:S(2)}, u32[]{:S(2)}) %collective-permute-start.8) | collective-permute-done | bytes 995360 | tf_op jit(solution)/shard_map/ppermute | solution.py:72
  117.5 21.3 %ffn_in.1 = (f32[512,768]{1,0:T(8,128)}, bf16[512,768]{1,0:T(8,128)(2,1)}, bf16[4,512,768]{2,1,0:T(8,128)(2,1)}, bf16[4,512,768]{2,1,0:T(8,128)(2,1)}, bf16[4,512,768]{2,1,0:T(8,128)(2,1)}) custom-call(s32[20]{0:T(128)} %copy-done.42, bf16[2048,768]{1,0:T(8,128)(2,1)} %x_ref.11, f32[1,768]{1,0:T(1,128)} %reshape.116.gain_ref.gffn_ref, ...), custom_call_target="tpu_custom_call" | custom-call | flops 5435817984 | bytes 25165824 | tf_op jit(solution)/shard_map/ffn_in/pallas_call | solution.py:537
  138.9 32.2 %middle.1 = (f32[32,32]{1,0:T(8,128)}, bf16[512,768]{1,0:T(8,128)(2,1)}, bf16[512,128]{1,0:T(8,128)(2,1)}, f32[1,768]{1,0:T(1,128)}, f32[1,768]{1,0:T(1,128)}, /...) custom-call(s32[20]{0:T(128)} %copy-done.42, ...), custom_call_target="tpu_custom_call" | custom-call | flops 10267656192 | bytes 33554432 | tf_op jit(solution)/shard_map/middle/pallas_call | solution.py:729
  171.2 1.9 copy-done.5
  173.1 6.8 %products_send.2 = bf16[4,384,1536]{2,1,0:T(8,128)(2,1)} custom-call(s32[20]{0:T(128)S(1)} %copy-done.43, bf16[512,768]{1,0:T(8,128)(2,1)S(1)} %copy-done.12, bf16[4,512,768]{2,1,0:T(8,128)(2,1)S(1)} %copy-done.5, bf16[4,512,768]{2,1,0:T(8,128)(2,1)} %get-tuple-element.113.refs_2_), custom_call_target="tpu_custom_call" | custom-call | flops 1048576 | bytes 65536 | tf_op jit(solution)/shard_map/products_send/pallas_call | solution.py:827
  180.4 4.5 products_send.3
  185.0 6.9 %collective-permute-done.15.refs_4_ = bf16[4,384,896]{2,1,0:T(8,128)(2,1)S(1)} collective-permute-done((bf16[4,384,896]{2,1,0:T(8,128)(2,1)S(1)}, bf16[4,384,896]{2,1,0:T(8,128)(2,1)S(1)}, u32[]{:S(2)}, u32[]{:S(2)}) %collective-permute-start.15) | collective-permute-done | bytes 2752544 | tf_op jit(solution)/shard_map/ppermute | solution.py:72
  193.4 5.2 %products_keep.3 = (bf16[4,2,48,896]{3,2,1,0:T(8,128)(2,1)S(1)}, bf16[4,2,48,896]{3,2,1,0:T(8,128)(2,1)S(1)}, bf16[4,2,48,896]{3,2,1,0:T(8,128)(2,1)S(1)}, bf16[4,2,48,896]{3,2,1,0:T(8,128)(2,1)S(1)}) custom-call(s32[20]{0:T(128)S(1)} %copy-done.43, bf16[4,512,768]{2,1,0:T(8,128)(2,1)} %get-tuple-element.107.inner_ref.refs_0_, ...), custom_call_target="tpu_custom_call" | custom-call | flops 1048576 | bytes 65536 | tf_op jit(solution)/shard_map/products_keep/pallas_call | solution.py:827
  200.8 2.2 copy-done.53
  203.0 7.0 %products_keep.2 = (bf16[4,2,48,1536]{3,2,1,0:T(8,128)(2,1)S(1)}, bf16[4,2,48,1536]{3,2,1,0:T(8,128)(2,1)S(1)}, bf16[4,2,48,1536]{3,2,1,0:T(8,128)(2,1)S(1)}, bf16[4,2,48,1536]{3,2,1,0:T(8,128)(2,1)S(1)}) custom-call(s32[20]{0:T(128)S(1)} %copy-done.43, bf16[512,768]{1,0:T(8,128)(2,1)S(1)} %copy-done.12, bf16[4,512,768]{2,1,0:T(8,128)(2,1)} %get-tuple-element.112.refs_1_, ...), custom_call_target="tpu_custom_call" | custom-call | flops 1048576 | bytes 65536 | tf_op jit(solution)/shard_map/products_keep/pallas_call | solution.py:827
  212.0 4.9 %collective-permute-done.16.ra = bf16[4,2,48,896]{3,2,1,0:T(8,128)(2,1)S(1)} collective-permute-done((bf16[4,2,48,896]{3,2,1,0:T(8,128)(2,1)S(1)}, bf16[4,2,48,896]{3,2,1,0:T(8,128)(2,1)S(1)}, u32[]{:S(2)}, u32[]{:S(2)}) %collective-permute-start.16) | collective-permute-done | bytes 688160 | tf_op jit(solution)/shard_map/ppermute | solution.py:72
  218.0 2.4 second_sums.3
  223.8 12.7 %attend_back0.1 = (bf16[4,4,512,192]{3,2,1,0:T(8,128)(2,1)}, f32[8,128]{1,0:T(8,128)}, f32[512,768]{1,0:T(8,128)}) custom-call(s32[20]{0:T(128)} %copy-done.42, bf16[2048,768]{1,0:T(8,128)(2,1)} %x_ref.11, f32[4,512]{1,0:T(4,128)} %copy-done.31, f32[4,512]{1,0:T(4,128)} %copy-done.38, f32[512,4]{1,0:T(8,128)} %bitcast.90, f32[1,768]{1,0:T(1,128)} %copy-done.46, ...), custom_call_target="tpu_custom_call" | custom-call | flops 1610612736 | bytes 16777216 | tf_op jit(solution)/shard_map/attend_back0/pallas_call | solution.py:455
  236.5 13.4 %collective-permute-done.18.ra = bf16[4,48,896]{2,1,0:T(8,128)(2,1)} collective-permute-done((bf16[4,48,896]{2,1,0:T(8,128)(2,1)}, bf16[4,48,896]{2,1,0:T(8,128)(2,1)}, u32[]{:S(2)}, u32[]{:S(2)}) %collective-permute-start.18) | collective-permute-done | bytes 344096 | tf_op jit(solution)/shard_map/ppermute | solution.py:72
  251.9 6.0 %collective-permute-start.49 = (bf16[96,896]{1,0:T(8,128)(2,1)S(1)}, bf16[96,896]{1,0:T(8,128)(2,1)S(1)}, u32[]{:S(2)}, u32[]{:S(2)}) collective-permute-start(bf16[96,896]{1,0:T(8,128)(2,1)S(1)} %get-tuple-element.130.refs_3_), channel_id=1, source_target_pairs={{0,3},{1,0},{2,1},{3,2},{4,7},{5,4},{6,5},{7,6},{8,11},{9,8},{10,9... | collective-permute-start | bytes 516104 | tf_op jit(solution)/shard_map/ppermute | solution.py:76
  259.0 13.2 %attend_back1.1 = (bf16[4,4,512,192]{3,2,1,0:T(8,128)(2,1)}, f32[8,128]{1,0:T(8,128)}, f32[512,768]{1,0:T(8,128)}) custom-call(s32[20]{0:T(128)} %copy-done.42, bf16[2048,768]{1,0:T(8,128)(2,1)} %x_ref.11, f32[4,512]{1,0:T(4,128)} %copy-done.31, f32[4,512]{1,0:T(4,128)} %copy-done.38, f32[512,4]{1,0:T(8,128)} %bitcast.91, ...), custom_call_target="tpu_custom_call", output_to_operand_aliasing={{0}: (11, {})} | custom-call | flops 1610612736 | bytes 16777216 | tf_op jit(solution)/shard_map/attend_back1/pallas_call | solution.py:455
  276.6 3.3 second_sums.4
  282.0 13.1 %attend_back2.1 = (bf16[4,4,512,192]{3,2,1,0:T(8,128)(2,1)}, f32[8,128]{1,0:T(8,128)}, f32[512,768]{1,0:T(8,128)}) custom-call(s32[20]{0:T(128)} %copy-done.42, bf16[2048,768]{1,0:T(8,128)(2,1)} %x_ref.11, f32[4,512]{1,0:T(4,128)} %copy-done.31, f32[4,512]{1,0:T(4,128)} %copy-done.38, f32[512,4]{1,0:T(8,128)} %bitcast.92, ...), custom_call_target="tpu_custom_call", output_to_operand_aliasing={{0}: (11, {})} | custom-call | flops 1610612736 | bytes 16777216 | tf_op jit(solution)/shard_map/attend_back2/pallas_call | solution.py:455
  295.9 2.7 collective-permute-done.23.rb
  301.7 15.3 %attend_back3.1 = (bf16[4,4,512,192]{3,2,1,0:T(8,128)(2,1)}, f32[8,128]{1,0:T(8,128)}, bf16[528,768]{1,0:T(8,128)(2,1)}, bf16[2,512,768]{2,1,0:T(8,128)(2,1)}, bf16[4,768,128]{2,1,0:T(8,128)(2,1)}) custom-call(s32[20]{0:T(128)} %copy-done.42, bf16[2048,768]{1,0:T(8,128)(2,1)} %x_ref.11, f32[4,512]{1,0:T(4,128)} %copy-done.31, ...), custom_call_target="tpu_custom_call", output_to_operand_aliasing={{0}: (19, {})} | custom-call | flops 1610612736 | bytes 16777216 | tf_op jit(solution)/shard_map/attend_back3/pallas_call | solution.py:455
  319.6 5.6 %attn_send.1 = bf16[4,384,896]{2,1,0:T(8,128)(2,1)} custom-call(s32[20]{0:T(128)S(1)} %copy-done.45, bf16[4,4,512,192]{3,2,1,0:T(8,128)(2,1)} %get-tuple-element.154.la.lb, bf16[4,4,512,192]{3,2,1,0:T(8,128)(2,1)} %get-tuple-element.154.la.lb, bf16[2,512,768]{2,1,0:T(8,128)(2,1)S(1)} %copy-done.3, bf16[2,512,768]{2,1,0:T(8,128)(2,1)S(1)} %copy-done.3, ...), custom_call_target="tpu_custom_call" | custom-call | flops 1048576 | bytes 65536 | tf_op jit(solution)/shard_map/attn_send/pallas_call | solution.py:888
  326.6 5.5 %collective-permute-start.24 = (bf16[528,768]{1,0:T(8,128)(2,1)S(1)}, bf16[528,768]{1,0:T(8,128)(2,1)}, u32[]{:S(2)}, u32[]{:S(2)}) collective-permute-start(bf16[528,768]{1,0:T(8,128)(2,1)S(1)} %copy-done.60), channel_id=1, source_target_pairs={{0,1},{1,2},{2,3},{4,5},{5,6},{6,7},{8,9},{9,10},{10,11},{12,13},{... | collective-permute-start | bytes 2433032 | tf_op jit(solution)/shard_map/ppermute | solution.py:1061
  332.2 2.4 collective-permute-start.47
  334.6 21.3 %collective-permute-done.46.refs_1_ = bf16[96,1536]{1,0:T(8,128)(2,1)S(1)} collective-permute-done((bf16[96,1536]{1,0:T(8,128)(2,1)S(1)}, bf16[96,1536]{1,0:T(8,128)(2,1)S(1)}, u32[]{:S(2)}, u32[]{:S(2)}) %collective-permute-start.46) | collective-permute-done | bytes 294944 | tf_op jit(solution)/shard_map/ppermute | solution.py:76
  355.9 13.1 %collective-permute-start.48 = (bf16[96,1536]{1,0:T(8,128)(2,1)S(1)}, bf16[96,1536]{1,0:T(8,128)(2,1)S(1)}, u32[]{:S(2)}, u32[]{:S(2)}) collective-permute-start(bf16[96,1536]{1,0:T(8,128)(2,1)S(1)} %copy-done.33), channel_id=1, source_target_pairs={{0,1},{1,2},{2,3},{3,0},{4,5},{5,6},{6,7},{7,4},{8,9},{9,10},{10,1... | collective-permute-start | bytes 884744 | tf_op jit(solution)/shard_map/ppermute | solution.py:76
  368.9 5.4 %collective-permute-done.47.refs_2_ = bf16[96,1536]{1,0:T(8,128)(2,1)S(1)} collective-permute-done((bf16[96,1536]{1,0:T(8,128)(2,1)S(1)}, bf16[96,1536]{1,0:T(8,128)(2,1)S(1)}, u32[]{:S(2)}, u32[]{:S(2)}) %collective-permute-start.47) | collective-permute-done | bytes 294944 | tf_op jit(solution)/shard_map/ppermute | solution.py:76
  376.5 5.5 %collective-permute-start.28 = (bf16[528,768]{1,0:T(8,128)(2,1)}, bf16[528,768]{1,0:T(8,128)(2,1)}, u32[]{:S(2)}, u32[]{:S(2)}) collective-permute-start(bf16[528,768]{1,0:T(8,128)(2,1)} %collective-permute-done.24), channel_id=1, source_target_pairs={{0,1},{1,2},{2,3},{4,5},{5,6},{6,7},{8,9},{9,10},{10,11},{12,13},{... | collective-permute-start | bytes 2433032 | tf_op jit(solution)/shard_map/ppermute | solution.py:1061
  382.0 14.9 %collective-permute-done.26 = bf16[528,768]{1,0:T(8,128)(2,1)} collective-permute-done((bf16[528,768]{1,0:T(8,128)(2,1)S(1)}, bf16[528,768]{1,0:T(8,128)(2,1)}, u32[]{:S(2)}, u32[]{:S(2)}) %collective-permute-start.26) | collective-permute-done | bytes 811040 | tf_op jit(solution)/shard_map/ppermute | solution.py:1062
  398.3 5.6 %collective-permute-start.29 = (bf16[528,768]{1,0:T(8,128)(2,1)}, bf16[528,768]{1,0:T(8,128)(2,1)}, u32[]{:S(2)}, u32[]{:S(2)}) collective-permute-start(bf16[528,768]{1,0:T(8,128)(2,1)} %collective-permute-done.28), channel_id=1, source_target_pairs={{0,1},{1,2},{2,3},{4,5},{5,6},{6,7},{8,9},{9,10},{10,11},{12,13},{... | collective-permute-start | bytes 2433032 | tf_op jit(solution)/shard_map/ppermute | solution.py:1061
  403.9 3.2 broadcast_in_dim.50
  408.5 5.7 %attn_keep.1 = (bf16[4,2,48,896]{3,2,1,0:T(8,128)(2,1)}, bf16[4,2,48,896]{3,2,1,0:T(8,128)(2,1)S(1)}, bf16[4,2,48,896]{3,2,1,0:T(8,128)(2,1)}, bf16[4,2,48,896]{3,2,1,0:T(8,128)(2,1)S(1)}) custom-call(s32[20]{0:T(128)S(1)} %copy-done.45, bf16[4,4,512,192]{3,2,1,0:T(8,128)(2,1)} %get-tuple-element.154.la.lb, ...), custom_call_target="tpu_custom_call" | custom-call | flops 1048576 | bytes 65536 | tf_op jit(solution)/shard_map/attn_keep/pallas_call | solution.py:888
  414.3 2.5 collective-permute-start.31
  422.5 1.9 add.103
  426.1 4.9 %collective-permute-done.31.ra = bf16[4,2,48,896]{3,2,1,0:T(8,128)(2,1)S(1)} collective-permute-done((bf16[4,2,48,896]{3,2,1,0:T(8,128)(2,1)}, bf16[4,2,48,896]{3,2,1,0:T(8,128)(2,1)S(1)}, u32[]{:S(2)}, u32[]{:S(2)}) %collective-permute-start.31) | collective-permute-done | bytes 688160 | tf_op jit(solution)/shard_map/ppermute | solution.py:72
  432.5 2.1 second_sums.5
  436.5 6.3 %collective-permute-done.33.ra = bf16[4,48,896]{2,1,0:T(8,128)(2,1)S(1)} collective-permute-done((bf16[4,48,896]{2,1,0:T(8,128)(2,1)}, bf16[4,48,896]{2,1,0:T(8,128)(2,1)S(1)}, u32[]{:S(2)}, u32[]{:S(2)}) %collective-permute-start.33) | collective-permute-done | bytes 344096 | tf_op jit(solution)/shard_map/ppermute | solution.py:72
  446.9 1.9 collective-permute-start.37
  448.8 2.4 convert_dynamic-update-slice_fusion.2
  452.1 5.9 %collective-permute-done.36.refs_2_ = bf16[96,896]{1,0:T(8,128)(2,1)S(1)} collective-permute-done((bf16[96,896]{1,0:T(8,128)(2,1)S(1)}, bf16[96,896]{1,0:T(8,128)(2,1)S(1)}, u32[]{:S(2)}, u32[]{:S(2)}) %collective-permute-start.36) | collective-permute-done | bytes 172064 | tf_op jit(solution)/shard_map/ppermute | solution.py:76
  472.0 2.2 unpack.1
  476.0 2.3 convert_bitcast_fusion
  478.7 2.5 fusion.5
  (274 shorter events, 90.9 us)
Async XLA Ops:
  7.2 131.7 %all-gather.9.cloned.1.call-start = ((), (), s32[]{:S(2)}) async-start(), calls=%async_computation | async-start | bytes 4866048 | tf_op jit(solution)/shard_map/all_gather | solution.py:1107
  9.2 214.6 %all-gather.11.cloned.1.call-start = ((), (), s32[]{:S(2)}) async-start(), calls=%async_computation.1 | async-start | bytes 4055040 | tf_op jit(solution)/shard_map/all_gather | solution.py:1107
  12.4 33.9 %collective-permute-start.3 = (bf16[96,1728]{1,0:T(8,128)(2,1)}, bf16[96,1728]{1,0:T(8,128)(2,1)}, u32[]{:S(2)}, u32[]{:S(2)}) collective-permute-start(bf16[96,1728]{1,0:T(8,128)(2,1)} %pad_maximum_fusion), channel_id=1, source_target_pairs={{0,1},{1,2},{2,3},{3,0},{4,5},{5,6},{6,7},{7,4},{8,9},{9,10},{10,1... | collective-permute-start | bytes 995336 | tf_op jit(solution)/shard_map/ppermute | solution.py:76
  15.4 30.9 %collective-permute-start.4 = (bf16[96,1728]{1,0:T(8,128)(2,1)}, bf16[96,1728]{1,0:T(8,128)(2,1)}, u32[]{:S(2)}, u32[]{:S(2)}) collective-permute-start(bf16[96,1728]{1,0:T(8,128)(2,1)} %pad_maximum_fusion), channel_id=1, source_target_pairs={{0,2},{1,3},{2,0},{3,1},{4,6},{5,7},{6,4},{7,5},{8,10},{9,11},{10,... | collective-permute-start | bytes 995336 | tf_op jit(solution)/shard_map/ppermute | solution.py:76
  18.0 28.3 %collective-permute-start.5 = (bf16[96,1728]{1,0:T(8,128)(2,1)}, bf16[96,1728]{1,0:T(8,128)(2,1)}, u32[]{:S(2)}, u32[]{:S(2)}) collective-permute-start(bf16[96,1728]{1,0:T(8,128)(2,1)} %pad_maximum_fusion), channel_id=1, source_target_pairs={{0,3},{1,0},{2,1},{3,2},{4,7},{5,4},{6,5},{7,6},{8,11},{9,8},{10,9... | collective-permute-start | bytes 995336 | tf_op jit(solution)/shard_map/ppermute | solution.py:76
  47.6 31.7 %collective-permute-start.6 = (bf16[3,48,1728]{2,1,0:T(8,128)(2,1)S(1)}, bf16[3,48,1728]{2,1,0:T(8,128)(2,1)S(1)}, u32[]{:S(2)}, u32[]{:S(2)}) collective-permute-start(bf16[3,48,1728]{2,1,0:T(8,128)(2,1)S(1)} %get-tuple-element.102.a), channel_id=1, source_target_pairs={{0,8},{8,0},{1,9},{9,1},{2,10},{10,2},{3,11},{11,3},{4,12},{12,4},... | collective-permute-start | bytes 1493000 | tf_op jit(solution)/shard_map/ppermute | solution.py:72
  49.2 30.1 %collective-permute-start.7 = (bf16[3,48,1728]{2,1,0:T(8,128)(2,1)S(1)}, bf16[3,48,1728]{2,1,0:T(8,128)(2,1)S(1)}, u32[]{:S(2)}, u32[]{:S(2)}) collective-permute-start(bf16[3,48,1728]{2,1,0:T(8,128)(2,1)S(1)} %get-tuple-element.103.b), channel_id=1, source_target_pairs={{0,16},{16,0},{1,17},{17,1},{2,18},{18,2},{3,19},{19,3},{4,20},{20... | collective-permute-start | bytes 1493000 | tf_op jit(solution)/shard_map/ppermute | solution.py:72
  51.5 15.5 %collective-permute-start = (bf16[528,192]{1,0:T(8,128)(2,1)S(1)}, bf16[528,192]{1,0:T(8,128)(2,1)S(1)}, u32[]{:S(2)}, u32[]{:S(2)}) collective-permute-start(bf16[528,192]{1,0:T(8,128)(2,1)S(1)} %get-tuple-element.241), channel_id=1, source_target_pairs={{0,1},{1,2},{2,3},{3,0},{4,5},{5,6},{6,7},{7,4},{8,9},{9,10},{10,1... | collective-permute-start | bytes 608264 | tf_op jit(solution)/shard_map/ppermute | solution.py:76
  56.8 22.5 %collective-permute-start.1 = (bf16[528,192]{1,0:T(8,128)(2,1)S(1)}, bf16[528,192]{1,0:T(8,128)(2,1)S(1)}, u32[]{:S(2)}, u32[]{:S(2)}) collective-permute-start(bf16[528,192]{1,0:T(8,128)(2,1)S(1)} %get-tuple-element.240), channel_id=1, source_target_pairs={{0,2},{1,3},{2,0},{3,1},{4,6},{5,7},{6,4},{7,5},{8,10},{9,11},{10,... | collective-permute-start | bytes 608264 | tf_op jit(solution)/shard_map/ppermute | solution.py:76
  58.4 20.8 %collective-permute-start.2 = (bf16[528,192]{1,0:T(8,128)(2,1)S(1)}, bf16[528,192]{1,0:T(8,128)(2,1)S(1)}, u32[]{:S(2)}, u32[]{:S(2)}) collective-permute-start(bf16[528,192]{1,0:T(8,128)(2,1)S(1)} %get-tuple-element.239), channel_id=1, source_target_pairs={{0,3},{1,0},{2,1},{3,2},{4,7},{5,4},{6,5},{7,6},{8,11},{9,8},{10,9... | collective-permute-start | bytes 608264 | tf_op jit(solution)/shard_map/ppermute | solution.py:76
  79.5 33.2 %collective-permute-start.8 = (bf16[2,3,48,1728]{3,2,1,0:T(8,128)(2,1)S(1)}, bf16[2,3,48,1728]{3,2,1,0:T(8,128)(2,1)}, u32[]{:S(2)}, u32[]{:S(2)}) collective-permute-start(bf16[2,3,48,1728]{3,2,1,0:T(8,128)(2,1)S(1)} %get-tuple-element.104.refs_7_.refs_3_), channel_id=1, source_target_pairs={{0,16},{16,0},{1,17},{17,1},{2,18},{18,2},{3,19},{19,3},{4,20},{20... | collective-permute-start | bytes 2985992 | tf_op jit(solution)/shard_map/ppermute | solution.py:72
  80.8 32.8 %collective-permute-start.9 = (bf16[2,3,48,1728]{3,2,1,0:T(8,128)(2,1)S(1)}, bf16[2,3,48,1728]{3,2,1,0:T(8,128)(2,1)}, u32[]{:S(2)}, u32[]{:S(2)}) collective-permute-start(bf16[2,3,48,1728]{3,2,1,0:T(8,128)(2,1)S(1)} %get-tuple-element.105.refs_8_.refs_4_), channel_id=1, source_target_pairs={{0,8},{8,0},{1,9},{9,1},{2,10},{10,2},{3,11},{11,3},{4,12},{12,4},... | collective-permute-start | bytes 2985992 | tf_op jit(solution)/shard_map/ppermute | solution.py:72
  81.9 35.6 %collective-permute-start.10 = (bf16[2,3,48,1728]{3,2,1,0:T(8,128)(2,1)S(1)}, bf16[2,3,48,1728]{3,2,1,0:T(8,128)(2,1)}, u32[]{:S(2)}, u32[]{:S(2)}) collective-permute-start(bf16[2,3,48,1728]{3,2,1,0:T(8,128)(2,1)S(1)} %get-tuple-element.104.refs_7_.refs_3_), channel_id=1, source_target_pairs={{0,4},{4,0},{1,5},{5,1},{2,6},{6,2},{3,7},{7,3},{8,12},{12,8},{9,1... | collective-permute-start | bytes 2985992 | tf_op jit(solution)/shard_map/ppermute | solution.py:72
  81.9 35.6 %collective-permute-start.11 = (bf16[2,3,48,1728]{3,2,1,0:T(8,128)(2,1)S(1)}, bf16[2,3,48,1728]{3,2,1,0:T(8,128)(2,1)}, u32[]{:S(2)}, u32[]{:S(2)}) collective-permute-start(bf16[2,3,48,1728]{3,2,1,0:T(8,128)(2,1)S(1)} %get-tuple-element.105.refs_8_.refs_4_), channel_id=1, source_target_pairs={{0,4},{4,0},{1,5},{5,1},{2,6},{6,2},{3,7},{7,3},{8,12},{12,8},{9,1... | collective-permute-start | bytes 2985992 | tf_op jit(solution)/shard_map/ppermute | solution.py:72
  115.2 301.5 %all-gather.15.cloned.1.call-start = ((), (), s32[]{:S(2)}) async-start(), calls=%async_computation.3 | async-start | bytes 1548288 | tf_op jit(solution)/shard_map/all_gather | solution.py:1020
  179.9 20.9 %collective-permute-start.14 = (bf16[4,384,1536]{2,1,0:T(8,128)(2,1)}, bf16[4,384,1536]{2,1,0:T(8,128)(2,1)S(1)}, u32[]{:S(2)}, u32[]{:S(2)}) collective-permute-start(bf16[4,384,1536]{2,1,0:T(8,128)(2,1)} %products_send.2), channel_id=1, source_target_pairs={{0,4},{4,0},{1,5},{5,1},{2,6},{6,2},{3,7},{7,3},{8,12},{12,8},{9,1... | collective-permute-start | bytes 14155784 | tf_op jit(solution)/shard_map/ppermute | solution.py:72
  184.9 7.0 %collective-permute-start.15 = (bf16[4,384,896]{2,1,0:T(8,128)(2,1)S(1)}, bf16[4,384,896]{2,1,0:T(8,128)(2,1)S(1)}, u32[]{:S(2)}, u32[]{:S(2)}) collective-permute-start(bf16[4,384,896]{2,1,0:T(8,128)(2,1)S(1)} %products_send.3), channel_id=1, source_target_pairs={{0,4},{4,0},{1,5},{5,1},{2,6},{6,2},{3,7},{7,3},{8,12},{12,8},{9,1... | collective-permute-start | bytes 8257544 | tf_op jit(solution)/shard_map/ppermute | solution.py:72
  198.6 18.3 %collective-permute-start.16 = (bf16[4,2,48,896]{3,2,1,0:T(8,128)(2,1)S(1)}, bf16[4,2,48,896]{3,2,1,0:T(8,128)(2,1)S(1)}, u32[]{:S(2)}, u32[]{:S(2)}) collective-permute-start(bf16[4,2,48,896]{3,2,1,0:T(8,128)(2,1)S(1)} %get-tuple-element.120), channel_id=1, source_target_pairs={{0,8},{8,0},{1,9},{9,1},{2,10},{10,2},{3,11},{11,3},{4,12},{12,4},... | collective-permute-start | bytes 2064392 | tf_op jit(solution)/shard_map/ppermute | solution.py:72
  199.7 18.3 %collective-permute-start.17 = (bf16[4,2,48,896]{3,2,1,0:T(8,128)(2,1)S(1)}, bf16[4,2,48,896]{3,2,1,0:T(8,128)(2,1)S(1)}, u32[]{:S(2)}, u32[]{:S(2)}) collective-permute-start(bf16[4,2,48,896]{3,2,1,0:T(8,128)(2,1)S(1)} %get-tuple-element.122), channel_id=1, source_target_pairs={{0,16},{16,0},{1,17},{17,1},{2,18},{18,2},{3,19},{19,3},{4,20},{20... | collective-permute-start | bytes 2064392 | tf_op jit(solution)/shard_map/ppermute | solution.py:72
  210.0 64.6 %collective-permute-start.20 = (bf16[4,2,48,1536]{3,2,1,0:T(8,128)(2,1)S(1)}, bf16[4,2,48,1536]{3,2,1,0:T(8,128)(2,1)}, u32[]{:S(2)}, u32[]{:S(2)}) collective-permute-start(bf16[4,2,48,1536]{3,2,1,0:T(8,128)(2,1)S(1)} %get-tuple-element.114.refs_0_.refs_1_), channel_id=1, source_target_pairs={{0,8},{8,0},{1,9},{9,1},{2,10},{10,2},{3,11},{11,3},{4,12},{12,4},... | collective-permute-start | bytes 3538952 | tf_op jit(solution)/shard_map/ppermute | solution.py:72
  210.8 63.8 %collective-permute-start.21 = (bf16[4,2,48,1536]{3,2,1,0:T(8,128)(2,1)S(1)}, bf16[4,2,48,1536]{3,2,1,0:T(8,128)(2,1)}, u32[]{:S(2)}, u32[]{:S(2)}) collective-permute-start(bf16[4,2,48,1536]{3,2,1,0:T(8,128)(2,1)S(1)} %get-tuple-element.115.refs_1_.refs_2_), channel_id=1, source_target_pairs={{0,16},{16,0},{1,17},{17,1},{2,18},{18,2},{3,19},{19,3},{4,20},{20... | collective-permute-start | bytes 3538952 | tf_op jit(solution)/shard_map/ppermute | solution.py:72
  221.9 28.0 %collective-permute-start.18 = (bf16[4,48,896]{2,1,0:T(8,128)(2,1)}, bf16[4,48,896]{2,1,0:T(8,128)(2,1)}, u32[]{:S(2)}, u32[]{:S(2)}) collective-permute-start(bf16[4,48,896]{2,1,0:T(8,128)(2,1)} %get-tuple-element.123.refs_3_), channel_id=1, source_target_pairs={{0,16},{16,0},{1,17},{17,1},{2,18},{18,2},{3,19},{19,3},{4,20},{20... | collective-permute-start | bytes 1032200 | tf_op jit(solution)/shard_map/ppermute | solution.py:72
  223.0 26.9 %collective-permute-start.19 = (bf16[4,48,896]{2,1,0:T(8,128)(2,1)}, bf16[4,48,896]{2,1,0:T(8,128)(2,1)}, u32[]{:S(2)}, u32[]{:S(2)}) collective-permute-start(bf16[4,48,896]{2,1,0:T(8,128)(2,1)} %get-tuple-element.124.refs_4_), channel_id=1, source_target_pairs={{0,8},{8,0},{1,9},{9,1},{2,10},{10,2},{3,11},{11,3},{4,12},{12,4},... | collective-permute-start | bytes 1032200 | tf_op jit(solution)/shard_map/ppermute | solution.py:72
  251.9 20.3 %collective-permute-start.49 = (bf16[96,896]{1,0:T(8,128)(2,1)S(1)}, bf16[96,896]{1,0:T(8,128)(2,1)S(1)}, u32[]{:S(2)}, u32[]{:S(2)}) collective-permute-start(bf16[96,896]{1,0:T(8,128)(2,1)S(1)} %get-tuple-element.130.refs_3_), channel_id=1, source_target_pairs={{0,3},{1,0},{2,1},{3,2},{4,7},{5,4},{6,5},{7,6},{8,11},{9,8},{10,9... | collective-permute-start | bytes 516104 | tf_op jit(solution)/shard_map/ppermute | solution.py:76
  257.8 15.3 %collective-permute-start.50 = (bf16[96,896]{1,0:T(8,128)(2,1)S(1)}, bf16[96,896]{1,0:T(8,128)(2,1)S(1)}, u32[]{:S(2)}, u32[]{:S(2)}) collective-permute-start(bf16[96,896]{1,0:T(8,128)(2,1)S(1)} %get-tuple-element.131.refs_4_), channel_id=1, source_target_pairs={{0,2},{1,3},{2,0},{3,1},{4,6},{5,7},{6,4},{7,5},{8,10},{9,11},{10,... | collective-permute-start | bytes 516104 | tf_op jit(solution)/shard_map/ppermute | solution.py:76
  258.6 14.4 %collective-permute-start.51 = (bf16[96,896]{1,0:T(8,128)(2,1)S(1)}, bf16[96,896]{1,0:T(8,128)(2,1)S(1)}, u32[]{:S(2)}, u32[]{:S(2)}) collective-permute-start(bf16[96,896]{1,0:T(8,128)(2,1)S(1)} %get-tuple-element.132.refs_5_), channel_id=1, source_target_pairs={{0,1},{1,2},{2,3},{3,0},{4,5},{5,6},{6,7},{7,4},{8,9},{9,10},{10,1... | collective-permute-start | bytes 516104 | tf_op jit(solution)/shard_map/ppermute | solution.py:76
  274.6 201.5 %all-gather.13.cloned.1.call-start = ((), (), s32[]{:S(2)}) async-start(), calls=%async_computation.2 | async-start | bytes 2654208 | tf_op jit(solution)/shard_map/all_gather | solution.py:1020
  280.0 15.9 %collective-permute-start.22 = (bf16[4,48,1536]{2,1,0:T(8,128)(2,1)S(1)}, bf16[4,48,1536]{2,1,0:T(8,128)(2,1)S(1)}, u32[]{:S(2)}, u32[]{:S(2)}) collective-permute-start(bf16[4,48,1536]{2,1,0:T(8,128)(2,1)S(1)} %get-tuple-element.138.refs_3_), channel_id=1, source_target_pairs={{0,16},{16,0},{1,17},{17,1},{2,18},{18,2},{3,19},{19,3},{4,20},{20... | collective-permute-start | bytes 1769480 | tf_op jit(solution)/shard_map/ppermute | solution.py:72
  280.6 18.0 %collective-permute-start.23 = (bf16[4,48,1536]{2,1,0:T(8,128)(2,1)S(1)}, bf16[4,48,1536]{2,1,0:T(8,128)(2,1)S(1)}, u32[]{:S(2)}, u32[]{:S(2)}) collective-permute-start(bf16[4,48,1536]{2,1,0:T(8,128)(2,1)S(1)} %get-tuple-element.139.refs_4_), channel_id=1, source_target_pairs={{0,8},{8,0},{1,9},{9,1},{2,10},{10,2},{3,11},{11,3},{4,12},{12,4},... | collective-permute-start | bytes 1769480 | tf_op jit(solution)/shard_map/ppermute | solution.py:72
  325.3 83.1 %collective-permute-start.30 = (bf16[4,384,896]{2,1,0:T(8,128)(2,1)}, bf16[4,384,896]{2,1,0:T(8,128)(2,1)}, u32[]{:S(2)}, u32[]{:S(2)}) collective-permute-start(bf16[4,384,896]{2,1,0:T(8,128)(2,1)} %attn_send.1), channel_id=1, source_target_pairs={{0,4},{4,0},{1,5},{5,1},{2,6},{6,2},{3,7},{7,3},{8,12},{12,8},{9,1... | collective-permute-start | bytes 8257544 | tf_op jit(solution)/shard_map/ppermute | solution.py:72
  325.3 49.9 %collective-permute-start.25 = (bf16[528,768]{1,0:T(8,128)(2,1)S(1)}, bf16[528,768]{1,0:T(8,128)(2,1)S(1)}, u32[]{:S(2)}, u32[]{:S(2)}) collective-permute-start(bf16[528,768]{1,0:T(8,128)(2,1)S(1)} %copy-done.60), channel_id=1, source_target_pairs={{1,0},{2,1},{3,2},{5,4},{6,5},{7,6},{9,8},{10,9},{11,10},{13,12},{... | collective-permute-start | bytes 2433032 | tf_op jit(solution)/shard_map/ppermute | solution.py:1062
  326.6 49.9 %collective-permute-start.24 = (bf16[528,768]{1,0:T(8,128)(2,1)S(1)}, bf16[528,768]{1,0:T(8,128)(2,1)}, u32[]{:S(2)}, u32[]{:S(2)}) collective-permute-start(bf16[528,768]{1,0:T(8,128)(2,1)S(1)} %copy-done.60), channel_id=1, source_target_pairs={{0,1},{1,2},{2,3},{4,5},{5,6},{6,7},{8,9},{9,10},{10,11},{12,13},{... | collective-permute-start | bytes 2433032 | tf_op jit(solution)/shard_map/ppermute | solution.py:1061
  332.1 23.8 %collective-permute-start.46 = (bf16[96,1536]{1,0:T(8,128)(2,1)S(1)}, bf16[96,1536]{1,0:T(8,128)(2,1)S(1)}, u32[]{:S(2)}, u32[]{:S(2)}) collective-permute-start(bf16[96,1536]{1,0:T(8,128)(2,1)S(1)} %copy-done.37), channel_id=1, source_target_pairs={{0,3},{1,0},{2,1},{3,2},{4,7},{5,4},{6,5},{7,6},{8,11},{9,8},{10,9... | collective-permute-start | bytes 884744 | tf_op jit(solution)/shard_map/ppermute | solution.py:76
  332.2 42.1 %collective-permute-start.47 = (bf16[96,1536]{1,0:T(8,128)(2,1)S(1)}, bf16[96,1536]{1,0:T(8,128)(2,1)S(1)}, u32[]{:S(2)}, u32[]{:S(2)}) collective-permute-start(bf16[96,1536]{1,0:T(8,128)(2,1)S(1)} %copy-done.35), channel_id=1, source_target_pairs={{0,2},{1,3},{2,0},{3,1},{4,6},{5,7},{6,4},{7,5},{8,10},{9,11},{10,... | collective-permute-start | bytes 884744 | tf_op jit(solution)/shard_map/ppermute | solution.py:76
  355.9 18.4 %collective-permute-start.48 = (bf16[96,1536]{1,0:T(8,128)(2,1)S(1)}, bf16[96,1536]{1,0:T(8,128)(2,1)S(1)}, u32[]{:S(2)}, u32[]{:S(2)}) collective-permute-start(bf16[96,1536]{1,0:T(8,128)(2,1)S(1)} %copy-done.33), channel_id=1, source_target_pairs={{0,1},{1,2},{2,3},{3,0},{4,5},{5,6},{6,7},{7,4},{8,9},{9,10},{10,1... | collective-permute-start | bytes 884744 | tf_op jit(solution)/shard_map/ppermute | solution.py:76
  375.2 21.7 %collective-permute-start.26 = (bf16[528,768]{1,0:T(8,128)(2,1)S(1)}, bf16[528,768]{1,0:T(8,128)(2,1)}, u32[]{:S(2)}, u32[]{:S(2)}) collective-permute-start(bf16[528,768]{1,0:T(8,128)(2,1)S(1)} %collective-permute-done.25), channel_id=1, source_target_pairs={{1,0},{2,1},{3,2},{5,4},{6,5},{7,6},{9,8},{10,9},{11,10},{13,12},{... | collective-permute-start | bytes 2433032 | tf_op jit(solution)/shard_map/ppermute | solution.py:1062
  376.5 21.8 %collective-permute-start.28 = (bf16[528,768]{1,0:T(8,128)(2,1)}, bf16[528,768]{1,0:T(8,128)(2,1)}, u32[]{:S(2)}, u32[]{:S(2)}) collective-permute-start(bf16[528,768]{1,0:T(8,128)(2,1)} %collective-permute-done.24), channel_id=1, source_target_pairs={{0,1},{1,2},{2,3},{4,5},{5,6},{6,7},{8,9},{9,10},{10,11},{12,13},{... | collective-permute-start | bytes 2433032 | tf_op jit(solution)/shard_map/ppermute | solution.py:1061
  396.9 25.6 %collective-permute-start.27 = (bf16[528,768]{1,0:T(8,128)(2,1)}, bf16[528,768]{1,0:T(8,128)(2,1)}, u32[]{:S(2)}, u32[]{:S(2)}) collective-permute-start(bf16[528,768]{1,0:T(8,128)(2,1)} %collective-permute-done.26), channel_id=1, source_target_pairs={{1,0},{2,1},{3,2},{5,4},{6,5},{7,6},{9,8},{10,9},{11,10},{13,12},{... | collective-permute-start | bytes 2433032 | tf_op jit(solution)/shard_map/ppermute | solution.py:1062
  398.3 26.1 %collective-permute-start.29 = (bf16[528,768]{1,0:T(8,128)(2,1)}, bf16[528,768]{1,0:T(8,128)(2,1)}, u32[]{:S(2)}, u32[]{:S(2)}) collective-permute-start(bf16[528,768]{1,0:T(8,128)(2,1)} %collective-permute-done.28), channel_id=1, source_target_pairs={{0,1},{1,2},{2,3},{4,5},{5,6},{6,7},{8,9},{9,10},{10,11},{12,13},{... | collective-permute-start | bytes 2433032 | tf_op jit(solution)/shard_map/ppermute | solution.py:1061
  414.3 16.8 %collective-permute-start.31 = (bf16[4,2,48,896]{3,2,1,0:T(8,128)(2,1)}, bf16[4,2,48,896]{3,2,1,0:T(8,128)(2,1)S(1)}, u32[]{:S(2)}, u32[]{:S(2)}) collective-permute-start(bf16[4,2,48,896]{3,2,1,0:T(8,128)(2,1)} %get-tuple-element.158), channel_id=1, source_target_pairs={{0,8},{8,0},{1,9},{9,1},{2,10},{10,2},{3,11},{11,3},{4,12},{12,4},... | collective-permute-start | bytes 2064392 | tf_op jit(solution)/shard_map/ppermute | solution.py:72
  416.7 15.8 %collective-permute-start.32 = (bf16[4,2,48,896]{3,2,1,0:T(8,128)(2,1)}, bf16[4,2,48,896]{3,2,1,0:T(8,128)(2,1)S(1)}, u32[]{:S(2)}, u32[]{:S(2)}) collective-permute-start(bf16[4,2,48,896]{3,2,1,0:T(8,128)(2,1)} %get-tuple-element.160), channel_id=1, source_target_pairs={{0,16},{16,0},{1,17},{17,1},{2,18},{18,2},{3,19},{19,3},{4,20},{20... | collective-permute-start | bytes 2064392 | tf_op jit(solution)/shard_map/ppermute | solution.py:72
  435.3 7.5 %collective-permute-start.33 = (bf16[4,48,896]{2,1,0:T(8,128)(2,1)}, bf16[4,48,896]{2,1,0:T(8,128)(2,1)S(1)}, u32[]{:S(2)}, u32[]{:S(2)}) collective-permute-start(bf16[4,48,896]{2,1,0:T(8,128)(2,1)} %get-tuple-element.162), channel_id=1, source_target_pairs={{0,16},{16,0},{1,17},{17,1},{2,18},{18,2},{3,19},{19,3},{4,20},{20... | collective-permute-start | bytes 1032200 | tf_op jit(solution)/shard_map/ppermute | solution.py:72
  435.6 7.5 %collective-permute-start.34 = (bf16[4,48,896]{2,1,0:T(8,128)(2,1)}, bf16[4,48,896]{2,1,0:T(8,128)(2,1)S(1)}, u32[]{:S(2)}, u32[]{:S(2)}) collective-permute-start(bf16[4,48,896]{2,1,0:T(8,128)(2,1)} %get-tuple-element.164), channel_id=1, source_target_pairs={{0,8},{8,0},{1,9},{9,1},{2,10},{10,2},{3,11},{11,3},{4,12},{12,4},... | collective-permute-start | bytes 1032200 | tf_op jit(solution)/shard_map/ppermute | solution.py:72
  444.2 7.9 %collective-permute-start.35 = (bf16[96,896]{1,0:T(8,128)(2,1)S(1)}, bf16[96,896]{1,0:T(8,128)(2,1)S(1)}, u32[]{:S(2)}, u32[]{:S(2)}) collective-permute-start(bf16[96,896]{1,0:T(8,128)(2,1)S(1)} %get-tuple-element.166), channel_id=1, source_target_pairs={{0,3},{1,0},{2,1},{3,2},{4,7},{5,4},{6,5},{7,6},{8,11},{9,8},{10,9... | collective-permute-start | bytes 516104 | tf_op jit(solution)/shard_map/ppermute | solution.py:76
  445.9 12.1 %collective-permute-start.36 = (bf16[96,896]{1,0:T(8,128)(2,1)S(1)}, bf16[96,896]{1,0:T(8,128)(2,1)S(1)}, u32[]{:S(2)}, u32[]{:S(2)}) collective-permute-start(bf16[96,896]{1,0:T(8,128)(2,1)S(1)} %get-tuple-element.167), channel_id=1, source_target_pairs={{0,2},{1,3},{2,0},{3,1},{4,6},{5,7},{6,4},{7,5},{8,10},{9,11},{10,... | collective-permute-start | bytes 516104 | tf_op jit(solution)/shard_map/ppermute | solution.py:76
  446.9 11.1 %collective-permute-start.37 = (bf16[96,896]{1,0:T(8,128)(2,1)S(1)}, bf16[96,896]{1,0:T(8,128)(2,1)S(1)}, u32[]{:S(2)}, u32[]{:S(2)}) collective-permute-start(bf16[96,896]{1,0:T(8,128)(2,1)S(1)} %get-tuple-element.168), channel_id=1, source_target_pairs={{0,1},{1,2},{2,3},{3,0},{4,5},{5,6},{6,7},{7,4},{8,9},{9,10},{10,1... | collective-permute-start | bytes 516104 | tf_op jit(solution)/shard_map/ppermute | solution.py:76
  463.5 5.5 %collective-permute-start.40 = (bf16[2,48,896]{2,1,0:T(8,128)(2,1)S(1)}, bf16[2,48,896]{2,1,0:T(8,128)(2,1)S(1)}, u32[]{:S(2)}, u32[]{:S(2)}) collective-permute-start(bf16[2,48,896]{2,1,0:T(8,128)(2,1)S(1)} %get-tuple-element.169.refs_0_), channel_id=1, source_target_pairs={{0,16},{16,0},{1,17},{17,1},{2,18},{18,2},{3,19},{19,3},{4,20},{20... | collective-permute-start | bytes 516104 | tf_op jit(solution)/shard_map/ppermute | solution.py:72
  465.1 5.4 %collective-permute-start.41 = (bf16[2,48,896]{2,1,0:T(8,128)(2,1)S(1)}, bf16[2,48,896]{2,1,0:T(8,128)(2,1)S(1)}, u32[]{:S(2)}, u32[]{:S(2)}) collective-permute-start(bf16[2,48,896]{2,1,0:T(8,128)(2,1)S(1)} %get-tuple-element.170.refs_1_), channel_id=1, source_target_pairs={{0,8},{8,0},{1,9},{9,1},{2,10},{10,2},{3,11},{11,3},{4,12},{12,4},... | collective-permute-start | bytes 516104 | tf_op jit(solution)/shard_map/ppermute | solution.py:72
  (75 other events, 1028.2 us)
Sparse Core Ops, SparseCore 0:
  11.4 101.0 all-gather.8
  115.3 64.2 all-gather.10
  274.7 27.0 all-gather.14
  375.3 30.3 all-gather.12

commit v2 on v1

v2 whole, which is shorter than its diff:
```python
import functools
import math

import jax
import jax.numpy as jnp
import numpy as np
from jax import lax
from jax.experimental import pallas as pl
from jax.experimental.pallas import tpu as pltpu
from jax.sharding import Mesh
from jax.sharding import PartitionSpec as P

f32 = jnp.float32
bf16 = jnp.bfloat16
eps = 1e-06
masked_logit = -1e30
gelu_c = math.sqrt(2.0 / math.pi)
CORE, XBIT, YBIT = "core", "x", "y"
group = ("y", "x", "core")
dp = ("out",) + group
span = 1024
tile = 128


def bucket_hot(buckets, length):
    column = np.arange(span)
    base = length - tile
    offset = np.where(column < base + length, column - base, column - span - base)
    distance = np.abs(offset)
    far = 8 + sum((distance >= t).astype(np.int32) for t in (12, 16, 23, 32, 46, 64, 91))
    bucket = np.where(distance < 8, distance, far) + 16 * (offset > 0)
    hot = (bucket[None, :] == np.arange(tile)[:, None]) & (np.arange(tile)[:, None] < buckets)
    return hot.astype(np.float32)


def dot(a, b, dims=((1,), (0,))):
    return lax.dot_general(a, b, (dims, ((), ())), preferred_element_type=f32)


def rms_scale(v):
    return lax.rsqrt(jnp.mean(v * v, axis=-1, keepdims=True) + eps)


def rms_back(v, gain, grad):
    s = rms_scale(v)
    w = grad * gain
    value = s * w - v * ((s * s * s) * jnp.mean(w * v, axis=-1, keepdims=True))
    return value, jnp.sum(grad * v * s, axis=0, keepdims=True)


def whole(shape):
    return pl.BlockSpec(shape, lambda *_: (0,) * len(shape))


ANY = pl.BlockSpec(memory_space=pl.ANY)
token_shape = (8, 128)


def launch(
    kernel, name, args, in_specs, out_specs, out_shape, grid=(1,), offs=None, scratch=(),
    cost=None, after=(), alias=None, n_alias=1, mib=16,
):
    first = 0 if offs is None else 1
    n_in, n_out, n_after = first + len(args), len(out_shape), len(after)

    def body(*refs):
        ins, rest = refs[:n_in], refs[n_in + n_after :]
        outs, token, own = rest[:n_out], rest[n_out], rest[n_out + 1 :]
        token[...] = jnp.zeros(token_shape, f32)
        kernel(*ins, *outs, *own)

    specs = dict(
        grid=grid,
        in_specs=list(in_specs) + [ANY] * n_after,
        out_specs=list(out_specs) + [whole(token_shape)],
        scratch_shapes=list(scratch),
    )
    if offs is None:
        specs = dict(specs)
        scalars = []
    else:
        specs = dict(grid_spec=pltpu.PrefetchScalarGridSpec(num_scalar_prefetch=1, **specs))
        scalars = [offs]
    *outs, token = pl.pallas_call(
        body,
        out_shape=list(out_shape) + [jax.ShapeDtypeStruct(token_shape, f32)],
        input_output_aliases=(
            {} if alias is None else {alias + first + i: i for i in range(n_alias)}
        ),
        compiler_params=pltpu.CompilerParams(
            vmem_limit_bytes=mib << 20, dimension_semantics=("arbitrary",)
        ),
        cost_estimate=cost or cheap,
        name=name,
        **specs,
    )(*scalars, *args, *after)
    return outs, token


cheap = pl.CostEstimate(flops=1 << 20, bytes_accessed=1 << 16, transcendentals=0)


def cost(flops, mib, transcendentals=0):
    return pl.CostEstimate(
        flops=flops, bytes_accessed=mib << 20, transcendentals=transcendentals
    )


def like(dtype, *shapes):
    return [jax.ShapeDtypeStruct(shape, dtype) for shape in shapes]


class Place:
    def __init__(self):
        self.n_out, self.n_mp = lax.axis_size("out"), lax.axis_size("mp")
        self.c, self.x, self.y = (lax.axis_index(name) for name in ("core", "x", "y"))
        self.z = lax.axis_index("mp")
        self.p = self.c * 4 + self.y * 2 + self.x

    def swap(self, v, name):
        return lax.ppermute(v, name, [(0, 1), (1, 0)])

    def shift(self, v, k):
        n = self.n_mp
        return lax.ppermute(v, "mp", [(i, (i + k) % n) for i in range(n)])

    def offsets(self, rows):
        half = rows // 2
        out = []
        for flip in (0, 4):
            p = self.p ^ flip
            for other, extra in (
                (0, 0), (1, 0), (0, half), (2, half), (2, 0), (3, 0), (1, half), (3, half),
            ):
                out.append((p ^ other) * rows + extra)
        return jnp.stack(out + [self.z, self.c, self.x, self.y]).astype(jnp.int32)

    def both_ways(self, right, left):
        n = self.n_mp
        right = lax.ppermute(right, "mp", [(i, i + 1) for i in range(n - 1)])
        return right, lax.ppermute(left, "mp", [(i + 1, i) for i in range(n - 1)])

    def first_round(self, a, b, after=()):
        return stack_pairs(a, self.swap(a, XBIT), b, self.swap(b, YBIT), after)

    def second_round(self, sa, sb, after=()):
        ya, xb = self.swap(sa, YBIT), self.swap(sb, XBIT)
        if after:
            ya, xb = relay(ya, xb, after)
        near = [sa, sb, ya, xb]
        return near + [self.swap(t, CORE) for t in near]


def pick(v, axis, index):
    return lax.dynamic_index_in_dim(v, index, axis, keepdims=False)


def halves(v, axis):
    half = v.shape[axis] // 2
    return (
        lax.slice_in_dim(v, 0, half, axis=axis),
        lax.slice_in_dim(v, half, 2 * half, axis=axis),
    )


def chunk_copies(offs, own, arrays, dst, sems, first=0, slot=0):
    slots, rows, width = dst.shape
    half = rows // 16
    skip = 0 if slot else 1
    pairs = [
        (ref, dst.at[0, :, pl.ds(column, ref.shape[1])]) for ref, column in own
    ]
    for at in range(16):
        src = arrays[at // 2].at[at % 2, pl.ds(slot + skip - 1, slots - skip)]
        if src.shape[2] != width:
            src = src.at[:, :, pl.ds(first, width)]
        start = pl.multiple_of(offs[at], 16)
        pairs.append((src, dst.at[pl.ds(skip, slots - skip), pl.ds(start, half), :]))
    return [pltpu.make_async_copy(s, d, sems.at[i]) for i, (s, d) in enumerate(pairs)]


copies_per_chunk = 20


def gathered_copies(gathered, dst, sems, shard=None):
    full = gathered.shape[4]
    out = []
    for at, (c, y, x) in enumerate(np.ndindex(2, 2, 2)):
        rows = pl.ds(at * full, full)
        if shard is None:
            out.append((gathered.at[y, x, c], dst.at[:, rows, :]))
        else:
            out.append((gathered.at[y, x, c, shard], dst.at[rows, :]))
    return [pltpu.make_async_copy(s, d, sems.at[i]) for i, (s, d) in enumerate(out)]


def split_kernel(sc, v_ref, a_ref, b_ref, *rest):
    half = a_ref.shape[1]
    n = v_ref.shape[0]
    for ref in rest:
        ref[...] = v_ref[:, 2 * half :, :]
    for k in range(1, n):
        at = lax.rem(sc[16] + n - k, n)
        a_ref[k - 1] = v_ref[at, :half, :]
        b_ref[k - 1] = v_ref[at, half : 2 * half, :]


def split(offs, v, rows, after=()):
    n, _, width = v.shape
    out = (n - 1, rows // 2, width)
    shapes = [out, out] + ([(n, v.shape[1] - rows, width)] if v.shape[1] > rows else [])
    return launch(
        split_kernel, "split", [v], [whole(v.shape)], [whole(shape) for shape in shapes],
        like(bf16, *shapes), offs=offs, after=after,
    )


def relay_kernel(a, b, c, d):
    c[...] = a[...]
    d[...] = b[...]


def relay(a, b, after):
    return launch(
        relay_kernel, "relay", [a, b], [whole(a.shape)] * 2, [whole(a.shape)] * 2,
        like(a.dtype, a.shape, a.shape), after=after,
    )[0]


def collect_kernel(step, n, sc, right, left, own, *refs):
    out, rest, *on = refs
    length = out.shape[1]
    side = pl.program_id(0)
    z = sc[16]

    @pl.when((side == 0) & (z >= step))
    def _():
        out[0] = right[:length, :].astype(f32)
        rest[0] = right[length:, :]

    @pl.when((side == 1) & (z + step < n))
    def _():
        out[0] = left[:length, :].astype(f32)
        rest[0] = left[length:, :]

    @pl.when(((side == 0) & (z < step)) | ((side == 1) & (z + step >= n)))
    def _():
        out[0] = own[:length, :].astype(f32)
        rest[0] = own[length:, :]

    @pl.when(side == 0)
    def _():
        for new, old in zip(on, (right, left)):
            new[...] = old[...]


def collect(step, n, offs, right, left, own, so_far, after):
    rows, d = own.shape
    length = rows // tile * tile

    def index(i, sc):
        z = sc[16]
        near, far = jnp.where(z >= step, z - step, z), jnp.where(z + step < n, z + step, z)
        return (jnp.where(i == 0, near, far), 0, 0)

    goes_on = step < n - 1
    kept = list(so_far or ())
    shapes = [(n, length, d), (n, rows - length, d)]
    out_shape = like(f32, shapes[0]) + like(bf16, shapes[1])
    out_specs = [pl.BlockSpec((1,) + shape[1:], index) for shape in shapes]
    if goes_on:
        out_shape += like(bf16, own.shape, own.shape)
        out_specs += [whole(own.shape)] * 2

    def kernel(sc, right, left, own, *refs):
        collect_kernel(step, n, sc, right, left, own, *refs[len(kept) :])

    return launch(
        kernel, f"collect{step}", [right, left, own, *kept],
        [whole(own.shape)] * 3 + [ANY] * len(kept), out_specs, out_shape, grid=(2,), offs=offs,
        after=after, alias=3 if kept else None, n_alias=2,
    )


def skew(base):
    t = jnp.broadcast_to(base, (8, span))
    row = lax.broadcasted_iota(jnp.int32, (8, span), 0)
    for step in (1, 2, 4):
        t = jnp.where((row & step) != 0, pltpu.roll(t, step, 1), t)
    while t.shape[0] < tile:
        t = jnp.concatenate([t, pltpu.roll(t, t.shape[0], 1)], axis=0)
    return t


def unskew(t):
    while t.shape[0] > 8:
        n = t.shape[0] // 2
        t = t[:n] + pltpu.roll(t[n:], span - n, 1)
    row = lax.broadcasted_iota(jnp.int32, (8, span), 0)
    for step in (1, 2, 4):
        t = jnp.where((row & step) != 0, pltpu.roll(t, span - step, 1), t)
    return jnp.sum(t, axis=0, keepdims=True)


def fill_mask(mask, segs, pads, seg_cols, row):
    length = mask.shape[0]
    rows = segs.shape[0]
    chosen = lax.broadcasted_iota(jnp.int32, (rows, length), 0) == row
    seg_k = jnp.sum(jnp.where(chosen, segs, 0.0), axis=0, keepdims=True)
    pad_k = jnp.sum(jnp.where(chosen, pads, 0.0), axis=0, keepdims=True)
    code = jnp.where(pad_k == 1.0, seg_k, -1.0)
    lane = lax.broadcasted_iota(jnp.int32, seg_cols.shape, 1)
    seg_q = jnp.sum(jnp.where(lane == row, seg_cols, 0.0), axis=1, keepdims=True)
    q = lax.broadcasted_iota(jnp.int32, (tile, length), 0)
    k = lax.broadcasted_iota(jnp.int32, (tile, length), 1)
    for a in range(length // tile):
        own = seg_q[a * tile : (a + 1) * tile]
        ok = (own == code) | (q + a * tile == k)
        mask[a * tile : (a + 1) * tile, :] = jnp.where(ok, 0.0, masked_logit)


def fill_bias(bias, table, hot, heads):
    base = dot(table, hot[0 : table.shape[1], :])
    for h in range(heads):
        bias[h] = skew(base[h : h + 1, :])


def normalize(x_ref, gain, normed):
    for a in range(x_ref.shape[0] // tile):
        rows = slice(a * tile, (a + 1) * tile)
        v = x_ref[rows, :].astype(f32)
        normed[rows, :] = (v * rms_scale(v) * gain).astype(bf16)


chunk = 32


def head_groups(heads, size):
    per = tile // size
    out = []
    for first in range(0, heads, per):
        members = range(first, min(heads, first + per))
        lanes = slice(first * size, (members[-1] + 1) * size)
        out.append((lanes, [(h, (h - first) * size) for h in members]))
    return out


def only(v, lane, size):
    if v.shape[1] == size:
        return v
    at = lax.broadcasted_iota(jnp.int32, v.shape, 1)
    return jnp.where((at >= lane) & (at < lane + size), v, jnp.zeros_like(v))


def merge(parts, size):
    out = parts[0]
    at = lax.broadcasted_iota(jnp.int32, out.shape, 1)
    for i, part in enumerate(parts[1:]):
        out = jnp.where(at >= (i + 1) * size, part, out)
    return out


def project_heads(normed_ref, w, parts):
    rows = parts[0].shape[1]
    for i, part in enumerate(parts):
        part[...] = dot(
            normed_ref[...], w[i * rows : (i + 1) * rows, :], ((1,), (1,))
        ).astype(bf16)


def softmax_chunks(length):
    for r in range(0, length, chunk):
        at = length - tile - r // tile * tile
        yield slice(r, r + chunk), slice(r % tile, r % tile + chunk), slice(at, at + length)


def attend_kernel(
    first, heads, size, sc, x_ref, seg_ref, pad_ref, segc_ref, gain_ref, w_ref, hot_ref,
    out_ref, normed, query, keys, values, mask, bias, logits, probs, inverse,
):
    length = x_ref.shape[0]
    wide = heads * size
    buckets = 32
    row = lax.rem(sc[16] + first + pl.program_id(0), seg_ref.shape[0])
    normalize(x_ref, gain_ref[...], normed)
    project_heads(normed, w_ref, (query, keys, values))
    fill_mask(mask, seg_ref[...], pad_ref[...], segc_ref[...], row)

    @pl.when(pl.program_id(0) == 0)
    def _():
        fill_bias(bias, w_ref[3 * wide : 3 * wide + 16, :tile][:, :buckets], hot_ref, heads)

    for lanes, members in head_groups(heads, size):
        parts = []
        for i, (h, lane) in enumerate(members):
            logits[i % 2] = dot(only(query[:, lanes], lane, size), keys[:, lanes], ((1,), (1,)))
            for rows, inner, at in softmax_chunks(length):
                v = logits[i % 2, rows, :] + bias[h, inner, at] + mask[rows, :]
                e = jnp.exp(v - jnp.max(v, axis=1, keepdims=True))
                total = jnp.sum(e, axis=1, keepdims=True)
                inverse[rows, :] = jnp.broadcast_to(1.0 / total, (chunk, tile))
                probs[i % 2, rows, :] = e.astype(bf16)
            part = dot(probs[i % 2], values[:, lanes])
            parts.append(part * inverse[:, : part.shape[1]])
        out_ref[0, :length, lanes] = merge(parts, size).astype(bf16)
    out_ref[0, length:, :] = w_ref[3 * wide : 3 * wide + 16, :wide]


def attend(first, offs, tokens, segs, pads, seg_cols, gain, w_qkv, hot, heads, size, after=()):
    rows, length = segs.shape
    d = tokens.shape[1]
    wide = heads * size
    args = [tokens, segs, pads, seg_cols, gain, w_qkv, hot]
    specs = [pl.BlockSpec((length, d), lambda i, sc: (lax.rem(sc[16] + first + i, rows), 0))]
    return launch(
        functools.partial(attend_kernel, first, heads, size), "attend", args,
        specs + [whole(v.shape) for v in args[1:]],
        [pl.BlockSpec((1, length + 16, wide), lambda i, sc: (i, 0, 0))],
        like(bf16, (rows, length + 16, wide)),
        grid=(rows,), offs=offs,
        scratch=[
            pltpu.VMEM((length, d), bf16),
            pltpu.VMEM((length, wide), bf16),
            pltpu.VMEM((length, wide), bf16),
            pltpu.VMEM((length, wide), bf16),
            pltpu.VMEM((length, length), f32),
            pltpu.VMEM((heads, tile, span), f32),
            pltpu.VMEM((2, length, length), f32),
            pltpu.VMEM((2, length, length), bf16),
            pltpu.VMEM((length, tile), f32),
        ],
        cost=cost(
            rows * (6 * length * d * wide + 4 * wide * length * length), 4,
            rows * heads * length * length,
        ),
        after=after,
    )


def high_low(v):
    high = v.astype(bf16)
    return high, (v - high.astype(f32)).astype(bf16)


def attend_back_slot(
    heads, size, mixed_ref, gm_ref, hot_ref, w, left_ref, table_out, acc,
    normed, query, keys, values, mask, bias, logits, gprobs, probs, dlog, skewed, diag,
):
    length = normed.shape[0]
    wide = heads * size
    fill_bias(bias, mixed_ref[length:, :tile][:, :32], hot_ref, heads)
    project_heads(normed, w, (query, keys, values))
    for lanes, members in head_groups(heads, size):
        q, k, v = query[:, lanes], keys[:, lanes], values[:, lanes]
        grad = gm_ref[:, lanes]
        results = []
        for h, lane in members:
            logits[...] = dot(only(q, lane, size), k, ((1,), (1,)))
            gprobs[...] = dot(only(grad, lane, size), v, ((1,), (1,)))
            skewed[...] = jnp.zeros_like(skewed)
            for rows, inner, at in softmax_chunks(length):
                t = logits[rows, :] + bias[h, inner, at] + mask[rows, :]
                e = jnp.exp(t - jnp.max(t, axis=1, keepdims=True))
                p = e * (1.0 / jnp.sum(e, axis=1, keepdims=True))
                probs[rows, :] = p.astype(bf16)
                gp = gprobs[rows, :]
                gl = p * (gp - jnp.sum(gp * p, axis=1, keepdims=True))
                dlog[rows, :] = gl.astype(bf16)
                skewed[inner, at] += gl
            diag[h : h + 1, :] = unskew(skewed[...])
            results.append(
                (
                    dot(dlog[...], k),
                    dot(dlog[...], q, ((0,), (0,))),
                    dot(probs[...], grad, ((0,), (0,))),
                )
            )
        for part in range(3):
            merged = merge([r[part] for r in results], size)
            left_ref[part, :, lanes] = merged.astype(bf16)
    left_ref[3] = mixed_ref[:length, :]
    high, low = high_low(diag[...])
    table = dot(high, hot_ref[...], ((1,), (1,))) + dot(low, hot_ref[...], ((1,), (1,)))
    table_out[...] = table
    value = sum(
        dot(left_ref[part], w[part * wide : (part + 1) * wide, :]) for part in range(3)
    )
    acc[...] += value


def attend_back_kernel(
    first, count, last, heads, size, sc, x_ref, seg_ref, pad_ref, segc_ref, gain_ref, hot_ref,
    gm_ref, *refs,
):
    mixed_refs, refs = refs[:count], list(refs[count:])
    acc_in = refs.pop(0) if first else None
    if last:
        gha_ref, gat_ref, fin_ref, mid_ref, score_ref = refs[:5]
        refs = refs[5:]
        tables = [refs.pop(0)] if first else []
    w_ref = refs[0]
    refs = refs[1 + (1 if first else 0) :]
    left_ref, table_out = refs[:2]
    if last:
        dx_ref, both_ref, small_ref, acc = refs[2:6]
        refs = refs[6:]
    else:
        acc, refs = refs[2], refs[3:]
    (
        w, sems, normed, query, keys, values, mask, bias, logits, gprobs, probs, dlog, skewed, diag,
    ) = refs
    length, d = x_ref.shape
    wide = heads * size
    row = sc[16]
    gain = gain_ref[...]
    blocks = length // tile
    copies = [
        gathered_copies(w_ref, w.at[i], sems.at[i], lax.rem(row + 4 - first - i, 4))
        for i in range(count)
    ]
    for copy in sum(copies, []):
        copy.start()
    normalize(x_ref, gain, normed)
    fill_mask(mask, seg_ref[...], pad_ref[...], segc_ref[...], row)
    diag[...] = jnp.zeros_like(diag)
    if acc_in is None:
        acc[...] = jnp.zeros_like(acc)
    else:
        acc[...] = acc_in[...]
    for i in range(count):
        for copy in copies[i]:
            copy.wait()
        attend_back_slot(
            heads, size, mixed_refs[i], gm_ref.at[i], hot_ref, w.at[i], left_ref.at[i],
            table_out.at[8 * i : 8 * i + 8], acc,
            normed, query, keys, values, mask, bias, logits, gprobs, probs, dlog, skewed, diag,
        )
    if not last:
        return
    total = jnp.zeros((1, d), f32)
    for a in range(blocks):
        rows = slice(a * tile, (a + 1) * tile)
        back, part = rms_back(x_ref[rows, :].astype(f32), gain, acc[rows, :])
        dx_ref[rows, :] = (gha_ref[rows, :] + back).astype(bf16)
        total = total + part
    both_ref[0] = normed[...]
    both_ref[1] = gat_ref[...]
    dx_ref[length:, :] = jnp.zeros((dx_ref.shape[0] - length, d), bf16)
    n = score_ref.shape[0] // 16
    cols = score_ref.shape[1]
    high, low = high_low(score_ref[...])
    for i in range(n):
        rows = slice(16 * i, 16 * i + 16)
        dx_ref[length : length + 16, 2 * i * tile : 2 * i * tile + cols] = high[rows]
        dx_ref[length : length + 16, (2 * i + 1) * tile : (2 * i + 1) * tile + cols] = low[rows]
    line = lax.broadcasted_iota(jnp.int32, (8, d), 0)
    gains = jnp.where(
        line == 0, total, jnp.where(line == 1, fin_ref[...], jnp.where(line == 2, mid_ref[...], 0.0))
    )
    line = lax.broadcasted_iota(jnp.int32, (8, tile), 0)
    column = lax.broadcasted_iota(jnp.int32, (8, tile), 1)

    def turned(value, at):
        place = jnp.where(column == line + at, 1.0, 0.0).astype(bf16)
        high, low = high_low(value)
        return dot(high, place, ((0,), (0,))) + dot(low, place, ((0,), (0,)))

    gains = turned(gains, 0)
    tables = [t[8 * i : 8 * i + 8] for t in tables + [table_out] for i in range(t.shape[0] // 8)]
    for k, value in enumerate(tables):
        small_ref[k] = gains.astype(bf16)
        small_ref[k, 0:tile, :] = (gains[0:tile] + turned(value, tile // 2)).astype(bf16)


def attend_back(
    first, count, common, grad_mixed, mixed, acc, left, finish, weights, heads, size, after=()
):
    offs, *shared = common
    rows, length = shared[1].shape
    d = shared[0].shape[1]
    slots = grad_mixed.shape[0]
    wide = heads * size
    last = first + count == slots
    mixed = mixed[first : first + count]
    args = [*shared, grad_mixed, *mixed]
    specs = [pl.BlockSpec((length, d), lambda i, sc: (sc[16], 0))]
    specs += [whole(v.shape) for v in shared[1:]]
    specs.append(pl.BlockSpec((count, length, wide), lambda i, sc: (first // count, 0, 0)))
    specs += [whole(m.shape) for m in mixed]
    if first:
        args.append(acc)
        specs.append(whole(acc.shape))
    if last:
        args += finish
        specs += [whole(v.shape) for v in finish]
    args += [weights] + ([left] if first else [])
    specs += [ANY] * (2 if first else 1)
    out_specs = [
        pl.BlockSpec((count, 4, length, wide), lambda i, sc: (first // count, 0, 0, 0)),
        whole((8 * count, tile)),
    ]
    out_shape = like(bf16, (slots, 4, length, wide)) + like(f32, (8 * count, tile))
    scratch = []
    if last:
        shapes = ((length + 16, d), (2, length, d), (slots, d, tile))
        out_specs += [whole(shape) for shape in shapes]
        out_shape += like(bf16, *shapes)
        scratch = [pltpu.VMEM((length, d), f32)]
    else:
        out_specs.append(whole((length, d)))
        out_shape += like(f32, (length, d))
    return launch(
        functools.partial(attend_back_kernel, first, count, last, heads, size),
        f"attend_back{first}",
        args, specs, out_specs, out_shape, offs=offs,
        scratch=scratch
        + [
            pltpu.VMEM((count, 8 * weights.shape[4], d), bf16),
            pltpu.SemaphoreType.DMA((count, 8)),
            pltpu.VMEM((length, d), bf16),
            pltpu.VMEM((length, wide), bf16),
            pltpu.VMEM((length, wide), bf16),
            pltpu.VMEM((length, wide), bf16),
            pltpu.VMEM((length, length), f32),
            pltpu.VMEM((heads, tile, span), f32),
            pltpu.VMEM((length, length), f32),
            pltpu.VMEM((length, length), f32),
            pltpu.VMEM((length, length), bf16),
            pltpu.VMEM((length, length), bf16),
            pltpu.VMEM((tile, span), f32),
            pltpu.VMEM((8, span), f32),
        ],
        cost=cost(
            count * (12 * length * d * wide + 14 * wide * length * length), 16,
            count * heads * length * length,
        ),
        after=after, alias=len(args) - 1 if first else None, mib=32,
    )


def ffn_in_first_kernel(count, sc, x_ref, gain_ref, *refs):
    slots = 4
    mixed, own, arrays = refs[:slots], refs[slots : slots + 3], refs[slots + 3 : slots + 11]
    hid_ref, normed_ref, *outs = refs[slots + 11 : slots + 16]
    w, wo, sems, o_sems = refs[slots + 16 :]
    length, d = x_ref.shape
    hidden = outs[0].shape[2]
    copies = chunk_copies(sc, zip(own, (0, hidden)), arrays, w, sems)
    o_copies = chunk_copies(sc, [(own[2], 0)], arrays, wo, o_sems, 2 * hidden)

    @pl.when(pl.program_id(0) == 0)
    def _():
        for copy in o_copies + copies:
            copy.start()
        for copy in o_copies:
            copy.wait()
        gain = gain_ref[...]
        for a in range(length // tile):
            rows = slice(a * tile, (a + 1) * tile)
            h = x_ref[rows, :].astype(f32)
            for k in range(slots):
                h = h + dot(mixed[k][rows, :], wo[k], ((1,), (1,)))
            hid_ref[rows, :] = h
            normed_ref[rows, :] = (h * rms_scale(h) * gain).astype(bf16)
        for copy in copies:
            copy.wait()

    gate_up(normed_ref, w.at[pl.program_id(0)], *outs)


def ffn_in_rest_kernel(first, sc, normed_ref, *refs):
    arrays, outs, (w, sems) = refs[:8], refs[8:11], refs[11:]
    copies = chunk_copies(sc, (), arrays, w, sems, 0, first)

    @pl.when(pl.program_id(0) == 0)
    def _():
        for copy in copies:
            copy.start()
        for copy in copies:
            copy.wait()

    gate_up(normed_ref, w.at[pl.program_id(0)], *outs)


def gate_up(normed_ref, w, act_ref, dact_ref, inner_ref):
    hidden = act_ref.shape[2]
    for n in range(hidden // 256):
        cols = slice(n * 256, (n + 1) * 256)
        normed = normed_ref[...]
        gate = dot(normed, w[:, cols])
        up = dot(normed, w[:, hidden + n * 256 : hidden + (n + 1) * 256])
        t = jnp.tanh(gelu_c * (gate + 0.044715 * gate * gate * gate))
        half = 0.5 * (1.0 + t)
        act = gate * half
        slope = half + 0.5 * gate * (1.0 - t * t) * (
            gelu_c * (1.0 + 3 * 0.044715 * gate * gate)
        )
        act_ref[0, :, cols] = act.astype(bf16)
        dact_ref[0, :, cols] = (up * slope).astype(bf16)
        inner_ref[0, :, cols] = (act * up).astype(bf16)


def ffn_in_first(count, offs, tokens, gain, mixed, own, arrays, length, after=()):
    d = tokens.shape[1]
    slots = len(mixed)
    hidden = own[0].shape[1]
    wide = own[2].shape[1]
    per_slot = pl.BlockSpec((1, length, hidden), lambda i, sc: (i, 0, 0))
    three = (slots, length, hidden)
    specs = [pl.BlockSpec((length, d), lambda i, sc: (sc[16], 0)), whole(gain.shape)]
    return launch(
        functools.partial(ffn_in_first_kernel, count), "ffn_in_first",
        [tokens, gain, *mixed, *own, *arrays],
        specs + [whole(m.shape) for m in mixed] + [ANY] * 11,
        [whole((length, d)), whole((length, d))] + [per_slot] * 3,
        like(f32, (length, d)) + like(bf16, (length, d), three, three, three),
        grid=(count,), offs=offs,
        scratch=[
            pltpu.VMEM((count, d, 2 * hidden), bf16),
            pltpu.VMEM((slots, d, wide), bf16),
            pltpu.SemaphoreType.DMA((copies_per_chunk,)),
            pltpu.SemaphoreType.DMA((copies_per_chunk,)),
        ],
        cost=cost(2 * length * d * (d + 2 * count * hidden), 16, count * length * hidden),
        after=after, mib=24,
    )


def ffn_in_rest(count, offs, normed, so_far, arrays, after=()):
    length, d = normed.shape
    slots, _, hidden = so_far[0].shape
    first = slots - count
    per_slot = pl.BlockSpec((1, length, hidden), lambda i, sc: (i + first, 0, 0))

    def kernel(sc, normed_ref, *refs):
        ffn_in_rest_kernel(first, sc, normed_ref, *refs[:8], *refs[11:])

    return launch(
        kernel, "ffn_in_rest", [normed, *arrays, *so_far],
        [whole(normed.shape)] + [ANY] * 11, [per_slot] * 3,
        like(bf16, *[v.shape for v in so_far]), grid=(count,), offs=offs,
        scratch=[
            pltpu.VMEM((count, d, 2 * hidden), bf16),
            pltpu.SemaphoreType.DMA((copies_per_chunk,)),
        ],
        cost=cost(4 * length * d * count * hidden, 16, count * length * hidden),
        after=after, mib=20, alias=9, n_alias=3,
    )


def ffn_out_kernel(
    sc, hid_ref, inner_ref, gain_ref, wp_ref, padc_ref, query_ref, cot_ref, top_ref, own, *refs
):
    arrays = refs[:8]
    score_ref, nfin, ge, total_ref, gft_ref, ghf_ref, wd, sems, acc, embed, unit = refs[8:]
    length, d = hid_ref.shape
    step = pl.program_id(0)
    copies = chunk_copies(sc, [(own, 0)], arrays, wd, sems)
    blocks = length // tile

    @pl.when(step == 0)
    def _():
        for copy in copies:
            copy.start()
        acc[...] = hid_ref[...]
        for copy in copies:
            copy.wait()

    acc[...] += dot(inner_ref[0], wd[step])

    @pl.when(step == pl.num_programs(0) - 1)
    def _():
        lane = lax.broadcasted_iota(jnp.int32, padc_ref.shape, 1)
        pad = jnp.sum(jnp.where(lane == sc[16], padc_ref[...], 0.0), axis=1, keepdims=True)
        gain = gain_ref[...]
        for a in range(blocks):
            rows = slice(a * tile, (a + 1) * tile)
            h = acc[rows, :]
            n = (h * rms_scale(h) * gain).astype(bf16)
            nfin[rows, :] = n
            e = dot(n, wp_ref[...])
            embed[rows, :] = e
            inverse = lax.rsqrt(jnp.sum(e * e, axis=1, keepdims=True) + eps)
            unit[rows, :] = (e * inverse * pad[rows]).astype(bf16)
        query = query_ref[0]
        cot = cot_ref[0]
        top = top_ref[0]
        scored = dot(query, unit[...], ((1,), (1,)))
        place = lax.broadcasted_iota(jnp.int32, scored.shape, 1)
        out_lane = lax.broadcasted_iota(jnp.int32, cot.shape, 1)
        chosen = jnp.zeros_like(cot)
        weight = jnp.zeros_like(scored)
        for j in range(top.shape[1]):
            here = place == top[:, j : j + 1]
            mine = jnp.sum(jnp.where(here, scored, 0.0), axis=1, keepdims=True)
            chosen = jnp.where(out_lane == j, mine, chosen)
            weight = weight + jnp.where(here, cot[:, j : j + 1], 0.0)
        score_ref[...] = chosen
        high, low = high_low(weight)
        gunit = dot(high, query, ((0,), (0,))) + dot(low, query, ((0,), (0,)))
        total = jnp.zeros((1, d), f32)
        for a in range(blocks):
            rows = slice(a * tile, (a + 1) * tile)
            e = embed[rows, :]
            inverse = lax.rsqrt(jnp.sum(e * e, axis=1, keepdims=True) + eps)
            u = gunit[rows] * pad[rows]
            cube = (inverse * inverse * inverse) * jnp.sum(u * e, axis=1, keepdims=True)
            g = (inverse * u - e * cube).astype(bf16)
            ge[rows, :] = g
            back, part = rms_back(acc[rows, :], gain, dot(g, wp_ref[...], ((1,), (1,))))
            total = total + part
            ghf_ref[rows, :] = back
            gft_ref[rows, :] = back.astype(bf16)
        total_ref[...] = total


def ffn_out(offs, hid, inner, gain, w_proj, pad_cols, query, cot, top, own, arrays):
    length, d = hid.shape
    slots, _, hidden = inner.shape
    e = w_proj.shape[1]

    def row_block(v):
        return pl.BlockSpec((1,) + v.shape[1:], lambda i, sc: (sc[16], 0, 0))

    score, low, embed, total = cot.shape[1:], (length, d), (length, e), (1, d)
    return launch(
        ffn_out_kernel, "ffn_out",
        [hid, inner, gain, w_proj, pad_cols, query, cot, top, own, *arrays],
        [whole(hid.shape), pl.BlockSpec((1, length, hidden), lambda i, sc: (i, 0, 0))]
        + [whole(v.shape) for v in (gain, w_proj, pad_cols)]
        + [row_block(v) for v in (query, cot, top)]
        + [ANY] * 9,
        [whole(v) for v in (score, low, embed, total, low, low)],
        like(f32, score) + like(bf16, low, embed) + like(f32, total) + like(bf16, low)
        + like(f32, low),
        grid=(slots,), offs=offs,
        scratch=[
            pltpu.VMEM((slots, hidden, d), bf16),
            pltpu.SemaphoreType.DMA((copies_per_chunk,)),
            pltpu.VMEM((length, d), f32),
            pltpu.VMEM((length, e), f32),
            pltpu.VMEM((length, e), bf16),
        ],
        cost=cost(2 * length * d * slots * hidden, 16), mib=24,
    )


def ffn_back_kernel(sc, hid_ref, gft_ref, ghf_ref, act_ref, dact_ref, gain_ref, *refs):
    slots = 4
    own, first, own_down, second = refs[:3], refs[3:11], refs[11], refs[12:20]
    refs = refs[20:]
    gg_ref, gu_ref, gha_ref, gat_ref, gm_ref, total_ref, w, wd, w_sems, d_sems, acc = refs
    length, d = hid_ref.shape
    hidden = wd.shape[1]
    step = pl.program_id(0)
    w_copies = chunk_copies(sc, zip(own, (0, hidden, 2 * hidden)), first, w, w_sems)
    d_copies = chunk_copies(sc, [(own_down, 0)], second, wd, d_sems)
    blocks = length // tile

    @pl.when(step == 0)
    def _():
        for copy in d_copies + w_copies:
            copy.start()
        acc[...] = jnp.zeros_like(acc)
        for copy in d_copies:
            copy.wait()

    def part(n, carry):
        cols = pl.ds(pl.multiple_of(n * 256, 256), 256)
        gi = dot(gft_ref[...], wd[step, cols, :], ((1,), (1,)))
        gg_ref[0, :, cols] = (gi * dact_ref[0, :, cols].astype(f32)).astype(bf16)
        gu_ref[0, :, cols] = (gi * act_ref[0, :, cols].astype(f32)).astype(bf16)
        return carry

    lax.fori_loop(0, hidden // 256, part, 0)

    @pl.when(step == 0)
    def _():
        for copy in w_copies:
            copy.wait()

    acc[...] += dot(gg_ref[0], w[step, :, :hidden], ((1,), (1,))) + dot(
        gu_ref[0], w[step, :, hidden : 2 * hidden], ((1,), (1,))
    )

    @pl.when(step == slots - 1)
    def _():
        gain = gain_ref[...]
        total = jnp.zeros((1, d), f32)
        for a in range(blocks):
            rows = slice(a * tile, (a + 1) * tile)
            back, part = rms_back(hid_ref[rows, :], gain, acc[rows, :])
            total = total + part
            g = ghf_ref[rows, :] + back
            gha_ref[rows, :] = g
            g = g.astype(bf16)
            gat_ref[rows, :] = g
            for k in range(slots):
                gm_ref[k, rows, :] = dot(g, w[k, :, 2 * hidden :]).astype(bf16)
        total_ref[...] = total


def ffn_back(offs, hid, gft, ghf, act, dact, gain, own, first, own_down, second, after=()):
    length, d = hid.shape
    slots, _, hidden = act.shape
    width = first[0].shape[3]
    mixed = (slots, length, width - 2 * hidden)
    block = pl.BlockSpec((1, length, hidden), lambda i, sc: (i, 0, 0))
    return launch(
        ffn_back_kernel, "ffn_back",
        [hid, gft, ghf, act, dact, gain, *own, *first, own_down, *second],
        [whole(v.shape) for v in (hid, gft, ghf)] + [block] * 2 + [whole(gain.shape)] + [ANY] * 20,
        [block, block] + [whole(v) for v in (hid.shape, hid.shape, mixed, (1, d))],
        like(bf16, act.shape, act.shape) + like(f32, hid.shape) + like(bf16, hid.shape, mixed)
        + like(f32, (1, d)),
        grid=(slots,), offs=offs,
        scratch=[
            pltpu.VMEM((slots, d, width), bf16),
            pltpu.VMEM((slots, hidden, d), bf16),
            pltpu.SemaphoreType.DMA((copies_per_chunk,)),
            pltpu.SemaphoreType.DMA((copies_per_chunk,)),
            pltpu.VMEM((length, d), f32),
        ],
        cost=cost(2 * length * d * (3 * slots * hidden + d), 24),
        after=after, mib=42,
    )


def keep_parts(sc, out, refs):
    send_a, keep_a, send_b, keep_b = refs
    half = send_a.shape[2]
    x, y = sc[18], sc[19]

    def rows(y, x, extra):
        at = pl.multiple_of((2 * y + x) * (2 * half) + extra, 16)
        return out[pl.ds(at, half), :]

    for other in range(2):
        send_a[0, other] = rows(other, 1 - x, 0)
        keep_a[0, other] = rows(other, x, 0)
        send_b[0, other] = rows(1 - y, other, half)
        keep_b[0, other] = rows(y, other, half)


def parts_of(slots, rows, width):
    part = (1, 2, rows // 8, width)
    spec = pl.BlockSpec(part, lambda i, sc: (i, 0, 0, 0))
    return [spec] * 4, [jax.ShapeDtypeStruct((slots,) + part[1:], bf16)] * 4


def product_kernel(lefts, pairs, keep, sc, *refs):
    left_refs, right_refs = refs[:lefts], refs[lefts : lefts + len(pairs)]
    refs = refs[lefts + len(pairs) :]
    out = refs[-1] if keep else refs[-1].at[0]
    at = 0
    for right_ref, which in zip(right_refs, pairs):
        right = right_ref[...]
        left = left_refs[which][...]
        left, right = (v.reshape(v.shape[-2:]) for v in (left, right))
        cols = slice(at, at + right.shape[1])
        value = dot(left, right, ((0,), (0,)))
        if keep:
            value = value + refs[0][0, :, cols].astype(f32)
        out[:, cols] = value.astype(bf16)
        at += right.shape[1]
    if keep:
        keep_parts(sc, out, refs[-5:-1])


def products(offs, lefts, rights, slots, got=None, after=()):
    keep = got is not None
    length, half = lefts[0].shape[-2], lefts[0].shape[-1] // 2
    width = sum(right.shape[-1] for right, _ in rights)

    def which(sc):
        return sc[17] if keep else 1 - sc[17]

    specs = []
    for left in lefts:
        if left.ndim == 3:
            specs.append(pl.BlockSpec((1, length, half), lambda i, sc: (i, 0, which(sc))))
        else:
            specs.append(pl.BlockSpec((length, half), lambda i, sc: (0, which(sc))))
    for right, _ in rights:
        if right.ndim == 3:
            specs.append(pl.BlockSpec((1,) + right.shape[1:], lambda i, sc: (i, 0, 0)))
        else:
            specs.append(whole(right.shape))
    args = list(lefts) + [right for right, _ in rights]
    block = pl.BlockSpec((1, half, width), lambda i, sc: (i, 0, 0))
    out_specs, out_shape, scratch = [block], like(bf16, (slots, half, width)), []
    if keep:
        specs.append(block)
        args.append(got)
        out_specs, out_shape = parts_of(slots, half, width)
        scratch = [pltpu.VMEM((half, width), bf16)]
    return launch(
        functools.partial(product_kernel, len(lefts), [i for _, i in rights], keep),
        "products_keep" if keep else "products_send",
        args, specs, out_specs, out_shape, grid=(slots,), offs=offs, scratch=scratch, after=after,
        mib=16,
    )


def attn_product_kernel(keep, sc, la, lb, ra, rb, small, *refs):
    out = refs[-1] if keep else refs[-1].at[0]
    quarter, d = la.shape[3], ra.shape[2]
    for left, right, at in ((la, ra, 0), (lb, rb, quarter)):
        value = dot(left[0, 0], right[0], ((0,), (0,)))
        if keep:
            value = value + refs[0][0, at : at + quarter, :d].astype(f32)
        out[at : at + quarter, :d] = value.astype(bf16)
    value = small[0]
    if keep:
        value = add(value, refs[0][0, :, d:])
    out[:, d:] = value
    if keep:
        keep_parts(sc, out, refs[1:5])


def attn_products(offs, left, both, small, got=None, after=()):
    keep = got is not None
    slots, _, length, quarter = left.shape
    d = both.shape[2]
    width = d + small.shape[2]
    half = 2 * quarter

    def which(sc):
        return sc[17] if keep else 1 - sc[17]

    block = pl.BlockSpec((1, half, width), lambda i, sc: (i, 0, 0))
    specs = [
        pl.BlockSpec((1, 1, length, quarter), lambda i, sc: (i, 2 * which(sc), 0, 0)),
        pl.BlockSpec((1, 1, length, quarter), lambda i, sc: (i, 2 * which(sc) + 1, 0, 0)),
        pl.BlockSpec((1, length, d), lambda i, sc: (0, 0, 0)),
        pl.BlockSpec((1, length, d), lambda i, sc: (which(sc), 0, 0)),
        pl.BlockSpec((1, half, small.shape[2]), lambda i, sc: (i, which(sc), 0)),
    ]
    args = [left, left, both, both, small]
    out_specs, out_shape, scratch = [block], like(bf16, (slots, half, width)), []
    if keep:
        specs.append(block)
        args.append(got)
        out_specs, out_shape = parts_of(slots, half, width)
        scratch = [pltpu.VMEM((half, width), bf16)]
    return launch(
        functools.partial(attn_product_kernel, keep), "attn_keep" if keep else "attn_send",
        args, specs, out_specs, out_shape, grid=(slots,), offs=offs, scratch=scratch, after=after,
        mib=16,
    )


def add(a, b):
    return (a.astype(f32) + b.astype(f32)).astype(bf16)


def second_kernel(sc, ka, ra, kb, rb, send_a, keep_a, send_b, keep_b):
    x, y = sc[18], sc[19]
    send_a[0] = add(ka[0, 1 - y], ra[0, 1 - y])
    keep_a[0] = add(ka[0, y], ra[0, y])
    send_b[0] = add(kb[0, 1 - x], rb[0, 1 - x])
    keep_b[0] = add(kb[0, x], rb[0, x])


def second_sums(offs, *arrays, after=()):
    slots, _, half, width = arrays[0].shape
    into = pl.BlockSpec((1, 2, half, width), lambda i, sc: (i, 0, 0, 0))
    out = pl.BlockSpec((1, half, width), lambda i, sc: (i, 0, 0))
    return launch(
        second_kernel, "second_sums", arrays, [into] * 4, [out] * 4,
        like(bf16, *[(slots, half, width)] * 4), grid=(slots,), offs=offs, after=after,
    )


def third_kernel(ka, ra, kb, rb, *outs):
    half = ka.shape[1]
    for k, out in enumerate(outs):
        out[:half, :] = add(ka[k], ra[k])
        out[half:, :] = add(kb[k], rb[k])


def third_sums(*arrays, after=()):
    slots, half, width = arrays[0].shape
    shape = (2 * half, width)
    return launch(
        third_kernel, "third_sums", arrays, [whole(arrays[0].shape)] * 4, [whole(shape)] * slots,
        like(bf16, *[shape] * slots), after=after,
    )


def third_stacked_kernel(sc, ka, ra, kb, rb, out):
    n, half, _ = ka.shape
    for k in range(n):
        to = lax.rem(sc[16] + n - k, n)
        out[to, :half, :] = add(ka[k], ra[k])
        out[to, half:, :] = add(kb[k], rb[k])


def third_stacked(offs, *arrays, after=()):
    slots, half, width = arrays[0].shape
    shape = (slots, 2 * half, width)
    (out,), token = launch(
        third_stacked_kernel, "third_stacked", arrays, [whole(arrays[0].shape)] * 4,
        [whole(shape)], like(bf16, shape), offs=offs, after=after,
    )
    return out, token


def last_kernel(*refs):
    t = [ref[...].astype(f32) for ref in refs[:4]]
    refs[4][...] = ((t[0] + t[2]) + (t[1] + t[3])).astype(refs[4].dtype)


def last_sum(arrays, dtype, after=()):
    shape = arrays[0].shape
    return launch(
        last_kernel, "last_sum", arrays, [whole(shape)] * 4, [whole(shape)], like(dtype, shape),
        after=after,
    )


def stack_kernel(a, xa, b, yb, sa, sb):
    sa[0], sa[1], sb[0], sb[1] = a[...], xa[...], b[...], yb[...]


def stack_pairs(a, xa, b, yb, after):
    out = (2,) + a.shape
    return launch(
        stack_kernel, "stack_pairs", [a, xa, b, yb], [whole(a.shape)] * 4, [whole(out)] * 2,
        like(bf16, out, out), after=after,
    )


class Reduce:
    def __init__(self, place, offs, kept):
        self.place, self.offs, self.kept = place, offs, kept

    def first(self, after=()):
        send_a, keep_a, send_b, keep_b = self.kept
        ra, rb = self.place.swap(send_a, XBIT), self.place.swap(send_b, YBIT)
        self.kept, token = second_sums(self.offs, keep_a, ra, keep_b, rb, after=after)
        return token

    def second(self, after=()):
        send_a, keep_a, send_b, keep_b = self.kept
        ra, rb = self.place.swap(send_a, YBIT), self.place.swap(send_b, XBIT)
        self.kept, token = third_sums(keep_a, ra, keep_b, rb, after=after)
        return token

    def second_and_third(self, after=()):
        send_a, keep_a, send_b, keep_b = self.kept
        ra, rb = self.place.swap(send_a, YBIT), self.place.swap(send_b, XBIT)
        v, token = third_stacked(self.offs, keep_a, ra, keep_b, rb, after=after)
        total = lax.psum_scatter(v, "mp", scatter_dimension=0, tiled=True)
        if self.place.n_out > 1:
            total = lax.psum(total.astype(f32), "out").astype(bf16)
        self.total = total.reshape(v.shape[1:])
        return token

    def third(self, after=()):
        p = self.place
        t = [self.kept[0]] + [p.shift(self.kept[k], -k) for k in range(1, p.n_mp)]
        if p.n_out > 1:
            (total,), token = last_sum(t, f32, after)
            self.total = lax.psum(total, "out").astype(bf16)
        else:
            (self.total,), token = last_sum(t, bf16, after)
        return token


def open_kernel(v_ref, *outs):
    rows = v_ref.shape[3]
    for at, (c, y, x) in enumerate(np.ndindex(2, 2, 2)):
        left = 0
        for out in outs:
            value = v_ref[y, x, c, :, left : left + out.shape[1]]
            out[at * rows : (at + 1) * rows, :] = value.astype(f32)
            left += out.shape[1]


def beside_kernel(a, b, out):
    out[:, : a.shape[1]] = a[...]
    out[:, a.shape[1] :] = b[...]


def gathered(a, b, cuts, start_after, after):
    rows, width = a.shape[0], a.shape[1] + b.shape[1]
    (v,), _ = launch(
        beside_kernel, "beside", [a, b], [whole(a.shape), whole(b.shape)],
        [whole((rows, width))], like(bf16, (rows, width)), after=start_after,
    )
    v = lax.all_gather(v, group, tiled=False).reshape(2, 2, 2, rows, width)
    shapes = [(8 * rows, cut) for cut in cuts]
    return launch(
        open_kernel, "open", [v], [whole(v.shape)], [whole(shape) for shape in shapes],
        like(f32, *shapes), after=after, mib=58,
    )


def unpack_kernel(offs, *refs):
    arrays, outs, small, full = refs[:8], refs[8:-2], refs[-2], refs[-1]
    for at in range(16):
        value = arrays[at // 2][at % 2]
        rows = pl.ds(pl.multiple_of(offs[at], 16), value.shape[0])
        full[rows, :] = value.astype(f32)
    rows, d = outs[0].shape
    for i, out in enumerate(outs):
        out[...] = full[i * rows : (i + 1) * rows, :d]
    small[...] = full[:, d:]


def unpack(offs, arrays, count, small):
    half, width = arrays[0].shape[1:]
    rows, d = 16 * half, width - small
    shapes = [(rows // count, d)] * count + [(rows, small)]
    outs, _ = launch(
        unpack_kernel, "unpack", arrays, [whole(v.shape) for v in arrays],
        [whole(v) for v in shapes], like(f32, *shapes), offs=offs,
        scratch=[pltpu.VMEM((rows, width), f32)],
    )
    return outs


def local(
    tokens, segment_ids, pad_mask, top_index, query_emb, score_cot, gain_attn, w_query, w_key,
    w_value, w_out, rel_table, gain_ffn, w_gate, w_up, w_down, gain_final, w_proj,
):
    place = Place()
    slots = place.n_mp
    rows, length = segment_ids.shape
    d = tokens.shape[1]
    heads = rel_table.shape[1]
    size = w_query.shape[1] // heads
    wide = heads * size
    hot = jnp.asarray(bucket_hot(rel_table.shape[0], length), bf16)
    segs, pads = segment_ids.astype(f32), pad_mask.astype(f32)
    seg_cols, pad_cols = segs.T, pads.T
    gain_a, gain_f, gain_l = (
        g.astype(f32).reshape(1, d) for g in (gain_attn, gain_ffn, gain_final)
    )
    offs = place.offsets(d // 8)

    buckets = rel_table.shape[0]
    table = jnp.zeros((64, d), bf16).at[:heads, :buckets].set(rel_table.T)
    w_qkv = jnp.concatenate([w_query.T, w_key.T, w_value.T, table])
    w_out_t = w_out.T
    eighth = d // 8
    hidden = w_gate.shape[1]

    def piece(*arrays):
        parts = []
        for v in arrays:
            rows = v.shape[0] // 8
            parts.append(lax.dynamic_slice_in_dim(v, place.p * rows, rows, 0))
        return jnp.concatenate(parts, axis=1) if len(parts) > 1 else parts[0]

    common = (offs, tokens, segs, pads, seg_cols, gain_a)
    z1 = lax.all_gather(piece(w_gate, w_up, w_out_t), "mp")
    piece2 = jnp.concatenate([piece(w_down), piece(w_qkv)])
    z2 = lax.all_gather(piece2, "mp")
    (attended,), done = attend(1, *common, w_qkv, hot, heads, size, (piece2,))
    mixed = [attended[slots - 1]] + [place.shift(attended[k - 1], k) for k in range(1, slots)]
    halved, _ = split(offs, z1, eighth, (done,))
    s1, done1 = place.first_round(*halved, mixed[1:])
    first = place.second_round(*s1)
    (*halved, z2), done = split(offs, z2, eighth, (done1,))
    all_qkv = lax.all_gather(z2, group)
    all_qkv = all_qkv.reshape((2, 2, 2) + all_qkv.shape[-3:])
    own = (w_gate, w_up, w_out_t)
    (hid, normed_ffn, *gates), done = ffn_in_first(
        slots // 2, offs, tokens, gain_f, mixed, own, first, length, (done,)
    )
    s2, done = place.first_round(*halved, (done,))
    (act, dact, inner), done = ffn_in_rest(slots // 2, offs, normed_ffn, gates, first, (done,))
    second = place.second_round(*s2, (done,))
    (score, nfin, ge, gain_fin, gft, ghf), _ = ffn_out(
        offs, hid, inner, gain_l, w_proj, pad_cols, query_emb, score_cot, top_index, w_down, second
    )
    down_sides = ([inner, nfin], [(gft, 0), (ge, 1)])
    (send,), _ = products(offs, *down_sides, slots)
    kept, kept_done = products(offs, *down_sides, slots, place.swap(send, CORE))
    down = Reduce(place, offs, kept)
    (gg, gu, gha, gat, gm, gain_mid), done = ffn_back(
        offs, hid, gft, ghf, act, dact, gain_f, own, first, w_down, second, (kept_done,)
    )
    done = down.first((done,))
    gu_sides = ([normed_ffn], [(gg, 0), (gu, 0)])
    (send,), _ = products(offs, *gu_sides, slots, None, (done,))
    got = place.swap(send, CORE)
    finish = [gha, gat, gain_fin, gain_mid, score]

    def back(first, acc, left, after):
        return attend_back(
            first, slots // 2, common + (hot,), gm, mixed, acc, left, finish, all_qkv, heads, size,
            after,
        )

    (left, tables, acc), done = back(0, None, None, (done,))
    done = down.second((done,))
    kept, done = products(offs, *gu_sides, slots, got, (done,))
    gate_up = Reduce(place, offs, kept)
    finish.append(tables)
    (left, _, dx, both, small), done = back(slots // 2, acc, left, (done,))
    right, left_ = place.both_ways(dx, dx)
    done = down.third((done,))
    done = gate_up.first((done,))
    (send,), _ = attn_products(offs, left, both, small, None, (done,))
    kept, done = attn_products(offs, left, both, small, place.swap(send, CORE))
    attn = Reduce(place, offs, kept)
    (*so_far, right, left_), done = collect(1, slots, offs, right, left_, dx, None, (done,))
    done = gate_up.second_and_third((done,))
    done = attn.first((done,))
    right, left_ = place.both_ways(right, left_)
    done = attn.second((done,))
    (*so_far, right, left_), done = collect(2, slots, offs, right, left_, dx, so_far, (done,))
    start_after = (done,)
    right, left_ = place.both_ways(right, left_)
    done = attn.third((done,))
    (input_grad, packed), done = collect(3, slots, offs, right, left_, dx, so_far, (done,))
    (grad_down, grad_proj, grad_gate, grad_up), done = gathered(
        down.total, gate_up.total, (d, w_proj.shape[1], hidden, hidden), start_after, (done,)
    )
    last, _ = place.first_round(*halves(attn.total, 0), (done,))
    grad_q, grad_k, grad_v, grad_out, small = unpack(
        offs, place.second_round(*last), 4, small.shape[2]
    )

    input_grad = input_grad.reshape(rows * length, d)
    n, m = score.shape
    packed = packed.astype(f32).reshape(slots, 16, d // 128, 128)[:, :, : 2 * (n // 16), :m]
    packed = packed[:, :, 0::2] + packed[:, :, 1::2]
    scores = packed.transpose(0, 2, 1, 3).reshape(slots, n, m)
    return (
        scores,
        input_grad,
        small[:, 0],
        grad_q.T,
        grad_k.T,
        grad_v.T,
        grad_out,
        small[:buckets, 64 : 64 + heads],
        small[:, 2],
        grad_gate,
        grad_up,
        grad_down,
        small[:, 1],
        grad_proj,
    )


def solution(mesh):
    n_dp, n_mp = mesh.shape["dp"], mesh.shape["mp"]
    mesh = Mesh(mesh.devices.reshape(n_dp // 8, 2, 2, 2, n_mp), dp + ("mp",))
    return jax.shard_map(
        local,
        mesh=mesh,
        in_specs=(
            P(dp, None),
            P(dp, None),
            P(dp, None),
            P(dp, None, None),
            P(dp, None, None),
            P(dp, None, None),
            P(),
            P(None, "mp"),
            P(None, "mp"),
            P(None, "mp"),
            P("mp", None),
            P(None, "mp"),
            P(),
            P(None, "mp"),
            P(None, "mp"),
            P("mp", None),
            P(),
            P(),
        ),
        out_specs=(
            P(dp, None, None),
            P(dp, None),
            P(),
            P(None, "mp"),
            P(None, "mp"),
            P(None, "mp"),
            P("mp", None),
            P(None, "mp"),
            P(),
            P(None, "mp"),
            P(None, "mp"),
            P("mp", None),
            P(),
            P(),
        ),
        check_vma=False,
    )
```

time: 495 us -> 451 us (0.911); the launches traced: 488 us -> 451 us
  Pallas kernels: 180 us -> 148 us
  local copies, waits for them, and re-layouts: 41.1 us -> 60.1 us
  other arithmetic: 17.9 us -> 1.97 us
  starting transfers between devices: 86.4 us -> 71.1 us
  waiting for transfers between devices: 148 us -> 154 us
    pallas_call x26 -> x33, Pallas kernels: 180 us -> 148 us  [launch(): pl.pallas_call(body, out_shape=list(out_shape) + [jax.ShapeDtypeStruct(to...]
    unnamed x136 -> x202, local copies, waits for them, and re-layouts: 22.8 us -> 53 us
    ppermute x15 -> x9, starting transfers between devices: 42 us -> 14.2 us  [shift(): return lax.ppermute(v, 'mp', [(i, (i + k) % n) for i in range(n)])]
    all_gather x4, waiting for transfers between devices: 0.03 us -> 25 us  [the longest x1 16.9 us: local(): z1 = lax.all_gather(piece(w_gate, w_up, w_out_t), 'mp')]
    ppermute x31 -> x39, waiting for transfers between devices: 78.6 us -> 53.8 us  [swap(): return lax.ppermute(v, name, [(0, 1), (1, 0)])]
    ppermute x6, waiting for transfers between devices: 15.1 us -> 30 us  [the longest x3 24.5 us: both_ways(): right = lax.ppermute(right, 'mp', [(i, i + 1) for i in range(n - 1)])]
    reduce_scatter x0 -> x1, starting transfers between devices: none -> 12.9 us  [second_and_third(): total = lax.psum_scatter(v, 'mp', scatter_dimension=0, tiled=True)]
    ppermute x15 -> x9, waiting for transfers between devices: 54.4 us -> 45.2 us  [shift(): return lax.ppermute(v, 'mp', [(i, (i + k) % n) for i in range(n)])]
  transfers between devices with their start and end apart: 56 -> 59, of which waited for: 26 -> 23; matrix products, arithmetic and copies ran while one was open for 7% -> 1% of each run, Pallas kernels for 37% -> 25%
where the time goes in v2:
time: 451 us
  waiting for transfers between devices  154 us (34%)
  Pallas kernels  148 us (33%)
  starting transfers between devices  71.1 us (16%)
  local copies, waits for them, and re-layouts  60.1 us (13%)
  between operations  15.1 us (3%)
    pallas_call x33, Pallas kernels, launch(): pl.pallas_call(body, out_shape=list(out_shape) + [jax.ShapeDtypeStruct(to...  148 us
    ppermute x39, waiting for transfers between devices, swap(): return lax.ppermute(v, name, [(0, 1), (1, 0)])  53.8 us
    unnamed x202, local copies, waits for them, and re-layouts  53 us
    ppermute x9, waiting for transfers between devices, shift(): return lax.ppermute(v, 'mp', [(i, (i + k) % n) for i in range(n)])  45.2 us
    ppermute x39, starting transfers between devices, swap(): return lax.ppermute(v, name, [(0, 1), (1, 0)])  28.5 us
    ppermute x3, waiting for transfers between devices, both_ways(): right = lax.ppermute(right, 'mp', [(i, i + 1) for i in range(n - 1)])  24.5 us
    all_gather x1, waiting for transfers between devices, local(): z1 = lax.all_gather(piece(w_gate, w_up, w_out_t), 'mp')  16.9 us
    ppermute x9, starting transfers between devices, shift(): return lax.ppermute(v, 'mp', [(i, (i + k) % n) for i in range(n)])  14.2 us
  transfers between devices with their start and end apart: 59, of which 23 were waited for; matrix products, arithmetic and copies ran while one was open for 1% of the time, Pallas kernels for 25%

profile of v2, /device:TPU:0, one launch (start us, length us, event | category | flops | bytes accessed | tf_op | source)
XLA Modules:
  0.0 450.5 jit_solution(8221299639890598536)
XLA Ops:
  17.8 10.7 %attend.1 = (bf16[4,528,192]{2,1,0:T(8,128)(2,1)S(1)}, f32[8,128]{1,0:T(8,128)S(1)}) custom-call(s32[20]{0:T(128)S(1)} %stack.83.refs_0_, bf16[2048,768]{1,0:T(8,128)(2,1)S(1)} %copy-done.4, f32[4,512]{1,0:T(4,128)S(1)} %convert_element_type.4.refs_2_, f32[4,512]{1,0:T(4,128)S(1)} %get-tuple-element.352.refs_3_, f32[512,4]{1,0:T(8,128)S(1)} %bitcast.56, ...), custom_call_target="tpu_custom_call" | custom-call | flops 2617245696 | bytes 4194304 | tf_op jit(solution)/shard_map/attend/pallas_call | solution.py:84
  30.1 16.9 %all-gather.9.cloned.1.call-done = bf16[384,1728]{1,0:T(8,128)(2,1)} async-done(((bf16[96,1728]{1,0:T(8,128)(2,1)}), bf16[384,1728]{1,0:T(8,128)(2,1)}) %all-gather.9.cloned.1.call-update) | async-done | bytes 1327120 | tf_op jit(solution)/shard_map/all_gather | solution.py:1258
  55.2 2.4 collective-permute-start.2
  57.6 7.0 %collective-permute-done.refs_4_.refs_9_ = bf16[528,192]{1,0:T(8,128)(2,1)S(1)} collective-permute-done((bf16[528,192]{1,0:T(8,128)(2,1)S(1)}, bf16[528,192]{1,0:T(8,128)(2,1)S(1)}, u32[]{:S(2)}, u32[]{:S(2)}) %collective-permute-start) | collective-permute-done | bytes 202784 | tf_op jit(solution)/shard_map/ppermute | solution.py:125
  64.6 9.2 %collective-permute-done.1.refs_5_.refs_8_ = bf16[528,192]{1,0:T(8,128)(2,1)S(1)} collective-permute-done((bf16[528,192]{1,0:T(8,128)(2,1)S(1)}, bf16[528,192]{1,0:T(8,128)(2,1)S(1)}, u32[]{:S(2)}, u32[]{:S(2)}) %collective-permute-start.1) | collective-permute-done | bytes 202784 | tf_op jit(solution)/shard_map/ppermute | solution.py:125
  77.2 21.4 %collective-permute-done.6.refs_13_.refs_5_ = bf16[2,3,48,1728]{3,2,1,0:T(8,128)(2,1)S(1)} collective-permute-done((bf16[2,3,48,1728]{3,2,1,0:T(8,128)(2,1)S(1)}, bf16[2,3,48,1728]{3,2,1,0:T(8,128)(2,1)S(1)}, u32[]{:S(2)}, u32[]{:S(2)}) %collective-permute-start.6) | collective-permute-done | bytes 995360 | tf_op jit(solution)/shard_map/ppermute | solution.py:121
  100.1 8.0 %all-gather.11.cloned.1.call-done = bf16[704,768]{1,0:T(8,128)(2,1)} async-done(((bf16[176,768]{1,0:T(8,128)(2,1)}), bf16[704,768]{1,0:T(8,128)(2,1)}) %all-gather.11.cloned.1.call-update) | async-done | bytes 1081360 | tf_op jit(solution)/shard_map/all_gather | solution.py:1260
  113.8 1.9 copy-done.5
  125.7 8.9 %ffn_in_first.1 = (f32[512,768]{1,0:T(8,128)S(1)}, bf16[512,768]{1,0:T(8,128)(2,1)S(1)}, bf16[4,512,768]{2,1,0:T(8,128)(2,1)S(1)}, bf16[4,512,768]{2,1,0:T(8,128...) custom-call(s32[20]{0:T(128)S(1)} %stack.83.refs_0_, bf16[2048,768]{1,0:T(8,128)(2,1)S(1)} %copy-done.5, ...), custom_call_target="tpu_custom_call" | custom-call | flops 3019898880 | bytes 16777216 | tf_op jit(solution)/shard_map/ffn_in_first/pallas_call | solution.py:84
  137.4 6.8 %ffn_in_rest.1 = (bf16[4,512,768]{2,1,0:T(8,128)(2,1)S(1)}, bf16[4,512,768]{2,1,0:T(8,128)(2,1)S(1)}, bf16[4,512,768]{2,1,0:T(8,128)(2,1)S(1)}, f32[8,128]{1,0:T(8,128)S(1)}) custom-call(s32[20]{0:T(128)S(1)} %stack.83.refs_0_, bf16[512,768]{1,0:T(8,128)(2,1)S(1)} %get-tuple-element.158.refs_1_, ...), custom_call_target="tpu_custom_call", output_to_operand_aliasing={{0}: (10, {}), {1}: (11, {}), {2}: (12, {})} | custom-call | flops 2415919104 | bytes 16777216 | tf_op jit(solution)/shard_map/ffn_in_rest/pallas_call | solution.py:84
  144.3 1.7 copy-done.31
  145.9 1.7 copy-done.32
  158.3 11.0 %ffn_out.1 = (f32[32,32]{1,0:T(8,128)S(1)}, bf16[512,768]{1,0:T(8,128)(2,1)S(1)}, bf16[512,128]{1,0:T(8,128)(2,1)S(1)}, f32[1,768]{1,0:T(1,128)S(1)}, bf16[512,7...) custom-call(s32[20]{0:T(128)S(1)} %stack.83.refs_0_, f32[512,768]{1,0:T(8,128)S(1)} %copy-done.41, ...), custom_call_target="tpu_custom_call" | custom-call | flops 2415919104 | bytes 16777216 | tf_op jit(solution)/shard_map/ffn_out/pallas_call | solution.py:84
  169.4 4.4 products_send.2
  174.0 12.9 %reduce-scatter.2.cloned.1.call-start = ((), (), s32[]{:S(2)}) async-start(), calls=%async_computation.1 | async-start | bytes 1474560 | tf_op jit(solution)/shard_map/reduce_scatter | solution.py:1154
  189.4 5.0 %products_keep.2 = (bf16[4,2,48,896]{3,2,1,0:T(8,128)(2,1)S(1)}, bf16[4,2,48,896]{3,2,1,0:T(8,128)(2,1)S(1)}, bf16[4,2,48,896]{3,2,1,0:T(8,128)(2,1)S(1)}, bf16[...) custom-call(s32[20]{0:T(128)S(1)} %stack.83.refs_0_, bf16[4,512,768]{2,1,0:T(8,128)(2,1)S(1)} %get-tuple-element.166.refs_2_.refs_1_, ...), custom_call_target="tpu_custom_call" | custom-call | flops 1048576 | bytes 65536 | tf_op jit(solution)/shard_map/products_keep/pallas_call | solution.py:84
  197.5 21.2 %ffn_back.1 = (bf16[4,512,768]{2,1,0:T(8,128)(2,1)}, bf16[4,512,768]{2,1,0:T(8,128)(2,1)}, f32[512,768]{1,0:T(8,128)}, bf16[512,768]{1,0:T(8,128)(2,1)S(1)}, bf1...) custom-call(s32[20]{0:T(128)S(1)} %stack.83.refs_0_, f32[512,768]{1,0:T(8,128)} %copy-done.40, ...), custom_call_target="tpu_custom_call" | custom-call | flops 7851737088 | bytes 25165824 | tf_op jit(solution)/shard_map/ffn_back/pallas_call | solution.py:84
  218.7 3.6 collective-permute-done.20.refs_2_
  222.3 2.1 second_sums.3
  225.9 1.9 copy-done
  227.8 1.9 copy-done.2
  229.7 5.1 %products_send.3 = (bf16[4,384,1536]{2,1,0:T(8,128)(2,1)}, f32[8,128]{1,0:T(8,128)}) custom-call(s32[20]{0:T(128)S(1)} %stack.83.refs_0_, bf16[512,768]{1,0:T(8,128)(2,1)S(1)} %copy-done.10, bf16[4,512,768]{2,1,0:T(8,128)(2,1)S(1)} %copy-done, bf16[4,512,768]{2,1,0:T(8,128)(2,1)S(1)} %copy-done.2, f32[8,128]{1,0:T(8,128)S(1)} %get-tuple-element.187.refs_11_.refs_4_), custom_call_target="tpu_custom_call" | custom-call | flops 1048576 | bytes 65536 | tf_op jit(solution)/shard_map/products_send/pallas_call | solution.py:84
  236.8 2.1 copy-done.24
  243.9 16.5 %attend_back0.1 = (bf16[4,4,512,192]{3,2,1,0:T(8,128)(2,1)S(1)}, f32[16,128]{1,0:T(8,128)S(1)}, f32[512,768]{1,0:T(8,128)S(1)}, f32[8,128]{1,0:T(8,128)S(1)}) custom-call(s32[20]{0:T(128)S(1)} %stack.83.refs_0_, bf16[2048,768]{1,0:T(8,128)(2,1)S(1)} %copy-done.6, f32[4,512]{1,0:T(4,128)S(1)} %copy-done.75, f32[4,512]{1,0:T(4,128)S(1)} %copy-done.80, ...), custom_call_target="tpu_custom_call" | custom-call | flops 3221225472 | bytes 16777216 | tf_op jit(solution)/shard_map/attend_back0/pallas_call | solution.py:84
  261.9 7.2 %products_keep.3 = (bf16[4,2,48,1536]{3,2,1,0:T(8,128)(2,1)}, bf16[4,2,48,1536]{3,2,1,0:T(8,128)(2,1)S(1)}, bf16[4,2,48,1536]{3,2,1,0:T(8,128)(2,1)}, bf16[4,2,48,1536]{3,2,1,0:T(8,128)(2,1)S(1)}, f32[8,128]{1,0:T(8,128)S(1)}) custom-call(s32[20]{0:T(128)S(1)} %stack.83.refs_0_, bf16[512,768]{1,0:T(8,128)(2,1)S(1)} %copy-done.11, ...), custom_call_target="tpu_custom_call" | custom-call | flops 1048576 | bytes 65536 | tf_op jit(solution)/shard_map/products_keep/pallas_call | solution.py:84
  271.1 3.3 collective-permute-start.29
  275.6 17.6 %attend_back2.1 = (bf16[4,4,512,192]{3,2,1,0:T(8,128)(2,1)S(1)}, f32[16,128]{1,0:T(8,128)}, bf16[528,768]{1,0:T(8,128)(2,1)S(1)}, bf16[2,512,768]{2,1,0:T(8,128)...) custom-call(s32[20]{0:T(128)S(1)} %stack.83.refs_0_, ...), custom_call_target="tpu_custom_call", output_to_operand_aliasing={{0}: (18, {})} | custom-call | flops 3221225472 | bytes 16777216 | tf_op jit(solution)/shard_map/attend_back2/pallas_call | solution.py:84
  293.4 3.8 collective-permute-done.27.refs_2_
  299.5 3.2 attn_send.1
  302.7 3.4 collective-permute-start.25
  309.4 2.9 attn_keep.1
  312.4 11.7 %collective-permute-done.25.refs_1_ = bf16[528,768]{1,0:T(8,128)(2,1)S(1)} collective-permute-done((bf16[528,768]{1,0:T(8,128)(2,1)S(1)}, bf16[528,768]{1,0:T(8,128)(2,1)S(1)}, u32[]{:S(2)}, u32[]{:S(2)}) %collective-permute-start.25) | collective-permute-done | bytes 811040 | tf_op jit(solution)/shard_map/ppermute | solution.py:140
  324.0 4.2 collective-permute-done.26.refs_2_
  328.2 2.5 collect1.1
  331.5 1.8 third_stacked.1
  335.5 3.4 collective-permute-start.33
  340.2 10.3 %collective-permute-done.35.refs_2_ = bf16[4,2,48,896]{3,2,1,0:T(8,128)(2,1)S(1)} collective-permute-done((bf16[4,2,48,896]{3,2,1,0:T(8,128)(2,1)}, bf16[4,2,48,896]{3,2,1,0:T(8,128)(2,1)S(1)}, u32[]{:S(2)}, u32[]{:S(2)}) %collective-permute-start.35) | collective-permute-done | bytes 688160 | tf_op jit(solution)/shard_map/ppermute | solution.py:121
  353.8 6.3 %collective-permute-done.39.refs_1_ = bf16[4,48,896]{2,1,0:T(8,128)(2,1)S(1)} collective-permute-done((bf16[4,48,896]{2,1,0:T(8,128)(2,1)S(1)}, bf16[4,48,896]{2,1,0:T(8,128)(2,1)S(1)}, u32[]{:S(2)}, u32[]{:S(2)}) %collective-permute-start.39) | collective-permute-done | bytes 344096 | tf_op jit(solution)/shard_map/ppermute | solution.py:121
  361.4 12.8 %collective-permute-done.33.refs_1_ = bf16[528,768]{1,0:T(8,128)(2,1)S(1)} collective-permute-done((bf16[528,768]{1,0:T(8,128)(2,1)}, bf16[528,768]{1,0:T(8,128)(2,1)S(1)}, u32[]{:S(2)}, u32[]{:S(2)}) %collective-permute-start.33) | collective-permute-done | bytes 811040 | tf_op jit(solution)/shard_map/ppermute | solution.py:140
  375.5 2.5 collect2.1
  379.8 4.2 collective-permute-start.41
  385.3 3.0 collective-permute-start.43
  390.8 17.8 %collective-permute-done.43.refs_1_ = bf16[96,896]{1,0:T(8,128)(2,1)S(1)} collective-permute-done((bf16[96,896]{1,0:T(8,128)(2,1)S(1)}, bf16[96,896]{1,0:T(8,128)(2,1)S(1)}, u32[]{:S(2)}, u32[]{:S(2)}) %collective-permute-start.43) | collective-permute-done | bytes 172064 | tf_op jit(solution)/shard_map/ppermute | solution.py:125
  408.7 11.1 %collective-permute-done.44.refs_2_ = bf16[96,896]{1,0:T(8,128)(2,1)S(1)} collective-permute-done((bf16[96,896]{1,0:T(8,128)(2,1)S(1)}, bf16[96,896]{1,0:T(8,128)(2,1)S(1)}, u32[]{:S(2)}, u32[]{:S(2)}) %collective-permute-start.44) | collective-permute-done | bytes 172064 | tf_op jit(solution)/shard_map/ppermute | solution.py:125
  422.7 2.4 collect3.1
  425.6 5.3 %open.1 = (f32[768,768]{1,0:T(8,128)}, f32[768,128]{1,0:T(8,128)}, f32[768,768]{1,0:T(8,128)}, f32[768,768]{1,0:T(8,128)}, f32[8,128]{1,0:T(8,128)}) custom-call(bf16[2,2,2,96,2432]{4,3,2,1,0:T(8,128)(2,1)} %bitcast.61, f32[8,128]{1,0:T(8,128)} %copy-done.86), custom_call_target="tpu_custom_call" | custom-call | flops 1048576 | bytes 65536 | tf_op jit(solution)/shard_map/open/pallas_call | solution.py:84
  434.6 3.0 collective-permute-done.48.refs_3_
  439.7 2.2 unpack.1
  (335 shorter events, 105.5 us)
Async XLA Ops:
  7.2 39.8 %all-gather.9.cloned.1.call-start = ((), (), s32[]{:S(2)}) async-start(), calls=%async_computation.2 | async-start | bytes 1720320 | tf_op jit(solution)/shard_map/all_gather | solution.py:1258
  10.4 97.8 %all-gather.11.cloned.1.call-start = ((), (), s32[]{:S(2)}) async-start(), calls=%async_computation.3 | async-start | bytes 1351680 | tf_op jit(solution)/shard_map/all_gather | solution.py:1260
  49.5 24.3 %collective-permute-start.3 = (bf16[3,48,1728]{2,1,0:T(8,128)(2,1)S(1)}, bf16[3,48,1728]{2,1,0:T(8,128)(2,1)S(1)}, u32[]{:S(2)}, u32[]{:S(2)}) collective-permute-start(bf16[3,48,1728]{2,1,0:T(8,128)(2,1)S(1)} %get-tuple-element.151.refs_0_), channel_id=1, source_target_pairs={{0,8},{8,0},{1,9},{9,1},{2,10},{10,2},{3,11},{11,3},{4,12},{12,4},... | collective-permute-start | bytes 1493000 | tf_op jit(solution)/shard_map/ppermute | solution.py:121
  51.0 22.8 %collective-permute-start.4 = (bf16[3,48,1728]{2,1,0:T(8,128)(2,1)S(1)}, bf16[3,48,1728]{2,1,0:T(8,128)(2,1)S(1)}, u32[]{:S(2)}, u32[]{:S(2)}) collective-permute-start(bf16[3,48,1728]{2,1,0:T(8,128)(2,1)S(1)} %get-tuple-element.152.refs_2_), channel_id=1, source_target_pairs={{0,16},{16,0},{1,17},{17,1},{2,18},{18,2},{3,19},{19,3},{4,20},{20... | collective-permute-start | bytes 1493000 | tf_op jit(solution)/shard_map/ppermute | solution.py:121
  53.3 11.3 %collective-permute-start = (bf16[528,192]{1,0:T(8,128)(2,1)S(1)}, bf16[528,192]{1,0:T(8,128)(2,1)S(1)}, u32[]{:S(2)}, u32[]{:S(2)}) collective-permute-start(bf16[528,192]{1,0:T(8,128)(2,1)S(1)} %get-tuple-element.347), channel_id=1, source_target_pairs={{0,1},{1,2},{2,3},{3,0},{4,5},{5,6},{6,7},{7,4},{8,9},{9,10},{10,1... | collective-permute-start | bytes 608264 | tf_op jit(solution)/shard_map/ppermute | solution.py:125
  54.0 19.8 %collective-permute-start.1 = (bf16[528,192]{1,0:T(8,128)(2,1)S(1)}, bf16[528,192]{1,0:T(8,128)(2,1)S(1)}, u32[]{:S(2)}, u32[]{:S(2)}) collective-permute-start(bf16[528,192]{1,0:T(8,128)(2,1)S(1)} %get-tuple-element.346), channel_id=1, source_target_pairs={{0,2},{1,3},{2,0},{3,1},{4,6},{5,7},{6,4},{7,5},{8,10},{9,11},{10,... | collective-permute-start | bytes 608264 | tf_op jit(solution)/shard_map/ppermute | solution.py:125
  55.2 18.6 %collective-permute-start.2 = (bf16[528,192]{1,0:T(8,128)(2,1)S(1)}, bf16[528,192]{1,0:T(8,128)(2,1)S(1)}, u32[]{:S(2)}, u32[]{:S(2)}) collective-permute-start(bf16[528,192]{1,0:T(8,128)(2,1)S(1)} %get-tuple-element.345), channel_id=1, source_target_pairs={{0,3},{1,0},{2,1},{3,2},{4,7},{5,4},{6,5},{7,6},{8,11},{9,8},{10,9... | collective-permute-start | bytes 608264 | tf_op jit(solution)/shard_map/ppermute | solution.py:125
  74.0 24.6 %collective-permute-start.6 = (bf16[2,3,48,1728]{3,2,1,0:T(8,128)(2,1)S(1)}, bf16[2,3,48,1728]{3,2,1,0:T(8,128)(2,1)S(1)}, u32[]{:S(2)}, u32[]{:S(2)}) collective-permute-start(bf16[2,3,48,1728]{3,2,1,0:T(8,128)(2,1)S(1)} %get-tuple-element.154.refs_11_.refs_3_), channel_id=1, source_target_pairs={{0,8},{8,0},{1,9},{9,1},{2,10},{10,2},{3,11},{11,3},{4,12},{12,4},... | collective-permute-start | bytes 2985992 | tf_op jit(solution)/shard_map/ppermute | solution.py:121
  74.6 25.0 %collective-permute-start.5 = (bf16[2,3,48,1728]{3,2,1,0:T(8,128)(2,1)S(1)}, bf16[2,3,48,1728]{3,2,1,0:T(8,128)(2,1)}, u32[]{:S(2)}, u32[]{:S(2)}) collective-permute-start(bf16[2,3,48,1728]{3,2,1,0:T(8,128)(2,1)S(1)} %get-tuple-element.153.refs_10_.refs_2_), channel_id=1, source_target_pairs={{0,16},{16,0},{1,17},{17,1},{2,18},{18,2},{3,19},{19,3},{4,20},{20... | collective-permute-start | bytes 2985992 | tf_op jit(solution)/shard_map/ppermute | solution.py:121
  75.2 161.6 %all-gather.13.cloned.1.call-start = ((), (), s32[]{:S(2)}) async-start(), calls=%async_computation.4 | async-start | bytes 4423680 | tf_op jit(solution)/shard_map/all_gather | solution.py:1267
  75.6 36.6 %collective-permute-start.7 = (bf16[2,3,48,1728]{3,2,1,0:T(8,128)(2,1)S(1)}, bf16[2,3,48,1728]{3,2,1,0:T(8,128)(2,1)}, u32[]{:S(2)}, u32[]{:S(2)}) collective-permute-start(bf16[2,3,48,1728]{3,2,1,0:T(8,128)(2,1)S(1)} %get-tuple-element.153.refs_10_.refs_2_), channel_id=1, source_target_pairs={{0,4},{4,0},{1,5},{5,1},{2,6},{6,2},{3,7},{7,3},{8,12},{12,8},{9,1... | collective-permute-start | bytes 2985992 | tf_op jit(solution)/shard_map/ppermute | solution.py:121
  75.7 38.0 %collective-permute-start.8 = (bf16[2,3,48,1728]{3,2,1,0:T(8,128)(2,1)S(1)}, bf16[2,3,48,1728]{3,2,1,0:T(8,128)(2,1)}, u32[]{:S(2)}, u32[]{:S(2)}) collective-permute-start(bf16[2,3,48,1728]{3,2,1,0:T(8,128)(2,1)S(1)} %get-tuple-element.154.refs_11_.refs_3_), channel_id=1, source_target_pairs={{0,4},{4,0},{1,5},{5,1},{2,6},{6,2},{3,7},{7,3},{8,12},{12,8},{9,1... | collective-permute-start | bytes 2985992 | tf_op jit(solution)/shard_map/ppermute | solution.py:121
  98.6 15.2 %collective-permute-start.10 = (bf16[2,3,48,1728]{3,2,1,0:T(8,128)(2,1)S(1)}, bf16[2,3,48,1728]{3,2,1,0:T(8,128)(2,1)}, u32[]{:S(2)}, u32[]{:S(2)}) collective-permute-start(bf16[2,3,48,1728]{3,2,1,0:T(8,128)(2,1)S(1)} %collective-permute-done.6.refs_13_.refs_5_), channel_id=1, source_target_pairs={{0,4},{4,0},{1,5},{5,1},{2,6},{6,2},{3,7},{7,3},{8,12},{12,8},{9,1... | collective-permute-start | bytes 2985992 | tf_op jit(solution)/shard_map/ppermute | solution.py:121
  99.6 14.1 %collective-permute-start.9 = (bf16[2,3,48,1728]{3,2,1,0:T(8,128)(2,1)}, bf16[2,3,48,1728]{3,2,1,0:T(8,128)(2,1)}, u32[]{:S(2)}, u32[]{:S(2)}) collective-permute-start(bf16[2,3,48,1728]{3,2,1,0:T(8,128)(2,1)} %collective-permute-done.5.refs_12_.refs_4_), channel_id=1, source_target_pairs={{0,4},{4,0},{1,5},{5,1},{2,6},{6,2},{3,7},{7,3},{8,12},{12,8},{9,1... | collective-permute-start | bytes 2985992 | tf_op jit(solution)/shard_map/ppermute | solution.py:121
  110.8 23.9 %collective-permute-start.11 = (bf16[3,48,768]{2,1,0:T(8,128)(2,1)S(1)}, bf16[3,48,768]{2,1,0:T(8,128)(2,1)S(1)}, u32[]{:S(2)}, u32[]{:S(2)}) collective-permute-start(bf16[3,48,768]{2,1,0:T(8,128)(2,1)S(1)} %get-tuple-element.162.refs_0_), channel_id=1, source_target_pairs={{0,8},{8,0},{1,9},{9,1},{2,10},{10,2},{3,11},{11,3},{4,12},{12,4},... | collective-permute-start | bytes 663560 | tf_op jit(solution)/shard_map/ppermute | solution.py:121
  112.3 22.4 %collective-permute-start.12 = (bf16[3,48,768]{2,1,0:T(8,128)(2,1)S(1)}, bf16[3,48,768]{2,1,0:T(8,128)(2,1)S(1)}, u32[]{:S(2)}, u32[]{:S(2)}) collective-permute-start(bf16[3,48,768]{2,1,0:T(8,128)(2,1)S(1)} %get-tuple-element.163.refs_2_), channel_id=1, source_target_pairs={{0,16},{16,0},{1,17},{17,1},{2,18},{18,2},{3,19},{19,3},{4,20},{20... | collective-permute-start | bytes 663560 | tf_op jit(solution)/shard_map/ppermute | solution.py:121
  135.8 11.8 %collective-permute-start.13 = (bf16[2,3,48,768]{3,2,1,0:T(8,128)(2,1)}, bf16[2,3,48,768]{3,2,1,0:T(8,128)(2,1)S(1)}, u32[]{:S(2)}, u32[]{:S(2)}) collective-permute-start(bf16[2,3,48,768]{3,2,1,0:T(8,128)(2,1)} %get-tuple-element.167.refs_10_.refs_19_), channel_id=1, source_target_pairs={{0,16},{16,0},{1,17},{17,1},{2,18},{18,2},{3,19},{19,3},{4,20},{20... | collective-permute-start | bytes 1327112 | tf_op jit(solution)/shard_map/ppermute | solution.py:121
  136.3 11.3 %collective-permute-start.14 = (bf16[2,3,48,768]{3,2,1,0:T(8,128)(2,1)}, bf16[2,3,48,768]{3,2,1,0:T(8,128)(2,1)S(1)}, u32[]{:S(2)}, u32[]{:S(2)}) collective-permute-start(bf16[2,3,48,768]{3,2,1,0:T(8,128)(2,1)} %get-tuple-element.168.refs_11_.refs_20_), channel_id=1, source_target_pairs={{0,8},{8,0},{1,9},{9,1},{2,10},{10,2},{3,11},{11,3},{4,12},{12,4},... | collective-permute-start | bytes 1327112 | tf_op jit(solution)/shard_map/ppermute | solution.py:121
  136.9 13.1 %collective-permute-start.15 = (bf16[2,3,48,768]{3,2,1,0:T(8,128)(2,1)}, bf16[2,3,48,768]{3,2,1,0:T(8,128)(2,1)}, u32[]{:S(2)}, u32[]{:S(2)}) collective-permute-start(bf16[2,3,48,768]{3,2,1,0:T(8,128)(2,1)} %get-tuple-element.167.refs_10_.refs_19_), channel_id=1, source_target_pairs={{0,4},{4,0},{1,5},{5,1},{2,6},{6,2},{3,7},{7,3},{8,12},{12,8},{9,1... | collective-permute-start | bytes 1327112 | tf_op jit(solution)/shard_map/ppermute | solution.py:121
  136.9 13.1 %collective-permute-start.16 = (bf16[2,3,48,768]{3,2,1,0:T(8,128)(2,1)}, bf16[2,3,48,768]{3,2,1,0:T(8,128)(2,1)}, u32[]{:S(2)}, u32[]{:S(2)}) collective-permute-start(bf16[2,3,48,768]{3,2,1,0:T(8,128)(2,1)} %get-tuple-element.168.refs_11_.refs_20_), channel_id=1, source_target_pairs={{0,4},{4,0},{1,5},{5,1},{2,6},{6,2},{3,7},{7,3},{8,12},{12,8},{9,1... | collective-permute-start | bytes 1327112 | tf_op jit(solution)/shard_map/ppermute | solution.py:121
  173.8 13.2 %collective-permute-start.19 = (bf16[4,384,896]{2,1,0:T(8,128)(2,1)}, bf16[4,384,896]{2,1,0:T(8,128)(2,1)}, u32[]{:S(2)}, u32[]{:S(2)}) collective-permute-start(bf16[4,384,896]{2,1,0:T(8,128)(2,1)} %get-tuple-element.178), channel_id=1, source_target_pairs={{0,4},{4,0},{1,5},{5,1},{2,6},{6,2},{3,7},{7,3},{8,12},{12,8},{9,1... | collective-permute-start | bytes 8257544 | tf_op jit(solution)/shard_map/ppermute | solution.py:121
  174.0 204.0 %reduce-scatter.2.cloned.1.call-start = ((), (), s32[]{:S(2)}) async-start(), calls=%async_computation.1 | async-start | bytes 1474560 | tf_op jit(solution)/shard_map/reduce_scatter | solution.py:1154
  194.4 27.9 %collective-permute-start.20 = (bf16[4,2,48,896]{3,2,1,0:T(8,128)(2,1)S(1)}, bf16[4,2,48,896]{3,2,1,0:T(8,128)(2,1)S(1)}, u32[]{:S(2)}, u32[]{:S(2)}) collective-permute-start(bf16[4,2,48,896]{3,2,1,0:T(8,128)(2,1)S(1)} %get-tuple-element.183), channel_id=1, source_target_pairs={{0,8},{8,0},{1,9},{9,1},{2,10},{10,2},{3,11},{11,3},{4,12},{12,4},... | collective-permute-start | bytes 2064392 | tf_op jit(solution)/shard_map/ppermute | solution.py:121
  196.0 26.4 %collective-permute-start.21 = (bf16[4,2,48,896]{3,2,1,0:T(8,128)(2,1)S(1)}, bf16[4,2,48,896]{3,2,1,0:T(8,128)(2,1)S(1)}, u32[]{:S(2)}, u32[]{:S(2)}) collective-permute-start(bf16[4,2,48,896]{3,2,1,0:T(8,128)(2,1)S(1)} %get-tuple-element.185), channel_id=1, source_target_pairs={{0,16},{16,0},{1,17},{17,1},{2,18},{18,2},{3,19},{19,3},{4,20},{20... | collective-permute-start | bytes 2064392 | tf_op jit(solution)/shard_map/ppermute | solution.py:121
  234.7 27.0 %collective-permute-start.22 = (bf16[4,384,1536]{2,1,0:T(8,128)(2,1)}, bf16[4,384,1536]{2,1,0:T(8,128)(2,1)}, u32[]{:S(2)}, u32[]{:S(2)}) collective-permute-start(bf16[4,384,1536]{2,1,0:T(8,128)(2,1)} %get-tuple-element.198), channel_id=1, source_target_pairs={{0,4},{4,0},{1,5},{5,1},{2,6},{6,2},{3,7},{7,3},{8,12},{12,8},{9,1... | collective-permute-start | bytes 14155784 | tf_op jit(solution)/shard_map/ppermute | solution.py:121
  234.7 25.7 %collective-permute-start.23 = (bf16[4,48,896]{2,1,0:T(8,128)(2,1)}, bf16[4,48,896]{2,1,0:T(8,128)(2,1)}, u32[]{:S(2)}, u32[]{:S(2)}) collective-permute-start(bf16[4,48,896]{2,1,0:T(8,128)(2,1)} %get-tuple-element.200), channel_id=1, source_target_pairs={{0,16},{16,0},{1,17},{17,1},{2,18},{18,2},{3,19},{19,3},{4,20},{20... | collective-permute-start | bytes 1032200 | tf_op jit(solution)/shard_map/ppermute | solution.py:121
  236.2 24.2 %collective-permute-start.24 = (bf16[4,48,896]{2,1,0:T(8,128)(2,1)}, bf16[4,48,896]{2,1,0:T(8,128)(2,1)}, u32[]{:S(2)}, u32[]{:S(2)}) collective-permute-start(bf16[4,48,896]{2,1,0:T(8,128)(2,1)} %get-tuple-element.202), channel_id=1, source_target_pairs={{0,8},{8,0},{1,9},{9,1},{2,10},{10,2},{3,11},{11,3},{4,12},{12,4},... | collective-permute-start | bytes 1032200 | tf_op jit(solution)/shard_map/ppermute | solution.py:121
  269.1 28.0 %collective-permute-start.27 = (bf16[4,2,48,1536]{3,2,1,0:T(8,128)(2,1)}, bf16[4,2,48,1536]{3,2,1,0:T(8,128)(2,1)S(1)}, u32[]{:S(2)}, u32[]{:S(2)}) collective-permute-start(bf16[4,2,48,1536]{3,2,1,0:T(8,128)(2,1)} %get-tuple-element.211), channel_id=1, source_target_pairs={{0,8},{8,0},{1,9},{9,1},{2,10},{10,2},{3,11},{11,3},{4,12},{12,4},... | collective-permute-start | bytes 3538952 | tf_op jit(solution)/shard_map/ppermute | solution.py:121
  270.6 27.8 %collective-permute-start.28 = (bf16[4,2,48,1536]{3,2,1,0:T(8,128)(2,1)}, bf16[4,2,48,1536]{3,2,1,0:T(8,128)(2,1)S(1)}, u32[]{:S(2)}, u32[]{:S(2)}) collective-permute-start(bf16[4,2,48,1536]{3,2,1,0:T(8,128)(2,1)} %get-tuple-element.213), channel_id=1, source_target_pairs={{0,16},{16,0},{1,17},{17,1},{2,18},{18,2},{3,19},{19,3},{4,20},{20... | collective-permute-start | bytes 3538952 | tf_op jit(solution)/shard_map/ppermute | solution.py:121
  271.1 22.1 %collective-permute-start.29 = (bf16[96,896]{1,0:T(8,128)(2,1)S(1)}, bf16[96,896]{1,0:T(8,128)(2,1)S(1)}, u32[]{:S(2)}, u32[]{:S(2)}) collective-permute-start(bf16[96,896]{1,0:T(8,128)(2,1)S(1)} %get-tuple-element.215), channel_id=1, source_target_pairs={{0,3},{1,0},{2,1},{3,2},{4,7},{5,4},{6,5},{7,6},{8,11},{9,8},{10,9... | collective-permute-start | bytes 516104 | tf_op jit(solution)/shard_map/ppermute | solution.py:125
  274.4 18.8 %collective-permute-start.30 = (bf16[96,896]{1,0:T(8,128)(2,1)S(1)}, bf16[96,896]{1,0:T(8,128)(2,1)S(1)}, u32[]{:S(2)}, u32[]{:S(2)}) collective-permute-start(bf16[96,896]{1,0:T(8,128)(2,1)S(1)} %get-tuple-element.216), channel_id=1, source_target_pairs={{0,2},{1,3},{2,0},{3,1},{4,6},{5,7},{6,4},{7,5},{8,10},{9,11},{10,... | collective-permute-start | bytes 516104 | tf_op jit(solution)/shard_map/ppermute | solution.py:125
  274.4 18.8 %collective-permute-start.31 = (bf16[96,896]{1,0:T(8,128)(2,1)S(1)}, bf16[96,896]{1,0:T(8,128)(2,1)S(1)}, u32[]{:S(2)}, u32[]{:S(2)}) collective-permute-start(bf16[96,896]{1,0:T(8,128)(2,1)S(1)} %get-tuple-element.217), channel_id=1, source_target_pairs={{0,1},{1,2},{2,3},{3,0},{4,5},{5,6},{6,7},{7,4},{8,9},{9,10},{10,1... | collective-permute-start | bytes 516104 | tf_op jit(solution)/shard_map/ppermute | solution.py:125
  302.7 21.4 %collective-permute-start.25 = (bf16[528,768]{1,0:T(8,128)(2,1)S(1)}, bf16[528,768]{1,0:T(8,128)(2,1)S(1)}, u32[]{:S(2)}, u32[]{:S(2)}) collective-permute-start(bf16[528,768]{1,0:T(8,128)(2,1)S(1)} %get-tuple-element.206.refs_3_), channel_id=1, source_target_pairs={{0,1},{1,2},{2,3},{4,5},{5,6},{6,7},{8,9},{9,10},{10,11},{12,13},{... | collective-permute-start | bytes 2433032 | tf_op jit(solution)/shard_map/ppermute | solution.py:140
  306.1 22.1 %collective-permute-start.26 = (bf16[528,768]{1,0:T(8,128)(2,1)S(1)}, bf16[528,768]{1,0:T(8,128)(2,1)S(1)}, u32[]{:S(2)}, u32[]{:S(2)}) collective-permute-start(bf16[528,768]{1,0:T(8,128)(2,1)S(1)} %get-tuple-element.206.refs_3_), channel_id=1, source_target_pairs={{1,0},{2,1},{3,2},{5,4},{6,5},{7,6},{9,8},{10,9},{11,10},{13,12},{... | collective-permute-start | bytes 2433032 | tf_op jit(solution)/shard_map/ppermute | solution.py:141
  307.4 24.1 %collective-permute-start.37 = (bf16[4,48,1536]{2,1,0:T(8,128)(2,1)S(1)}, bf16[4,48,1536]{2,1,0:T(8,128)(2,1)S(1)}, u32[]{:S(2)}, u32[]{:S(2)}) collective-permute-start(bf16[4,48,1536]{2,1,0:T(8,128)(2,1)S(1)} %get-tuple-element.232), channel_id=1, source_target_pairs={{0,16},{16,0},{1,17},{17,1},{2,18},{18,2},{3,19},{19,3},{4,20},{20... | collective-permute-start | bytes 1769480 | tf_op jit(solution)/shard_map/ppermute | solution.py:121
  308.0 23.5 %collective-permute-start.38 = (bf16[4,48,1536]{2,1,0:T(8,128)(2,1)S(1)}, bf16[4,48,1536]{2,1,0:T(8,128)(2,1)S(1)}, u32[]{:S(2)}, u32[]{:S(2)}) collective-permute-start(bf16[4,48,1536]{2,1,0:T(8,128)(2,1)S(1)} %get-tuple-element.234), channel_id=1, source_target_pairs={{0,8},{8,0},{1,9},{9,1},{2,10},{10,2},{3,11},{11,3},{4,12},{12,4},... | collective-permute-start | bytes 1769480 | tf_op jit(solution)/shard_map/ppermute | solution.py:121
  333.4 91.8 %all-gather.15.cloned.1.call-start = ((), (), s32[]{:S(2)}) async-start(), calls=%async_computation.5 | async-start | bytes 4202496 | tf_op jit(solution)/shard_map/all_gather | solution.py:1192
  333.4 17.0 %collective-permute-start.35 = (bf16[4,2,48,896]{3,2,1,0:T(8,128)(2,1)}, bf16[4,2,48,896]{3,2,1,0:T(8,128)(2,1)S(1)}, u32[]{:S(2)}, u32[]{:S(2)}) collective-permute-start(bf16[4,2,48,896]{3,2,1,0:T(8,128)(2,1)} %copy-done.92), channel_id=1, source_target_pairs={{0,8},{8,0},{1,9},{9,1},{2,10},{10,2},{3,11},{11,3},{4,12},{12,4},... | collective-permute-start | bytes 2064392 | tf_op jit(solution)/shard_map/ppermute | solution.py:121
  334.1 16.7 %collective-permute-start.36 = (bf16[4,2,48,896]{3,2,1,0:T(8,128)(2,1)}, bf16[4,2,48,896]{3,2,1,0:T(8,128)(2,1)S(1)}, u32[]{:S(2)}, u32[]{:S(2)}) collective-permute-start(bf16[4,2,48,896]{3,2,1,0:T(8,128)(2,1)} %copy-done.91), channel_id=1, source_target_pairs={{0,16},{16,0},{1,17},{17,1},{2,18},{18,2},{3,19},{19,3},{4,20},{20... | collective-permute-start | bytes 2064392 | tf_op jit(solution)/shard_map/ppermute | solution.py:121
  335.5 38.7 %collective-permute-start.33 = (bf16[528,768]{1,0:T(8,128)(2,1)}, bf16[528,768]{1,0:T(8,128)(2,1)S(1)}, u32[]{:S(2)}, u32[]{:S(2)}) collective-permute-start(bf16[528,768]{1,0:T(8,128)(2,1)} %copy-done.90), channel_id=1, source_target_pairs={{0,1},{1,2},{2,3},{4,5},{5,6},{6,7},{8,9},{9,10},{10,11},{12,13},{... | collective-permute-start | bytes 2433032 | tf_op jit(solution)/shard_map/ppermute | solution.py:140
  338.9 36.6 %collective-permute-start.34 = (bf16[528,768]{1,0:T(8,128)(2,1)S(1)}, bf16[528,768]{1,0:T(8,128)(2,1)S(1)}, u32[]{:S(2)}, u32[]{:S(2)}) collective-permute-start(bf16[528,768]{1,0:T(8,128)(2,1)S(1)} %get-tuple-element.224), channel_id=1, source_target_pairs={{1,0},{2,1},{3,2},{5,4},{6,5},{7,6},{9,8},{10,9},{11,10},{13,12},{... | collective-permute-start | bytes 2433032 | tf_op jit(solution)/shard_map/ppermute | solution.py:141
  379.8 42.9 %collective-permute-start.41 = (bf16[528,768]{1,0:T(8,128)(2,1)S(1)}, bf16[528,768]{1,0:T(8,128)(2,1)S(1)}, u32[]{:S(2)}, u32[]{:S(2)}) collective-permute-start(bf16[528,768]{1,0:T(8,128)(2,1)S(1)} %get-tuple-element.243), channel_id=1, source_target_pairs={{0,1},{1,2},{2,3},{4,5},{5,6},{6,7},{8,9},{9,10},{10,11},{12,13},{... | collective-permute-start | bytes 2433032 | tf_op jit(solution)/shard_map/ppermute | solution.py:140
  384.0 38.7 %collective-permute-start.42 = (bf16[528,768]{1,0:T(8,128)(2,1)S(1)}, bf16[528,768]{1,0:T(8,128)(2,1)S(1)}, u32[]{:S(2)}, u32[]{:S(2)}) collective-permute-start(bf16[528,768]{1,0:T(8,128)(2,1)S(1)} %get-tuple-element.244), channel_id=1, source_target_pairs={{1,0},{2,1},{3,2},{5,4},{6,5},{7,6},{9,8},{10,9},{11,10},{13,12},{... | collective-permute-start | bytes 2433032 | tf_op jit(solution)/shard_map/ppermute | solution.py:141
  385.3 23.4 %collective-permute-start.43 = (bf16[96,896]{1,0:T(8,128)(2,1)S(1)}, bf16[96,896]{1,0:T(8,128)(2,1)S(1)}, u32[]{:S(2)}, u32[]{:S(2)}) collective-permute-start(bf16[96,896]{1,0:T(8,128)(2,1)S(1)} %get-tuple-element.248), channel_id=1, source_target_pairs={{0,3},{1,0},{2,1},{3,2},{4,7},{5,4},{6,5},{7,6},{8,11},{9,8},{10,9... | collective-permute-start | bytes 516104 | tf_op jit(solution)/shard_map/ppermute | solution.py:125
  388.3 31.5 %collective-permute-start.44 = (bf16[96,896]{1,0:T(8,128)(2,1)S(1)}, bf16[96,896]{1,0:T(8,128)(2,1)S(1)}, u32[]{:S(2)}, u32[]{:S(2)}) collective-permute-start(bf16[96,896]{1,0:T(8,128)(2,1)S(1)} %get-tuple-element.249), channel_id=1, source_target_pairs={{0,2},{1,3},{2,0},{3,1},{4,6},{5,7},{6,4},{7,5},{8,10},{9,11},{10,... | collective-permute-start | bytes 516104 | tf_op jit(solution)/shard_map/ppermute | solution.py:125
  389.5 30.3 %collective-permute-start.45 = (bf16[96,896]{1,0:T(8,128)(2,1)S(1)}, bf16[96,896]{1,0:T(8,128)(2,1)S(1)}, u32[]{:S(2)}, u32[]{:S(2)}) collective-permute-start(bf16[96,896]{1,0:T(8,128)(2,1)S(1)} %get-tuple-element.250), channel_id=1, source_target_pairs={{0,1},{1,2},{2,3},{3,0},{4,5},{5,6},{6,7},{7,4},{8,9},{9,10},{10,1... | collective-permute-start | bytes 516104 | tf_op jit(solution)/shard_map/ppermute | solution.py:125
  419.9 11.0 %collective-permute-start.46 = (bf16[48,896]{1,0:T(8,128)(2,1)S(1)}, bf16[48,896]{1,0:T(8,128)(2,1)S(1)}, u32[]{:S(2)}, u32[]{:S(2)}) collective-permute-start(bf16[48,896]{1,0:T(8,128)(2,1)S(1)} %get-tuple-element.350.refs_0_), channel_id=1, source_target_pairs={{0,8},{8,0},{1,9},{9,1},{2,10},{10,2},{3,11},{11,3},{4,12},{12,4},... | collective-permute-start | bytes 258056 | tf_op jit(solution)/shard_map/ppermute | solution.py:121
  421.3 9.6 %collective-permute-start.47 = (bf16[48,896]{1,0:T(8,128)(2,1)S(1)}, bf16[48,896]{1,0:T(8,128)(2,1)S(1)}, u32[]{:S(2)}, u32[]{:S(2)}) collective-permute-start(bf16[48,896]{1,0:T(8,128)(2,1)S(1)} %get-tuple-element.349.refs_2_), channel_id=1, source_target_pairs={{0,16},{16,0},{1,17},{17,1},{2,18},{18,2},{3,19},{19,3},{4,20},{20... | collective-permute-start | bytes 258056 | tf_op jit(solution)/shard_map/ppermute | solution.py:121
  (111 other events, 781.2 us)
Sparse Core Ops, SparseCore 0:
  10.5 36.4 all-gather.8
  75.3 32.8 all-gather.10
  174.1 45.4 all-gather.12
  333.5 44.4 reduce-scatter.1
  380.3 34.2 all-gather.14

commit v3 on v2

--- a/solution.py
+++ b/solution.py
@@ -143,11 +143,8 @@
     def first_round(self, a, b, after=()):
         return stack_pairs(a, self.swap(a, XBIT), b, self.swap(b, YBIT), after)
 
-    def second_round(self, sa, sb, after=()):
-        ya, xb = self.swap(sa, YBIT), self.swap(sb, XBIT)
-        if after:
-            ya, xb = relay(ya, xb, after)
-        near = [sa, sb, ya, xb]
+    def second_round(self, sa, sb):
+        near = [sa, sb, self.swap(sa, YBIT), self.swap(sb, XBIT)]
         return near + [self.swap(t, CORE) for t in near]
 
 
@@ -215,16 +212,16 @@
     )
 
 
-def relay_kernel(a, b, c, d):
-    c[...] = a[...]
-    d[...] = b[...]
-
-
-def relay(a, b, after):
-    return launch(
-        relay_kernel, "relay", [a, b], [whole(a.shape)] * 2, [whole(a.shape)] * 2,
-        like(a.dtype, a.shape, a.shape), after=after,
-    )[0]
+def relay_kernel(a, b):
+    b[...] = a[...]
+
+
+def relay(a, after):
+    (a,), _ = launch(
+        relay_kernel, "relay", [a], [whole(a.shape)], [whole(a.shape)], like(a.dtype, a.shape),
+        after=after,
+    )
+    return a
 
 
 def collect_kernel(step, n, sc, right, left, own, *refs):
@@ -638,50 +635,6 @@
     )
 
 
-def ffn_in_first_kernel(count, sc, x_ref, gain_ref, *refs):
-    slots = 4
-    mixed, own, arrays = refs[:slots], refs[slots : slots + 3], refs[slots + 3 : slots + 11]
-    hid_ref, normed_ref, *outs = refs[slots + 11 : slots + 16]
-    w, wo, sems, o_sems = refs[slots + 16 :]
-    length, d = x_ref.shape
-    hidden = outs[0].shape[2]
-    copies = chunk_copies(sc, zip(own, (0, hidden)), arrays, w, sems)
-    o_copies = chunk_copies(sc, [(own[2], 0)], arrays, wo, o_sems, 2 * hidden)
-
-    @pl.when(pl.program_id(0) == 0)
-    def _():
-        for copy in o_copies + copies:
-            copy.start()
-        for copy in o_copies:
-            copy.wait()
-        gain = gain_ref[...]
-        for a in range(length // tile):
-            rows = slice(a * tile, (a + 1) * tile)
-            h = x_ref[rows, :].astype(f32)
-            for k in range(slots):
-                h = h + dot(mixed[k][rows, :], wo[k], ((1,), (1,)))
-            hid_ref[rows, :] = h
-            normed_ref[rows, :] = (h * rms_scale(h) * gain).astype(bf16)
-        for copy in copies:
-            copy.wait()
-
-    gate_up(normed_ref, w.at[pl.program_id(0)], *outs)
-
-
-def ffn_in_rest_kernel(first, sc, normed_ref, *refs):
-    arrays, outs, (w, sems) = refs[:8], refs[8:11], refs[11:]
-    copies = chunk_copies(sc, (), arrays, w, sems, 0, first)
-
-    @pl.when(pl.program_id(0) == 0)
-    def _():
-        for copy in copies:
-            copy.start()
-        for copy in copies:
-            copy.wait()
-
-    gate_up(normed_ref, w.at[pl.program_id(0)], *outs)
-
-
 def gate_up(normed_ref, w, act_ref, dact_ref, inner_ref):
     hidden = act_ref.shape[2]
     for n in range(hidden // 256):
@@ -700,79 +653,53 @@
         inner_ref[0, :, cols] = (act * up).astype(bf16)
 
 
-def ffn_in_first(count, offs, tokens, gain, mixed, own, arrays, length, after=()):
-    d = tokens.shape[1]
-    slots = len(mixed)
-    hidden = own[0].shape[1]
-    wide = own[2].shape[1]
-    per_slot = pl.BlockSpec((1, length, hidden), lambda i, sc: (i, 0, 0))
-    three = (slots, length, hidden)
-    specs = [pl.BlockSpec((length, d), lambda i, sc: (sc[16], 0)), whole(gain.shape)]
-    return launch(
-        functools.partial(ffn_in_first_kernel, count), "ffn_in_first",
-        [tokens, gain, *mixed, *own, *arrays],
-        specs + [whole(m.shape) for m in mixed] + [ANY] * 11,
-        [whole((length, d)), whole((length, d))] + [per_slot] * 3,
-        like(f32, (length, d)) + like(bf16, (length, d), three, three, three),
-        grid=(count,), offs=offs,
-        scratch=[
-            pltpu.VMEM((count, d, 2 * hidden), bf16),
-            pltpu.VMEM((slots, d, wide), bf16),
-            pltpu.SemaphoreType.DMA((copies_per_chunk,)),
-            pltpu.SemaphoreType.DMA((copies_per_chunk,)),
-        ],
-        cost=cost(2 * length * d * (d + 2 * count * hidden), 16, count * length * hidden),
-        after=after, mib=24,
-    )
-
-
-def ffn_in_rest(count, offs, normed, so_far, arrays, after=()):
-    length, d = normed.shape
-    slots, _, hidden = so_far[0].shape
-    first = slots - count
-    per_slot = pl.BlockSpec((1, length, hidden), lambda i, sc: (i + first, 0, 0))
-
-    def kernel(sc, normed_ref, *refs):
-        ffn_in_rest_kernel(first, sc, normed_ref, *refs[:8], *refs[11:])
-
-    return launch(
-        kernel, "ffn_in_rest", [normed, *arrays, *so_far],
-        [whole(normed.shape)] + [ANY] * 11, [per_slot] * 3,
-        like(bf16, *[v.shape for v in so_far]), grid=(count,), offs=offs,
-        scratch=[
-            pltpu.VMEM((count, d, 2 * hidden), bf16),
-            pltpu.SemaphoreType.DMA((copies_per_chunk,)),
-        ],
-        cost=cost(4 * length * d * count * hidden, 16, count * length * hidden),
-        after=after, mib=20, alias=9, n_alias=3,
-    )
-
-
-def ffn_out_kernel(
-    sc, hid_ref, inner_ref, gain_ref, wp_ref, padc_ref, query_ref, cot_ref, top_ref, own, *refs
+def forward_kernel(
+    sc, x_ref, gain_ref, gain_l_ref, wp_ref, padc_ref, query_ref, cot_ref, top_ref, *refs
 ):
-    arrays = refs[:8]
-    score_ref, nfin, ge, total_ref, gft_ref, ghf_ref, wd, sems, acc, embed, unit = refs[8:]
-    length, d = hid_ref.shape
+    slots = 4
+    mixed, own, arrays = refs[:slots], refs[slots : slots + 4], refs[slots + 4 : slots + 12]
+    hid_ref, normed_ref, act_ref, dact_ref, inner_ref = refs[slots + 12 : slots + 17]
+    score_ref, nfin, ge, total_ref, gft_ref, ghf_ref = refs[slots + 17 : slots + 23]
+    w, wd, wo, w_sems, d_sems, o_sems, acc, embed, unit = refs[slots + 23 :]
+    length, d = x_ref.shape
+    hidden = act_ref.shape[2]
     step = pl.program_id(0)
-    copies = chunk_copies(sc, [(own, 0)], arrays, wd, sems)
     blocks = length // tile
+    w_copies = chunk_copies(sc, zip(own, (0, hidden)), arrays, w, w_sems)
+    d_copies = chunk_copies(sc, [(own[2], 0)], arrays, wd, d_sems, 2 * hidden)
+    o_copies = chunk_copies(sc, [(own[3], 0)], arrays, wo, o_sems, 3 * hidden)
 
     @pl.when(step == 0)
     def _():
-        for copy in copies:
+        for copy in o_copies + w_copies + d_copies:
             copy.start()
-        acc[...] = hid_ref[...]
-        for copy in copies:
+        for copy in o_copies:
             copy.wait()
-
+        gain = gain_ref[...]
+        for a in range(blocks):
+            rows = slice(a * tile, (a + 1) * tile)
+            h = x_ref[rows, :].astype(f32)
+            for k in range(slots):
+                h = h + dot(mixed[k][rows, :], wo[k], ((1,), (1,)))
+            hid_ref[rows, :] = h
+            acc[rows, :] = h
+            normed_ref[rows, :] = (h * rms_scale(h) * gain).astype(bf16)
+        for copy in w_copies[:2] + d_copies[:1]:
+            copy.wait()
+
+    @pl.when(step == 1)
+    def _():
+        for copy in w_copies[2:] + d_copies[1:]:
+            copy.wait()
+
+    gate_up(normed_ref, w.at[step], act_ref, dact_ref, inner_ref)
     acc[...] += dot(inner_ref[0], wd[step])
 
-    @pl.when(step == pl.num_programs(0) - 1)
+    @pl.when(step == slots - 1)
     def _():
         lane = lax.broadcasted_iota(jnp.int32, padc_ref.shape, 1)
         pad = jnp.sum(jnp.where(lane == sc[16], padc_ref[...], 0.0), axis=1, keepdims=True)
-        gain = gain_ref[...]
+        gain = gain_l_ref[...]
         for a in range(blocks):
             rows = slice(a * tile, (a + 1) * tile)
             h = acc[rows, :]
@@ -814,55 +741,73 @@
         total_ref[...] = total
 
 
-def ffn_out(offs, hid, inner, gain, w_proj, pad_cols, query, cot, top, own, arrays):
-    length, d = hid.shape
-    slots, _, hidden = inner.shape
+def forward(
+    offs, tokens, gain, gain_l, w_proj, pad_cols, query, cot, top, mixed, own, arrays, length
+):
+    d = tokens.shape[1]
+    slots = len(mixed)
+    hidden = own[0].shape[1]
+    wide = own[3].shape[1]
     e = w_proj.shape[1]
+    three = (slots, length, hidden)
+    score, low, embed, total = cot.shape[1:], (length, d), (length, e), (1, d)
+    per_slot = pl.BlockSpec((1, length, hidden), lambda i, sc: (i, 0, 0))
 
     def row_block(v):
         return pl.BlockSpec((1,) + v.shape[1:], lambda i, sc: (sc[16], 0, 0))
 
-    score, low, embed, total = cot.shape[1:], (length, d), (length, e), (1, d)
     return launch(
-        ffn_out_kernel, "ffn_out",
-        [hid, inner, gain, w_proj, pad_cols, query, cot, top, own, *arrays],
-        [whole(hid.shape), pl.BlockSpec((1, length, hidden), lambda i, sc: (i, 0, 0))]
-        + [whole(v.shape) for v in (gain, w_proj, pad_cols)]
+        forward_kernel, "forward",
+        [tokens, gain, gain_l, w_proj, pad_cols, query, cot, top, *mixed, *own, *arrays],
+        [pl.BlockSpec((length, d), lambda i, sc: (sc[16], 0))]
+        + [whole(v.shape) for v in (gain, gain_l, w_proj, pad_cols)]
         + [row_block(v) for v in (query, cot, top)]
-        + [ANY] * 9,
-        [whole(v) for v in (score, low, embed, total, low, low)],
-        like(f32, score) + like(bf16, low, embed) + like(f32, total) + like(bf16, low)
-        + like(f32, low),
+        + [whole(m.shape) for m in mixed]
+        + [ANY] * 12,
+        [whole(low), whole(low)] + [per_slot] * 3
+        + [whole(v) for v in (score, low, embed, total, low, low)],
+        like(f32, low) + like(bf16, low, three, three, three) + like(f32, score)
+        + like(bf16, low, embed) + like(f32, total) + like(bf16, low) + like(f32, low),
         grid=(slots,), offs=offs,
         scratch=[
+            pltpu.VMEM((slots, d, 2 * hidden), bf16),
             pltpu.VMEM((slots, hidden, d), bf16),
+            pltpu.VMEM((slots, d, wide), bf16),
+            pltpu.SemaphoreType.DMA((copies_per_chunk,)),
+            pltpu.SemaphoreType.DMA((copies_per_chunk,)),
             pltpu.SemaphoreType.DMA((copies_per_chunk,)),
             pltpu.VMEM((length, d), f32),
             pltpu.VMEM((length, e), f32),
             pltpu.VMEM((length, e), bf16),
         ],
-        cost=cost(2 * length * d * slots * hidden, 16), mib=24,
+        cost=cost(2 * length * d * (d + 3 * slots * hidden), 24, slots * length * hidden),
+        mib=58,
     )
 
 
 def ffn_back_kernel(sc, hid_ref, gft_ref, ghf_ref, act_ref, dact_ref, gain_ref, *refs):
     slots = 4
-    own, first, own_down, second = refs[:3], refs[3:11], refs[11], refs[12:20]
-    refs = refs[20:]
-    gg_ref, gu_ref, gha_ref, gat_ref, gm_ref, total_ref, w, wd, w_sems, d_sems, acc = refs
+    own, arrays, refs = refs[:4], refs[4:12], refs[12:]
+    gg_ref, gu_ref, gha_ref, gat_ref, gm_ref, total_ref, w, wd, wo, w_sems, d_sems, acc = refs
     length, d = hid_ref.shape
     hidden = wd.shape[1]
     step = pl.program_id(0)
-    w_copies = chunk_copies(sc, zip(own, (0, hidden, 2 * hidden)), first, w, w_sems)
-    d_copies = chunk_copies(sc, [(own_down, 0)], second, wd, d_sems)
+    w_copies = chunk_copies(sc, zip(own, (0, hidden)), arrays, w, w_sems.at[0])
+    w_copies += chunk_copies(sc, [(own[3], 0)], arrays, wo, w_sems.at[1], 3 * hidden)
+    d_copies = chunk_copies(sc, [(own[2], 0)], arrays, wd, d_sems, 2 * hidden)
     blocks = length // tile
 
     @pl.when(step == 0)
     def _():
-        for copy in d_copies + w_copies:
+        for copy in d_copies[:1] + w_copies[:2] + d_copies[1:] + w_copies[2:]:
             copy.start()
         acc[...] = jnp.zeros_like(acc)
-        for copy in d_copies:
+        for copy in d_copies[:1] + w_copies[:2]:
+            copy.wait()
+
+    @pl.when(step == 1)
+    def _():
+        for copy in d_copies[1:] + w_copies[2:]:
             copy.wait()
 
     def part(n, carry):
@@ -873,12 +818,6 @@
         return carry
 
     lax.fori_loop(0, hidden // 256, part, 0)
-
-    @pl.when(step == 0)
-    def _():
-        for copy in w_copies:
-            copy.wait()
-
     acc[...] += dot(gg_ref[0], w[step, :, :hidden], ((1,), (1,))) + dot(
         gu_ref[0], w[step, :, hidden : 2 * hidden], ((1,), (1,))
     )
@@ -896,28 +835,29 @@
             g = g.astype(bf16)
             gat_ref[rows, :] = g
             for k in range(slots):
-                gm_ref[k, rows, :] = dot(g, w[k, :, 2 * hidden :]).astype(bf16)
+                gm_ref[k, rows, :] = dot(g, wo[k]).astype(bf16)
         total_ref[...] = total
 
 
-def ffn_back(offs, hid, gft, ghf, act, dact, gain, own, first, own_down, second, after=()):
+def ffn_back(offs, hid, gft, ghf, act, dact, gain, own, arrays, after=()):
     length, d = hid.shape
     slots, _, hidden = act.shape
-    width = first[0].shape[3]
-    mixed = (slots, length, width - 2 * hidden)
+    wide = own[3].shape[1]
+    mixed = (slots, length, wide)
     block = pl.BlockSpec((1, length, hidden), lambda i, sc: (i, 0, 0))
     return launch(
         ffn_back_kernel, "ffn_back",
-        [hid, gft, ghf, act, dact, gain, *own, *first, own_down, *second],
-        [whole(v.shape) for v in (hid, gft, ghf)] + [block] * 2 + [whole(gain.shape)] + [ANY] * 20,
+        [hid, gft, ghf, act, dact, gain, *own, *arrays],
+        [whole(v.shape) for v in (hid, gft, ghf)] + [block] * 2 + [whole(gain.shape)] + [ANY] * 12,
         [block, block] + [whole(v) for v in (hid.shape, hid.shape, mixed, (1, d))],
         like(bf16, act.shape, act.shape) + like(f32, hid.shape) + like(bf16, hid.shape, mixed)
         + like(f32, (1, d)),
         grid=(slots,), offs=offs,
         scratch=[
-            pltpu.VMEM((slots, d, width), bf16),
+            pltpu.VMEM((slots, d, 2 * hidden), bf16),
             pltpu.VMEM((slots, hidden, d), bf16),
-            pltpu.SemaphoreType.DMA((copies_per_chunk,)),
+            pltpu.VMEM((slots, d, wide), bf16),
+            pltpu.SemaphoreType.DMA((2, copies_per_chunk)),
             pltpu.SemaphoreType.DMA((copies_per_chunk,)),
             pltpu.VMEM((length, d), f32),
         ],
@@ -967,7 +907,7 @@
         keep_parts(sc, out, refs[-5:-1])
 
 
-def products(offs, lefts, rights, slots, got=None, after=()):
+def products(offs, lefts, rights, slots, got=None, after=(), mib=16):
     keep = got is not None
     length, half = lefts[0].shape[-2], lefts[0].shape[-1] // 2
     width = sum(right.shape[-1] for right, _ in rights)
@@ -998,7 +938,7 @@
         functools.partial(product_kernel, len(lefts), [i for _, i in rights], keep),
         "products_keep" if keep else "products_send",
         args, specs, out_specs, out_shape, grid=(slots,), offs=offs, scratch=scratch, after=after,
-        mib=16,
+        mib=mib,
     )
 
 
@@ -1255,38 +1195,33 @@
         return jnp.concatenate(parts, axis=1) if len(parts) > 1 else parts[0]
 
     common = (offs, tokens, segs, pads, seg_cols, gain_a)
-    z1 = lax.all_gather(piece(w_gate, w_up, w_out_t), "mp")
-    piece2 = jnp.concatenate([piece(w_down), piece(w_qkv)])
-    z2 = lax.all_gather(piece2, "mp")
-    (attended,), done = attend(1, *common, w_qkv, hot, heads, size, (piece2,))
+    own = (w_gate, w_up, w_down, w_out_t)
+    z1 = lax.all_gather(piece(*own), "mp")
+    (attended,), done = attend(1, *common, w_qkv, hot, heads, size)
     mixed = [attended[slots - 1]] + [place.shift(attended[k - 1], k) for k in range(1, slots)]
     halved, _ = split(offs, z1, eighth, (done,))
-    s1, done1 = place.first_round(*halved, mixed[1:])
-    first = place.second_round(*s1)
-    (*halved, z2), done = split(offs, z2, eighth, (done1,))
-    all_qkv = lax.all_gather(z2, group)
-    all_qkv = all_qkv.reshape((2, 2, 2) + all_qkv.shape[-3:])
-    own = (w_gate, w_up, w_out_t)
-    (hid, normed_ffn, *gates), done = ffn_in_first(
-        slots // 2, offs, tokens, gain_f, mixed, own, first, length, (done,)
-    )
-    s2, done = place.first_round(*halved, (done,))
-    (act, dact, inner), done = ffn_in_rest(slots // 2, offs, normed_ffn, gates, first, (done,))
-    second = place.second_round(*s2, (done,))
-    (score, nfin, ge, gain_fin, gft, ghf), _ = ffn_out(
-        offs, hid, inner, gain_l, w_proj, pad_cols, query_emb, score_cot, top_index, w_down, second
-    )
+    s1, _ = place.first_round(*halved, mixed[1:])
+    arrays = place.second_round(*s1)
+    (hid, normed_ffn, act, dact, inner, score, nfin, ge, gain_fin, gft, ghf), done = forward(
+        offs, tokens, gain_f, gain_l, w_proj, pad_cols, query_emb, score_cot, top_index, mixed,
+        own, arrays, length,
+    )
+    all_qkv = lax.all_gather(relay(piece(w_qkv), (done,)), group + ("mp",))
+    all_qkv = all_qkv.reshape((2, 2, 2, slots) + all_qkv.shape[-2:])
     down_sides = ([inner, nfin], [(gft, 0), (ge, 1)])
-    (send,), _ = products(offs, *down_sides, slots)
+    (send,), _ = products(offs, *down_sides, slots, mib=58)
     kept, kept_done = products(offs, *down_sides, slots, place.swap(send, CORE))
     down = Reduce(place, offs, kept)
     (gg, gu, gha, gat, gm, gain_mid), done = ffn_back(
-        offs, hid, gft, ghf, act, dact, gain_f, own, first, w_down, second, (kept_done,)
-    )
+        offs, hid, gft, ghf, act, dact, gain_f, own, arrays, (kept_done,)
+    )
+    gu_sides = ([normed_ffn], [(gg, 0), (gu, 0)])
     done = down.first((done,))
-    gu_sides = ([normed_ffn], [(gg, 0), (gu, 0)])
-    (send,), _ = products(offs, *gu_sides, slots, None, (done,))
+    (send,), done = products(offs, *gu_sides, slots, None, (done,))
     got = place.swap(send, CORE)
+    done = down.second((done,))
+    kept, done = products(offs, *gu_sides, slots, got, (done,))
+    gate_up = Reduce(place, offs, kept)
     finish = [gha, gat, gain_fin, gain_mid, score]
 
     def back(first, acc, left, after):
@@ -1296,30 +1231,27 @@
         )
 
     (left, tables, acc), done = back(0, None, None, (done,))
-    done = down.second((done,))
-    kept, done = products(offs, *gu_sides, slots, got, (done,))
-    gate_up = Reduce(place, offs, kept)
     finish.append(tables)
+    done = down.third((done,))
+    done = gate_up.first((done,))
     (left, _, dx, both, small), done = back(slots // 2, acc, left, (done,))
     right, left_ = place.both_ways(dx, dx)
-    done = down.third((done,))
-    done = gate_up.first((done,))
+    done = gate_up.second_and_third((done,))
     (send,), _ = attn_products(offs, left, both, small, None, (done,))
     kept, done = attn_products(offs, left, both, small, place.swap(send, CORE))
     attn = Reduce(place, offs, kept)
     (*so_far, right, left_), done = collect(1, slots, offs, right, left_, dx, None, (done,))
-    done = gate_up.second_and_third((done,))
-    done = attn.first((done,))
     right, left_ = place.both_ways(right, left_)
+    done = start_after = attn.first((done,))
     done = attn.second((done,))
     (*so_far, right, left_), done = collect(2, slots, offs, right, left_, dx, so_far, (done,))
-    start_after = (done,)
     right, left_ = place.both_ways(right, left_)
+    (grad_down, grad_proj, grad_gate, grad_up), done = gathered(
+        down.total, gate_up.total, (d, w_proj.shape[1], hidden, hidden), (start_after,),
+        (done,),
+    )
     done = attn.third((done,))
     (input_grad, packed), done = collect(3, slots, offs, right, left_, dx, so_far, (done,))
-    (grad_down, grad_proj, grad_gate, grad_up), done = gathered(
-        down.total, gate_up.total, (d, w_proj.shape[1], hidden, hidden), start_after, (done,)
-    )
     last, _ = place.first_round(*halves(attn.total, 0), (done,))
     grad_q, grad_k, grad_v, grad_out, small = unpack(
         offs, place.second_round(*last), 4, small.shape[2]

time: 451 us -> 433 us (0.960)
  local copies, waits for them, and re-layouts: 60.1 us -> 34.9 us
  waiting for transfers between devices: 154 us -> 174 us
  starting transfers between devices: 71.1 us -> 54.3 us
    unnamed x202 -> x142, local copies, waits for them, and re-layouts: 53 us -> 26.5 us
    ppermute x39 -> x31, waiting for transfers between devices: 53.8 us -> 69.4 us  [swap(): return lax.ppermute(v, name, [(0, 1), (1, 0)])]
    reduce_scatter x1, starting transfers between devices: 12.9 us -> 0.57 us  [second_and_third(): total = lax.psum_scatter(v, 'mp', scatter_dimension=0, tiled=True)]
    all_gather x3 -> x2, waiting for transfers between devices: 25 us -> 31.1 us  [the longest x1 31.1 us: local(): z1 = lax.all_gather(piece(*own), 'mp')]
    ppermute x39 -> x31, starting transfers between devices: 28.5 us -> 22.8 us  [swap(): return lax.ppermute(v, name, [(0, 1), (1, 0)])]
    ppermute x9, waiting for transfers between devices: 45.2 us -> 39.6 us  [shift(): return lax.ppermute(v, 'mp', [(i, (i + k) % n) for i in range(n)])]
    pallas_call x33 -> x29, Pallas kernels: 148 us -> 148 us  [launch(): pl.pallas_call(body, out_shape=list(out_shape) + [jax.ShapeDtypeStruct(to...]
  transfers between devices with their start and end apart: 59 -> 50, of which waited for: 23 -> 24; matrix products, arithmetic and copies ran while one was open for 1% -> 1% of each run, Pallas kernels for 25% -> 24%
where the time goes in v3:
time: 433 us; the launch traced here: 429 us
  waiting for transfers between devices  174 us (40%)
  Pallas kernels  148 us (34%)
  starting transfers between devices  54.3 us (13%)
  local copies, waits for them, and re-layouts  34.9 us (8%)
  between operations  15.2 us (4%)
    pallas_call x29, Pallas kernels, launch(): pl.pallas_call(body, out_shape=list(out_shape) + [jax.ShapeDtypeStruct(to...  148 us
    ppermute x31, waiting for transfers between devices, swap(): return lax.ppermute(v, name, [(0, 1), (1, 0)])  69.4 us
    ppermute x9, waiting for transfers between devices, shift(): return lax.ppermute(v, 'mp', [(i, (i + k) % n) for i in range(n)])  39.6 us
    all_gather x1, waiting for transfers between devices, local(): z1 = lax.all_gather(piece(*own), 'mp')  31.1 us
    unnamed x142, local copies, waits for them, and re-layouts  26.5 us
    ppermute x3, waiting for transfers between devices, both_ways(): right = lax.ppermute(right, 'mp', [(i, i + 1) for i in range(n - 1)])  25.3 us
    ppermute x31, starting transfers between devices, swap(): return lax.ppermute(v, name, [(0, 1), (1, 0)])  22.8 us
    ppermute x9, starting transfers between devices, shift(): return lax.ppermute(v, 'mp', [(i, (i + k) % n) for i in range(n)])  17 us
  transfers between devices with their start and end apart: 50, of which 24 were waited for; matrix products, arithmetic and copies ran while one was open for 1% of the time, Pallas kernels for 24%

profile of v3, /device:TPU:0, one launch (start us, length us, event | category | flops | bytes accessed | tf_op | source)
XLA Modules:
  0.0 428.6 jit_solution(10050792686344506787)
XLA Ops:
  14.9 10.8 %attend.1 = (bf16[4,528,192]{2,1,0:T(8,128)(2,1)S(1)}, f32[8,128]{1,0:T(8,128)S(1)}) custom-call(s32[20]{0:T(128)S(1)} %stack.83.refs_0_, bf16[2048,768]{1,0:T(8,128)(2,1)S(1)} %copy-done.11, f32[4,512]{1,0:T(4,128)S(1)} %convert_element_type.4.refs_2_, f32[4,512]{1,0:T(4,128)S(1)} %get-tuple-element.314.refs_3_, f32[512,4]{1,0:T(8,128)S(1)} %bitcast.52, ...), custom_call_target="tpu_custom_call" | custom-call | flops 2617245696 | bytes 4194304 | tf_op jit(solution)/shard_map/attend/pallas_call | solution.py:84
  26.7 31.1 %all-gather.7.cloned.1.call-done = bf16[384,2496]{1,0:T(8,128)(2,1)} async-done(((bf16[96,2496]{1,0:T(8,128)(2,1)}), bf16[384,2496]{1,0:T(8,128)(2,1)}) %all-gather.7.cloned.1.call-update) | async-done | bytes 1916944 | tf_op jit(solution)/shard_map/all_gather | solution.py:1199
  57.8 1.5 copy-done.15
  64.4 1.6 collective-permute-start.1
  66.0 2.7 collective-permute-start.2
  68.7 6.9 %collective-permute-done.refs_4_.refs_10_.refs_9_ = bf16[528,192]{1,0:T(8,128)(2,1)S(1)} collective-permute-done((bf16[528,192]{1,0:T(8,128)(2,1)S(1)}, bf16[528,192]{1,0:T(8,128)(2,1)S(1)}, u32[]{:S(2)}, u32[]{:S(2)}) %collective-permute-start) | collective-permute-done | bytes 202784 | tf_op jit(solution)/shard_map/ppermute | solution.py:125
  75.5 9.9 %collective-permute-done.1.refs_5_.refs_11_.refs_8_ = bf16[528,192]{1,0:T(8,128)(2,1)S(1)} collective-permute-done((bf16[528,192]{1,0:T(8,128)(2,1)S(1)}, bf16[528,192]{1,0:T(8,128)(2,1)S(1)}, u32[]{:S(2)}, u32[]{:S(2)}) %collective-permute-start.1) | collective-permute-done | bytes 202784 | tf_op jit(solution)/shard_map/ppermute | solution.py:125
  85.5 1.8 stack_pairs.2
  88.9 30.8 %collective-permute-done.6.refs_20_.refs_14_ = bf16[2,3,48,2496]{3,2,1,0:T(8,128)(2,1)S(1)} collective-permute-done((bf16[2,3,48,2496]{3,2,1,0:T(8,128)(2,1)}, bf16[2,3,48,2496]{3,2,1,0:T(8,128)(2,1)S(1)}, u32[]{:S(2)}, u32[]{:S(2)}) %collective-permute-start.6) | collective-permute-done | bytes 1437728 | tf_op jit(solution)/shard_map/ppermute | solution.py:121
  123.1 2.3 collective-permute-done.9.refs_23_.refs_17_
  125.4 24.8 %forward.1 = (f32[512,768]{1,0:T(8,128)}, bf16[512,768]{1,0:T(8,128)(2,1)}, bf16[4,512,768]{2,1,0:T(8,128)(2,1)}, bf16[4,512,768]{2,1,0:T(8,128)(2,1)}, bf16[4,5...) custom-call(s32[20]{0:T(128)} %copy-done.49, ...), custom_call_target="tpu_custom_call" | custom-call | flops 7851737088 | bytes 25165824 | tf_op jit(solution)/shard_map/forward/pallas_call | solution.py:84
  150.2 6.3 %products_send.2 = (bf16[4,384,896]{2,1,0:T(8,128)(2,1)}, f32[8,128]{1,0:T(8,128)}) custom-call(s32[20]{0:T(128)} %copy-done.49, bf16[4,512,768]{2,1,0:T(8,128)(2,1)} %get-tuple-element.148.refs_1_, bf16[512,768]{1,0:T(8,128)(2,1)} %get-tuple-element.149.refs_2_, bf16[512,768]{1,0:T(8,128)(2,1)} %get-tuple-element.144.refs_3_.refs_2_, ...), custom_call_target="tpu_custom_call" | custom-call | flops 1048576 | bytes 65536 | tf_op jit(solution)/shard_map/products_send/pallas_call | solution.py:84
  158.9 3.1 collective-permute-done.11.refs_5_
  164.3 5.3 %products_keep.2 = (bf16[4,2,48,896]{3,2,1,0:T(8,128)(2,1)S(1)}, bf16[4,2,48,896]{3,2,1,0:T(8,128)(2,1)S(1)}, bf16[4,2,48,896]{3,2,1,0:T(8,128)(2,1)S(1)}, bf16[...) custom-call(s32[20]{0:T(128)S(1)} %copy-done.50, bf16[4,512,768]{2,1,0:T(8,128)(2,1)S(1)} %copy-done.5, ...), custom_call_target="tpu_custom_call" | custom-call | flops 1048576 | bytes 65536 | tf_op jit(solution)/shard_map/products_keep/pallas_call | solution.py:84
  170.8 19.4 %ffn_back.1 = (bf16[4,512,768]{2,1,0:T(8,128)(2,1)}, bf16[4,512,768]{2,1,0:T(8,128)(2,1)}, f32[512,768]{1,0:T(8,128)}, bf16[512,768]{1,0:T(8,128)(2,1)S(1)}, bf1...) custom-call(s32[20]{0:T(128)S(1)} %copy-done.50, ...), custom_call_target="tpu_custom_call" | custom-call | flops 7851737088 | bytes 25165824 | tf_op jit(solution)/shard_map/ffn_back/pallas_call | solution.py:84
  192.0 1.9 copy-done.2
  193.9 1.9 copy-done.4
  195.8 3.9 products_send.3
  202.8 11.4 %collective-permute-done.15.refs_1_ = bf16[4,48,896]{2,1,0:T(8,128)(2,1)S(1)} collective-permute-done((bf16[4,48,896]{2,1,0:T(8,128)(2,1)S(1)}, bf16[4,48,896]{2,1,0:T(8,128)(2,1)S(1)}, u32[]{:S(2)}, u32[]{:S(2)}) %collective-permute-start.15) | collective-permute-done | bytes 344096 | tf_op jit(solution)/shard_map/ppermute | solution.py:121
  214.2 2.9 collective-permute-done.16.refs_3_
  218.0 5.1 %products_keep.3 = (bf16[4,2,48,1536]{3,2,1,0:T(8,128)(2,1)}, bf16[4,2,48,1536]{3,2,1,0:T(8,128)(2,1)S(1)}, bf16[4,2,48,1536]{3,2,1,0:T(8,128)(2,1)}, bf16[4,2,48,1536]{3,2,1,0:T(8,128)(2,1)S(1)}, f32[8,128]{1,0:T(8,128)S(1)}) custom-call(s32[20]{0:T(128)S(1)} %copy-done.50, bf16[512,768]{1,0:T(8,128)(2,1)S(1)} %copy-done.14, ...), custom_call_target="tpu_custom_call" | custom-call | flops 1048576 | bytes 65536 | tf_op jit(solution)/shard_map/products_keep/pallas_call | solution.py:84
  225.2 2.5 collective-permute-start.17
  227.7 7.0 %collective-permute-start.19 = (bf16[96,896]{1,0:T(8,128)(2,1)}, bf16[96,896]{1,0:T(8,128)(2,1)}, u32[]{:S(2)}, u32[]{:S(2)}) collective-permute-start(bf16[96,896]{1,0:T(8,128)(2,1)} %get-tuple-element.186), channel_id=1, source_target_pairs={{0,3},{1,0},{2,1},{3,2},{4,7},{5,4},{6,5},{7,6},{8,11},{9,8},{10,9... | collective-permute-start | bytes 516104 | tf_op jit(solution)/shard_map/ppermute | solution.py:125
  235.9 2.1 copy-done.6
  242.1 16.5 %attend_back0.1 = (bf16[4,4,512,192]{3,2,1,0:T(8,128)(2,1)S(1)}, f32[16,128]{1,0:T(8,128)S(1)}, f32[512,768]{1,0:T(8,128)S(1)}, f32[8,128]{1,0:T(8,128)S(1)}) custom-call(s32[20]{0:T(128)S(1)} %copy-done.50, bf16[2048,768]{1,0:T(8,128)(2,1)S(1)} %copy-done.12, f32[4,512]{1,0:T(4,128)S(1)} %convert_element_type.4.refs_2_, ...), custom_call_target="tpu_custom_call" | custom-call | flops 3221225472 | bytes 16777216 | tf_op jit(solution)/shard_map/attend_back0/pallas_call | solution.py:84
  260.0 3.5 second_sums.4
  265.7 17.5 %attend_back2.1 = (bf16[4,4,512,192]{3,2,1,0:T(8,128)(2,1)S(1)}, f32[16,128]{1,0:T(8,128)}, bf16[528,768]{1,0:T(8,128)(2,1)S(1)}, bf16[2,512,768]{2,1,0:T(8,128)...) custom-call(s32[20]{0:T(128)S(1)} %copy-done.50, ...), custom_call_target="tpu_custom_call", output_to_operand_aliasing={{0}: (18, {})} | custom-call | flops 3221225472 | bytes 16777216 | tf_op jit(solution)/shard_map/attend_back2/pallas_call | solution.py:84
  284.0 3.9 attn_send.1
  288.0 4.3 %collective-permute-start.22 = (bf16[528,768]{1,0:T(8,128)(2,1)S(1)}, bf16[528,768]{1,0:T(8,128)(2,1)S(1)}, u32[]{:S(2)}, u32[]{:S(2)}) collective-permute-start(bf16[528,768]{1,0:T(8,128)(2,1)S(1)} %get-tuple-element.192.refs_3_), channel_id=1, source_target_pairs={{0,1},{1,2},{2,3},{4,5},{5,6},{6,7},{8,9},{9,10},{10,11},{12,13},{... | collective-permute-start | bytes 2433032 | tf_op jit(solution)/shard_map/ppermute | solution.py:140
  293.7 2.2 copy-done.1
  295.9 4.6 %attn_keep.1 = (bf16[4,2,48,896]{3,2,1,0:T(8,128)(2,1)S(1)}, bf16[4,2,48,896]{3,2,1,0:T(8,128)(2,1)S(1)}, bf16[4,2,48,896]{3,2,1,0:T(8,128)(2,1)S(1)}, bf16[4,2,48,896]{3,2,1,0:T(8,128)(2,1)S(1)}, f32[8,128]{1,0:T(8,128)S(1)}) custom-call(s32[20]{0:T(128)S(1)} %copy-done.50, bf16[4,4,512,192]{3,2,1,0:T(8,128)(2,1)S(1)} %copy-done.1, ...), custom_call_target="tpu_custom_call" | custom-call | flops 1048576 | bytes 65536 | tf_op jit(solution)/shard_map/attn_keep/pallas_call | solution.py:84
  302.8 24.8 %collective-permute-done.22.refs_1_ = bf16[528,768]{1,0:T(8,128)(2,1)S(1)} collective-permute-done((bf16[528,768]{1,0:T(8,128)(2,1)S(1)}, bf16[528,768]{1,0:T(8,128)(2,1)S(1)}, u32[]{:S(2)}, u32[]{:S(2)}) %collective-permute-start.22) | collective-permute-done | bytes 811040 | tf_op jit(solution)/shard_map/ppermute | solution.py:140
  327.6 3.6 collective-permute-done.23.refs_2_
  331.2 2.5 collect1.1
  337.6 3.5 collective-permute-start.27
  343.4 2.0 collective-permute-start.32
  345.4 11.8 %collective-permute-done.31.refs_1_ = bf16[4,48,896]{2,1,0:T(8,128)(2,1)S(1)} collective-permute-done((bf16[4,48,896]{2,1,0:T(8,128)(2,1)S(1)}, bf16[4,48,896]{2,1,0:T(8,128)(2,1)S(1)}, u32[]{:S(2)}, u32[]{:S(2)}) %collective-permute-start.31) | collective-permute-done | bytes 344096 | tf_op jit(solution)/shard_map/ppermute | solution.py:121
  358.9 4.1 collective-permute-done.28.refs_2_
  362.9 3.0 collect2.1
  366.0 2.2 collective-permute-start.33
  369.4 1.8 collective-permute-start.35
  371.2 2.4 collective-permute-start.36
  375.0 5.3 %open.1 = (f32[768,768]{1,0:T(8,128)}, f32[768,128]{1,0:T(8,128)}, f32[768,768]{1,0:T(8,128)}, f32[768,768]{1,0:T(8,128)}, f32[8,128]{1,0:T(8,128)}) custom-call(bf16[2,2,2,96,2432]{4,3,2,1,0:T(8,128)(2,1)} %bitcast.59, f32[8,128]{1,0:T(8,128)} %copy-done.57), custom_call_target="tpu_custom_call" | custom-call | flops 1048576 | bytes 65536 | tf_op jit(solution)/shard_map/open/pallas_call | solution.py:84
  380.3 12.8 %collective-permute-done.35.refs_1_ = bf16[96,896]{1,0:T(8,128)(2,1)S(1)} collective-permute-done((bf16[96,896]{1,0:T(8,128)(2,1)}, bf16[96,896]{1,0:T(8,128)(2,1)S(1)}, u32[]{:S(2)}, u32[]{:S(2)}) %collective-permute-start.35) | collective-permute-done | bytes 172064 | tf_op jit(solution)/shard_map/ppermute | solution.py:125
  393.1 10.0 %collective-permute-done.36.refs_2_ = bf16[96,896]{1,0:T(8,128)(2,1)S(1)} collective-permute-done((bf16[96,896]{1,0:T(8,128)(2,1)}, bf16[96,896]{1,0:T(8,128)(2,1)S(1)}, u32[]{:S(2)}, u32[]{:S(2)}) %collective-permute-start.36) | collective-permute-done | bytes 172064 | tf_op jit(solution)/shard_map/ppermute | solution.py:125
  405.0 2.4 collect3.1
  413.0 2.2 collective-permute-done.40.refs_3_
  417.5 2.2 unpack.1
  (251 shorter events, 67.6 us)
Async XLA Ops:
  7.2 50.6 %all-gather.7.cloned.1.call-start = ((), (), s32[]{:S(2)}) async-start(), calls=%async_computation.2 | async-start | bytes 2457600 | tf_op jit(solution)/shard_map/all_gather | solution.py:1199
  11.4 224.5 %all-gather.9.cloned.1.call-start = ((), (), s32[]{:S(2)}) async-start(), calls=%async_computation.3 | async-start | bytes 4055040 | tf_op jit(solution)/shard_map/all_gather | solution.py:1209
  60.5 25.0 %collective-permute-start.3 = (bf16[3,48,2496]{2,1,0:T(8,128)(2,1)S(1)}, bf16[3,48,2496]{2,1,0:T(8,128)(2,1)S(1)}, u32[]{:S(2)}, u32[]{:S(2)}) collective-permute-start(bf16[3,48,2496]{2,1,0:T(8,128)(2,1)S(1)} %get-tuple-element.139.refs_0_), channel_id=1, source_target_pairs={{0,8},{8,0},{1,9},{9,1},{2,10},{10,2},{3,11},{11,3},{4,12},{12,4},... | collective-permute-start | bytes 2156552 | tf_op jit(solution)/shard_map/ppermute | solution.py:121
  61.9 23.5 %collective-permute-start.4 = (bf16[3,48,2496]{2,1,0:T(8,128)(2,1)S(1)}, bf16[3,48,2496]{2,1,0:T(8,128)(2,1)S(1)}, u32[]{:S(2)}, u32[]{:S(2)}) collective-permute-start(bf16[3,48,2496]{2,1,0:T(8,128)(2,1)S(1)} %get-tuple-element.140.refs_2_), channel_id=1, source_target_pairs={{0,16},{16,0},{1,17},{17,1},{2,18},{18,2},{3,19},{19,3},{4,20},{20... | collective-permute-start | bytes 2156552 | tf_op jit(solution)/shard_map/ppermute | solution.py:121
  64.2 11.3 %collective-permute-start = (bf16[528,192]{1,0:T(8,128)(2,1)S(1)}, bf16[528,192]{1,0:T(8,128)(2,1)S(1)}, u32[]{:S(2)}, u32[]{:S(2)}) collective-permute-start(bf16[528,192]{1,0:T(8,128)(2,1)S(1)} %get-tuple-element.309), channel_id=1, source_target_pairs={{0,1},{1,2},{2,3},{3,0},{4,5},{5,6},{6,7},{7,4},{8,9},{9,10},{10,1... | collective-permute-start | bytes 608264 | tf_op jit(solution)/shard_map/ppermute | solution.py:125
  64.4 21.1 %collective-permute-start.1 = (bf16[528,192]{1,0:T(8,128)(2,1)S(1)}, bf16[528,192]{1,0:T(8,128)(2,1)S(1)}, u32[]{:S(2)}, u32[]{:S(2)}) collective-permute-start(bf16[528,192]{1,0:T(8,128)(2,1)S(1)} %get-tuple-element.308), channel_id=1, source_target_pairs={{0,2},{1,3},{2,0},{3,1},{4,6},{5,7},{6,4},{7,5},{8,10},{9,11},{10,... | collective-permute-start | bytes 608264 | tf_op jit(solution)/shard_map/ppermute | solution.py:125
  66.0 19.5 %collective-permute-start.2 = (bf16[528,192]{1,0:T(8,128)(2,1)S(1)}, bf16[528,192]{1,0:T(8,128)(2,1)S(1)}, u32[]{:S(2)}, u32[]{:S(2)}) collective-permute-start(bf16[528,192]{1,0:T(8,128)(2,1)S(1)} %get-tuple-element.307), channel_id=1, source_target_pairs={{0,3},{1,0},{2,1},{3,2},{4,7},{5,4},{6,5},{7,6},{8,11},{9,8},{10,9... | collective-permute-start | bytes 608264 | tf_op jit(solution)/shard_map/ppermute | solution.py:125
  87.3 32.4 %collective-permute-start.6 = (bf16[2,3,48,2496]{3,2,1,0:T(8,128)(2,1)}, bf16[2,3,48,2496]{3,2,1,0:T(8,128)(2,1)S(1)}, u32[]{:S(2)}, u32[]{:S(2)}) collective-permute-start(bf16[2,3,48,2496]{3,2,1,0:T(8,128)(2,1)} %get-tuple-element.142.refs_18_.refs_12_), channel_id=1, source_target_pairs={{0,8},{8,0},{1,9},{9,1},{2,10},{10,2},{3,11},{11,3},{4,12},{12,4},... | collective-permute-start | bytes 4313096 | tf_op jit(solution)/shard_map/ppermute | solution.py:121
  87.8 32.2 %collective-permute-start.5 = (bf16[2,3,48,2496]{3,2,1,0:T(8,128)(2,1)}, bf16[2,3,48,2496]{3,2,1,0:T(8,128)(2,1)}, u32[]{:S(2)}, u32[]{:S(2)}) collective-permute-start(bf16[2,3,48,2496]{3,2,1,0:T(8,128)(2,1)} %get-tuple-element.141.refs_17_.refs_11_), channel_id=1, source_target_pairs={{0,16},{16,0},{1,17},{17,1},{2,18},{18,2},{3,19},{19,3},{4,20},{20... | collective-permute-start | bytes 4313096 | tf_op jit(solution)/shard_map/ppermute | solution.py:121
  88.4 33.9 %collective-permute-start.7 = (bf16[2,3,48,2496]{3,2,1,0:T(8,128)(2,1)}, bf16[2,3,48,2496]{3,2,1,0:T(8,128)(2,1)}, u32[]{:S(2)}, u32[]{:S(2)}) collective-permute-start(bf16[2,3,48,2496]{3,2,1,0:T(8,128)(2,1)} %get-tuple-element.141.refs_17_.refs_11_), channel_id=1, source_target_pairs={{0,4},{4,0},{1,5},{5,1},{2,6},{6,2},{3,7},{7,3},{8,12},{12,8},{9,1... | collective-permute-start | bytes 4313096 | tf_op jit(solution)/shard_map/ppermute | solution.py:121
  88.4 33.9 %collective-permute-start.8 = (bf16[2,3,48,2496]{3,2,1,0:T(8,128)(2,1)}, bf16[2,3,48,2496]{3,2,1,0:T(8,128)(2,1)}, u32[]{:S(2)}, u32[]{:S(2)}) collective-permute-start(bf16[2,3,48,2496]{3,2,1,0:T(8,128)(2,1)} %get-tuple-element.142.refs_18_.refs_12_), channel_id=1, source_target_pairs={{0,4},{4,0},{1,5},{5,1},{2,6},{6,2},{3,7},{7,3},{8,12},{12,8},{9,1... | collective-permute-start | bytes 4313096 | tf_op jit(solution)/shard_map/ppermute | solution.py:121
  119.7 3.4 collective-permute-start.10
  120.1 5.3 %collective-permute-start.9 = (bf16[2,3,48,2496]{3,2,1,0:T(8,128)(2,1)}, bf16[2,3,48,2496]{3,2,1,0:T(8,128)(2,1)}, u32[]{:S(2)}, u32[]{:S(2)}) collective-permute-start(bf16[2,3,48,2496]{3,2,1,0:T(8,128)(2,1)} %collective-permute-done.5.refs_19_.refs_13_), channel_id=1, source_target_pairs={{0,4},{4,0},{1,5},{5,1},{2,6},{6,2},{3,7},{7,3},{8,12},{12,8},{9,1... | collective-permute-start | bytes 4313096 | tf_op jit(solution)/shard_map/ppermute | solution.py:121
  156.6 5.4 %collective-permute-start.11 = (bf16[4,384,896]{2,1,0:T(8,128)(2,1)}, bf16[4,384,896]{2,1,0:T(8,128)(2,1)}, u32[]{:S(2)}, u32[]{:S(2)}) collective-permute-start(bf16[4,384,896]{2,1,0:T(8,128)(2,1)} %get-tuple-element.151), channel_id=1, source_target_pairs={{0,4},{4,0},{1,5},{5,1},{2,6},{6,2},{3,7},{7,3},{8,12},{12,8},{9,1... | collective-permute-start | bytes 8257544 | tf_op jit(solution)/shard_map/ppermute | solution.py:121
  158.3 177.5 %reduce-scatter.2.cloned.1.call-start = ((), (), s32[]{:S(2)}) async-start(), calls=%async_computation.1 | async-start | bytes 1474560 | tf_op jit(solution)/shard_map/reduce_scatter | solution.py:1094
  169.6 20.7 %collective-permute-start.12 = (bf16[4,2,48,896]{3,2,1,0:T(8,128)(2,1)S(1)}, bf16[4,2,48,896]{3,2,1,0:T(8,128)(2,1)S(1)}, u32[]{:S(2)}, u32[]{:S(2)}) collective-permute-start(bf16[4,2,48,896]{3,2,1,0:T(8,128)(2,1)S(1)} %get-tuple-element.160), channel_id=1, source_target_pairs={{0,8},{8,0},{1,9},{9,1},{2,10},{10,2},{3,11},{11,3},{4,12},{12,4},... | collective-permute-start | bytes 2064392 | tf_op jit(solution)/shard_map/ppermute | solution.py:121
  170.3 20.1 %collective-permute-start.13 = (bf16[4,2,48,896]{3,2,1,0:T(8,128)(2,1)S(1)}, bf16[4,2,48,896]{3,2,1,0:T(8,128)(2,1)S(1)}, u32[]{:S(2)}, u32[]{:S(2)}) collective-permute-start(bf16[4,2,48,896]{3,2,1,0:T(8,128)(2,1)S(1)} %get-tuple-element.162), channel_id=1, source_target_pairs={{0,16},{16,0},{1,17},{17,1},{2,18},{18,2},{3,19},{19,3},{4,20},{20... | collective-permute-start | bytes 2064392 | tf_op jit(solution)/shard_map/ppermute | solution.py:121
  199.7 18.2 %collective-permute-start.14 = (bf16[4,384,1536]{2,1,0:T(8,128)(2,1)S(1)}, bf16[4,384,1536]{2,1,0:T(8,128)(2,1)S(1)}, u32[]{:S(2)}, u32[]{:S(2)}) collective-permute-start(bf16[4,384,1536]{2,1,0:T(8,128)(2,1)S(1)} %get-tuple-element.165), channel_id=1, source_target_pairs={{0,4},{4,0},{1,5},{5,1},{2,6},{6,2},{3,7},{7,3},{8,12},{12,8},{9,1... | collective-permute-start | bytes 14155784 | tf_op jit(solution)/shard_map/ppermute | solution.py:121
  199.8 14.4 %collective-permute-start.15 = (bf16[4,48,896]{2,1,0:T(8,128)(2,1)S(1)}, bf16[4,48,896]{2,1,0:T(8,128)(2,1)S(1)}, u32[]{:S(2)}, u32[]{:S(2)}) collective-permute-start(bf16[4,48,896]{2,1,0:T(8,128)(2,1)S(1)} %get-tuple-element.167), channel_id=1, source_target_pairs={{0,16},{16,0},{1,17},{17,1},{2,18},{18,2},{3,19},{19,3},{4,20},{20... | collective-permute-start | bytes 1032200 | tf_op jit(solution)/shard_map/ppermute | solution.py:121
  201.3 15.8 %collective-permute-start.16 = (bf16[4,48,896]{2,1,0:T(8,128)(2,1)S(1)}, bf16[4,48,896]{2,1,0:T(8,128)(2,1)S(1)}, u32[]{:S(2)}, u32[]{:S(2)}) collective-permute-start(bf16[4,48,896]{2,1,0:T(8,128)(2,1)S(1)} %get-tuple-element.169), channel_id=1, source_target_pairs={{0,8},{8,0},{1,9},{9,1},{2,10},{10,2},{3,11},{11,3},{4,12},{12,4},... | collective-permute-start | bytes 1032200 | tf_op jit(solution)/shard_map/ppermute | solution.py:121
  225.2 34.7 %collective-permute-start.17 = (bf16[4,2,48,1536]{3,2,1,0:T(8,128)(2,1)}, bf16[4,2,48,1536]{3,2,1,0:T(8,128)(2,1)}, u32[]{:S(2)}, u32[]{:S(2)}) collective-permute-start(bf16[4,2,48,1536]{3,2,1,0:T(8,128)(2,1)} %get-tuple-element.182), channel_id=1, source_target_pairs={{0,8},{8,0},{1,9},{9,1},{2,10},{10,2},{3,11},{11,3},{4,12},{12,4},... | collective-permute-start | bytes 3538952 | tf_op jit(solution)/shard_map/ppermute | solution.py:121
  227.7 32.2 %collective-permute-start.18 = (bf16[4,2,48,1536]{3,2,1,0:T(8,128)(2,1)}, bf16[4,2,48,1536]{3,2,1,0:T(8,128)(2,1)}, u32[]{:S(2)}, u32[]{:S(2)}) collective-permute-start(bf16[4,2,48,1536]{3,2,1,0:T(8,128)(2,1)} %get-tuple-element.184), channel_id=1, source_target_pairs={{0,16},{16,0},{1,17},{17,1},{2,18},{18,2},{3,19},{19,3},{4,20},{20... | collective-permute-start | bytes 3538952 | tf_op jit(solution)/shard_map/ppermute | solution.py:121
  227.7 30.9 %collective-permute-start.19 = (bf16[96,896]{1,0:T(8,128)(2,1)}, bf16[96,896]{1,0:T(8,128)(2,1)}, u32[]{:S(2)}, u32[]{:S(2)}) collective-permute-start(bf16[96,896]{1,0:T(8,128)(2,1)} %get-tuple-element.186), channel_id=1, source_target_pairs={{0,3},{1,0},{2,1},{3,2},{4,7},{5,4},{6,5},{7,6},{8,11},{9,8},{10,9... | collective-permute-start | bytes 516104 | tf_op jit(solution)/shard_map/ppermute | solution.py:125
  234.7 23.9 %collective-permute-start.20 = (bf16[96,896]{1,0:T(8,128)(2,1)}, bf16[96,896]{1,0:T(8,128)(2,1)}, u32[]{:S(2)}, u32[]{:S(2)}) collective-permute-start(bf16[96,896]{1,0:T(8,128)(2,1)} %get-tuple-element.187), channel_id=1, source_target_pairs={{0,2},{1,3},{2,0},{3,1},{4,6},{5,7},{6,4},{7,5},{8,10},{9,11},{10,... | collective-permute-start | bytes 516104 | tf_op jit(solution)/shard_map/ppermute | solution.py:125
  234.7 23.9 %collective-permute-start.21 = (bf16[96,896]{1,0:T(8,128)(2,1)}, bf16[96,896]{1,0:T(8,128)(2,1)}, u32[]{:S(2)}, u32[]{:S(2)}) collective-permute-start(bf16[96,896]{1,0:T(8,128)(2,1)} %get-tuple-element.188), channel_id=1, source_target_pairs={{0,1},{1,2},{2,3},{3,0},{4,5},{5,6},{6,7},{7,4},{8,9},{9,10},{10,1... | collective-permute-start | bytes 516104 | tf_op jit(solution)/shard_map/ppermute | solution.py:125
  263.5 19.7 %collective-permute-start.24 = (bf16[4,48,1536]{2,1,0:T(8,128)(2,1)S(1)}, bf16[4,48,1536]{2,1,0:T(8,128)(2,1)S(1)}, u32[]{:S(2)}, u32[]{:S(2)}) collective-permute-start(bf16[4,48,1536]{2,1,0:T(8,128)(2,1)S(1)} %get-tuple-element.197), channel_id=1, source_target_pairs={{0,16},{16,0},{1,17},{17,1},{2,18},{18,2},{3,19},{19,3},{4,20},{20... | collective-permute-start | bytes 1769480 | tf_op jit(solution)/shard_map/ppermute | solution.py:121
  264.2 19.0 %collective-permute-start.25 = (bf16[4,48,1536]{2,1,0:T(8,128)(2,1)S(1)}, bf16[4,48,1536]{2,1,0:T(8,128)(2,1)S(1)}, u32[]{:S(2)}, u32[]{:S(2)}) collective-permute-start(bf16[4,48,1536]{2,1,0:T(8,128)(2,1)S(1)} %get-tuple-element.199), channel_id=1, source_target_pairs={{0,8},{8,0},{1,9},{9,1},{2,10},{10,2},{3,11},{11,3},{4,12},{12,4},... | collective-permute-start | bytes 1769480 | tf_op jit(solution)/shard_map/ppermute | solution.py:121
  287.9 5.7 %collective-permute-start.26 = (bf16[4,384,896]{2,1,0:T(8,128)(2,1)}, bf16[4,384,896]{2,1,0:T(8,128)(2,1)}, u32[]{:S(2)}, u32[]{:S(2)}) collective-permute-start(bf16[4,384,896]{2,1,0:T(8,128)(2,1)} %get-tuple-element.202), channel_id=1, source_target_pairs={{0,4},{4,0},{1,5},{5,1},{2,6},{6,2},{3,7},{7,3},{8,12},{12,8},{9,1... | collective-permute-start | bytes 8257544 | tf_op jit(solution)/shard_map/ppermute | solution.py:121
  287.9 87.1 %all-gather.11.cloned.1.call-start = ((), (), s32[]{:S(2)}) async-start(), calls=%async_computation.4 | async-start | bytes 4202496 | tf_op jit(solution)/shard_map/all_gather | solution.py:1132
  288.0 39.6 %collective-permute-start.22 = (bf16[528,768]{1,0:T(8,128)(2,1)S(1)}, bf16[528,768]{1,0:T(8,128)(2,1)S(1)}, u32[]{:S(2)}, u32[]{:S(2)}) collective-permute-start(bf16[528,768]{1,0:T(8,128)(2,1)S(1)} %get-tuple-element.192.refs_3_), channel_id=1, source_target_pairs={{0,1},{1,2},{2,3},{4,5},{5,6},{6,7},{8,9},{9,10},{10,11},{12,13},{... | collective-permute-start | bytes 2433032 | tf_op jit(solution)/shard_map/ppermute | solution.py:140
  292.3 38.9 %collective-permute-start.23 = (bf16[528,768]{1,0:T(8,128)(2,1)S(1)}, bf16[528,768]{1,0:T(8,128)(2,1)S(1)}, u32[]{:S(2)}, u32[]{:S(2)}) collective-permute-start(bf16[528,768]{1,0:T(8,128)(2,1)S(1)} %get-tuple-element.192.refs_3_), channel_id=1, source_target_pairs={{1,0},{2,1},{3,2},{5,4},{6,5},{7,6},{9,8},{10,9},{11,10},{13,12},{... | collective-permute-start | bytes 2433032 | tf_op jit(solution)/shard_map/ppermute | solution.py:141
  300.5 33.2 %collective-permute-start.29 = (bf16[4,2,48,896]{3,2,1,0:T(8,128)(2,1)S(1)}, bf16[4,2,48,896]{3,2,1,0:T(8,128)(2,1)S(1)}, u32[]{:S(2)}, u32[]{:S(2)}) collective-permute-start(bf16[4,2,48,896]{3,2,1,0:T(8,128)(2,1)S(1)} %get-tuple-element.209), channel_id=1, source_target_pairs={{0,8},{8,0},{1,9},{9,1},{2,10},{10,2},{3,11},{11,3},{4,12},{12,4},... | collective-permute-start | bytes 2064392 | tf_op jit(solution)/shard_map/ppermute | solution.py:121
  301.3 32.4 %collective-permute-start.30 = (bf16[4,2,48,896]{3,2,1,0:T(8,128)(2,1)S(1)}, bf16[4,2,48,896]{3,2,1,0:T(8,128)(2,1)S(1)}, u32[]{:S(2)}, u32[]{:S(2)}) collective-permute-start(bf16[4,2,48,896]{3,2,1,0:T(8,128)(2,1)S(1)} %get-tuple-element.211), channel_id=1, source_target_pairs={{0,16},{16,0},{1,17},{17,1},{2,18},{18,2},{3,19},{19,3},{4,20},{20... | collective-permute-start | bytes 2064392 | tf_op jit(solution)/shard_map/ppermute | solution.py:121
  337.6 21.3 %collective-permute-start.27 = (bf16[528,768]{1,0:T(8,128)(2,1)}, bf16[528,768]{1,0:T(8,128)(2,1)S(1)}, u32[]{:S(2)}, u32[]{:S(2)}) collective-permute-start(bf16[528,768]{1,0:T(8,128)(2,1)} %copy-done.63), channel_id=1, source_target_pairs={{0,1},{1,2},{2,3},{4,5},{5,6},{6,7},{8,9},{9,10},{10,11},{12,13},{... | collective-permute-start | bytes 2433032 | tf_op jit(solution)/shard_map/ppermute | solution.py:140
  341.1 21.9 %collective-permute-start.28 = (bf16[528,768]{1,0:T(8,128)(2,1)}, bf16[528,768]{1,0:T(8,128)(2,1)S(1)}, u32[]{:S(2)}, u32[]{:S(2)}) collective-permute-start(bf16[528,768]{1,0:T(8,128)(2,1)} %copy-done.62), channel_id=1, source_target_pairs={{1,0},{2,1},{3,2},{5,4},{6,5},{7,6},{9,8},{10,9},{11,10},{13,12},{... | collective-permute-start | bytes 2433032 | tf_op jit(solution)/shard_map/ppermute | solution.py:141
  342.4 14.8 %collective-permute-start.31 = (bf16[4,48,896]{2,1,0:T(8,128)(2,1)S(1)}, bf16[4,48,896]{2,1,0:T(8,128)(2,1)S(1)}, u32[]{:S(2)}, u32[]{:S(2)}) collective-permute-start(bf16[4,48,896]{2,1,0:T(8,128)(2,1)S(1)} %get-tuple-element.214), channel_id=1, source_target_pairs={{0,16},{16,0},{1,17},{17,1},{2,18},{18,2},{3,19},{19,3},{4,20},{20... | collective-permute-start | bytes 1032200 | tf_op jit(solution)/shard_map/ppermute | solution.py:121
  343.4 14.2 %collective-permute-start.32 = (bf16[4,48,896]{2,1,0:T(8,128)(2,1)S(1)}, bf16[4,48,896]{2,1,0:T(8,128)(2,1)S(1)}, u32[]{:S(2)}, u32[]{:S(2)}) collective-permute-start(bf16[4,48,896]{2,1,0:T(8,128)(2,1)S(1)} %get-tuple-element.216), channel_id=1, source_target_pairs={{0,8},{8,0},{1,9},{9,1},{2,10},{10,2},{3,11},{11,3},{4,12},{12,4},... | collective-permute-start | bytes 1032200 | tf_op jit(solution)/shard_map/ppermute | solution.py:121
  366.0 39.0 %collective-permute-start.33 = (bf16[528,768]{1,0:T(8,128)(2,1)}, bf16[528,768]{1,0:T(8,128)(2,1)S(1)}, u32[]{:S(2)}, u32[]{:S(2)}) collective-permute-start(bf16[528,768]{1,0:T(8,128)(2,1)} %get-tuple-element.219), channel_id=1, source_target_pairs={{0,1},{1,2},{2,3},{4,5},{5,6},{6,7},{8,9},{9,10},{10,11},{12,13},{... | collective-permute-start | bytes 2433032 | tf_op jit(solution)/shard_map/ppermute | solution.py:140
  368.1 36.9 %collective-permute-start.34 = (bf16[528,768]{1,0:T(8,128)(2,1)}, bf16[528,768]{1,0:T(8,128)(2,1)S(1)}, u32[]{:S(2)}, u32[]{:S(2)}) collective-permute-start(bf16[528,768]{1,0:T(8,128)(2,1)} %get-tuple-element.220), channel_id=1, source_target_pairs={{1,0},{2,1},{3,2},{5,4},{6,5},{7,6},{9,8},{10,9},{11,10},{13,12},{... | collective-permute-start | bytes 2433032 | tf_op jit(solution)/shard_map/ppermute | solution.py:141
  369.4 23.7 %collective-permute-start.35 = (bf16[96,896]{1,0:T(8,128)(2,1)}, bf16[96,896]{1,0:T(8,128)(2,1)S(1)}, u32[]{:S(2)}, u32[]{:S(2)}) collective-permute-start(bf16[96,896]{1,0:T(8,128)(2,1)} %get-tuple-element.224), channel_id=1, source_target_pairs={{0,3},{1,0},{2,1},{3,2},{4,7},{5,4},{6,5},{7,6},{8,11},{9,8},{10,9... | collective-permute-start | bytes 516104 | tf_op jit(solution)/shard_map/ppermute | solution.py:125
  371.2 31.9 %collective-permute-start.36 = (bf16[96,896]{1,0:T(8,128)(2,1)}, bf16[96,896]{1,0:T(8,128)(2,1)S(1)}, u32[]{:S(2)}, u32[]{:S(2)}) collective-permute-start(bf16[96,896]{1,0:T(8,128)(2,1)} %get-tuple-element.225), channel_id=1, source_target_pairs={{0,2},{1,3},{2,0},{3,1},{4,6},{5,7},{6,4},{7,5},{8,10},{9,11},{10,... | collective-permute-start | bytes 516104 | tf_op jit(solution)/shard_map/ppermute | solution.py:125
  373.6 29.5 %collective-permute-start.37 = (bf16[96,896]{1,0:T(8,128)(2,1)}, bf16[96,896]{1,0:T(8,128)(2,1)S(1)}, u32[]{:S(2)}, u32[]{:S(2)}) collective-permute-start(bf16[96,896]{1,0:T(8,128)(2,1)} %get-tuple-element.226), channel_id=1, source_target_pairs={{0,1},{1,2},{2,3},{3,0},{4,5},{5,6},{6,7},{7,4},{8,9},{9,10},{10,1... | collective-permute-start | bytes 516104 | tf_op jit(solution)/shard_map/ppermute | solution.py:125
  404.0 4.6 %collective-permute-start.38 = (bf16[48,896]{1,0:T(8,128)(2,1)S(1)}, bf16[48,896]{1,0:T(8,128)(2,1)S(1)}, u32[]{:S(2)}, u32[]{:S(2)}) collective-permute-start(bf16[48,896]{1,0:T(8,128)(2,1)S(1)} %get-tuple-element.312.refs_0_), channel_id=1, source_target_pairs={{0,8},{8,0},{1,9},{9,1},{2,10},{10,2},{3,11},{11,3},{4,12},{12,4},... | collective-permute-start | bytes 258056 | tf_op jit(solution)/shard_map/ppermute | solution.py:121
  404.0 5.1 %collective-permute-start.39 = (bf16[48,896]{1,0:T(8,128)(2,1)S(1)}, bf16[48,896]{1,0:T(8,128)(2,1)S(1)}, u32[]{:S(2)}, u32[]{:S(2)}) collective-permute-start(bf16[48,896]{1,0:T(8,128)(2,1)S(1)} %get-tuple-element.311.refs_2_), channel_id=1, source_target_pairs={{0,16},{16,0},{1,17},{17,1},{2,18},{18,2},{3,19},{19,3},{4,20},{20... | collective-permute-start | bytes 258056 | tf_op jit(solution)/shard_map/ppermute | solution.py:121
  409.8 5.4 %collective-permute-start.40 = (bf16[2,48,896]{2,1,0:T(8,128)(2,1)S(1)}, bf16[2,48,896]{2,1,0:T(8,128)(2,1)S(1)}, u32[]{:S(2)}, u32[]{:S(2)}) collective-permute-start(bf16[2,48,896]{2,1,0:T(8,128)(2,1)S(1)} %get-tuple-element.237.refs_1_), channel_id=1, source_target_pairs={{0,16},{16,0},{1,17},{17,1},{2,18},{18,2},{3,19},{19,3},{4,20},{20... | collective-permute-start | bytes 516104 | tf_op jit(solution)/shard_map/ppermute | solution.py:121
  410.7 5.4 %collective-permute-start.41 = (bf16[2,48,896]{2,1,0:T(8,128)(2,1)S(1)}, bf16[2,48,896]{2,1,0:T(8,128)(2,1)S(1)}, u32[]{:S(2)}, u32[]{:S(2)}) collective-permute-start(bf16[2,48,896]{2,1,0:T(8,128)(2,1)S(1)} %get-tuple-element.238.refs_2_), channel_id=1, source_target_pairs={{0,8},{8,0},{1,9},{9,1},{2,10},{10,2},{3,11},{11,3},{4,12},{12,4},... | collective-permute-start | bytes 516104 | tf_op jit(solution)/shard_map/ppermute | solution.py:121
  412.4 4.4 %collective-permute-start.42 = (bf16[2,48,896]{2,1,0:T(8,128)(2,1)S(1)}, bf16[2,48,896]{2,1,0:T(8,128)(2,1)S(1)}, u32[]{:S(2)}, u32[]{:S(2)}) collective-permute-start(bf16[2,48,896]{2,1,0:T(8,128)(2,1)S(1)} %get-tuple-element.237.refs_1_), channel_id=1, source_target_pairs={{0,4},{4,0},{1,5},{5,1},{2,6},{6,2},{3,7},{7,3},{8,12},{12,8},{9,1... | collective-permute-start | bytes 516104 | tf_op jit(solution)/shard_map/ppermute | solution.py:121
  412.5 4.3 %collective-permute-start.43 = (bf16[2,48,896]{2,1,0:T(8,128)(2,1)S(1)}, bf16[2,48,896]{2,1,0:T(8,128)(2,1)S(1)}, u32[]{:S(2)}, u32[]{:S(2)}) collective-permute-start(bf16[2,48,896]{2,1,0:T(8,128)(2,1)S(1)} %get-tuple-element.238.refs_2_), channel_id=1, source_target_pairs={{0,4},{4,0},{1,5},{5,1},{2,6},{6,2},{3,7},{7,3},{8,12},{12,8},{9,1... | collective-permute-start | bytes 516104 | tf_op jit(solution)/shard_map/ppermute | solution.py:121
  (72 other events, 704.1 us)
Sparse Core Ops, SparseCore 0:
  11.5 46.2 all-gather.6
  158.5 70.8 all-gather.8
  288.1 45.7 reduce-scatter.1
  337.7 37.2 all-gather.10

commit v4 on v3

--- a/solution.py
+++ b/solution.py
@@ -143,8 +143,11 @@
     def first_round(self, a, b, after=()):
         return stack_pairs(a, self.swap(a, XBIT), b, self.swap(b, YBIT), after)
 
-    def second_round(self, sa, sb):
-        near = [sa, sb, self.swap(sa, YBIT), self.swap(sb, XBIT)]
+    def second_round(self, sa, sb, after=()):
+        ya, xb = self.swap(sa, YBIT), self.swap(sb, XBIT)
+        if after:
+            ya, xb = relay([ya, xb], after)
+        near = [sa, sb, ya, xb]
         return near + [self.swap(t, CORE) for t in near]
 
 
@@ -191,37 +194,39 @@
     return [pltpu.make_async_copy(s, d, sems.at[i]) for i, (s, d) in enumerate(out)]
 
 
-def split_kernel(sc, v_ref, a_ref, b_ref, *rest):
+def split_kernel(sc, v_ref, *refs):
+    *others, a_ref, b_ref = refs
     half = a_ref.shape[1]
-    n = v_ref.shape[0]
-    for ref in rest:
-        ref[...] = v_ref[:, 2 * half :, :]
+    n, _, width = v_ref.shape
     for k in range(1, n):
         at = lax.rem(sc[16] + n - k, n)
-        a_ref[k - 1] = v_ref[at, :half, :]
-        b_ref[k - 1] = v_ref[at, half : 2 * half, :]
-
-
-def split(offs, v, rows, after=()):
-    n, _, width = v.shape
-    out = (n - 1, rows // 2, width)
-    shapes = [out, out] + ([(n, v.shape[1] - rows, width)] if v.shape[1] > rows else [])
+        a_ref[k - 1, :, :width] = v_ref[at, :half, :]
+        b_ref[k - 1, :, :width] = v_ref[at, half:, :]
+        a_ref[k - 1, :, width:] = others[k - 1][:half, :]
+        b_ref[k - 1, :, width:] = others[k - 1][half:, :]
+
+
+def split(offs, v, others, after=()):
+    n, rows, width = v.shape
+    out = (n - 1, rows // 2, width + others[0].shape[1])
     return launch(
-        split_kernel, "split", [v], [whole(v.shape)], [whole(shape) for shape in shapes],
-        like(bf16, *shapes), offs=offs, after=after,
-    )
-
-
-def relay_kernel(a, b):
-    b[...] = a[...]
-
-
-def relay(a, after):
-    (a,), _ = launch(
-        relay_kernel, "relay", [a], [whole(a.shape)], [whole(a.shape)], like(a.dtype, a.shape),
-        after=after,
-    )
-    return a
+        split_kernel, "split", [v, *others], [whole(x.shape) for x in (v, *others)],
+        [whole(out)] * 2, like(bf16, out, out), offs=offs, after=after,
+    )
+
+
+def relay_kernel(*refs):
+    half = len(refs) // 2
+    for a, b in zip(refs[:half], refs[half:]):
+        b[...] = a[...]
+
+
+def relay(arrays, after):
+    specs = [whole(a.shape) for a in arrays]
+    return launch(
+        relay_kernel, "relay", arrays, specs, specs,
+        [jax.ShapeDtypeStruct(a.shape, a.dtype) for a in arrays], after=after,
+    )[0]
 
 
 def collect_kernel(step, n, sc, right, left, own, *refs):
@@ -1196,17 +1201,19 @@
 
     common = (offs, tokens, segs, pads, seg_cols, gain_a)
     own = (w_gate, w_up, w_down, w_out_t)
-    z1 = lax.all_gather(piece(*own), "mp")
+    z1 = lax.all_gather(piece(*own[:2]), "mp")
+    piece2 = piece(*own[2:])
+    z2 = [place.shift(piece2, k) for k in range(1, slots)]
     (attended,), done = attend(1, *common, w_qkv, hot, heads, size)
     mixed = [attended[slots - 1]] + [place.shift(attended[k - 1], k) for k in range(1, slots)]
-    halved, _ = split(offs, z1, eighth, (done,))
-    s1, _ = place.first_round(*halved, mixed[1:])
-    arrays = place.second_round(*s1)
+    halved, _ = split(offs, z1, z2, (done,))
+    s1, _ = place.first_round(*halved)
+    arrays = place.second_round(*s1, mixed[1:])
     (hid, normed_ffn, act, dact, inner, score, nfin, ge, gain_fin, gft, ghf), done = forward(
         offs, tokens, gain_f, gain_l, w_proj, pad_cols, query_emb, score_cot, top_index, mixed,
         own, arrays, length,
     )
-    all_qkv = lax.all_gather(relay(piece(w_qkv), (done,)), group + ("mp",))
+    all_qkv = lax.all_gather(relay([piece(w_qkv)], (done,))[0], group + ("mp",))
     all_qkv = all_qkv.reshape((2, 2, 2, slots) + all_qkv.shape[-2:])
     down_sides = ([inner, nfin], [(gft, 0), (ge, 1)])
     (send,), _ = products(offs, *down_sides, slots, mib=58)

time: 433 us -> 425 us (0.982)
  waiting for transfers between devices: 174 us -> 157 us
  starting transfers between devices: 54.3 us -> 59 us
    all_gather x2, waiting for transfers between devices: 31.1 us -> 13.6 us  [the longest x1 13.6 us: local(): z1 = lax.all_gather(piece(*own[:2]), 'mp')]
    ppermute x9 -> x12, starting transfers between devices: 17 us -> 21.1 us  [shift(): return lax.ppermute(v, 'mp', [(i, (i + k) % n) for i in range(n)])]
    ppermute x9 -> x12, waiting for transfers between devices: 39.6 us -> 42.7 us  [shift(): return lax.ppermute(v, 'mp', [(i, (i + k) % n) for i in range(n)])]
    pallas_call x29 -> x30, Pallas kernels: 148 us -> 150 us  [launch(): pl.pallas_call(body, out_shape=list(out_shape) + [jax.ShapeDtypeStruct(to...]
    unnamed x142 -> x136, local copies, waits for them, and re-layouts: 26.5 us -> 25.8 us
  transfers between devices with their start and end apart: 50 -> 53, of which waited for: 24 -> 28; matrix products, arithmetic and copies ran while one was open for 1% -> 3% of each run, Pallas kernels for 24% -> 25%
where the time goes in v4:
time: 425 us; the launch traced here: 420 us
  waiting for transfers between devices  157 us (37%)
  Pallas kernels  150 us (35%)
  starting transfers between devices  59 us (14%)
  local copies, waits for them, and re-layouts  35 us (8%)
  between operations  15.1 us (4%)
    pallas_call x30, Pallas kernels, launch(): pl.pallas_call(body, out_shape=list(out_shape) + [jax.ShapeDtypeStruct(to...  150 us
    ppermute x31, waiting for transfers between devices, swap(): return lax.ppermute(v, name, [(0, 1), (1, 0)])  66.9 us
    ppermute x12, waiting for transfers between devices, shift(): return lax.ppermute(v, 'mp', [(i, (i + k) % n) for i in range(n)])  42.7 us
    unnamed x136, local copies, waits for them, and re-layouts  25.8 us
    ppermute x3, waiting for transfers between devices, both_ways(): right = lax.ppermute(right, 'mp', [(i, i + 1) for i in range(n - 1)])  25.3 us
    ppermute x31, starting transfers between devices, swap(): return lax.ppermute(v, name, [(0, 1), (1, 0)])  23.4 us
    ppermute x12, starting transfers between devices, shift(): return lax.ppermute(v, 'mp', [(i, (i + k) % n) for i in range(n)])  21.1 us
    all_gather x1, waiting for transfers between devices, local(): z1 = lax.all_gather(piece(*own[:2]), 'mp')  13.6 us
  transfers between devices with their start and end apart: 53, of which 28 were waited for; matrix products, arithmetic and copies ran while one was open for 3% of the time, Pallas kernels for 25%

profile of v4, /device:TPU:0, one launch (start us, length us, event | category | flops | bytes accessed | tf_op | source)
XLA Modules:
  0.0 420.1 jit_solution(224522411813060604)
XLA Ops:
  12.1 3.0 collective-permute-start.3
  15.2 2.6 collective-permute-start.4
  23.2 10.8 %attend.1 = (bf16[4,528,192]{2,1,0:T(8,128)(2,1)S(1)}, f32[8,128]{1,0:T(8,128)S(1)}) custom-call(s32[20]{0:T(128)S(1)} %stack.83.refs_0_, bf16[2048,768]{1,0:T(8,128)(2,1)S(1)} %copy-done.11, f32[4,512]{1,0:T(4,128)S(1)} %convert_element_type.4.refs_2_, f32[4,512]{1,0:T(4,128)S(1)} %get-tuple-element.318.refs_3_, f32[512,4]{1,0:T(8,128)S(1)} %bitcast.52, ...), custom_call_target="tpu_custom_call" | custom-call | flops 2617245696 | bytes 4194304 | tf_op jit(solution)/shard_map/attend/pallas_call | solution.py:84
  35.1 4.9 %collective-permute-done.4.refs_3_ = bf16[96,960]{1,0:T(8,128)(2,1)} collective-permute-done((bf16[96,960]{1,0:T(8,128)(2,1)}, bf16[96,960]{1,0:T(8,128)(2,1)}, u32[]{:S(2)}, u32[]{:S(2)}) %collective-permute-start.4) | collective-permute-done | bytes 184352 | tf_op jit(solution)/shard_map/ppermute | solution.py:125
  39.9 13.6 %all-gather.7.cloned.1.call-done = bf16[384,1536]{1,0:T(8,128)(2,1)} async-done(((bf16[96,1536]{1,0:T(8,128)(2,1)}), bf16[384,1536]{1,0:T(8,128)(2,1)}) %all-gather.7.cloned.1.call-update) | async-done | bytes 1179664 | tf_op jit(solution)/shard_map/all_gather | solution.py:1204
  54.8 2.2 split.1
  60.0 15.4 %collective-permute-done.6.refs_1_ = bf16[3,48,2496]{2,1,0:T(8,128)(2,1)S(1)} collective-permute-done((bf16[3,48,2496]{2,1,0:T(8,128)(2,1)S(1)}, bf16[3,48,2496]{2,1,0:T(8,128)(2,1)S(1)}, u32[]{:S(2)}, u32[]{:S(2)}) %collective-permute-start.6) | collective-permute-done | bytes 718880 | tf_op jit(solution)/shard_map/ppermute | solution.py:121
  83.8 2.3 collective-permute-start.2
  86.1 6.0 %collective-permute-done.refs_2_.refs_10_.refs_9_ = bf16[528,192]{1,0:T(8,128)(2,1)S(1)} collective-permute-done((bf16[528,192]{1,0:T(8,128)(2,1)S(1)}, bf16[528,192]{1,0:T(8,128)(2,1)S(1)}, u32[]{:S(2)}, u32[]{:S(2)}) %collective-permute-start) | collective-permute-done | bytes 202784 | tf_op jit(solution)/shard_map/ppermute | solution.py:125
  92.1 9.0 %collective-permute-done.1.refs_3_.refs_11_.refs_8_ = bf16[528,192]{1,0:T(8,128)(2,1)S(1)} collective-permute-done((bf16[528,192]{1,0:T(8,128)(2,1)S(1)}, bf16[528,192]{1,0:T(8,128)(2,1)S(1)}, u32[]{:S(2)}, u32[]{:S(2)}) %collective-permute-start.1) | collective-permute-done | bytes 202784 | tf_op jit(solution)/shard_map/ppermute | solution.py:125
  101.2 9.9 %collective-permute-done.8.refs_0_ = bf16[2,3,48,2496]{3,2,1,0:T(8,128)(2,1)S(1)} collective-permute-done((bf16[2,3,48,2496]{3,2,1,0:T(8,128)(2,1)S(1)}, bf16[2,3,48,2496]{3,2,1,0:T(8,128)(2,1)S(1)}, u32[]{:S(2)}, u32[]{:S(2)}) %collective-permute-start.8) | collective-permute-done | bytes 1437728 | tf_op jit(solution)/shard_map/ppermute | solution.py:121
  112.5 1.8 relay.2
  117.9 2.1 collective-permute-done.13.refs_24_.refs_18_
  120.0 24.8 %forward.1 = (f32[512,768]{1,0:T(8,128)}, bf16[512,768]{1,0:T(8,128)(2,1)}, bf16[4,512,768]{2,1,0:T(8,128)(2,1)}, bf16[4,512,768]{2,1,0:T(8,128)(2,1)}, bf16[4,5...) custom-call(s32[20]{0:T(128)} %copy-done.49, ...), custom_call_target="tpu_custom_call" | custom-call | flops 7851737088 | bytes 25165824 | tf_op jit(solution)/shard_map/forward/pallas_call | solution.py:84
  144.9 6.3 %products_send.2 = (bf16[4,384,896]{2,1,0:T(8,128)(2,1)}, f32[8,128]{1,0:T(8,128)}) custom-call(s32[20]{0:T(128)} %copy-done.49, bf16[4,512,768]{2,1,0:T(8,128)(2,1)} %get-tuple-element.152.refs_1_, bf16[512,768]{1,0:T(8,128)(2,1)} %get-tuple-element.153.refs_2_, bf16[512,768]{1,0:T(8,128)(2,1)} %get-tuple-element.148.refs_3_.refs_2_, ...), custom_call_target="tpu_custom_call" | custom-call | flops 1048576 | bytes 65536 | tf_op jit(solution)/shard_map/products_send/pallas_call | solution.py:84
  153.5 3.1 collective-permute-done.14.refs_5_
  158.9 5.4 %products_keep.2 = (bf16[4,2,48,896]{3,2,1,0:T(8,128)(2,1)S(1)}, bf16[4,2,48,896]{3,2,1,0:T(8,128)(2,1)S(1)}, bf16[4,2,48,896]{3,2,1,0:T(8,128)(2,1)S(1)}, bf16[...) custom-call(s32[20]{0:T(128)S(1)} %copy-done.50, bf16[4,512,768]{2,1,0:T(8,128)(2,1)S(1)} %copy-done.5, ...), custom_call_target="tpu_custom_call" | custom-call | flops 1048576 | bytes 65536 | tf_op jit(solution)/shard_map/products_keep/pallas_call | solution.py:84
  165.5 19.4 %ffn_back.1 = (bf16[4,512,768]{2,1,0:T(8,128)(2,1)}, bf16[4,512,768]{2,1,0:T(8,128)(2,1)}, f32[512,768]{1,0:T(8,128)}, bf16[512,768]{1,0:T(8,128)(2,1)S(1)}, bf1...) custom-call(s32[20]{0:T(128)S(1)} %copy-done.50, ...), custom_call_target="tpu_custom_call" | custom-call | flops 7851737088 | bytes 25165824 | tf_op jit(solution)/shard_map/ffn_back/pallas_call | solution.py:84
  186.7 1.9 copy-done.2
  188.6 1.9 copy-done.4
  190.5 3.9 products_send.3
  197.5 14.4 %collective-permute-done.18.refs_1_ = bf16[4,48,896]{2,1,0:T(8,128)(2,1)S(1)} collective-permute-done((bf16[4,48,896]{2,1,0:T(8,128)(2,1)S(1)}, bf16[4,48,896]{2,1,0:T(8,128)(2,1)S(1)}, u32[]{:S(2)}, u32[]{:S(2)}) %collective-permute-start.18) | collective-permute-done | bytes 344096 | tf_op jit(solution)/shard_map/ppermute | solution.py:121
  212.9 5.1 %products_keep.3 = (bf16[4,2,48,1536]{3,2,1,0:T(8,128)(2,1)}, bf16[4,2,48,1536]{3,2,1,0:T(8,128)(2,1)S(1)}, bf16[4,2,48,1536]{3,2,1,0:T(8,128)(2,1)}, bf16[4,2,48,1536]{3,2,1,0:T(8,128)(2,1)S(1)}, f32[8,128]{1,0:T(8,128)S(1)}) custom-call(s32[20]{0:T(128)S(1)} %copy-done.50, bf16[512,768]{1,0:T(8,128)(2,1)S(1)} %copy-done.14, ...), custom_call_target="tpu_custom_call" | custom-call | flops 1048576 | bytes 65536 | tf_op jit(solution)/shard_map/products_keep/pallas_call | solution.py:84
  222.2 3.3 collective-permute-start.22
  226.8 2.1 copy-done.6
  233.0 16.4 %attend_back0.1 = (bf16[4,4,512,192]{3,2,1,0:T(8,128)(2,1)S(1)}, f32[16,128]{1,0:T(8,128)S(1)}, f32[512,768]{1,0:T(8,128)S(1)}, f32[8,128]{1,0:T(8,128)S(1)}) custom-call(s32[20]{0:T(128)S(1)} %copy-done.50, bf16[2048,768]{1,0:T(8,128)(2,1)S(1)} %copy-done.12, f32[4,512]{1,0:T(4,128)S(1)} %convert_element_type.4.refs_2_, ...), custom_call_target="tpu_custom_call" | custom-call | flops 3221225472 | bytes 16777216 | tf_op jit(solution)/shard_map/attend_back0/pallas_call | solution.py:84
  250.9 3.5 second_sums.4
  256.5 17.5 %attend_back2.1 = (bf16[4,4,512,192]{3,2,1,0:T(8,128)(2,1)S(1)}, f32[16,128]{1,0:T(8,128)}, bf16[528,768]{1,0:T(8,128)(2,1)S(1)}, bf16[2,512,768]{2,1,0:T(8,128)...) custom-call(s32[20]{0:T(128)S(1)} %copy-done.50, ...), custom_call_target="tpu_custom_call", output_to_operand_aliasing={{0}: (18, {})} | custom-call | flops 3221225472 | bytes 16777216 | tf_op jit(solution)/shard_map/attend_back2/pallas_call | solution.py:84
  274.9 3.9 attn_send.1
  278.9 4.3 %collective-permute-start.25 = (bf16[528,768]{1,0:T(8,128)(2,1)S(1)}, bf16[528,768]{1,0:T(8,128)(2,1)S(1)}, u32[]{:S(2)}, u32[]{:S(2)}) collective-permute-start(bf16[528,768]{1,0:T(8,128)(2,1)S(1)} %get-tuple-element.196.refs_3_), channel_id=1, source_target_pairs={{0,1},{1,2},{2,3},{4,5},{5,6},{6,7},{8,9},{9,10},{10,11},{12,13},{... | collective-permute-start | bytes 2433032 | tf_op jit(solution)/shard_map/ppermute | solution.py:140
  284.5 2.2 copy-done.1
  286.7 4.6 %attn_keep.1 = (bf16[4,2,48,896]{3,2,1,0:T(8,128)(2,1)S(1)}, bf16[4,2,48,896]{3,2,1,0:T(8,128)(2,1)S(1)}, bf16[4,2,48,896]{3,2,1,0:T(8,128)(2,1)S(1)}, bf16[4,2,48,896]{3,2,1,0:T(8,128)(2,1)S(1)}, f32[8,128]{1,0:T(8,128)S(1)}) custom-call(s32[20]{0:T(128)S(1)} %copy-done.50, bf16[4,4,512,192]{3,2,1,0:T(8,128)(2,1)S(1)} %copy-done.1, ...), custom_call_target="tpu_custom_call" | custom-call | flops 1048576 | bytes 65536 | tf_op jit(solution)/shard_map/attn_keep/pallas_call | solution.py:84
  293.6 24.8 %collective-permute-done.25.refs_1_ = bf16[528,768]{1,0:T(8,128)(2,1)S(1)} collective-permute-done((bf16[528,768]{1,0:T(8,128)(2,1)S(1)}, bf16[528,768]{1,0:T(8,128)(2,1)S(1)}, u32[]{:S(2)}, u32[]{:S(2)}) %collective-permute-start.25) | collective-permute-done | bytes 811040 | tf_op jit(solution)/shard_map/ppermute | solution.py:140
  318.4 3.6 collective-permute-done.26.refs_2_
  322.1 2.5 collect1.1
  329.1 3.5 collective-permute-start.30
  333.9 1.8 collective-permute-start.34
  336.9 11.8 %collective-permute-done.34.refs_1_ = bf16[4,48,896]{2,1,0:T(8,128)(2,1)S(1)} collective-permute-done((bf16[4,48,896]{2,1,0:T(8,128)(2,1)S(1)}, bf16[4,48,896]{2,1,0:T(8,128)(2,1)S(1)}, u32[]{:S(2)}, u32[]{:S(2)}) %collective-permute-start.34) | collective-permute-done | bytes 344096 | tf_op jit(solution)/shard_map/ppermute | solution.py:121
  350.4 4.1 collective-permute-done.31.refs_2_
  354.4 3.0 collect2.1
  357.4 2.2 collective-permute-start.36
  362.7 2.4 collective-permute-start.39
  366.5 5.3 %open.1 = (f32[768,768]{1,0:T(8,128)}, f32[768,128]{1,0:T(8,128)}, f32[768,768]{1,0:T(8,128)}, f32[768,768]{1,0:T(8,128)}, f32[8,128]{1,0:T(8,128)}) custom-call(bf16[2,2,2,96,2432]{4,3,2,1,0:T(8,128)(2,1)} %bitcast.59, f32[8,128]{1,0:T(8,128)} %copy-done.57), custom_call_target="tpu_custom_call" | custom-call | flops 1048576 | bytes 65536 | tf_op jit(solution)/shard_map/open/pallas_call | solution.py:84
  371.8 12.9 %collective-permute-done.38.refs_1_ = bf16[96,896]{1,0:T(8,128)(2,1)S(1)} collective-permute-done((bf16[96,896]{1,0:T(8,128)(2,1)}, bf16[96,896]{1,0:T(8,128)(2,1)S(1)}, u32[]{:S(2)}, u32[]{:S(2)}) %collective-permute-start.38) | collective-permute-done | bytes 172064 | tf_op jit(solution)/shard_map/ppermute | solution.py:125
  384.7 9.9 %collective-permute-done.39.refs_2_ = bf16[96,896]{1,0:T(8,128)(2,1)S(1)} collective-permute-done((bf16[96,896]{1,0:T(8,128)(2,1)}, bf16[96,896]{1,0:T(8,128)(2,1)S(1)}, u32[]{:S(2)}, u32[]{:S(2)}) %collective-permute-start.39) | collective-permute-done | bytes 172064 | tf_op jit(solution)/shard_map/ppermute | solution.py:125
  396.5 2.4 collect3.1
  404.4 2.2 collective-permute-done.43.refs_3_
  409.1 2.2 unpack.1
  (253 shorter events, 82.8 us)
Async XLA Ops:
  7.2 46.3 %all-gather.7.cloned.1.call-start = ((), (), s32[]{:S(2)}) async-start(), calls=%async_computation.2 | async-start | bytes 1474560 | tf_op jit(solution)/shard_map/all_gather | solution.py:1204
  9.0 217.7 %all-gather.9.cloned.1.call-start = ((), (), s32[]{:S(2)}) async-start(), calls=%async_computation.3 | async-start | bytes 4055040 | tf_op jit(solution)/shard_map/all_gather | solution.py:1216
  12.1 22.9 %collective-permute-start.3 = (bf16[96,960]{1,0:T(8,128)(2,1)}, bf16[96,960]{1,0:T(8,128)(2,1)}, u32[]{:S(2)}, u32[]{:S(2)}) collective-permute-start(bf16[96,960]{1,0:T(8,128)(2,1)} %pad_maximum_fusion.1), channel_id=1, source_target_pairs={{0,1},{1,2},{2,3},{3,0},{4,5},{5,6},{6,7},{7,4},{8,9},{9,10},{10,1... | collective-permute-start | bytes 552968 | tf_op jit(solution)/shard_map/ppermute | solution.py:125
  15.2 24.8 %collective-permute-start.4 = (bf16[96,960]{1,0:T(8,128)(2,1)}, bf16[96,960]{1,0:T(8,128)(2,1)}, u32[]{:S(2)}, u32[]{:S(2)}) collective-permute-start(bf16[96,960]{1,0:T(8,128)(2,1)} %pad_maximum_fusion.1), channel_id=1, source_target_pairs={{0,2},{1,3},{2,0},{3,1},{4,6},{5,7},{6,4},{7,5},{8,10},{9,11},{10,... | collective-permute-start | bytes 552968 | tf_op jit(solution)/shard_map/ppermute | solution.py:125
  17.8 22.2 %collective-permute-start.5 = (bf16[96,960]{1,0:T(8,128)(2,1)}, bf16[96,960]{1,0:T(8,128)(2,1)}, u32[]{:S(2)}, u32[]{:S(2)}) collective-permute-start(bf16[96,960]{1,0:T(8,128)(2,1)} %pad_maximum_fusion.1), channel_id=1, source_target_pairs={{0,3},{1,0},{2,1},{3,2},{4,7},{5,4},{6,5},{7,6},{8,11},{9,8},{10,9... | collective-permute-start | bytes 552968 | tf_op jit(solution)/shard_map/ppermute | solution.py:125
  57.0 18.4 %collective-permute-start.6 = (bf16[3,48,2496]{2,1,0:T(8,128)(2,1)S(1)}, bf16[3,48,2496]{2,1,0:T(8,128)(2,1)S(1)}, u32[]{:S(2)}, u32[]{:S(2)}) collective-permute-start(bf16[3,48,2496]{2,1,0:T(8,128)(2,1)S(1)} %get-tuple-element.141.refs_0_), channel_id=1, source_target_pairs={{0,8},{8,0},{1,9},{9,1},{2,10},{10,2},{3,11},{11,3},{4,12},{12,4},... | collective-permute-start | bytes 2156552 | tf_op jit(solution)/shard_map/ppermute | solution.py:121
  58.5 18.1 %collective-permute-start.7 = (bf16[3,48,2496]{2,1,0:T(8,128)(2,1)S(1)}, bf16[3,48,2496]{2,1,0:T(8,128)(2,1)S(1)}, u32[]{:S(2)}, u32[]{:S(2)}) collective-permute-start(bf16[3,48,2496]{2,1,0:T(8,128)(2,1)S(1)} %get-tuple-element.142.refs_2_), channel_id=1, source_target_pairs={{0,16},{16,0},{1,17},{17,1},{2,18},{18,2},{3,19},{19,3},{4,20},{20... | collective-permute-start | bytes 2156552 | tf_op jit(solution)/shard_map/ppermute | solution.py:121
  78.0 33.1 %collective-permute-start.8 = (bf16[2,3,48,2496]{3,2,1,0:T(8,128)(2,1)S(1)}, bf16[2,3,48,2496]{3,2,1,0:T(8,128)(2,1)S(1)}, u32[]{:S(2)}, u32[]{:S(2)}) collective-permute-start(bf16[2,3,48,2496]{3,2,1,0:T(8,128)(2,1)S(1)} %get-tuple-element.143.refs_17_.refs_11_), channel_id=1, source_target_pairs={{0,16},{16,0},{1,17},{17,1},{2,18},{18,2},{3,19},{19,3},{4,20},{20... | collective-permute-start | bytes 4313096 | tf_op jit(solution)/shard_map/ppermute | solution.py:121
  79.5 33.0 %collective-permute-start.9 = (bf16[2,3,48,2496]{3,2,1,0:T(8,128)(2,1)}, bf16[2,3,48,2496]{3,2,1,0:T(8,128)(2,1)S(1)}, u32[]{:S(2)}, u32[]{:S(2)}) collective-permute-start(bf16[2,3,48,2496]{3,2,1,0:T(8,128)(2,1)} %get-tuple-element.144.refs_18_.refs_12_), channel_id=1, source_target_pairs={{0,8},{8,0},{1,9},{9,1},{2,10},{10,2},{3,11},{11,3},{4,12},{12,4},... | collective-permute-start | bytes 4313096 | tf_op jit(solution)/shard_map/ppermute | solution.py:121
  80.8 11.3 %collective-permute-start = (bf16[528,192]{1,0:T(8,128)(2,1)S(1)}, bf16[528,192]{1,0:T(8,128)(2,1)S(1)}, u32[]{:S(2)}, u32[]{:S(2)}) collective-permute-start(bf16[528,192]{1,0:T(8,128)(2,1)S(1)} %get-tuple-element.313), channel_id=1, source_target_pairs={{0,1},{1,2},{2,3},{3,0},{4,5},{5,6},{6,7},{7,4},{8,9},{9,10},{10,1... | collective-permute-start | bytes 608264 | tf_op jit(solution)/shard_map/ppermute | solution.py:125
  82.1 19.0 %collective-permute-start.1 = (bf16[528,192]{1,0:T(8,128)(2,1)S(1)}, bf16[528,192]{1,0:T(8,128)(2,1)S(1)}, u32[]{:S(2)}, u32[]{:S(2)}) collective-permute-start(bf16[528,192]{1,0:T(8,128)(2,1)S(1)} %get-tuple-element.312), channel_id=1, source_target_pairs={{0,2},{1,3},{2,0},{3,1},{4,6},{5,7},{6,4},{7,5},{8,10},{9,11},{10,... | collective-permute-start | bytes 608264 | tf_op jit(solution)/shard_map/ppermute | solution.py:125
  83.8 17.3 %collective-permute-start.2 = (bf16[528,192]{1,0:T(8,128)(2,1)S(1)}, bf16[528,192]{1,0:T(8,128)(2,1)S(1)}, u32[]{:S(2)}, u32[]{:S(2)}) collective-permute-start(bf16[528,192]{1,0:T(8,128)(2,1)S(1)} %get-tuple-element.311), channel_id=1, source_target_pairs={{0,3},{1,0},{2,1},{3,2},{4,7},{5,4},{6,5},{7,6},{8,11},{9,8},{10,9... | collective-permute-start | bytes 608264 | tf_op jit(solution)/shard_map/ppermute | solution.py:125
  92.1 24.8 %collective-permute-start.10 = (bf16[2,3,48,2496]{3,2,1,0:T(8,128)(2,1)S(1)}, bf16[2,3,48,2496]{3,2,1,0:T(8,128)(2,1)}, u32[]{:S(2)}, u32[]{:S(2)}) collective-permute-start(bf16[2,3,48,2496]{3,2,1,0:T(8,128)(2,1)S(1)} %get-tuple-element.143.refs_17_.refs_11_), channel_id=1, source_target_pairs={{0,4},{4,0},{1,5},{5,1},{2,6},{6,2},{3,7},{7,3},{8,12},{12,8},{9,1... | collective-permute-start | bytes 4313096 | tf_op jit(solution)/shard_map/ppermute | solution.py:121
  101.1 15.7 %collective-permute-start.11 = (bf16[2,3,48,2496]{3,2,1,0:T(8,128)(2,1)}, bf16[2,3,48,2496]{3,2,1,0:T(8,128)(2,1)}, u32[]{:S(2)}, u32[]{:S(2)}) collective-permute-start(bf16[2,3,48,2496]{3,2,1,0:T(8,128)(2,1)} %get-tuple-element.144.refs_18_.refs_12_), channel_id=1, source_target_pairs={{0,4},{4,0},{1,5},{5,1},{2,6},{6,2},{3,7},{7,3},{8,12},{12,8},{9,1... | collective-permute-start | bytes 4313096 | tf_op jit(solution)/shard_map/ppermute | solution.py:121
  114.3 5.7 %collective-permute-start.13 = (bf16[2,3,48,2496]{3,2,1,0:T(8,128)(2,1)}, bf16[2,3,48,2496]{3,2,1,0:T(8,128)(2,1)}, u32[]{:S(2)}, u32[]{:S(2)}) collective-permute-start(bf16[2,3,48,2496]{3,2,1,0:T(8,128)(2,1)} %get-tuple-element.146.refs_20_.refs_14_), channel_id=1, source_target_pairs={{0,4},{4,0},{1,5},{5,1},{2,6},{6,2},{3,7},{7,3},{8,12},{12,8},{9,1... | collective-permute-start | bytes 4313096 | tf_op jit(solution)/shard_map/ppermute | solution.py:121
  151.2 5.4 %collective-permute-start.14 = (bf16[4,384,896]{2,1,0:T(8,128)(2,1)}, bf16[4,384,896]{2,1,0:T(8,128)(2,1)}, u32[]{:S(2)}, u32[]{:S(2)}) collective-permute-start(bf16[4,384,896]{2,1,0:T(8,128)(2,1)} %get-tuple-element.155), channel_id=1, source_target_pairs={{0,4},{4,0},{1,5},{5,1},{2,6},{6,2},{3,7},{7,3},{8,12},{12,8},{9,1... | collective-permute-start | bytes 8257544 | tf_op jit(solution)/shard_map/ppermute | solution.py:121
  152.9 174.4 %reduce-scatter.2.cloned.1.call-start = ((), (), s32[]{:S(2)}) async-start(), calls=%async_computation.1 | async-start | bytes 1474560 | tf_op jit(solution)/shard_map/reduce_scatter | solution.py:1099
  164.3 21.1 %collective-permute-start.15 = (bf16[4,2,48,896]{3,2,1,0:T(8,128)(2,1)S(1)}, bf16[4,2,48,896]{3,2,1,0:T(8,128)(2,1)S(1)}, u32[]{:S(2)}, u32[]{:S(2)}) collective-permute-start(bf16[4,2,48,896]{3,2,1,0:T(8,128)(2,1)S(1)} %get-tuple-element.164), channel_id=1, source_target_pairs={{0,8},{8,0},{1,9},{9,1},{2,10},{10,2},{3,11},{11,3},{4,12},{12,4},... | collective-permute-start | bytes 2064392 | tf_op jit(solution)/shard_map/ppermute | solution.py:121
  165.0 20.4 %collective-permute-start.16 = (bf16[4,2,48,896]{3,2,1,0:T(8,128)(2,1)S(1)}, bf16[4,2,48,896]{3,2,1,0:T(8,128)(2,1)S(1)}, u32[]{:S(2)}, u32[]{:S(2)}) collective-permute-start(bf16[4,2,48,896]{3,2,1,0:T(8,128)(2,1)S(1)} %get-tuple-element.166), channel_id=1, source_target_pairs={{0,16},{16,0},{1,17},{17,1},{2,18},{18,2},{3,19},{19,3},{4,20},{20... | collective-permute-start | bytes 2064392 | tf_op jit(solution)/shard_map/ppermute | solution.py:121
  194.4 18.5 %collective-permute-start.17 = (bf16[4,384,1536]{2,1,0:T(8,128)(2,1)S(1)}, bf16[4,384,1536]{2,1,0:T(8,128)(2,1)S(1)}, u32[]{:S(2)}, u32[]{:S(2)}) collective-permute-start(bf16[4,384,1536]{2,1,0:T(8,128)(2,1)S(1)} %get-tuple-element.169), channel_id=1, source_target_pairs={{0,4},{4,0},{1,5},{5,1},{2,6},{6,2},{3,7},{7,3},{8,12},{12,8},{9,1... | collective-permute-start | bytes 14155784 | tf_op jit(solution)/shard_map/ppermute | solution.py:121
  194.5 17.5 %collective-permute-start.18 = (bf16[4,48,896]{2,1,0:T(8,128)(2,1)S(1)}, bf16[4,48,896]{2,1,0:T(8,128)(2,1)S(1)}, u32[]{:S(2)}, u32[]{:S(2)}) collective-permute-start(bf16[4,48,896]{2,1,0:T(8,128)(2,1)S(1)} %get-tuple-element.171), channel_id=1, source_target_pairs={{0,16},{16,0},{1,17},{17,1},{2,18},{18,2},{3,19},{19,3},{4,20},{20... | collective-permute-start | bytes 1032200 | tf_op jit(solution)/shard_map/ppermute | solution.py:121
  196.1 16.0 %collective-permute-start.19 = (bf16[4,48,896]{2,1,0:T(8,128)(2,1)S(1)}, bf16[4,48,896]{2,1,0:T(8,128)(2,1)S(1)}, u32[]{:S(2)}, u32[]{:S(2)}) collective-permute-start(bf16[4,48,896]{2,1,0:T(8,128)(2,1)S(1)} %get-tuple-element.173), channel_id=1, source_target_pairs={{0,8},{8,0},{1,9},{9,1},{2,10},{10,2},{3,11},{11,3},{4,12},{12,4},... | collective-permute-start | bytes 1032200 | tf_op jit(solution)/shard_map/ppermute | solution.py:121
  220.1 30.6 %collective-permute-start.20 = (bf16[4,2,48,1536]{3,2,1,0:T(8,128)(2,1)}, bf16[4,2,48,1536]{3,2,1,0:T(8,128)(2,1)}, u32[]{:S(2)}, u32[]{:S(2)}) collective-permute-start(bf16[4,2,48,1536]{3,2,1,0:T(8,128)(2,1)} %get-tuple-element.186), channel_id=1, source_target_pairs={{0,8},{8,0},{1,9},{9,1},{2,10},{10,2},{3,11},{11,3},{4,12},{12,4},... | collective-permute-start | bytes 3538952 | tf_op jit(solution)/shard_map/ppermute | solution.py:121
  221.5 29.3 %collective-permute-start.21 = (bf16[4,2,48,1536]{3,2,1,0:T(8,128)(2,1)}, bf16[4,2,48,1536]{3,2,1,0:T(8,128)(2,1)}, u32[]{:S(2)}, u32[]{:S(2)}) collective-permute-start(bf16[4,2,48,1536]{3,2,1,0:T(8,128)(2,1)} %get-tuple-element.188), channel_id=1, source_target_pairs={{0,16},{16,0},{1,17},{17,1},{2,18},{18,2},{3,19},{19,3},{4,20},{20... | collective-permute-start | bytes 3538952 | tf_op jit(solution)/shard_map/ppermute | solution.py:121
  222.2 27.3 %collective-permute-start.22 = (bf16[96,896]{1,0:T(8,128)(2,1)}, bf16[96,896]{1,0:T(8,128)(2,1)}, u32[]{:S(2)}, u32[]{:S(2)}) collective-permute-start(bf16[96,896]{1,0:T(8,128)(2,1)} %get-tuple-element.190), channel_id=1, source_target_pairs={{0,3},{1,0},{2,1},{3,2},{4,7},{5,4},{6,5},{7,6},{8,11},{9,8},{10,9... | collective-permute-start | bytes 516104 | tf_op jit(solution)/shard_map/ppermute | solution.py:125
  225.5 23.9 %collective-permute-start.23 = (bf16[96,896]{1,0:T(8,128)(2,1)}, bf16[96,896]{1,0:T(8,128)(2,1)}, u32[]{:S(2)}, u32[]{:S(2)}) collective-permute-start(bf16[96,896]{1,0:T(8,128)(2,1)} %get-tuple-element.191), channel_id=1, source_target_pairs={{0,2},{1,3},{2,0},{3,1},{4,6},{5,7},{6,4},{7,5},{8,10},{9,11},{10,... | collective-permute-start | bytes 516104 | tf_op jit(solution)/shard_map/ppermute | solution.py:125
  225.5 23.9 %collective-permute-start.24 = (bf16[96,896]{1,0:T(8,128)(2,1)}, bf16[96,896]{1,0:T(8,128)(2,1)}, u32[]{:S(2)}, u32[]{:S(2)}) collective-permute-start(bf16[96,896]{1,0:T(8,128)(2,1)} %get-tuple-element.192), channel_id=1, source_target_pairs={{0,1},{1,2},{2,3},{3,0},{4,5},{5,6},{6,7},{7,4},{8,9},{9,10},{10,1... | collective-permute-start | bytes 516104 | tf_op jit(solution)/shard_map/ppermute | solution.py:125
  254.4 19.7 %collective-permute-start.27 = (bf16[4,48,1536]{2,1,0:T(8,128)(2,1)S(1)}, bf16[4,48,1536]{2,1,0:T(8,128)(2,1)S(1)}, u32[]{:S(2)}, u32[]{:S(2)}) collective-permute-start(bf16[4,48,1536]{2,1,0:T(8,128)(2,1)S(1)} %get-tuple-element.201), channel_id=1, source_target_pairs={{0,16},{16,0},{1,17},{17,1},{2,18},{18,2},{3,19},{19,3},{4,20},{20... | collective-permute-start | bytes 1769480 | tf_op jit(solution)/shard_map/ppermute | solution.py:121
  255.0 19.1 %collective-permute-start.28 = (bf16[4,48,1536]{2,1,0:T(8,128)(2,1)S(1)}, bf16[4,48,1536]{2,1,0:T(8,128)(2,1)S(1)}, u32[]{:S(2)}, u32[]{:S(2)}) collective-permute-start(bf16[4,48,1536]{2,1,0:T(8,128)(2,1)S(1)} %get-tuple-element.203), channel_id=1, source_target_pairs={{0,8},{8,0},{1,9},{9,1},{2,10},{10,2},{3,11},{11,3},{4,12},{12,4},... | collective-permute-start | bytes 1769480 | tf_op jit(solution)/shard_map/ppermute | solution.py:121
  278.8 5.7 %collective-permute-start.29 = (bf16[4,384,896]{2,1,0:T(8,128)(2,1)}, bf16[4,384,896]{2,1,0:T(8,128)(2,1)}, u32[]{:S(2)}, u32[]{:S(2)}) collective-permute-start(bf16[4,384,896]{2,1,0:T(8,128)(2,1)} %get-tuple-element.206), channel_id=1, source_target_pairs={{0,4},{4,0},{1,5},{5,1},{2,6},{6,2},{3,7},{7,3},{8,12},{12,8},{9,1... | collective-permute-start | bytes 8257544 | tf_op jit(solution)/shard_map/ppermute | solution.py:121
  278.8 87.7 %all-gather.11.cloned.1.call-start = ((), (), s32[]{:S(2)}) async-start(), calls=%async_computation.4 | async-start | bytes 4202496 | tf_op jit(solution)/shard_map/all_gather | solution.py:1137
  278.9 39.6 %collective-permute-start.25 = (bf16[528,768]{1,0:T(8,128)(2,1)S(1)}, bf16[528,768]{1,0:T(8,128)(2,1)S(1)}, u32[]{:S(2)}, u32[]{:S(2)}) collective-permute-start(bf16[528,768]{1,0:T(8,128)(2,1)S(1)} %get-tuple-element.196.refs_3_), channel_id=1, source_target_pairs={{0,1},{1,2},{2,3},{4,5},{5,6},{6,7},{8,9},{9,10},{10,11},{12,13},{... | collective-permute-start | bytes 2433032 | tf_op jit(solution)/shard_map/ppermute | solution.py:140
  283.2 38.9 %collective-permute-start.26 = (bf16[528,768]{1,0:T(8,128)(2,1)S(1)}, bf16[528,768]{1,0:T(8,128)(2,1)S(1)}, u32[]{:S(2)}, u32[]{:S(2)}) collective-permute-start(bf16[528,768]{1,0:T(8,128)(2,1)S(1)} %get-tuple-element.196.refs_3_), channel_id=1, source_target_pairs={{1,0},{2,1},{3,2},{5,4},{6,5},{7,6},{9,8},{10,9},{11,10},{13,12},{... | collective-permute-start | bytes 2433032 | tf_op jit(solution)/shard_map/ppermute | solution.py:141
  291.3 34.1 %collective-permute-start.32 = (bf16[4,2,48,896]{3,2,1,0:T(8,128)(2,1)S(1)}, bf16[4,2,48,896]{3,2,1,0:T(8,128)(2,1)S(1)}, u32[]{:S(2)}, u32[]{:S(2)}) collective-permute-start(bf16[4,2,48,896]{3,2,1,0:T(8,128)(2,1)S(1)} %get-tuple-element.213), channel_id=1, source_target_pairs={{0,8},{8,0},{1,9},{9,1},{2,10},{10,2},{3,11},{11,3},{4,12},{12,4},... | collective-permute-start | bytes 2064392 | tf_op jit(solution)/shard_map/ppermute | solution.py:121
  292.1 33.3 %collective-permute-start.33 = (bf16[4,2,48,896]{3,2,1,0:T(8,128)(2,1)S(1)}, bf16[4,2,48,896]{3,2,1,0:T(8,128)(2,1)S(1)}, u32[]{:S(2)}, u32[]{:S(2)}) collective-permute-start(bf16[4,2,48,896]{3,2,1,0:T(8,128)(2,1)S(1)} %get-tuple-element.215), channel_id=1, source_target_pairs={{0,16},{16,0},{1,17},{17,1},{2,18},{18,2},{3,19},{19,3},{4,20},{20... | collective-permute-start | bytes 2064392 | tf_op jit(solution)/shard_map/ppermute | solution.py:121
  329.1 21.3 %collective-permute-start.30 = (bf16[528,768]{1,0:T(8,128)(2,1)}, bf16[528,768]{1,0:T(8,128)(2,1)S(1)}, u32[]{:S(2)}, u32[]{:S(2)}) collective-permute-start(bf16[528,768]{1,0:T(8,128)(2,1)} %copy-done.63), channel_id=1, source_target_pairs={{0,1},{1,2},{2,3},{4,5},{5,6},{6,7},{8,9},{9,10},{10,11},{12,13},{... | collective-permute-start | bytes 2433032 | tf_op jit(solution)/shard_map/ppermute | solution.py:140
  332.6 21.9 %collective-permute-start.31 = (bf16[528,768]{1,0:T(8,128)(2,1)}, bf16[528,768]{1,0:T(8,128)(2,1)S(1)}, u32[]{:S(2)}, u32[]{:S(2)}) collective-permute-start(bf16[528,768]{1,0:T(8,128)(2,1)} %copy-done.62), channel_id=1, source_target_pairs={{1,0},{2,1},{3,2},{5,4},{6,5},{7,6},{9,8},{10,9},{11,10},{13,12},{... | collective-permute-start | bytes 2433032 | tf_op jit(solution)/shard_map/ppermute | solution.py:141
  333.9 14.8 %collective-permute-start.34 = (bf16[4,48,896]{2,1,0:T(8,128)(2,1)S(1)}, bf16[4,48,896]{2,1,0:T(8,128)(2,1)S(1)}, u32[]{:S(2)}, u32[]{:S(2)}) collective-permute-start(bf16[4,48,896]{2,1,0:T(8,128)(2,1)S(1)} %get-tuple-element.218), channel_id=1, source_target_pairs={{0,16},{16,0},{1,17},{17,1},{2,18},{18,2},{3,19},{19,3},{4,20},{20... | collective-permute-start | bytes 1032200 | tf_op jit(solution)/shard_map/ppermute | solution.py:121
  335.7 13.4 %collective-permute-start.35 = (bf16[4,48,896]{2,1,0:T(8,128)(2,1)S(1)}, bf16[4,48,896]{2,1,0:T(8,128)(2,1)S(1)}, u32[]{:S(2)}, u32[]{:S(2)}) collective-permute-start(bf16[4,48,896]{2,1,0:T(8,128)(2,1)S(1)} %get-tuple-element.220), channel_id=1, source_target_pairs={{0,8},{8,0},{1,9},{9,1},{2,10},{10,2},{3,11},{11,3},{4,12},{12,4},... | collective-permute-start | bytes 1032200 | tf_op jit(solution)/shard_map/ppermute | solution.py:121
  357.4 39.1 %collective-permute-start.36 = (bf16[528,768]{1,0:T(8,128)(2,1)}, bf16[528,768]{1,0:T(8,128)(2,1)S(1)}, u32[]{:S(2)}, u32[]{:S(2)}) collective-permute-start(bf16[528,768]{1,0:T(8,128)(2,1)} %get-tuple-element.223), channel_id=1, source_target_pairs={{0,1},{1,2},{2,3},{4,5},{5,6},{6,7},{8,9},{9,10},{10,11},{12,13},{... | collective-permute-start | bytes 2433032 | tf_op jit(solution)/shard_map/ppermute | solution.py:140
  359.6 36.9 %collective-permute-start.37 = (bf16[528,768]{1,0:T(8,128)(2,1)}, bf16[528,768]{1,0:T(8,128)(2,1)S(1)}, u32[]{:S(2)}, u32[]{:S(2)}) collective-permute-start(bf16[528,768]{1,0:T(8,128)(2,1)} %get-tuple-element.224), channel_id=1, source_target_pairs={{1,0},{2,1},{3,2},{5,4},{6,5},{7,6},{9,8},{10,9},{11,10},{13,12},{... | collective-permute-start | bytes 2433032 | tf_op jit(solution)/shard_map/ppermute | solution.py:141
  360.9 23.7 %collective-permute-start.38 = (bf16[96,896]{1,0:T(8,128)(2,1)}, bf16[96,896]{1,0:T(8,128)(2,1)S(1)}, u32[]{:S(2)}, u32[]{:S(2)}) collective-permute-start(bf16[96,896]{1,0:T(8,128)(2,1)} %get-tuple-element.228), channel_id=1, source_target_pairs={{0,3},{1,0},{2,1},{3,2},{4,7},{5,4},{6,5},{7,6},{8,11},{9,8},{10,9... | collective-permute-start | bytes 516104 | tf_op jit(solution)/shard_map/ppermute | solution.py:125
  362.7 31.9 %collective-permute-start.39 = (bf16[96,896]{1,0:T(8,128)(2,1)}, bf16[96,896]{1,0:T(8,128)(2,1)S(1)}, u32[]{:S(2)}, u32[]{:S(2)}) collective-permute-start(bf16[96,896]{1,0:T(8,128)(2,1)} %get-tuple-element.229), channel_id=1, source_target_pairs={{0,2},{1,3},{2,0},{3,1},{4,6},{5,7},{6,4},{7,5},{8,10},{9,11},{10,... | collective-permute-start | bytes 516104 | tf_op jit(solution)/shard_map/ppermute | solution.py:125
  365.1 29.5 %collective-permute-start.40 = (bf16[96,896]{1,0:T(8,128)(2,1)}, bf16[96,896]{1,0:T(8,128)(2,1)S(1)}, u32[]{:S(2)}, u32[]{:S(2)}) collective-permute-start(bf16[96,896]{1,0:T(8,128)(2,1)} %get-tuple-element.230), channel_id=1, source_target_pairs={{0,1},{1,2},{2,3},{3,0},{4,5},{5,6},{6,7},{7,4},{8,9},{9,10},{10,1... | collective-permute-start | bytes 516104 | tf_op jit(solution)/shard_map/ppermute | solution.py:125
  395.4 4.6 %collective-permute-start.41 = (bf16[48,896]{1,0:T(8,128)(2,1)S(1)}, bf16[48,896]{1,0:T(8,128)(2,1)S(1)}, u32[]{:S(2)}, u32[]{:S(2)}) collective-permute-start(bf16[48,896]{1,0:T(8,128)(2,1)S(1)} %get-tuple-element.316.refs_0_), channel_id=1, source_target_pairs={{0,8},{8,0},{1,9},{9,1},{2,10},{10,2},{3,11},{11,3},{4,12},{12,4},... | collective-permute-start | bytes 258056 | tf_op jit(solution)/shard_map/ppermute | solution.py:121
  395.4 5.2 %collective-permute-start.42 = (bf16[48,896]{1,0:T(8,128)(2,1)S(1)}, bf16[48,896]{1,0:T(8,128)(2,1)S(1)}, u32[]{:S(2)}, u32[]{:S(2)}) collective-permute-start(bf16[48,896]{1,0:T(8,128)(2,1)S(1)} %get-tuple-element.315.refs_2_), channel_id=1, source_target_pairs={{0,16},{16,0},{1,17},{17,1},{2,18},{18,2},{3,19},{19,3},{4,20},{20... | collective-permute-start | bytes 258056 | tf_op jit(solution)/shard_map/ppermute | solution.py:121
  401.2 5.4 %collective-permute-start.43 = (bf16[2,48,896]{2,1,0:T(8,128)(2,1)S(1)}, bf16[2,48,896]{2,1,0:T(8,128)(2,1)S(1)}, u32[]{:S(2)}, u32[]{:S(2)}) collective-permute-start(bf16[2,48,896]{2,1,0:T(8,128)(2,1)S(1)} %get-tuple-element.241.refs_1_), channel_id=1, source_target_pairs={{0,16},{16,0},{1,17},{17,1},{2,18},{18,2},{3,19},{19,3},{4,20},{20... | collective-permute-start | bytes 516104 | tf_op jit(solution)/shard_map/ppermute | solution.py:121
  402.3 5.4 %collective-permute-start.44 = (bf16[2,48,896]{2,1,0:T(8,128)(2,1)S(1)}, bf16[2,48,896]{2,1,0:T(8,128)(2,1)S(1)}, u32[]{:S(2)}, u32[]{:S(2)}) collective-permute-start(bf16[2,48,896]{2,1,0:T(8,128)(2,1)S(1)} %get-tuple-element.242.refs_2_), channel_id=1, source_target_pairs={{0,8},{8,0},{1,9},{9,1},{2,10},{10,2},{3,11},{11,3},{4,12},{12,4},... | collective-permute-start | bytes 516104 | tf_op jit(solution)/shard_map/ppermute | solution.py:121
  (72 other events, 661.8 us)
Sparse Core Ops, SparseCore 0:
  10.2 43.3 all-gather.6
  153.1 67.2 all-gather.8
  278.9 45.7 reduce-scatter.1
  329.2 37.1 all-gather.10

commit v5 on v4

--- a/solution.py
+++ b/solution.py
@@ -676,7 +676,7 @@
 
     @pl.when(step == 0)
     def _():
-        for copy in o_copies + w_copies + d_copies:
+        for copy in o_copies + w_copies[:2] + d_copies[:1] + w_copies[2:] + d_copies[1:]:
             copy.start()
         for copy in o_copies:
             copy.wait()

time: 425 us -> 424 us (level)
  no operation moved by 1% of the time
where the time goes in v5:
time: 424 us; the launch traced here: 419 us
  waiting for transfers between devices  157 us (37%)
  Pallas kernels  149 us (35%)
  starting transfers between devices  59.1 us (14%)
  local copies, waits for them, and re-layouts  35 us (8%)
  between operations  15.1 us (4%)
    pallas_call x30, Pallas kernels, launch(): pl.pallas_call(body, out_shape=list(out_shape) + [jax.ShapeDtypeStruct(to...  149 us
    ppermute x31, waiting for transfers between devices, swap(): return lax.ppermute(v, name, [(0, 1), (1, 0)])  66.9 us
    ppermute x12, waiting for transfers between devices, shift(): return lax.ppermute(v, 'mp', [(i, (i + k) % n) for i in range(n)])  42.7 us
    unnamed x136, local copies, waits for them, and re-layouts  25.8 us
    ppermute x3, waiting for transfers between devices, both_ways(): right = lax.ppermute(right, 'mp', [(i, i + 1) for i in range(n - 1)])  25.2 us
    ppermute x31, starting transfers between devices, swap(): return lax.ppermute(v, name, [(0, 1), (1, 0)])  23.4 us
    ppermute x12, starting transfers between devices, shift(): return lax.ppermute(v, 'mp', [(i, (i + k) % n) for i in range(n)])  21.1 us
    all_gather x1, waiting for transfers between devices, local(): z1 = lax.all_gather(piece(*own[:2]), 'mp')  13.6 us
  transfers between devices with their start and end apart: 53, of which 28 were waited for; matrix products, arithmetic and copies ran while one was open for 3% of the time, Pallas kernels for 25%

profile of v5, /device:TPU:0, one launch (start us, length us, event | category | flops | bytes accessed | tf_op | source)
XLA Modules:
  0.0 419.2 jit_solution(8404901812552302439)
XLA Ops:
  12.1 3.0 collective-permute-start.3
  15.2 2.6 collective-permute-start.4
  23.2 10.8 %attend.1 = (bf16[4,528,192]{2,1,0:T(8,128)(2,1)S(1)}, f32[8,128]{1,0:T(8,128)S(1)}) custom-call(s32[20]{0:T(128)S(1)} %stack.83.refs_0_, bf16[2048,768]{1,0:T(8,128)(2,1)S(1)} %copy-done.11, f32[4,512]{1,0:T(4,128)S(1)} %convert_element_type.4.refs_2_, f32[4,512]{1,0:T(4,128)S(1)} %get-tuple-element.318.refs_3_, f32[512,4]{1,0:T(8,128)S(1)} %bitcast.52, ...), custom_call_target="tpu_custom_call" | custom-call | flops 2617245696 | bytes 4194304 | tf_op jit(solution)/shard_map/attend/pallas_call | solution.py:84
  35.1 4.9 %collective-permute-done.4.refs_3_ = bf16[96,960]{1,0:T(8,128)(2,1)} collective-permute-done((bf16[96,960]{1,0:T(8,128)(2,1)}, bf16[96,960]{1,0:T(8,128)(2,1)}, u32[]{:S(2)}, u32[]{:S(2)}) %collective-permute-start.4) | collective-permute-done | bytes 184352 | tf_op jit(solution)/shard_map/ppermute | solution.py:125
  39.9 13.6 %all-gather.7.cloned.1.call-done = bf16[384,1536]{1,0:T(8,128)(2,1)} async-done(((bf16[96,1536]{1,0:T(8,128)(2,1)}), bf16[384,1536]{1,0:T(8,128)(2,1)}) %all-gather.7.cloned.1.call-update) | async-done | bytes 1179664 | tf_op jit(solution)/shard_map/all_gather | solution.py:1204
  54.8 2.2 split.1
  60.0 15.4 %collective-permute-done.6.refs_1_ = bf16[3,48,2496]{2,1,0:T(8,128)(2,1)S(1)} collective-permute-done((bf16[3,48,2496]{2,1,0:T(8,128)(2,1)S(1)}, bf16[3,48,2496]{2,1,0:T(8,128)(2,1)S(1)}, u32[]{:S(2)}, u32[]{:S(2)}) %collective-permute-start.6) | collective-permute-done | bytes 718880 | tf_op jit(solution)/shard_map/ppermute | solution.py:121
  83.8 2.3 collective-permute-start.2
  86.1 6.0 %collective-permute-done.refs_2_.refs_10_.refs_9_ = bf16[528,192]{1,0:T(8,128)(2,1)S(1)} collective-permute-done((bf16[528,192]{1,0:T(8,128)(2,1)S(1)}, bf16[528,192]{1,0:T(8,128)(2,1)S(1)}, u32[]{:S(2)}, u32[]{:S(2)}) %collective-permute-start) | collective-permute-done | bytes 202784 | tf_op jit(solution)/shard_map/ppermute | solution.py:125
  92.1 9.0 %collective-permute-done.1.refs_3_.refs_11_.refs_8_ = bf16[528,192]{1,0:T(8,128)(2,1)S(1)} collective-permute-done((bf16[528,192]{1,0:T(8,128)(2,1)S(1)}, bf16[528,192]{1,0:T(8,128)(2,1)S(1)}, u32[]{:S(2)}, u32[]{:S(2)}) %collective-permute-start.1) | collective-permute-done | bytes 202784 | tf_op jit(solution)/shard_map/ppermute | solution.py:125
  101.2 9.9 %collective-permute-done.8.refs_0_ = bf16[2,3,48,2496]{3,2,1,0:T(8,128)(2,1)S(1)} collective-permute-done((bf16[2,3,48,2496]{3,2,1,0:T(8,128)(2,1)S(1)}, bf16[2,3,48,2496]{3,2,1,0:T(8,128)(2,1)S(1)}, u32[]{:S(2)}, u32[]{:S(2)}) %collective-permute-start.8) | collective-permute-done | bytes 1437728 | tf_op jit(solution)/shard_map/ppermute | solution.py:121
  112.5 1.8 relay.2
  117.9 2.1 collective-permute-done.13.refs_24_.refs_18_
  120.0 23.8 %forward.1 = (f32[512,768]{1,0:T(8,128)}, bf16[512,768]{1,0:T(8,128)(2,1)}, bf16[4,512,768]{2,1,0:T(8,128)(2,1)}, bf16[4,512,768]{2,1,0:T(8,128)(2,1)}, bf16[4,5...) custom-call(s32[20]{0:T(128)} %copy-done.49, ...), custom_call_target="tpu_custom_call" | custom-call | flops 7851737088 | bytes 25165824 | tf_op jit(solution)/shard_map/forward/pallas_call | solution.py:84
  143.9 6.3 %products_send.2 = (bf16[4,384,896]{2,1,0:T(8,128)(2,1)}, f32[8,128]{1,0:T(8,128)}) custom-call(s32[20]{0:T(128)} %copy-done.49, bf16[4,512,768]{2,1,0:T(8,128)(2,1)} %get-tuple-element.152.refs_1_, bf16[512,768]{1,0:T(8,128)(2,1)} %get-tuple-element.153.refs_2_, bf16[512,768]{1,0:T(8,128)(2,1)} %get-tuple-element.148.refs_3_.refs_2_, ...), custom_call_target="tpu_custom_call" | custom-call | flops 1048576 | bytes 65536 | tf_op jit(solution)/shard_map/products_send/pallas_call | solution.py:84
  152.6 3.1 collective-permute-done.14.refs_5_
  158.0 5.4 %products_keep.2 = (bf16[4,2,48,896]{3,2,1,0:T(8,128)(2,1)S(1)}, bf16[4,2,48,896]{3,2,1,0:T(8,128)(2,1)S(1)}, bf16[4,2,48,896]{3,2,1,0:T(8,128)(2,1)S(1)}, bf16[...) custom-call(s32[20]{0:T(128)S(1)} %copy-done.50, bf16[4,512,768]{2,1,0:T(8,128)(2,1)S(1)} %copy-done.5, ...), custom_call_target="tpu_custom_call" | custom-call | flops 1048576 | bytes 65536 | tf_op jit(solution)/shard_map/products_keep/pallas_call | solution.py:84
  164.5 19.4 %ffn_back.1 = (bf16[4,512,768]{2,1,0:T(8,128)(2,1)}, bf16[4,512,768]{2,1,0:T(8,128)(2,1)}, f32[512,768]{1,0:T(8,128)}, bf16[512,768]{1,0:T(8,128)(2,1)S(1)}, bf1...) custom-call(s32[20]{0:T(128)S(1)} %copy-done.50, ...), custom_call_target="tpu_custom_call" | custom-call | flops 7851737088 | bytes 25165824 | tf_op jit(solution)/shard_map/ffn_back/pallas_call | solution.py:84
  185.7 1.9 copy-done.2
  187.6 1.9 copy-done.4
  189.5 3.9 products_send.3
  196.6 14.4 %collective-permute-done.18.refs_1_ = bf16[4,48,896]{2,1,0:T(8,128)(2,1)S(1)} collective-permute-done((bf16[4,48,896]{2,1,0:T(8,128)(2,1)S(1)}, bf16[4,48,896]{2,1,0:T(8,128)(2,1)S(1)}, u32[]{:S(2)}, u32[]{:S(2)}) %collective-permute-start.18) | collective-permute-done | bytes 344096 | tf_op jit(solution)/shard_map/ppermute | solution.py:121
  212.0 5.1 %products_keep.3 = (bf16[4,2,48,1536]{3,2,1,0:T(8,128)(2,1)}, bf16[4,2,48,1536]{3,2,1,0:T(8,128)(2,1)S(1)}, bf16[4,2,48,1536]{3,2,1,0:T(8,128)(2,1)}, bf16[4,2,48,1536]{3,2,1,0:T(8,128)(2,1)S(1)}, f32[8,128]{1,0:T(8,128)S(1)}) custom-call(s32[20]{0:T(128)S(1)} %copy-done.50, bf16[512,768]{1,0:T(8,128)(2,1)S(1)} %copy-done.14, ...), custom_call_target="tpu_custom_call" | custom-call | flops 1048576 | bytes 65536 | tf_op jit(solution)/shard_map/products_keep/pallas_call | solution.py:84
  221.2 3.3 collective-permute-start.22
  225.8 2.1 copy-done.6
  232.0 16.4 %attend_back0.1 = (bf16[4,4,512,192]{3,2,1,0:T(8,128)(2,1)S(1)}, f32[16,128]{1,0:T(8,128)S(1)}, f32[512,768]{1,0:T(8,128)S(1)}, f32[8,128]{1,0:T(8,128)S(1)}) custom-call(s32[20]{0:T(128)S(1)} %copy-done.50, bf16[2048,768]{1,0:T(8,128)(2,1)S(1)} %copy-done.12, f32[4,512]{1,0:T(4,128)S(1)} %convert_element_type.4.refs_2_, ...), custom_call_target="tpu_custom_call" | custom-call | flops 3221225472 | bytes 16777216 | tf_op jit(solution)/shard_map/attend_back0/pallas_call | solution.py:84
  249.9 3.5 second_sums.4
  255.6 17.5 %attend_back2.1 = (bf16[4,4,512,192]{3,2,1,0:T(8,128)(2,1)S(1)}, f32[16,128]{1,0:T(8,128)}, bf16[528,768]{1,0:T(8,128)(2,1)S(1)}, bf16[2,512,768]{2,1,0:T(8,128)...) custom-call(s32[20]{0:T(128)S(1)} %copy-done.50, ...), custom_call_target="tpu_custom_call", output_to_operand_aliasing={{0}: (18, {})} | custom-call | flops 3221225472 | bytes 16777216 | tf_op jit(solution)/shard_map/attend_back2/pallas_call | solution.py:84
  273.9 3.9 attn_send.1
  277.9 4.3 %collective-permute-start.25 = (bf16[528,768]{1,0:T(8,128)(2,1)S(1)}, bf16[528,768]{1,0:T(8,128)(2,1)S(1)}, u32[]{:S(2)}, u32[]{:S(2)}) collective-permute-start(bf16[528,768]{1,0:T(8,128)(2,1)S(1)} %get-tuple-element.196.refs_3_), channel_id=1, source_target_pairs={{0,1},{1,2},{2,3},{4,5},{5,6},{6,7},{8,9},{9,10},{10,11},{12,13},{... | collective-permute-start | bytes 2433032 | tf_op jit(solution)/shard_map/ppermute | solution.py:140
  283.6 2.2 copy-done.1
  285.8 4.6 %attn_keep.1 = (bf16[4,2,48,896]{3,2,1,0:T(8,128)(2,1)S(1)}, bf16[4,2,48,896]{3,2,1,0:T(8,128)(2,1)S(1)}, bf16[4,2,48,896]{3,2,1,0:T(8,128)(2,1)S(1)}, bf16[4,2,48,896]{3,2,1,0:T(8,128)(2,1)S(1)}, f32[8,128]{1,0:T(8,128)S(1)}) custom-call(s32[20]{0:T(128)S(1)} %copy-done.50, bf16[4,4,512,192]{3,2,1,0:T(8,128)(2,1)S(1)} %copy-done.1, ...), custom_call_target="tpu_custom_call" | custom-call | flops 1048576 | bytes 65536 | tf_op jit(solution)/shard_map/attn_keep/pallas_call | solution.py:84
  292.7 24.8 %collective-permute-done.25.refs_1_ = bf16[528,768]{1,0:T(8,128)(2,1)S(1)} collective-permute-done((bf16[528,768]{1,0:T(8,128)(2,1)S(1)}, bf16[528,768]{1,0:T(8,128)(2,1)S(1)}, u32[]{:S(2)}, u32[]{:S(2)}) %collective-permute-start.25) | collective-permute-done | bytes 811040 | tf_op jit(solution)/shard_map/ppermute | solution.py:140
  317.5 3.6 collective-permute-done.26.refs_2_
  321.1 2.5 collect1.1
  328.1 3.5 collective-permute-start.30
  332.9 1.9 collective-permute-start.34
  336.0 11.8 %collective-permute-done.34.refs_1_ = bf16[4,48,896]{2,1,0:T(8,128)(2,1)S(1)} collective-permute-done((bf16[4,48,896]{2,1,0:T(8,128)(2,1)S(1)}, bf16[4,48,896]{2,1,0:T(8,128)(2,1)S(1)}, u32[]{:S(2)}, u32[]{:S(2)}) %collective-permute-start.34) | collective-permute-done | bytes 344096 | tf_op jit(solution)/shard_map/ppermute | solution.py:121
  349.4 4.1 collective-permute-done.31.refs_2_
  353.5 3.0 collect2.1
  356.5 2.2 collective-permute-start.36
  361.7 2.4 collective-permute-start.39
  365.5 5.3 %open.1 = (f32[768,768]{1,0:T(8,128)}, f32[768,128]{1,0:T(8,128)}, f32[768,768]{1,0:T(8,128)}, f32[768,768]{1,0:T(8,128)}, f32[8,128]{1,0:T(8,128)}) custom-call(bf16[2,2,2,96,2432]{4,3,2,1,0:T(8,128)(2,1)} %bitcast.59, f32[8,128]{1,0:T(8,128)} %copy-done.57), custom_call_target="tpu_custom_call" | custom-call | flops 1048576 | bytes 65536 | tf_op jit(solution)/shard_map/open/pallas_call | solution.py:84
  370.8 12.9 %collective-permute-done.38.refs_1_ = bf16[96,896]{1,0:T(8,128)(2,1)S(1)} collective-permute-done((bf16[96,896]{1,0:T(8,128)(2,1)}, bf16[96,896]{1,0:T(8,128)(2,1)S(1)}, u32[]{:S(2)}, u32[]{:S(2)}) %collective-permute-start.38) | collective-permute-done | bytes 172064 | tf_op jit(solution)/shard_map/ppermute | solution.py:125
  383.7 9.9 %collective-permute-done.39.refs_2_ = bf16[96,896]{1,0:T(8,128)(2,1)S(1)} collective-permute-done((bf16[96,896]{1,0:T(8,128)(2,1)}, bf16[96,896]{1,0:T(8,128)(2,1)S(1)}, u32[]{:S(2)}, u32[]{:S(2)}) %collective-permute-start.39) | collective-permute-done | bytes 172064 | tf_op jit(solution)/shard_map/ppermute | solution.py:125
  395.5 2.4 collect3.1
  403.5 2.2 collective-permute-done.43.refs_3_
  408.1 2.2 unpack.1
  (253 shorter events, 82.8 us)
Async XLA Ops:
  7.2 46.3 %all-gather.7.cloned.1.call-start = ((), (), s32[]{:S(2)}) async-start(), calls=%async_computation.2 | async-start | bytes 1474560 | tf_op jit(solution)/shard_map/all_gather | solution.py:1204
  9.0 216.8 %all-gather.9.cloned.1.call-start = ((), (), s32[]{:S(2)}) async-start(), calls=%async_computation.3 | async-start | bytes 4055040 | tf_op jit(solution)/shard_map/all_gather | solution.py:1216
  12.1 22.9 %collective-permute-start.3 = (bf16[96,960]{1,0:T(8,128)(2,1)}, bf16[96,960]{1,0:T(8,128)(2,1)}, u32[]{:S(2)}, u32[]{:S(2)}) collective-permute-start(bf16[96,960]{1,0:T(8,128)(2,1)} %pad_maximum_fusion.1), channel_id=1, source_target_pairs={{0,1},{1,2},{2,3},{3,0},{4,5},{5,6},{6,7},{7,4},{8,9},{9,10},{10,1... | collective-permute-start | bytes 552968 | tf_op jit(solution)/shard_map/ppermute | solution.py:125
  15.2 24.8 %collective-permute-start.4 = (bf16[96,960]{1,0:T(8,128)(2,1)}, bf16[96,960]{1,0:T(8,128)(2,1)}, u32[]{:S(2)}, u32[]{:S(2)}) collective-permute-start(bf16[96,960]{1,0:T(8,128)(2,1)} %pad_maximum_fusion.1), channel_id=1, source_target_pairs={{0,2},{1,3},{2,0},{3,1},{4,6},{5,7},{6,4},{7,5},{8,10},{9,11},{10,... | collective-permute-start | bytes 552968 | tf_op jit(solution)/shard_map/ppermute | solution.py:125
  17.8 22.2 %collective-permute-start.5 = (bf16[96,960]{1,0:T(8,128)(2,1)}, bf16[96,960]{1,0:T(8,128)(2,1)}, u32[]{:S(2)}, u32[]{:S(2)}) collective-permute-start(bf16[96,960]{1,0:T(8,128)(2,1)} %pad_maximum_fusion.1), channel_id=1, source_target_pairs={{0,3},{1,0},{2,1},{3,2},{4,7},{5,4},{6,5},{7,6},{8,11},{9,8},{10,9... | collective-permute-start | bytes 552968 | tf_op jit(solution)/shard_map/ppermute | solution.py:125
  57.0 18.4 %collective-permute-start.6 = (bf16[3,48,2496]{2,1,0:T(8,128)(2,1)S(1)}, bf16[3,48,2496]{2,1,0:T(8,128)(2,1)S(1)}, u32[]{:S(2)}, u32[]{:S(2)}) collective-permute-start(bf16[3,48,2496]{2,1,0:T(8,128)(2,1)S(1)} %get-tuple-element.141.refs_0_), channel_id=1, source_target_pairs={{0,8},{8,0},{1,9},{9,1},{2,10},{10,2},{3,11},{11,3},{4,12},{12,4},... | collective-permute-start | bytes 2156552 | tf_op jit(solution)/shard_map/ppermute | solution.py:121
  58.5 18.1 %collective-permute-start.7 = (bf16[3,48,2496]{2,1,0:T(8,128)(2,1)S(1)}, bf16[3,48,2496]{2,1,0:T(8,128)(2,1)S(1)}, u32[]{:S(2)}, u32[]{:S(2)}) collective-permute-start(bf16[3,48,2496]{2,1,0:T(8,128)(2,1)S(1)} %get-tuple-element.142.refs_2_), channel_id=1, source_target_pairs={{0,16},{16,0},{1,17},{17,1},{2,18},{18,2},{3,19},{19,3},{4,20},{20... | collective-permute-start | bytes 2156552 | tf_op jit(solution)/shard_map/ppermute | solution.py:121
  78.0 33.1 %collective-permute-start.8 = (bf16[2,3,48,2496]{3,2,1,0:T(8,128)(2,1)S(1)}, bf16[2,3,48,2496]{3,2,1,0:T(8,128)(2,1)S(1)}, u32[]{:S(2)}, u32[]{:S(2)}) collective-permute-start(bf16[2,3,48,2496]{3,2,1,0:T(8,128)(2,1)S(1)} %get-tuple-element.143.refs_17_.refs_11_), channel_id=1, source_target_pairs={{0,16},{16,0},{1,17},{17,1},{2,18},{18,2},{3,19},{19,3},{4,20},{20... | collective-permute-start | bytes 4313096 | tf_op jit(solution)/shard_map/ppermute | solution.py:121
  79.5 33.0 %collective-permute-start.9 = (bf16[2,3,48,2496]{3,2,1,0:T(8,128)(2,1)}, bf16[2,3,48,2496]{3,2,1,0:T(8,128)(2,1)S(1)}, u32[]{:S(2)}, u32[]{:S(2)}) collective-permute-start(bf16[2,3,48,2496]{3,2,1,0:T(8,128)(2,1)} %get-tuple-element.144.refs_18_.refs_12_), channel_id=1, source_target_pairs={{0,8},{8,0},{1,9},{9,1},{2,10},{10,2},{3,11},{11,3},{4,12},{12,4},... | collective-permute-start | bytes 4313096 | tf_op jit(solution)/shard_map/ppermute | solution.py:121
  80.8 11.3 %collective-permute-start = (bf16[528,192]{1,0:T(8,128)(2,1)S(1)}, bf16[528,192]{1,0:T(8,128)(2,1)S(1)}, u32[]{:S(2)}, u32[]{:S(2)}) collective-permute-start(bf16[528,192]{1,0:T(8,128)(2,1)S(1)} %get-tuple-element.313), channel_id=1, source_target_pairs={{0,1},{1,2},{2,3},{3,0},{4,5},{5,6},{6,7},{7,4},{8,9},{9,10},{10,1... | collective-permute-start | bytes 608264 | tf_op jit(solution)/shard_map/ppermute | solution.py:125
  82.1 19.0 %collective-permute-start.1 = (bf16[528,192]{1,0:T(8,128)(2,1)S(1)}, bf16[528,192]{1,0:T(8,128)(2,1)S(1)}, u32[]{:S(2)}, u32[]{:S(2)}) collective-permute-start(bf16[528,192]{1,0:T(8,128)(2,1)S(1)} %get-tuple-element.312), channel_id=1, source_target_pairs={{0,2},{1,3},{2,0},{3,1},{4,6},{5,7},{6,4},{7,5},{8,10},{9,11},{10,... | collective-permute-start | bytes 608264 | tf_op jit(solution)/shard_map/ppermute | solution.py:125
  83.8 17.3 %collective-permute-start.2 = (bf16[528,192]{1,0:T(8,128)(2,1)S(1)}, bf16[528,192]{1,0:T(8,128)(2,1)S(1)}, u32[]{:S(2)}, u32[]{:S(2)}) collective-permute-start(bf16[528,192]{1,0:T(8,128)(2,1)S(1)} %get-tuple-element.311), channel_id=1, source_target_pairs={{0,3},{1,0},{2,1},{3,2},{4,7},{5,4},{6,5},{7,6},{8,11},{9,8},{10,9... | collective-permute-start | bytes 608264 | tf_op jit(solution)/shard_map/ppermute | solution.py:125
  92.1 24.8 %collective-permute-start.10 = (bf16[2,3,48,2496]{3,2,1,0:T(8,128)(2,1)S(1)}, bf16[2,3,48,2496]{3,2,1,0:T(8,128)(2,1)}, u32[]{:S(2)}, u32[]{:S(2)}) collective-permute-start(bf16[2,3,48,2496]{3,2,1,0:T(8,128)(2,1)S(1)} %get-tuple-element.143.refs_17_.refs_11_), channel_id=1, source_target_pairs={{0,4},{4,0},{1,5},{5,1},{2,6},{6,2},{3,7},{7,3},{8,12},{12,8},{9,1... | collective-permute-start | bytes 4313096 | tf_op jit(solution)/shard_map/ppermute | solution.py:121
  101.1 15.7 %collective-permute-start.11 = (bf16[2,3,48,2496]{3,2,1,0:T(8,128)(2,1)}, bf16[2,3,48,2496]{3,2,1,0:T(8,128)(2,1)}, u32[]{:S(2)}, u32[]{:S(2)}) collective-permute-start(bf16[2,3,48,2496]{3,2,1,0:T(8,128)(2,1)} %get-tuple-element.144.refs_18_.refs_12_), channel_id=1, source_target_pairs={{0,4},{4,0},{1,5},{5,1},{2,6},{6,2},{3,7},{7,3},{8,12},{12,8},{9,1... | collective-permute-start | bytes 4313096 | tf_op jit(solution)/shard_map/ppermute | solution.py:121
  114.3 5.7 %collective-permute-start.13 = (bf16[2,3,48,2496]{3,2,1,0:T(8,128)(2,1)}, bf16[2,3,48,2496]{3,2,1,0:T(8,128)(2,1)}, u32[]{:S(2)}, u32[]{:S(2)}) collective-permute-start(bf16[2,3,48,2496]{3,2,1,0:T(8,128)(2,1)} %get-tuple-element.146.refs_20_.refs_14_), channel_id=1, source_target_pairs={{0,4},{4,0},{1,5},{5,1},{2,6},{6,2},{3,7},{7,3},{8,12},{12,8},{9,1... | collective-permute-start | bytes 4313096 | tf_op jit(solution)/shard_map/ppermute | solution.py:121
  150.2 5.4 %collective-permute-start.14 = (bf16[4,384,896]{2,1,0:T(8,128)(2,1)}, bf16[4,384,896]{2,1,0:T(8,128)(2,1)}, u32[]{:S(2)}, u32[]{:S(2)}) collective-permute-start(bf16[4,384,896]{2,1,0:T(8,128)(2,1)} %get-tuple-element.155), channel_id=1, source_target_pairs={{0,4},{4,0},{1,5},{5,1},{2,6},{6,2},{3,7},{7,3},{8,12},{12,8},{9,1... | collective-permute-start | bytes 8257544 | tf_op jit(solution)/shard_map/ppermute | solution.py:121
  152.0 174.3 %reduce-scatter.2.cloned.1.call-start = ((), (), s32[]{:S(2)}) async-start(), calls=%async_computation.1 | async-start | bytes 1474560 | tf_op jit(solution)/shard_map/reduce_scatter | solution.py:1099
  163.4 21.1 %collective-permute-start.15 = (bf16[4,2,48,896]{3,2,1,0:T(8,128)(2,1)S(1)}, bf16[4,2,48,896]{3,2,1,0:T(8,128)(2,1)S(1)}, u32[]{:S(2)}, u32[]{:S(2)}) collective-permute-start(bf16[4,2,48,896]{3,2,1,0:T(8,128)(2,1)S(1)} %get-tuple-element.164), channel_id=1, source_target_pairs={{0,8},{8,0},{1,9},{9,1},{2,10},{10,2},{3,11},{11,3},{4,12},{12,4},... | collective-permute-start | bytes 2064392 | tf_op jit(solution)/shard_map/ppermute | solution.py:121
  164.0 20.4 %collective-permute-start.16 = (bf16[4,2,48,896]{3,2,1,0:T(8,128)(2,1)S(1)}, bf16[4,2,48,896]{3,2,1,0:T(8,128)(2,1)S(1)}, u32[]{:S(2)}, u32[]{:S(2)}) collective-permute-start(bf16[4,2,48,896]{3,2,1,0:T(8,128)(2,1)S(1)} %get-tuple-element.166), channel_id=1, source_target_pairs={{0,16},{16,0},{1,17},{17,1},{2,18},{18,2},{3,19},{19,3},{4,20},{20... | collective-permute-start | bytes 2064392 | tf_op jit(solution)/shard_map/ppermute | solution.py:121
  193.4 18.5 %collective-permute-start.17 = (bf16[4,384,1536]{2,1,0:T(8,128)(2,1)S(1)}, bf16[4,384,1536]{2,1,0:T(8,128)(2,1)S(1)}, u32[]{:S(2)}, u32[]{:S(2)}) collective-permute-start(bf16[4,384,1536]{2,1,0:T(8,128)(2,1)S(1)} %get-tuple-element.169), channel_id=1, source_target_pairs={{0,4},{4,0},{1,5},{5,1},{2,6},{6,2},{3,7},{7,3},{8,12},{12,8},{9,1... | collective-permute-start | bytes 14155784 | tf_op jit(solution)/shard_map/ppermute | solution.py:121
  193.5 17.5 %collective-permute-start.18 = (bf16[4,48,896]{2,1,0:T(8,128)(2,1)S(1)}, bf16[4,48,896]{2,1,0:T(8,128)(2,1)S(1)}, u32[]{:S(2)}, u32[]{:S(2)}) collective-permute-start(bf16[4,48,896]{2,1,0:T(8,128)(2,1)S(1)} %get-tuple-element.171), channel_id=1, source_target_pairs={{0,16},{16,0},{1,17},{17,1},{2,18},{18,2},{3,19},{19,3},{4,20},{20... | collective-permute-start | bytes 1032200 | tf_op jit(solution)/shard_map/ppermute | solution.py:121
  195.1 15.9 %collective-permute-start.19 = (bf16[4,48,896]{2,1,0:T(8,128)(2,1)S(1)}, bf16[4,48,896]{2,1,0:T(8,128)(2,1)S(1)}, u32[]{:S(2)}, u32[]{:S(2)}) collective-permute-start(bf16[4,48,896]{2,1,0:T(8,128)(2,1)S(1)} %get-tuple-element.173), channel_id=1, source_target_pairs={{0,8},{8,0},{1,9},{9,1},{2,10},{10,2},{3,11},{11,3},{4,12},{12,4},... | collective-permute-start | bytes 1032200 | tf_op jit(solution)/shard_map/ppermute | solution.py:121
  219.2 30.6 %collective-permute-start.20 = (bf16[4,2,48,1536]{3,2,1,0:T(8,128)(2,1)}, bf16[4,2,48,1536]{3,2,1,0:T(8,128)(2,1)}, u32[]{:S(2)}, u32[]{:S(2)}) collective-permute-start(bf16[4,2,48,1536]{3,2,1,0:T(8,128)(2,1)} %get-tuple-element.186), channel_id=1, source_target_pairs={{0,8},{8,0},{1,9},{9,1},{2,10},{10,2},{3,11},{11,3},{4,12},{12,4},... | collective-permute-start | bytes 3538952 | tf_op jit(solution)/shard_map/ppermute | solution.py:121
  220.6 29.2 %collective-permute-start.21 = (bf16[4,2,48,1536]{3,2,1,0:T(8,128)(2,1)}, bf16[4,2,48,1536]{3,2,1,0:T(8,128)(2,1)}, u32[]{:S(2)}, u32[]{:S(2)}) collective-permute-start(bf16[4,2,48,1536]{3,2,1,0:T(8,128)(2,1)} %get-tuple-element.188), channel_id=1, source_target_pairs={{0,16},{16,0},{1,17},{17,1},{2,18},{18,2},{3,19},{19,3},{4,20},{20... | collective-permute-start | bytes 3538952 | tf_op jit(solution)/shard_map/ppermute | solution.py:121
  221.2 27.3 %collective-permute-start.22 = (bf16[96,896]{1,0:T(8,128)(2,1)}, bf16[96,896]{1,0:T(8,128)(2,1)}, u32[]{:S(2)}, u32[]{:S(2)}) collective-permute-start(bf16[96,896]{1,0:T(8,128)(2,1)} %get-tuple-element.190), channel_id=1, source_target_pairs={{0,3},{1,0},{2,1},{3,2},{4,7},{5,4},{6,5},{7,6},{8,11},{9,8},{10,9... | collective-permute-start | bytes 516104 | tf_op jit(solution)/shard_map/ppermute | solution.py:125
  224.6 23.9 %collective-permute-start.23 = (bf16[96,896]{1,0:T(8,128)(2,1)}, bf16[96,896]{1,0:T(8,128)(2,1)}, u32[]{:S(2)}, u32[]{:S(2)}) collective-permute-start(bf16[96,896]{1,0:T(8,128)(2,1)} %get-tuple-element.191), channel_id=1, source_target_pairs={{0,2},{1,3},{2,0},{3,1},{4,6},{5,7},{6,4},{7,5},{8,10},{9,11},{10,... | collective-permute-start | bytes 516104 | tf_op jit(solution)/shard_map/ppermute | solution.py:125
  224.6 23.9 %collective-permute-start.24 = (bf16[96,896]{1,0:T(8,128)(2,1)}, bf16[96,896]{1,0:T(8,128)(2,1)}, u32[]{:S(2)}, u32[]{:S(2)}) collective-permute-start(bf16[96,896]{1,0:T(8,128)(2,1)} %get-tuple-element.192), channel_id=1, source_target_pairs={{0,1},{1,2},{2,3},{3,0},{4,5},{5,6},{6,7},{7,4},{8,9},{9,10},{10,1... | collective-permute-start | bytes 516104 | tf_op jit(solution)/shard_map/ppermute | solution.py:125
  253.4 19.7 %collective-permute-start.27 = (bf16[4,48,1536]{2,1,0:T(8,128)(2,1)S(1)}, bf16[4,48,1536]{2,1,0:T(8,128)(2,1)S(1)}, u32[]{:S(2)}, u32[]{:S(2)}) collective-permute-start(bf16[4,48,1536]{2,1,0:T(8,128)(2,1)S(1)} %get-tuple-element.201), channel_id=1, source_target_pairs={{0,16},{16,0},{1,17},{17,1},{2,18},{18,2},{3,19},{19,3},{4,20},{20... | collective-permute-start | bytes 1769480 | tf_op jit(solution)/shard_map/ppermute | solution.py:121
  254.1 19.0 %collective-permute-start.28 = (bf16[4,48,1536]{2,1,0:T(8,128)(2,1)S(1)}, bf16[4,48,1536]{2,1,0:T(8,128)(2,1)S(1)}, u32[]{:S(2)}, u32[]{:S(2)}) collective-permute-start(bf16[4,48,1536]{2,1,0:T(8,128)(2,1)S(1)} %get-tuple-element.203), channel_id=1, source_target_pairs={{0,8},{8,0},{1,9},{9,1},{2,10},{10,2},{3,11},{11,3},{4,12},{12,4},... | collective-permute-start | bytes 1769480 | tf_op jit(solution)/shard_map/ppermute | solution.py:121
  277.8 5.7 %collective-permute-start.29 = (bf16[4,384,896]{2,1,0:T(8,128)(2,1)}, bf16[4,384,896]{2,1,0:T(8,128)(2,1)}, u32[]{:S(2)}, u32[]{:S(2)}) collective-permute-start(bf16[4,384,896]{2,1,0:T(8,128)(2,1)} %get-tuple-element.206), channel_id=1, source_target_pairs={{0,4},{4,0},{1,5},{5,1},{2,6},{6,2},{3,7},{7,3},{8,12},{12,8},{9,1... | collective-permute-start | bytes 8257544 | tf_op jit(solution)/shard_map/ppermute | solution.py:121
  277.8 87.7 %all-gather.11.cloned.1.call-start = ((), (), s32[]{:S(2)}) async-start(), calls=%async_computation.4 | async-start | bytes 4202496 | tf_op jit(solution)/shard_map/all_gather | solution.py:1137
  277.9 39.6 %collective-permute-start.25 = (bf16[528,768]{1,0:T(8,128)(2,1)S(1)}, bf16[528,768]{1,0:T(8,128)(2,1)S(1)}, u32[]{:S(2)}, u32[]{:S(2)}) collective-permute-start(bf16[528,768]{1,0:T(8,128)(2,1)S(1)} %get-tuple-element.196.refs_3_), channel_id=1, source_target_pairs={{0,1},{1,2},{2,3},{4,5},{5,6},{6,7},{8,9},{9,10},{10,11},{12,13},{... | collective-permute-start | bytes 2433032 | tf_op jit(solution)/shard_map/ppermute | solution.py:140
  282.2 38.9 %collective-permute-start.26 = (bf16[528,768]{1,0:T(8,128)(2,1)S(1)}, bf16[528,768]{1,0:T(8,128)(2,1)S(1)}, u32[]{:S(2)}, u32[]{:S(2)}) collective-permute-start(bf16[528,768]{1,0:T(8,128)(2,1)S(1)} %get-tuple-element.196.refs_3_), channel_id=1, source_target_pairs={{1,0},{2,1},{3,2},{5,4},{6,5},{7,6},{9,8},{10,9},{11,10},{13,12},{... | collective-permute-start | bytes 2433032 | tf_op jit(solution)/shard_map/ppermute | solution.py:141
  290.4 34.1 %collective-permute-start.32 = (bf16[4,2,48,896]{3,2,1,0:T(8,128)(2,1)S(1)}, bf16[4,2,48,896]{3,2,1,0:T(8,128)(2,1)S(1)}, u32[]{:S(2)}, u32[]{:S(2)}) collective-permute-start(bf16[4,2,48,896]{3,2,1,0:T(8,128)(2,1)S(1)} %get-tuple-element.213), channel_id=1, source_target_pairs={{0,8},{8,0},{1,9},{9,1},{2,10},{10,2},{3,11},{11,3},{4,12},{12,4},... | collective-permute-start | bytes 2064392 | tf_op jit(solution)/shard_map/ppermute | solution.py:121
  291.2 33.3 %collective-permute-start.33 = (bf16[4,2,48,896]{3,2,1,0:T(8,128)(2,1)S(1)}, bf16[4,2,48,896]{3,2,1,0:T(8,128)(2,1)S(1)}, u32[]{:S(2)}, u32[]{:S(2)}) collective-permute-start(bf16[4,2,48,896]{3,2,1,0:T(8,128)(2,1)S(1)} %get-tuple-element.215), channel_id=1, source_target_pairs={{0,16},{16,0},{1,17},{17,1},{2,18},{18,2},{3,19},{19,3},{4,20},{20... | collective-permute-start | bytes 2064392 | tf_op jit(solution)/shard_map/ppermute | solution.py:121
  328.1 21.3 %collective-permute-start.30 = (bf16[528,768]{1,0:T(8,128)(2,1)}, bf16[528,768]{1,0:T(8,128)(2,1)S(1)}, u32[]{:S(2)}, u32[]{:S(2)}) collective-permute-start(bf16[528,768]{1,0:T(8,128)(2,1)} %copy-done.63), channel_id=1, source_target_pairs={{0,1},{1,2},{2,3},{4,5},{5,6},{6,7},{8,9},{9,10},{10,11},{12,13},{... | collective-permute-start | bytes 2433032 | tf_op jit(solution)/shard_map/ppermute | solution.py:140
  331.6 21.9 %collective-permute-start.31 = (bf16[528,768]{1,0:T(8,128)(2,1)}, bf16[528,768]{1,0:T(8,128)(2,1)S(1)}, u32[]{:S(2)}, u32[]{:S(2)}) collective-permute-start(bf16[528,768]{1,0:T(8,128)(2,1)} %copy-done.62), channel_id=1, source_target_pairs={{1,0},{2,1},{3,2},{5,4},{6,5},{7,6},{9,8},{10,9},{11,10},{13,12},{... | collective-permute-start | bytes 2433032 | tf_op jit(solution)/shard_map/ppermute | solution.py:141
  332.9 14.8 %collective-permute-start.34 = (bf16[4,48,896]{2,1,0:T(8,128)(2,1)S(1)}, bf16[4,48,896]{2,1,0:T(8,128)(2,1)S(1)}, u32[]{:S(2)}, u32[]{:S(2)}) collective-permute-start(bf16[4,48,896]{2,1,0:T(8,128)(2,1)S(1)} %get-tuple-element.218), channel_id=1, source_target_pairs={{0,16},{16,0},{1,17},{17,1},{2,18},{18,2},{3,19},{19,3},{4,20},{20... | collective-permute-start | bytes 1032200 | tf_op jit(solution)/shard_map/ppermute | solution.py:121
  334.8 13.4 %collective-permute-start.35 = (bf16[4,48,896]{2,1,0:T(8,128)(2,1)S(1)}, bf16[4,48,896]{2,1,0:T(8,128)(2,1)S(1)}, u32[]{:S(2)}, u32[]{:S(2)}) collective-permute-start(bf16[4,48,896]{2,1,0:T(8,128)(2,1)S(1)} %get-tuple-element.220), channel_id=1, source_target_pairs={{0,8},{8,0},{1,9},{9,1},{2,10},{10,2},{3,11},{11,3},{4,12},{12,4},... | collective-permute-start | bytes 1032200 | tf_op jit(solution)/shard_map/ppermute | solution.py:121
  356.5 39.1 %collective-permute-start.36 = (bf16[528,768]{1,0:T(8,128)(2,1)}, bf16[528,768]{1,0:T(8,128)(2,1)S(1)}, u32[]{:S(2)}, u32[]{:S(2)}) collective-permute-start(bf16[528,768]{1,0:T(8,128)(2,1)} %get-tuple-element.223), channel_id=1, source_target_pairs={{0,1},{1,2},{2,3},{4,5},{5,6},{6,7},{8,9},{9,10},{10,11},{12,13},{... | collective-permute-start | bytes 2433032 | tf_op jit(solution)/shard_map/ppermute | solution.py:140
  358.7 36.9 %collective-permute-start.37 = (bf16[528,768]{1,0:T(8,128)(2,1)}, bf16[528,768]{1,0:T(8,128)(2,1)S(1)}, u32[]{:S(2)}, u32[]{:S(2)}) collective-permute-start(bf16[528,768]{1,0:T(8,128)(2,1)} %get-tuple-element.224), channel_id=1, source_target_pairs={{1,0},{2,1},{3,2},{5,4},{6,5},{7,6},{9,8},{10,9},{11,10},{13,12},{... | collective-permute-start | bytes 2433032 | tf_op jit(solution)/shard_map/ppermute | solution.py:141
  360.0 23.7 %collective-permute-start.38 = (bf16[96,896]{1,0:T(8,128)(2,1)}, bf16[96,896]{1,0:T(8,128)(2,1)S(1)}, u32[]{:S(2)}, u32[]{:S(2)}) collective-permute-start(bf16[96,896]{1,0:T(8,128)(2,1)} %get-tuple-element.228), channel_id=1, source_target_pairs={{0,3},{1,0},{2,1},{3,2},{4,7},{5,4},{6,5},{7,6},{8,11},{9,8},{10,9... | collective-permute-start | bytes 516104 | tf_op jit(solution)/shard_map/ppermute | solution.py:125
  361.7 31.9 %collective-permute-start.39 = (bf16[96,896]{1,0:T(8,128)(2,1)}, bf16[96,896]{1,0:T(8,128)(2,1)S(1)}, u32[]{:S(2)}, u32[]{:S(2)}) collective-permute-start(bf16[96,896]{1,0:T(8,128)(2,1)} %get-tuple-element.229), channel_id=1, source_target_pairs={{0,2},{1,3},{2,0},{3,1},{4,6},{5,7},{6,4},{7,5},{8,10},{9,11},{10,... | collective-permute-start | bytes 516104 | tf_op jit(solution)/shard_map/ppermute | solution.py:125
  364.1 29.5 %collective-permute-start.40 = (bf16[96,896]{1,0:T(8,128)(2,1)}, bf16[96,896]{1,0:T(8,128)(2,1)S(1)}, u32[]{:S(2)}, u32[]{:S(2)}) collective-permute-start(bf16[96,896]{1,0:T(8,128)(2,1)} %get-tuple-element.230), channel_id=1, source_target_pairs={{0,1},{1,2},{2,3},{3,0},{4,5},{5,6},{6,7},{7,4},{8,9},{9,10},{10,1... | collective-permute-start | bytes 516104 | tf_op jit(solution)/shard_map/ppermute | solution.py:125
  394.4 4.6 %collective-permute-start.41 = (bf16[48,896]{1,0:T(8,128)(2,1)S(1)}, bf16[48,896]{1,0:T(8,128)(2,1)S(1)}, u32[]{:S(2)}, u32[]{:S(2)}) collective-permute-start(bf16[48,896]{1,0:T(8,128)(2,1)S(1)} %get-tuple-element.316.refs_0_), channel_id=1, source_target_pairs={{0,8},{8,0},{1,9},{9,1},{2,10},{10,2},{3,11},{11,3},{4,12},{12,4},... | collective-permute-start | bytes 258056 | tf_op jit(solution)/shard_map/ppermute | solution.py:121
  394.5 5.2 %collective-permute-start.42 = (bf16[48,896]{1,0:T(8,128)(2,1)S(1)}, bf16[48,896]{1,0:T(8,128)(2,1)S(1)}, u32[]{:S(2)}, u32[]{:S(2)}) collective-permute-start(bf16[48,896]{1,0:T(8,128)(2,1)S(1)} %get-tuple-element.315.refs_2_), channel_id=1, source_target_pairs={{0,16},{16,0},{1,17},{17,1},{2,18},{18,2},{3,19},{19,3},{4,20},{20... | collective-permute-start | bytes 258056 | tf_op jit(solution)/shard_map/ppermute | solution.py:121
  400.3 5.4 %collective-permute-start.43 = (bf16[2,48,896]{2,1,0:T(8,128)(2,1)S(1)}, bf16[2,48,896]{2,1,0:T(8,128)(2,1)S(1)}, u32[]{:S(2)}, u32[]{:S(2)}) collective-permute-start(bf16[2,48,896]{2,1,0:T(8,128)(2,1)S(1)} %get-tuple-element.241.refs_1_), channel_id=1, source_target_pairs={{0,16},{16,0},{1,17},{17,1},{2,18},{18,2},{3,19},{19,3},{4,20},{20... | collective-permute-start | bytes 516104 | tf_op jit(solution)/shard_map/ppermute | solution.py:121
  401.3 5.4 %collective-permute-start.44 = (bf16[2,48,896]{2,1,0:T(8,128)(2,1)S(1)}, bf16[2,48,896]{2,1,0:T(8,128)(2,1)S(1)}, u32[]{:S(2)}, u32[]{:S(2)}) collective-permute-start(bf16[2,48,896]{2,1,0:T(8,128)(2,1)S(1)} %get-tuple-element.242.refs_2_), channel_id=1, source_target_pairs={{0,8},{8,0},{1,9},{9,1},{2,10},{10,2},{3,11},{11,3},{4,12},{12,4},... | collective-permute-start | bytes 516104 | tf_op jit(solution)/shard_map/ppermute | solution.py:121
  (72 other events, 661.9 us)
Sparse Core Ops, SparseCore 0:
  10.2 43.3 all-gather.6
  152.1 67.2 all-gather.8
  278.0 45.7 reduce-scatter.1
  328.3 37.2 all-gather.10
